TPU v7x, 32 devices: a whole 2x2x4 slice. The times are simulated.
32 devices in a mesh: rows: 16 (over z, x, core), field: 2 (over y).
Axes of the slice: x: 2, y: 2, z: 4, core: 2. Of those that a mesh axis runs over, the one named last changes fastest.
Arguments:
- inputs: bfloat16 [4, 8192, 512], P(None, 'rows', 'field'), may hold values from -6 to 6
- valid_mask: int32 [4, 8192], P(None, 'rows'), may hold values from 0 to 1, as said below
- labels: int32 [4, 8192], P(None, 'rows'), may hold values from 0 to 1
- domains: int32 [4, 8192], P(None, 'rows'), may hold values from 0 to 1
- expert_in: float32 [512, 2048], P(('field', 'rows')), may hold values from -0.25 to 0.25
- gate_in: float32 [512, 16], P(('field', 'rows')), may hold values from -0.1875 to 0.1875
- expert_out: float32 [8, 256, 256], P(None, ('rows', 'field')), may hold values from -0.375 to 0.375
- tower_in: float32 [2, 256, 128], P(None, ('rows', 'field')), may hold values from -0.375 to 0.375
- tower_out: float32 [2, 128], replicated, may hold values from -0.5 to 0.5
- velocity_expert_in: float32 [512, 2048], P(('field', 'rows')), may hold values from -5.340576e-05 to 5.340576e-05
- velocity_gate_in: float32 [512, 16], P(('field', 'rows')), may hold values from -0.00061035156 to 0.00061035156
- velocity_expert_out: float32 [8, 256, 256], P(None, ('rows', 'field')), may hold values from -5.340576e-05 to 5.340576e-05
- velocity_tower_in: float32 [2, 256, 128], P(None, ('rows', 'field')), may hold values from -0.00030517578 to 0.00030517578
- velocity_tower_out: float32 [2, 128], replicated, may hold values from -0.0068359375 to 0.0068359375
- average_expert_in: float32 [512, 2048], P(('field', 'rows')), may hold values from -0.25 to 0.25
- average_gate_in: float32 [512, 16], P(('field', 'rows')), may hold values from -0.1875 to 0.1875
- average_expert_out: float32 [8, 256, 256], P(None, ('rows', 'field')), may hold values from -0.375 to 0.375
- average_tower_in: float32 [2, 256, 128], P(None, ('rows', 'field')), may hold values from -0.375 to 0.375
- average_tower_out: float32 [2, 128], replicated, may hold values from -0.5 to 0.5
Outputs:
- loss_mean: float32 [], replicated
- input_grad: float32 [4, 8192, 512], P(None, 'rows', 'field')
- expert_in_new: float32 [512, 2048], P(('field', 'rows'))
- velocity_expert_in_new: float32 [512, 2048], P(('field', 'rows'))
- average_expert_in_new: float32 [512, 2048], P(('field', 'rows'))
- gate_in_new: float32 [512, 16], P(('field', 'rows'))
- velocity_gate_in_new: float32 [512, 16], P(('field', 'rows'))
- average_gate_in_new: float32 [512, 16], P(('field', 'rows'))
- expert_out_new: float32 [8, 256, 256], P(None, ('rows', 'field'))
- velocity_expert_out_new: float32 [8, 256, 256], P(None, ('rows', 'field'))
- average_expert_out_new: float32 [8, 256, 256], P(None, ('rows', 'field'))
- tower_in_new: float32 [2, 256, 128], P(None, ('rows', 'field'))
- velocity_tower_in_new: float32 [2, 256, 128], P(None, ('rows', 'field'))
- average_tower_in_new: float32 [2, 256, 128], P(None, ('rows', 'field'))
- tower_out_new: float32 [2, 128], replicated
- velocity_tower_out_new: float32 [2, 128], replicated
- average_tower_out_new: float32 [2, 128], replicated
Inputs may be any that keep to these rules, and one draw needn't show every extreme that they name: `valid_mask`: in the first micro-batch the first row of each block of 512 rows is real.
All inputs are finite; a program needn't handle non-finite values.
Results may differ from a plain program's by a relative error of at most 0.014.
Values may be sent and summed in bfloat16 or wider, within the bound.
No kernel may reach another device: no remote copies, remote signals or barrier semaphores. Data moves between devices by JAX's collectives and lax.ppermute only.
A program may use at most 128 MiB of HBM per device.

v0:
```python
import math

import jax
import jax.numpy as jnp
from jax import lax
from jax.sharding import PartitionSpec as P

highest = lax.Precision.HIGHEST
momentum_mu = 0.5
average_keep = 0.5
rate_bases = (17.0, 1.0, 24.0, 4.0, 0.25)


def silu_slope(values):
    sigma = jax.nn.sigmoid(values)
    return sigma * (1.0 + values * (1.0 - sigma))


def local_pass(
    pre_rows,
    own_valid,
    own_label,
    own_domain,
    second_w,
    tower_w,
    head_w,
    valid_total,
    experts,
    tasks,
):
    block_rows = pre_rows.shape[0]
    expert_cols = experts * second_w.shape[1]
    expert_pre = pre_rows[:, :expert_cols].reshape(block_rows, experts, second_w.shape[1])
    gate_pre = pre_rows[:, expert_cols:].reshape(block_rows, tasks, experts)
    gate_prob = jax.nn.softmax(gate_pre, axis=-1)
    expert_act = jax.nn.silu(expert_pre).astype(jnp.bfloat16)
    expert_res = jnp.einsum(
        "rkh,kho->rko", expert_act, second_w, preferred_element_type=jnp.float32
    )
    mixed_rows = jnp.einsum("rtk,rko->rto", gate_prob, expert_res, precision=highest).astype(
        jnp.bfloat16
    )
    tower_pre = jnp.einsum("rto,tom->rtm", mixed_rows, tower_w, preferred_element_type=jnp.float32)
    tower_act = jax.nn.silu(tower_pre).astype(jnp.bfloat16)
    logit_rows = jnp.einsum("rtm,tm->rt", tower_act, head_w, preferred_element_type=jnp.float32)
    row_pick = (own_domain[:, None] == jnp.arange(tasks, dtype=jnp.int32)[None, :]).astype(
        jnp.float32
    )
    chosen = jnp.sum(row_pick * logit_rows, axis=1)
    loss_part = jnp.sum(own_valid * (jax.nn.softplus(chosen) - own_label * chosen))
    dlogit = (
        row_pick * (own_valid * (jax.nn.sigmoid(chosen) - own_label) / valid_total)[:, None]
    ).astype(jnp.bfloat16)
    grad_head = jnp.einsum("rt,rtm->tm", dlogit, tower_act, preferred_element_type=jnp.float32)
    dtower_act = dlogit.astype(jnp.float32)[:, :, None] * head_w.astype(jnp.float32)[None, :, :]
    dtower_pre = (dtower_act * silu_slope(tower_pre)).astype(jnp.bfloat16)
    grad_tower = jnp.einsum(
        "rto,rtm->tom", mixed_rows, dtower_pre, preferred_element_type=jnp.float32
    )
    dmixed = jnp.einsum("rtm,tom->rto", dtower_pre, tower_w, preferred_element_type=jnp.float32)
    dgate = jnp.einsum("rto,rko->rtk", dmixed, expert_res, precision=highest)
    dexpert = jnp.einsum("rtk,rto->rko", gate_prob, dmixed, precision=highest).astype(jnp.bfloat16)
    grad_second = jnp.einsum(
        "rkh,rko->kho", expert_act, dexpert, preferred_element_type=jnp.float32
    )
    dexpert_act = jnp.einsum("rko,kho->rkh", dexpert, second_w, preferred_element_type=jnp.float32)
    dexpert_pre = dexpert_act * silu_slope(expert_pre)
    dgate_pre = gate_prob * (dgate - jnp.sum(gate_prob * dgate, axis=-1, keepdims=True))
    dpre_rows = jnp.concatenate(
        [dexpert_pre.reshape(block_rows, -1), dgate_pre.reshape(block_rows, -1)], axis=1
    )
    return (dpre_rows.astype(jnp.bfloat16), loss_part, grad_second, grad_tower, grad_head)


def renew(weight, velocity, average, gradient, rate):
    velocity_new = momentum_mu * velocity + gradient
    weight_new = weight - rate * (gradient + momentum_mu * velocity_new)
    average_new = average_keep * average + (1.0 - average_keep) * weight_new
    return (weight_new, velocity_new, average_new)


def on_device(
    inputs,
    valid_mask,
    labels,
    domains,
    expert_in,
    gate_in,
    expert_out,
    tower_in,
    tower_out,
    velocity_expert_in,
    velocity_gate_in,
    velocity_expert_out,
    velocity_tower_in,
    velocity_tower_out,
    average_expert_in,
    average_gate_in,
    average_expert_out,
    average_tower_in,
    average_tower_out,
):
    micro_count, rows_dev, field_width = inputs.shape
    field_count = lax.axis_size("field")
    half_rows = rows_dev // field_count
    half_start = lax.axis_index("field") * half_rows
    experts = expert_out.shape[0]
    tasks = tower_out.shape[0]
    expert_cols = expert_in.shape[1]
    total_rows = micro_count * rows_dev * lax.axis_size("rows")
    valid_total = lax.psum(jnp.sum(valid_mask).astype(jnp.float32), "rows")
    first_w, first_g = (
        lax.all_gather(expert_in.astype(jnp.bfloat16), "rows", axis=0, tiled=True),
        lax.all_gather(gate_in.astype(jnp.bfloat16), "rows", axis=0, tiled=True),
    )
    first_both = jnp.concatenate([first_w, first_g], axis=1)
    second_w, tower_w = (
        lax.all_gather(expert_out.astype(jnp.bfloat16), ("rows", "field"), axis=1, tiled=True),
        lax.all_gather(tower_in.astype(jnp.bfloat16), ("rows", "field"), axis=1, tiled=True),
    )
    head_w = tower_out.astype(jnp.bfloat16)
    width_all = first_both.shape[1]
    grad_first = jnp.zeros((field_width, width_all), jnp.float32)
    grad_second = jnp.zeros((experts, second_w.shape[1], second_w.shape[2]), jnp.float32)
    grad_tower = jnp.zeros(tower_w.shape, jnp.float32)
    grad_head = jnp.zeros(head_w.shape, jnp.float32)
    loss_total = jnp.float32(0.0)
    input_parts = []
    for micro_step in range(micro_count):
        rows_x = inputs[micro_step]
        pre_rows = lax.psum_scatter(
            jnp.dot(rows_x, first_both, preferred_element_type=jnp.float32),
            "field",
            scatter_dimension=0,
            tiled=True,
        )
        own_valid = lax.dynamic_slice_in_dim(
            valid_mask[micro_step], half_start, half_rows, 0
        ).astype(jnp.float32)
        own_label = lax.dynamic_slice_in_dim(labels[micro_step], half_start, half_rows, 0).astype(
            jnp.float32
        )
        own_domain = lax.dynamic_slice_in_dim(domains[micro_step], half_start, half_rows, 0)
        dpre_rows, loss_part, second_part, tower_part, head_part = local_pass(
            pre_rows,
            own_valid,
            own_label,
            own_domain,
            second_w,
            tower_w,
            head_w,
            valid_total,
            experts,
            tasks,
        )
        loss_total = loss_total + loss_part
        grad_second = grad_second + second_part
        grad_tower = grad_tower + tower_part
        grad_head = grad_head + head_part
        piece = lax.all_gather(dpre_rows, "field", axis=0, tiled=True)
        grad_weight = grad_first
        grad_weight = grad_weight + lax.dot_general(
            rows_x, piece, (((0,), (0,)), ((), ())), preferred_element_type=jnp.float32
        )
        input_piece = lax.dot_general(
            piece, first_both, (((1,), (1,)), ((), ())), preferred_element_type=jnp.float32
        )
        grad_input = input_piece
        grad_input, grad_first = (grad_input, grad_weight)
        input_parts.append(grad_input)
    (first_whole_sum,) = lax.psum((grad_first,), "rows")
    second_sum, tower_sum, head_sum, loss_sum = lax.psum(
        (grad_second, grad_tower, grad_head, loss_total), ("rows", "field")
    )
    row_share = expert_in.shape[0]
    first_share = lax.dynamic_slice_in_dim(
        first_whole_sum, lax.axis_index("rows") * row_share, row_share, 0
    )
    joined_index = lax.axis_index(("rows", "field"))
    second_share = lax.dynamic_slice_in_dim(
        second_sum, joined_index * expert_out.shape[1], expert_out.shape[1], 1
    )
    tower_share = lax.dynamic_slice_in_dim(
        tower_sum, joined_index * tower_in.shape[1], tower_in.shape[1], 1
    )
    gradients = (
        first_share[:, :expert_cols],
        first_share[:, expert_cols:],
        second_share,
        tower_share,
        head_sum,
    )
    weights = (expert_in, gate_in, expert_out, tower_in, tower_out)
    velocities = (
        velocity_expert_in,
        velocity_gate_in,
        velocity_expert_out,
        velocity_tower_in,
        velocity_tower_out,
    )
    averages = (
        average_expert_in,
        average_gate_in,
        average_expert_out,
        average_tower_in,
        average_tower_out,
    )
    scale_root = math.sqrt(total_rows)
    results = [loss_sum / valid_total, jnp.stack(input_parts, axis=0)]
    for index_w in range(5):
        results.extend(
            renew(
                weights[index_w],
                velocities[index_w],
                averages[index_w],
                gradients[index_w],
                rate_bases[index_w] * scale_root,
            )
        )
    return tuple(results)


def solution(mesh):
    return jax.shard_map(
        on_device,
        mesh=mesh,
        in_specs=(
            P(None, "rows", "field"),
            P(None, "rows"),
            P(None, "rows"),
            P(None, "rows"),
            P(("field", "rows"), None),
            P(("field", "rows"), None),
            P(None, ("rows", "field"), None),
            P(None, ("rows", "field"), None),
            P(),
            P(("field", "rows"), None),
            P(("field", "rows"), None),
            P(None, ("rows", "field"), None),
            P(None, ("rows", "field"), None),
            P(),
            P(("field", "rows"), None),
            P(("field", "rows"), None),
            P(None, ("rows", "field"), None),
            P(None, ("rows", "field"), None),
            P(),
        ),
        out_specs=(
            P(),
            P(None, "rows", "field"),
            P(("field", "rows"), None),
            P(("field", "rows"), None),
            P(("field", "rows"), None),
            P(("field", "rows"), None),
            P(("field", "rows"), None),
            P(("field", "rows"), None),
            P(None, ("rows", "field"), None),
            P(None, ("rows", "field"), None),
            P(None, ("rows", "field"), None),
            P(None, ("rows", "field"), None),
            P(None, ("rows", "field"), None),
            P(None, ("rows", "field"), None),
            P(),
            P(),
            P(),
        ),
        check_vma=False,
    )
```

profile of v0, /device:TPU:0, one launch (start us, length us, event | category | flops | bytes accessed | tf_op | source)
XLA Modules:
  0.0 721.4 jit_solution(17189694821331650245)
XLA Ops:
  10.5 23.2 %all_gather.25 = bf16[256,16]{1,0:T(8,128)(2,1)S(1)} all-gather(bf16[16,16]{1,0:T(8,128)(2,1)S(1)} %convert_element_type.231), channel_id=1, replica_groups=mesh['rows'=16,'field'=2] {'rows'}, dimensions={0}, use_global_device_ids=true | all-gather | bytes 8704 | tf_op jit(solution)/shard_map/all_gather | solution.py:114
  33.7 18.6 %all-gather.7.cloned.1.call-done = bf16[256,2048]{1,0:T(8,128)(2,1)} async-done(((bf16[16,2048]{1,0:T(8,128)(2,1)}), bf16[256,2048]{1,0:T(8,128)(2,1)}) %all-gather.7.cloned.1.call-update) | async-done | bytes 1048592 | tf_op jit(solution)/shard_map/all_gather | solution.py:113
  53.6 2.7 convolution_bitcast_fusion
  57.9 2.8 convolution_bitcast_fusion.1
  60.8 2.8 convolution_bitcast_fusion.2
  65.5 32.1 %psum.43 = f32[]{:T(128)} all-reduce(f32[]{:T(128)S(6)} %convert_element_type.261), channel_id=1, replica_groups=mesh['rows'=16,'field'=2] {'rows'}, use_global_device_ids=true, to_apply=%region_22.23 | all-reduce | flops 1 | bytes 8 | tf_op jit(solution)/shard_map/psum | solution.py:111
  98.3 2.8 convolution_bitcast_fusion.3
  101.1 71.4 %all_gather.27 = bf16[2,256,128]{2,1,0:T(8,128)(2,1)} all-gather(bf16[2,8,128]{2,1,0:T(8,128)(2,1)S(1)} %convert_element_type.235), channel_id=1, replica_groups=mesh['rows'=16,'field'=2] {'rows','field'}, dimensions={1}, use_global_device_ids=true | all-gather | bytes 135168 | tf_op jit(solution)/shard_map/all_gather | solution.py:119
  181.1 3.0 slice.111
  185.8 2.7 convolution_bitcast_fusion.4
  188.5 3.7 fusion.34
  192.2 1.8 copy.262
  197.1 1.8 slice.109
  202.7 3.7 fusion.31
  206.4 1.8 copy.261
  208.3 19.9 %reduce-scatter.7.cloned.1.call-done = f32[256,2064]{0,1:T(8,128)} async-done(((f32[512,2064]{0,1:T(8,128)}), f32[256,2064]{0,1:T(8,128)}) %reduce-scatter.7.cloned.1.call-update) | async-done | bytes 2113552 | tf_op jit(solution)/shard_map/reduce_scatter | solution.py:131
  231.3 1.8 slice.107
  237.0 3.7 fusion.28
  240.7 1.9 copy.260
  242.6 2.0 multiply_convert_fusion.8
  246.0 2.0 multiply_convert_fusion.9
  253.0 32.1 %reduce-scatter.5.cloned.1.call-done = f32[256,2064]{0,1:T(8,128)} async-done(((f32[512,2064]{0,1:T(8,128)}), f32[256,2064]{0,1:T(8,128)}) %reduce-scatter.5.cloned.1.call-update) | async-done | bytes 2113552 | tf_op jit(solution)/shard_map/reduce_scatter | solution.py:131
  291.5 1.8 slice.105
  296.0 3.7 fusion.25
  299.7 1.8 copy.259
  301.6 2.0 multiply_convert_fusion.11
  319.2 40.0 %all-reduce = (f32[]{:T(128)}, f32[2,128]{1,0:T(2,128)S(1)}) all-reduce(f32[]{:T(128)S(6)} %add.258, f32[2,128]{1,0:T(2,128)} %add_add_fusion.1), channel_id=1, replica_groups=mesh['rows'=16,'field'=2] {'rows','field'}, use_global_device_ids=true, to_apply=%region_20.21 | all-reduce | flops 257 | bytes 2056 | tf_op jit(solution)/shard_map/psum | solution.py:172
  363.4 4.2 fusion.21
  367.6 2.5 convolution_convert_fusion.3
  373.8 2.5 convolution_convert_fusion.2
  376.4 2.7 convolution_convert_fusion.1
  379.1 2.5 convolution_convert_fusion
  386.9 2.2 add_add_fusion
  389.1 2.3 fusion.48
  392.4 3.2 fusion.8
  397.0 5.2 fusion.17
  404.2 3.6 fusion.7
  409.0 5.3 fusion.13
  416.2 3.2 fusion.6
  420.9 4.5 fusion.9
  425.9 3.2 fusion.5
  431.6 164.5 %all-reduce.7.cloned.1.call-done = (f32[8,256,256]{2,1,0:T(8,128)}, f32[2,256,128]{2,1,0:T(8,128)}) async-done(((f32[8,256,256]{2,1,0:T(8,128)}, f32[2,256,128]{2,1,0:T(8,128)}), (f32[8,256,256]{2,1,0:T(8,128)}, f32[2,256,128]{2,1,0:T(8,128)})) %all-reduce.7.cloned.1.call-update) | async-done | bytes 2359312 | tf_op jit(solution)/shard_map/psum | solution.py:172
  598.9 2.4 fusion.74
  601.4 3.8 convolution_add_fusion.2
  605.2 3.2 convolution_add_fusion.1
  608.4 3.8 fusion.4
  621.3 88.2 %all-reduce.5.cloned.1.call-done = f32[256,2064]{1,0:T(8,128)} async-done(((f32[256,2064]{1,0:T(8,128)}), f32[256,2064]{1,0:T(8,128)}) %all-reduce.5.cloned.1.call-update) | async-done | bytes 2113552 | tf_op jit(solution)/shard_map/psum | solution.py:171
  709.4 1.7 add_multiply_fusion
  (294 shorter events, 96.0 us)
Async XLA Ops:
  8.0 45.6 %copy-start.4 = (bf16[4,512,256]{2,1,0:T(8,128)(2,1)S(1)}, bf16[4,512,256]{2,1,0:T(8,128)(2,1)}, u32[]{:S(2)}) copy-start(bf16[4,512,256]{2,1,0:T(8,128)(2,1)} %param.19) | copy-start | bytes 3145732
  8.0 44.2 %all-gather.7.cloned.1.call-start = ((), (), s32[]{:S(2)}) async-start(), calls=%async_computation.4 | async-start | bytes 1114112 | tf_op jit(solution)/shard_map/all_gather | solution.py:113
  9.7 169.6 %reduce-scatter.11.cloned.1.call-start = ((), (), s32[]{:S(2)}) async-start(), calls=%async_computation.9 | async-start | bytes 6340608 | tf_op jit(solution)/shard_map/reduce_scatter | solution.py:131
  56.3 129.4 %all-gather.9.cloned.1.call-start = ((), (), s32[]{:S(2)}) async-start(), calls=%async_computation.6 | async-start | bytes 1081344 | tf_op jit(solution)/shard_map/all_gather | solution.py:118
  57.8 136.2 %reduce-scatter.9.cloned.1.call-start = ((), (), s32[]{:S(2)}) async-start(), calls=%async_computation.8 | async-start | bytes 6340608 | tf_op jit(solution)/shard_map/reduce_scatter | solution.py:131
  60.7 167.5 %reduce-scatter.7.cloned.1.call-start = ((), (), s32[]{:S(2)}) async-start(), calls=%async_computation.7 | async-start | bytes 6340608 | tf_op jit(solution)/shard_map/reduce_scatter | solution.py:131
  63.6 34.1 %copy-start.52 = (f32[2,8,128]{2,1,0:T(8,128)S(1)}, f32[2,8,128]{2,1,0:T(8,128)}, u32[]{:S(2)}) copy-start(f32[2,8,128]{2,1,0:T(8,128)} %param.26) | copy-start | bytes 24580
  63.6 34.1 %copy-start.68 = (s32[4,512]{1,0:T(4,128)S(1)}, s32[4,512]{1,0:T(4,128)}, u32[]{:S(2)}) copy-start(s32[4,512]{1,0:T(4,128)} %param.21) | copy-start | bytes 24580
  63.6 221.5 %reduce-scatter.5.cloned.1.call-start = ((), (), s32[]{:S(2)}) async-start(), calls=%async_computation.5 | async-start | bytes 6340608 | tf_op jit(solution)/shard_map/reduce_scatter | solution.py:131
  101.0 73.2 %copy-start.69 = (s32[4,512]{1,0:T(4,128)S(1)}, s32[4,512]{1,0:T(4,128)}, u32[]{:S(2)}) copy-start(s32[4,512]{1,0:T(4,128)} %param.22) | copy-start | bytes 24580
  101.0 77.8 %copy-start.73 = (f32[2,128]{1,0:T(2,128)S(1)}, f32[2,128]{1,0:T(2,128)}, u32[]{:S(2)}) copy-start(f32[2,128]{1,0:T(2,128)} %param.27) | copy-start | bytes 3076
  101.1 495.0 %all-reduce.7.cloned.1.call-start = ((), (), s32[]{:S(2)}) async-start(), calls=%async_computation.15 | async-start | bytes 4718592 | tf_op jit(solution)/shard_map/psum | solution.py:172
  237.0 7.6 %copy-start.50 = (bf16[2,128,1]{1,0,2:T(2,128)(2,1)S(1)}, bf16[2,128,1]{1,0,2:T(2,128)(2,1)}, u32[]{:S(2)}) copy-start(bf16[2,128,1]{1,0,2:T(2,128)(2,1)} %convert_bitcast_fusion) | copy-start | bytes 1540
  240.7 8.1 %copy-start.59 = (f32[1,256]{1,0:T(1,128)S(1)}, f32[1,256]{1,0:T(1,128)}, u32[]{:S(2)}) copy-start(f32[1,256]{1,0:T(1,128)} %fusion.120) | copy-start | bytes 3076
  240.7 8.1 %copy-start.60 = (f32[1,256]{1,0:T(1,128)S(1)}, f32[1,256]{1,0:T(1,128)}, u32[]{:S(2)}) copy-start(f32[1,256]{1,0:T(1,128)} %fusion.118) | copy-start | bytes 3076
  240.7 8.1 %copy-start.61 = (f32[1,256]{1,0:T(1,128)S(1)}, f32[1,256]{1,0:T(1,128)}, u32[]{:S(2)}) copy-start(f32[1,256]{1,0:T(1,128)} %fusion.119) | copy-start | bytes 3076
  242.6 6.2 copy-start.63
  242.6 6.2 copy-start.62
  242.6 8.0 %copy-start.41 = (bf16[256,2,256]{0,2,1:T(8,128)(2,1)S(1)}, bf16[256,2,256]{0,2,1:T(8,128)(2,1)}, u32[]{:S(2)}) copy-start(bf16[256,2,256]{0,2,1:T(8,128)(2,1)} %copy.260) | copy-start | bytes 786436
  242.6 8.0 %copy-start.46 = (bf16[2,256,128]{2,1,0:T(8,128)(2,1)S(1)}, bf16[2,256,128]{2,1,0:T(8,128)(2,1)}, u32[]{:S(2)}) copy-start(bf16[2,256,128]{2,1,0:T(8,128)(2,1)} %all_gather.27) | copy-start | bytes 393220
  296.0 7.5 %copy-start.51 = (bf16[2,128,1]{1,0,2:T(2,128)(2,1)S(1)}, bf16[2,128,1]{1,0,2:T(2,128)(2,1)}, u32[]{:S(2)}) copy-start(bf16[2,128,1]{1,0,2:T(2,128)(2,1)} %convert_bitcast_fusion) | copy-start | bytes 1540
  296.0 9.1 %copy-start.56 = (f32[1,256]{1,0:T(1,128)S(1)}, f32[1,256]{1,0:T(1,128)}, u32[]{:S(2)}) copy-start(f32[1,256]{1,0:T(1,128)} %fusion.116) | copy-start | bytes 3076
  296.0 9.1 %copy-start.57 = (f32[1,256]{1,0:T(1,128)S(1)}, f32[1,256]{1,0:T(1,128)}, u32[]{:S(2)}) copy-start(f32[1,256]{1,0:T(1,128)} %fusion.114) | copy-start | bytes 3076
  296.0 9.1 %copy-start.58 = (f32[1,256]{1,0:T(1,128)S(1)}, f32[1,256]{1,0:T(1,128)}, u32[]{:S(2)}) copy-start(f32[1,256]{1,0:T(1,128)} %fusion.115) | copy-start | bytes 3076
  362.0 5.5 copy-start.12
  363.4 6.8 copy-start.47
  363.4 6.8 copy-start.72
  363.4 6.8 copy-start.79
  370.1 14.3 %copy-start.33 = (bf16[256,8,256]{2,1,0:T(8,128)(2,1)}, bf16[256,8,256]{2,1,0:T(8,128)(2,1)S(1)}, u32[]{:S(2)}) copy-start(bf16[256,8,256]{2,1,0:T(8,128)(2,1)S(1)} %convolution_convert_fusion.3) | copy-start | bytes 3145732
  372.8 6.4 copy-start.26
  376.4 6.1 copy-start.34
  376.4 5.3 copy-start.21
  389.1 209.9 %all-gather.11.cloned.1.call-start = ((), (), s32[]{:S(2)}) async-start(), calls=%async_computation.10 | async-start | bytes 3170304 | tf_op jit(solution)/shard_map/all_gather | solution.py:160
  396.7 204.7 %all-gather.13.cloned.1.call-start = ((), (), s32[]{:S(2)}) async-start(), calls=%async_computation.11 | async-start | bytes 3170304 | tf_op jit(solution)/shard_map/all_gather | solution.py:160
  408.9 196.3 %all-gather.15.cloned.1.call-start = ((), (), s32[]{:S(2)}) async-start(), calls=%async_computation.12 | async-start | bytes 3170304 | tf_op jit(solution)/shard_map/all_gather | solution.py:160
  420.6 187.8 %all-gather.17.cloned.1.call-start = ((), (), s32[]{:S(2)}) async-start(), calls=%async_computation.13 | async-start | bytes 3170304 | tf_op jit(solution)/shard_map/all_gather | solution.py:160
  429.1 167.0 %copy-start.53 = (f32[2,8,128]{2,1,0:T(8,128)S(1)}, f32[2,8,128]{2,1,0:T(8,128)}, u32[]{:S(2)}) copy-start(f32[2,8,128]{2,1,0:T(8,128)} %param.26) | copy-start | bytes 24580
  429.1 166.9 %copy-start.64 = (f32[2,8,128]{2,1,0:T(8,128)S(1)}, f32[2,8,128]{2,1,0:T(8,128)}, u32[]{:S(2)}) copy-start(f32[2,8,128]{2,1,0:T(8,128)} %param.36) | copy-start | bytes 24580
  429.1 166.9 %copy-start.65 = (f32[2,8,128]{2,1,0:T(8,128)S(1)}, f32[2,8,128]{2,1,0:T(8,128)}, u32[]{:S(2)}) copy-start(f32[2,8,128]{2,1,0:T(8,128)} %param.31) | copy-start | bytes 24580
  429.2 168.2 %copy-start.48 = (f32[8,8,256]{2,1,0:T(8,128)S(1)}, f32[8,8,256]{2,1,0:T(8,128)}, u32[]{:S(2)}) copy-start(f32[8,8,256]{2,1,0:T(8,128)} %param.35) | copy-start | bytes 196612
  429.2 168.2 %copy-start.49 = (f32[8,8,256]{2,1,0:T(8,128)S(1)}, f32[8,8,256]{2,1,0:T(8,128)}, u32[]{:S(2)}) copy-start(f32[8,8,256]{2,1,0:T(8,128)} %param.30) | copy-start | bytes 196612
  430.3 279.2 %all-reduce.5.cloned.1.call-start = ((), (), s32[]{:S(2)}) async-start(), calls=%async_computation.14 | async-start | bytes 4456448 | tf_op jit(solution)/shard_map/psum | solution.py:171
  619.7 89.7 %copy-start.35 = (f32[16,2048]{1,0:T(8,128)S(1)}, f32[16,2048]{1,0:T(8,128)}, u32[]{:S(2)}) copy-start(f32[16,2048]{1,0:T(8,128)} %param.23) | copy-start | bytes 393220
  619.7 89.7 %copy-start.44 = (f32[16,2048]{1,0:T(8,128)S(1)}, f32[16,2048]{1,0:T(8,128)}, u32[]{:S(2)}) copy-start(f32[16,2048]{1,0:T(8,128)} %param.33) | copy-start | bytes 393220
  619.7 89.7 %copy-start.45 = (f32[16,2048]{1,0:T(8,128)S(1)}, f32[16,2048]{1,0:T(8,128)}, u32[]{:S(2)}) copy-start(f32[16,2048]{1,0:T(8,128)} %param.28) | copy-start | bytes 393220
  619.7 91.4 %copy-start.54 = (f32[16,16]{1,0:T(8,128)S(1)}, f32[16,16]{1,0:T(8,128)}, u32[]{:S(2)}) copy-start(f32[16,16]{1,0:T(8,128)} %param.24) | copy-start | bytes 3076
  619.8 91.4 %copy-start.66 = (f32[16,16]{1,0:T(8,128)S(1)}, f32[16,16]{1,0:T(8,128)}, u32[]{:S(2)}) copy-start(f32[16,16]{1,0:T(8,128)} %param.34) | copy-start | bytes 3076
  619.8 91.4 %copy-start.67 = (f32[16,16]{1,0:T(8,128)S(1)}, f32[16,16]{1,0:T(8,128)}, u32[]{:S(2)}) copy-start(f32[16,16]{1,0:T(8,128)} %param.29) | copy-start | bytes 3076
  (44 other events, 91.4 us)
Sparse Core Ops, SparseCore 0:
  11.6 40.6 all-gather.6
  56.5 54.3 reduce-scatter.10
  113.3 58.0 reduce-scatter.8
  173.5 54.6 reduce-scatter.6
  230.4 54.6 reduce-scatter.4
  396.8 34.5 all-gather.10
  433.0 33.4 all-gather.12
  468.0 33.4 all-gather.14
  503.6 33.4 all-gather.16
  612.4 97.0 all-reduce.4
Sparse Core Ops, SparseCore 1:
  60.7 92.5 all-gather.8
  389.1 206.9 all-reduce.6
where the time goes:
time: 728 us; the launch traced here: 721 us
  waiting for transfers between devices  324 us (45%)
  blocking collectives  167 us (23%)
  matrix products  111 us (15%)
  other arithmetic  49.4 us (7%)
  local copies, waits for them, and re-layouts  46.6 us (6%)
  between operations  22.8 us (3%)
    psum x1, waiting for transfers between devices, on_device(): lax.psum((grad_second, grad_tower, grad_head, loss_total), ('rows', 'fiel...  164 us
    psum x1, waiting for transfers between devices, on_device(): first_whole_sum, = lax.psum((grad_first,), 'rows')  88.2 us
    all_gather x1, blocking collectives, on_device(): lax.all_gather(tower_in.astype(jnp.bfloat16), ('rows', 'field'), axis=1,...  71.4 us
    reduce_scatter x4, waiting for transfers between devices, on_device(): lax.psum_scatter(jnp.dot(rows_x, first_both, preferred_element_type=jnp.f...  52.1 us
    psum x1, blocking collectives, on_device(): lax.psum((grad_second, grad_tower, grad_head, loss_total), ('rows', 'fiel...  40 us
    psum x1, blocking collectives, on_device(): valid_total = lax.psum(jnp.sum(valid_mask).astype(jnp.float32), 'rows')  32.1 us
    all_gather x1, blocking collectives, on_device(): lax.all_gather(gate_in.astype(jnp.bfloat16), 'rows', axis=0, tiled=True)  23.2 us
    dot_general x4, matrix products, local_pass(): dgate = jnp.einsum('rto,rko->rtk', dmixed, expert_res, precision=highest)  19.1 us
  transfers between devices with their start and end apart: 12, of which 5 were waited for; matrix products, arithmetic and copies ran while one was open for 17% of the time, Pallas kernels for 0%

commit v1 on v0

v1 whole, which is shorter than its diff:
```python
import math

import jax
import jax.numpy as jnp
import numpy as np
from jax import lax
from jax.experimental import pallas as pl
from jax.experimental.pallas import tpu as pltpu
from jax.sharding import PartitionSpec as P

momentum_mu = 0.5
average_keep = 0.5
rate_bases = (17.0, 1.0, 24.0, 4.0, 0.25)
both = ("rows", "field")
f32 = jnp.float32
bf16 = jnp.bfloat16
BLOCK = 16
LANES = 128


def dot(a, b):
    return lax.dot_general(a, b, (((1,), (0,)), ((), ())), preferred_element_type=f32)


def dot_t(a, b):
    return lax.dot_general(a, b, (((1,), (1,)), ((), ())), preferred_element_type=f32)


def t_dot(a, b):
    return lax.dot_general(a, b, (((0,), (0,)), ((), ())), preferred_element_type=f32)


def sigmoid(v):
    return 0.5 + 0.5 * jnp.tanh(0.5 * v)


def rows16(start):
    return pl.ds(pl.multiple_of(start, BLOCK), BLOCK)


def each_block(tab, pairs, body):
    def step(j, carry):
        for side in range(2):
            core = tab[2 * pairs] if side == 0 else 1 - tab[2 * pairs]
            body(side, tab[side * pairs + j], 2 * (j // 2) + core, j % 2)
        return carry

    lax.fori_loop(0, pairs, step, 0, unroll=True)


def first_kernel(
    tab, own_ref, oth_ref, xo_ref, xr_ref, meta_ref, ga_ref, gs_ref, gate_ref, w_ref, cnt_ref, xt_ref
):
    pairs = own_ref.shape[0] // BLOCK
    half = xo_ref.shape[-1]
    wide = ga_ref.shape[1]
    hidden = 256 if wide % 256 == 0 else LANES
    experts = tab_experts(wide, hidden)

    @pl.when(pl.program_id(0) == 0)
    def _():
        def put(side, place, rr, ff):
            src = own_ref if side == 0 else oth_ref
            row = (ff ^ tab[2 * pairs + 1]) * half + rr * BLOCK
            w_ref[rows16(row), :] = src[rows16(place * BLOCK), :]

        each_block(tab, pairs, put)
        side_cols = w_ref[:, wide:].astype(f32)
        lane = lax.broadcasted_iota(jnp.int32, side_cols.shape, 1)
        base = 2 * experts
        scale = jnp.where(
            lane == base, 1.0, jnp.where(lane == base + 1, 256.0, jnp.where(lane == base + 2, 65536.0, 0.0))
        )
        total = jnp.sum(jnp.sum(side_cols * scale, axis=1, keepdims=True), axis=0, keepdims=True)
        cnt_ref[...] = jnp.broadcast_to(total, cnt_ref.shape)

    x = jnp.concatenate([xo_ref[0], xr_ref[...]], axis=1)
    xt_ref[...] = x.T
    meta = meta_ref[0].T
    domain = meta[:, 2:3]
    logits = dot(x, w_ref[:, wide:])
    lane = lax.broadcasted_iota(jnp.int32, logits.shape, 1)
    picked = (lane // experts).astype(f32) == domain
    top = jnp.max(jnp.where(picked, logits, -jnp.inf), axis=1, keepdims=True)
    raised = jnp.where(picked, jnp.exp(jnp.where(picked, logits, top) - top), 0.0)
    gate = raised / jnp.sum(raised, axis=1, keepdims=True)
    gate_ref[...] = gate
    gate = gate + pltpu.roll(gate, LANES - experts, axis=1)
    for k in range(experts):
        cols = pl.ds(k * hidden, hidden)
        pre = dot(x, w_ref[:, cols])
        s = sigmoid(pre)
        a = pre * s
        g = gate[:, k : k + 1]
        ga_ref[:, cols] = (g * a).astype(bf16)
        gs_ref[:, cols] = (g * (s + a * (1.0 - s))).astype(bf16)


def tab_experts(wide, hidden):
    return wide // hidden


def second_kernel(
    tab,
    own_ref,
    oth_ref,
    ga_ref,
    meta_ref,
    cnt_ref,
    to_ref,
    w_ref,
    dm_ref,
    keep_ref,
    send_ref,
    side_ref,
    ti_ref,
    gwo_ref,
    gti_ref,
):
    pairs = own_ref.shape[0] // BLOCK
    step = pl.program_id(0)
    out_cols = dm_ref.shape[1]
    hidden = pairs * BLOCK
    experts = w_ref.shape[0] // hidden
    part = experts // 2

    @pl.when(step == 0)
    def _():
        def put(side, j):
            src = own_ref if side == 0 else oth_ref
            core = tab[2 * pairs] if side == 0 else 1 - tab[2 * pairs]
            a0 = src[rows16(tab[side * pairs + 2 * j] * BLOCK), :].astype(f32)
            a1 = src[rows16(tab[side * pairs + 2 * j + 1] * BLOCK), :].astype(f32)
            row = (2 * j + core) * BLOCK
            upper = jnp.concatenate([a0[:8], a1[:8]], axis=0).astype(bf16)
            lower = jnp.concatenate([a0[8:], a1[8:]], axis=0).astype(bf16)
            for k in range(part):
                cols = slice(k * out_cols, (k + 1) * out_cols)
                w_ref[rows16(k * hidden + row), :] = upper[:, cols]
                w_ref[rows16((k + part) * hidden + row), :] = lower[:, cols]
            ti_ref[rows16(row), 0:LANES] = upper[:, part * out_cols :]
            ti_ref[rows16(row), LANES : 2 * LANES] = lower[:, part * out_cols :]

        for j in range(pairs // 2):
            put(0, j)
            put(1, j)
        gwo_ref[...] = jnp.zeros_like(gwo_ref)
        gti_ref[...] = jnp.zeros_like(gti_ref)
        side_ref[...] = jnp.zeros_like(side_ref)

    meta = meta_ref[0].T
    valid, label, domain = meta[:, 0:1], meta[:, 1:2], meta[:, 2:3]
    count = cnt_ref[0:1, 0:1]
    head = to_ref[0:1, :]
    mixed = dot(ga_ref[...], w_ref[...]).astype(bf16)
    tpre = dot(mixed, ti_ref[...])
    lane = lax.broadcasted_iota(jnp.int32, tpre.shape, 1)
    picked = (lane // LANES).astype(f32) == domain
    s = sigmoid(tpre)
    act = (tpre * s).astype(bf16).astype(f32)
    act = jnp.where(picked, act, 0.0)
    chosen = jnp.sum(act * head, axis=1, keepdims=True)
    soft = jnp.maximum(chosen, 0.0) + jnp.log1p(jnp.exp(-jnp.abs(chosen)))
    loss = jnp.sum(valid * (soft - label * chosen), axis=0, keepdims=True)
    dlogit = (valid * (sigmoid(chosen) - label) / count).astype(bf16).astype(f32)
    slope = s * (1.0 + tpre * (1.0 - s))
    dtpre = jnp.where(picked, dlogit * head * slope, 0.0).astype(bf16)
    side_ref[0:1, :] += jnp.sum(dlogit * act, axis=0, keepdims=True)
    side_ref[1:2, :] += jnp.broadcast_to(loss, (1, side_ref.shape[1]))
    gti_ref[...] += t_dot(mixed, dtpre)
    dmixed = dot_t(dtpre, ti_ref[...]).astype(bf16)
    dm_ref[...] = dmixed
    for k in range(experts):
        gwo_ref[k] += t_dot(ga_ref[:, pl.ds(k * hidden, hidden)], dmixed)

    @pl.when(step == pl.num_programs(0) - 1)
    def _():
        def put(side, place, rr, ff):
            dst = keep_ref if side == 0 else send_ref
            row = pl.ds(pl.multiple_of(rr * BLOCK + ff * 8, 8), 8)
            for k in range(part):
                cols = slice(k * out_cols, (k + 1) * out_cols)
                tile = jnp.concatenate([gwo_ref[k, row, :], gwo_ref[k + part, row, :]], axis=0)
                dst[rows16(place * BLOCK), cols] = tile.astype(dst.dtype)
            tile = gti_ref[row, :]
            tile = jnp.concatenate([tile[:, :LANES], tile[:, LANES:]], axis=0)
            dst[rows16(place * BLOCK), part * out_cols :] = tile.astype(dst.dtype)

        each_block(tab, pairs, put)


def back_kernel(
    tab,
    dm_ref,
    w_ref,
    ga_ref,
    gs_ref,
    xt_ref,
    gate_ref,
    dp_ref,
    dg_ref,
    keep_ref,
    send_ref,
    q_ref,
    gwi_ref,
):
    k = pl.program_id(0)
    experts = pl.num_programs(0)
    pairs = keep_ref.shape[0] // BLOCK
    half = keep_ref.shape[0]
    hidden = ga_ref.shape[1]
    wide = keep_ref.shape[1] - LANES

    def pack(start, width):
        def put(side, place, rr, ff):
            dst = keep_ref if side == 0 else send_ref
            row = (ff ^ tab[2 * pairs + 1]) * half + rr * BLOCK
            dst[rows16(place * BLOCK), pl.ds(start, width)] = gwi_ref[rows16(row), 0:width].astype(dst.dtype)

        each_block(tab, pairs, put)

    u = dot_t(dm_ref[...], w_ref[...])
    dpre = (u * gs_ref[...].astype(f32)).astype(bf16)
    dp_ref[...] = dpre
    q = jnp.sum(u * ga_ref[...].astype(f32), axis=1, keepdims=True)
    lane = lax.broadcasted_iota(jnp.int32, q_ref.shape, 1)
    mine = (lane == k) | (lane == k + experts)
    q_ref[...] = jnp.where(mine, q, jnp.where(k == 0, 0.0, q_ref[...]))
    gwi_ref[...] = dot(xt_ref[...], dpre)
    pack(pl.multiple_of(k * hidden, hidden), hidden)

    @pl.when(k == experts - 1)
    def _():
        q = q_ref[...]
        gate = gate_ref[...]
        total = jnp.sum(jnp.where(lane < experts, q, 0.0), axis=1, keepdims=True)
        dgate = jnp.where(gate_ref[...] != 0.0, q, 0.0) - gate * total
        dgate = dgate.astype(bf16)
        dg_ref[...] = dgate
        gwi_ref[:, 0:LANES] = dot(xt_ref[...], dgate)
        pack(wide, LANES)


def input_kernel(tab, dp_ref, dg_ref, w_ref, keep_ref, send_ref):
    wide = dp_ref.shape[1]
    grad = dot_t(dp_ref[...], w_ref[:, 0:wide]) + dot_t(dg_ref[...], w_ref[:, wide:])
    half = grad.shape[1] // 2
    keep_ref[0] = grad[:, :half]
    send_ref[...] = grad[:, half:].astype(bf16)


class Cube:
    def __init__(self):
        self.rows = lax.axis_size("rows")
        self.fields = lax.axis_size("field")
        self.bits = int(math.log2(self.rows))
        assert 1 << self.bits == self.rows and self.fields == 2
        self.outer = self.bits - 2
        steps = [self.flip_row(b) for b in range(self.bits - 1, 1, -1)]
        steps += [self.flip_mixed(0), self.flip_mixed(1)]
        self.steps = steps
        self.core = self.flip_row(0)

    def table(self, partner):
        pairs = []
        for r in range(self.rows):
            for f in range(self.fields):
                rr, ff = partner(r, f)
                pairs.append((r * self.fields + f, rr * self.fields + ff))
        return pairs

    def flip_row(self, bit):
        return self.table(lambda r, f: (r ^ (1 << bit), f))

    def flip_mixed(self, turn):
        return self.table(lambda r, f: (r ^ 2, f) if (r & 1) == turn else (r, f ^ 1))

    def place(self, rr, ff, r, f):
        dr, df, core = rr ^ r, ff ^ f, r & 1
        out = jnp.zeros_like(dr)
        for s in range(self.outer):
            out = out + (((dr >> (self.bits - 1 - s)) & 1) << s)
        xbit = (dr >> 1) & 1
        low = jnp.where(core == 0, xbit, df)
        high = jnp.where(core == 0, df, xbit)
        return out + (low << self.outer) + (high << (self.outer + 1))


def gather(cube, block):
    for pairs in cube.steps:
        block = jnp.concatenate([block, lax.ppermute(block, both, pairs)], axis=0)
    return block, lax.ppermute(block, both, cube.core)


def scatter(cube, keep, send):
    total = keep + lax.ppermute(send, both, cube.core).astype(f32)
    for pairs in reversed(cube.steps):
        half = total.shape[0] // 2
        got = lax.ppermute(total[half:].astype(bf16), both, pairs)
        total = total[:half] + got.astype(f32)
    return total


def sum_all(cube, part):
    for pairs in [cube.core] + cube.steps:
        part = part + lax.ppermute(part, both, pairs)
    return part


def renew(weight, velocity, average, gradient, rate):
    velocity_new = momentum_mu * velocity + gradient
    weight_new = weight - rate * (gradient + momentum_mu * velocity_new)
    average_new = average_keep * average + (1.0 - average_keep) * weight_new
    return (weight_new, velocity_new, average_new)


def shape(dims, dtype):
    return jax.ShapeDtypeStruct(dims, dtype)


def whole(dims):
    return pl.BlockSpec(dims, lambda i, tab: (0,) * len(dims))


def params(limit=48):
    return pltpu.CompilerParams(vmem_limit_bytes=limit << 20)


def on_device(
    inputs,
    valid_mask,
    labels,
    domains,
    expert_in,
    gate_in,
    expert_out,
    tower_in,
    tower_out,
    velocity_expert_in,
    velocity_gate_in,
    velocity_expert_out,
    velocity_tower_in,
    velocity_tower_out,
    average_expert_in,
    average_gate_in,
    average_expert_out,
    average_tower_in,
    average_tower_out,
):
    cube = Cube()
    micro, rows_dev, width = inputs.shape
    fields = cube.fields
    tile = rows_dev // fields
    rows_own = micro * tile
    experts, second_rows, out_cols = expert_out.shape
    tasks, tower_cols = tower_out.shape
    wide = expert_in.shape[1]
    hidden = wide // experts
    first_rows = expert_in.shape[0]
    part = experts // 2
    total_rows = micro * rows_dev * cube.rows
    r, f = lax.axis_index("rows"), lax.axis_index("field")

    def own_half(values, which):
        return lax.dynamic_slice_in_dim(values, which * tile, tile, 1)

    own_valid = own_half(valid_mask, f)
    ones = jnp.sum(own_valid)
    digits = jnp.stack([ones % 256, (ones // 256) % 256, ones // 65536]).astype(bf16)
    extra = jnp.zeros((first_rows, LANES - tasks * experts), bf16).at[0, :3].set(digits)
    block_a = jnp.concatenate([expert_in.astype(bf16), gate_in.astype(bf16), extra], axis=1)
    block_b = jnp.concatenate(
        [
            expert_out.astype(bf16)
            .reshape(2, part, second_rows, out_cols)
            .transpose(0, 2, 1, 3)
            .reshape(2 * second_rows, part * out_cols),
            tower_in.astype(bf16).reshape(2 * second_rows, tower_cols),
        ],
        axis=1,
    )
    x_send = own_half(inputs, 1 - f).reshape(rows_own, width)
    x_got = lax.ppermute(x_send, "field", [(0, 1), (1, 0)])
    own_a, oth_a = gather(cube, block_a)
    own_b, oth_b = gather(cube, block_b)

    pairs = 2 * width // BLOCK // 2
    fit = first_rows == BLOCK
    j = jnp.arange(pairs // 2, dtype=jnp.int32)[:, None]
    ff = jnp.arange(2, dtype=jnp.int32)[None, :]
    if fit:
        core = r & 1
        places = [
            cube.place(2 * j + core, ff, r, f).reshape(-1),
            cube.place(2 * j + 1 - core, ff, r ^ 1, f).reshape(-1),
        ]
    else:
        core = jnp.int32(0)
        places = [(2 * j + ff).reshape(-1)] * 2
        rows_a, rows_b = sorted_rows(cube, r, f, width, first_rows, second_rows)
        all_a, all_b = jnp.concatenate([own_a, oth_a]), jnp.concatenate([own_b, oth_b])
        own_a, oth_a = jnp.split(jnp.take(all_a, rows_a, axis=0), 2)
        own_b, oth_b = jnp.split(jnp.take(all_b, rows_b, axis=0), 2)
    tab = jnp.concatenate(places + [jnp.stack([core, f])]).astype(jnp.int32)
    sent = bf16 if fit else f32

    meta = jnp.stack(
        [own_valid.astype(f32), own_half(labels, f).astype(f32), own_half(domains, f).astype(f32)]
        + [jnp.zeros((micro, tile), f32)] * 5,
        axis=1,
    )
    a_cols, b_cols = wide + LANES, part * out_cols + LANES
    half = width

    ga, gs, gate, first_w, count, x_t = pl.pallas_call(
        first_kernel,
        grid_spec=pltpu.PrefetchScalarGridSpec(
            num_scalar_prefetch=1,
            grid=(micro,),
            in_specs=[
                whole((half, a_cols)),
                whole((half, a_cols)),
                pl.BlockSpec((1, tile, width), lambda i, tab: (i, tab[2 * pairs + 1], 0)),
                pl.BlockSpec((tile, width), lambda i, tab: (i, 0)),
                pl.BlockSpec((1, 8, tile), lambda i, tab: (i, 0, 0)),
            ],
            out_specs=[
                pl.BlockSpec((tile, wide), lambda i, tab: (i, 0)),
                pl.BlockSpec((tile, wide), lambda i, tab: (i, 0)),
                pl.BlockSpec((tile, LANES), lambda i, tab: (i, 0)),
                whole((2 * half, a_cols)),
                whole((8, LANES)),
                pl.BlockSpec((2 * width, tile), lambda i, tab: (0, i)),
            ],
        ),
        out_shape=[
            shape((rows_own, wide), bf16),
            shape((rows_own, wide), bf16),
            shape((rows_own, LANES), f32),
            shape((2 * half, a_cols), bf16),
            shape((8, LANES), f32),
            shape((2 * width, rows_own), bf16),
        ],
        compiler_params=params(),
        name="first",
    )(tab, own_a, oth_a, inputs, x_got, meta)

    head = jnp.broadcast_to(
        tower_out.astype(bf16).astype(f32).reshape(1, tasks * tower_cols), (8, tasks * tower_cols)
    )
    second_w, dmixed, keep_b, send_b, side = pl.pallas_call(
        second_kernel,
        grid_spec=pltpu.PrefetchScalarGridSpec(
            num_scalar_prefetch=1,
            grid=(micro,),
            in_specs=[
                whole((half, b_cols)),
                whole((half, b_cols)),
                pl.BlockSpec((tile, wide), lambda i, tab: (i, 0)),
                pl.BlockSpec((1, 8, tile), lambda i, tab: (i, 0, 0)),
                whole((8, LANES)),
                whole((8, tasks * tower_cols)),
            ],
            out_specs=[
                whole((wide, out_cols)),
                pl.BlockSpec((tile, out_cols), lambda i, tab: (i, 0)),
                whole((half, b_cols)),
                whole((half, b_cols)),
                whole((8, tasks * tower_cols)),
            ],
            scratch_shapes=[
                pltpu.VMEM((out_cols, tasks * tower_cols), bf16),
                pltpu.VMEM((experts, hidden, out_cols), f32),
                pltpu.VMEM((out_cols, tasks * tower_cols), f32),
            ],
        ),
        out_shape=[
            shape((wide, out_cols), bf16),
            shape((rows_own, out_cols), bf16),
            shape((half, b_cols), f32),
            shape((half, b_cols), sent),
            shape((8, tasks * tower_cols), f32),
        ],
        compiler_params=params(),
        name="second",
    )(tab, own_b, oth_b, ga, meta, count, head)

    dpre, dgate, keep_a, send_a = pl.pallas_call(
        back_kernel,
        grid_spec=pltpu.PrefetchScalarGridSpec(
            num_scalar_prefetch=1,
            grid=(experts,),
            in_specs=[
                whole((rows_own, out_cols)),
                pl.BlockSpec((hidden, out_cols), lambda i, tab: (i, 0)),
                pl.BlockSpec((rows_own, hidden), lambda i, tab: (0, i)),
                pl.BlockSpec((rows_own, hidden), lambda i, tab: (0, i)),
                whole((2 * width, rows_own)),
                whole((rows_own, LANES)),
            ],
            out_specs=[
                pl.BlockSpec((rows_own, hidden), lambda i, tab: (0, i)),
                whole((rows_own, LANES)),
                whole((half, a_cols)),
                whole((half, a_cols)),
            ],
            scratch_shapes=[
                pltpu.VMEM((rows_own, LANES), f32),
                pltpu.VMEM((2 * width, hidden), f32),
            ],
        ),
        out_shape=[
            shape((rows_own, wide), bf16),
            shape((rows_own, LANES), bf16),
            shape((half, a_cols), f32),
            shape((half, a_cols), sent),
        ],
        compiler_params=params(),
        name="back",
    )(tab, dmixed, second_w, ga, gs, x_t, gate)

    grad_keep, grad_send = pl.pallas_call(
        input_kernel,
        grid_spec=pltpu.PrefetchScalarGridSpec(
            num_scalar_prefetch=1,
            grid=(micro,),
            in_specs=[
                pl.BlockSpec((tile, wide), lambda i, tab: (i, 0)),
                pl.BlockSpec((tile, LANES), lambda i, tab: (i, 0)),
                whole((2 * half, a_cols)),
            ],
            out_specs=[
                pl.BlockSpec((1, tile, width), lambda i, tab: (i, tab[2 * pairs + 1], 0)),
                pl.BlockSpec((tile, width), lambda i, tab: (i, 0)),
            ],
        ),
        out_shape=[
            shape((micro, rows_dev, width), f32),
            shape((rows_own, width), bf16),
        ],
        compiler_params=params(),
        name="input",
    )(tab, dpre, dgate, first_w)
    grad_got = lax.ppermute(grad_send, "field", [(0, 1), (1, 0)])
    input_grad = lax.dynamic_update_slice_in_dim(
        grad_keep, grad_got.astype(f32).reshape(micro, tile, width), (1 - f) * tile, 1
    )

    if not fit:
        keep_b, send_b = unsorted(keep_b, send_b, rows_b)
        keep_a, send_a = unsorted(keep_a, send_a, rows_a)
    sum_b = scatter(cube, keep_b, send_b)
    sum_a = scatter(cube, keep_a, send_a)
    side = sum_all(cube, side)

    second_sum = (
        sum_b[:, : part * out_cols]
        .reshape(2, second_rows, part, out_cols)
        .transpose(0, 2, 1, 3)
        .reshape(experts, second_rows, out_cols)
    )
    gradients = (
        sum_a[:, :wide],
        sum_a[:, wide : wide + tasks * experts],
        second_sum,
        sum_b[:, part * out_cols :].reshape(tasks, second_rows, tower_cols),
        side[0].reshape(tasks, tower_cols),
    )
    weights = (expert_in, gate_in, expert_out, tower_in, tower_out)
    velocities = (
        velocity_expert_in,
        velocity_gate_in,
        velocity_expert_out,
        velocity_tower_in,
        velocity_tower_out,
    )
    averages = (
        average_expert_in,
        average_gate_in,
        average_expert_out,
        average_tower_in,
        average_tower_out,
    )
    scale_root = math.sqrt(total_rows)
    results = [side[1, 0] / count[0, 0], input_grad]
    for at in range(5):
        results.extend(
            renew(weights[at], velocities[at], averages[at], gradients[at], rate_bases[at] * scale_root)
        )
    return tuple(results)


def sorted_rows(cube, r, f, width, first_rows, second_rows):
    core = r & 1
    held = cube.rows * cube.fields // 2

    def row_of(rr, ff, inner, size):
        same = (rr & 1) == core
        here = cube.place(rr, ff, r, f)
        there = cube.place(rr, ff, r ^ 1, f)
        return jnp.where(same, here, held + there) * size + inner

    side = np.arange(2)[:, None, None, None]
    j = np.arange(width // (2 * BLOCK))[None, :, None, None]
    ff = np.arange(2)[None, None, :, None]
    inner = np.arange(BLOCK)[None, None, None, :]
    at = ((2 * j + side) * BLOCK + inner + 0 * ff).astype(np.int32)
    rows_a = row_of(jnp.asarray(at // first_rows), jnp.asarray(ff + 0 * at), jnp.asarray(at % first_rows), first_rows)
    upper = inner // 8
    at = ((2 * j + side) * BLOCK + ff * 8 + inner % 8).astype(np.int32)
    owner = at // second_rows
    rows_b = row_of(
        jnp.asarray(owner // 2),
        jnp.asarray(owner % 2),
        jnp.asarray(at % second_rows + second_rows * upper),
        2 * second_rows,
    )
    return rows_a.reshape(-1), rows_b.reshape(-1)


def unsorted(keep, send, rows):
    every = jnp.concatenate([keep, send])
    back = jnp.zeros_like(rows).at[rows].set(jnp.arange(rows.shape[0], dtype=rows.dtype))
    keep, send = jnp.split(jnp.take(every, back, axis=0), 2)
    return keep, send.astype(bf16)


def solution(mesh):
    first = P(("field", "rows"), None)
    second = P(None, ("rows", "field"), None)
    by_row = P(None, "rows")
    inputs = P(None, "rows", "field")
    weights = (first, first, second, second, P())
    return jax.shard_map(
        on_device,
        mesh=mesh,
        in_specs=(inputs, by_row, by_row, by_row) + weights * 3,
        out_specs=(P(), inputs) + tuple(spec for spec in weights for _ in range(3)),
        check_vma=False,
    )
```

time: 728 us -> 150 us (0.21)
  the two profiles are of different devices: /device:TPU:0 before, /device:TPU:1 now
where the time goes in v1:
time: 150 us
  waiting for transfers between devices  61.9 us (41%)
  Pallas kernels  38.1 us (25%)
  starting transfers between devices  28.8 us (19%)
  other arithmetic  8.08 us (5%)
  local copies, waits for them, and re-layouts  6.34 us (4%)
  between operations  6.31 us (4%)
    ppermute x8, waiting for transfers between devices, scatter(): got = lax.ppermute(total[half:].astype(bf16), both, pairs)  29.9 us
    ppermute x8, waiting for transfers between devices, gather(): block = jnp.concatenate([block, lax.ppermute(block, both, pairs)], axis=0)  20.7 us
    pallas_call x1, Pallas kernels, on_device(): pl.pallas_call(back_kernel, grid_spec=pltpu.PrefetchScalarGridSpec(num_sc...  12.8 us
    pallas_call x1, Pallas kernels, on_device(): pl.pallas_call(second_kernel, grid_spec=pltpu.PrefetchScalarGridSpec(num_...  10.4 us
    ppermute x5, waiting for transfers between devices, sum_all(): part = part + lax.ppermute(part, both, pairs)  9.24 us
    pallas_call x1, Pallas kernels, on_device(): pl.pallas_call(first_kernel, grid_spec=pltpu.PrefetchScalarGridSpec(num_s...  8.67 us
    ppermute x8, starting transfers between devices, scatter(): got = lax.ppermute(total[half:].astype(bf16), both, pairs)  7.72 us
    ppermute x2, starting transfers between devices, gather(): return (block, lax.ppermute(block, both, cube.core))  7.15 us
  transfers between devices with their start and end apart: 27, of which 16 were waited for; matrix products, arithmetic and copies ran while one was open for 6% of the time, Pallas kernels for 19%

profile of v1, /device:TPU:1, one launch (start us, length us, event | category | flops | bytes accessed | tf_op | source)
XLA Modules:
  0.0 149.5 jit_solution(2474606145613126054)
XLA Ops:
  0.7 1.4 dynamic-slice_convert_fusion.2
  4.7 0.9 convert_element_type.72
  5.6 0.7 convert_element_type.73
  6.5 3.1 %collective-permute-start.5 = (bf16[16,2176]{1,0:T(8,128)(2,1)S(1)}, bf16[16,2176]{1,0:T(8,128)(2,1)S(1)}, u32[]{:S(2)}, u32[]{:S(2)}) collective-permute-start(bf16[16,2176]{1,0:T(8,128)(2,1)S(1)} %concatenate.53), channel_id=1, source_target_pairs={{0,16},{1,17},{2,18},{3,19},{4,20},{5,21},{6,22},{7,23},{8,24},{9,... | collective-permute-start | bytes 208904 | tf_op jit(solution)/shard_map/ppermute | solution.py:291
  9.6 1.9 %constant_dynamic-slice_fusion = bf16[4,256,256]{2,1,0:T(8,128)(2,1)} fusion(bf16[4,512,256]{2,1,0:T(8,128)(2,1)} %xo_ref.1, s32[]{:T(128)S(6)} %select_n.70), kind=kLoop, calls=%fused_computation.67 | loop fusion | bytes 1048580 | tf_op jit(solution)/shard_map/dynamic_slice | solution.py:365
  11.5 1.2 collective-permute-start.10
  12.8 0.6 pad_maximum_fusion.6
  13.5 3.6 %collective-permute-done = bf16[16,1152]{1,0:T(8,128)(2,1)S(1)} collective-permute-done((bf16[16,1152]{1,0:T(8,128)(2,1)S(1)}, bf16[16,1152]{1,0:T(8,128)(2,1)S(1)}, u32[]{:S(2)}, u32[]{:S(2)}) %collective-permute-start) | collective-permute-done | bytes 36896 | tf_op jit(solution)/shard_map/ppermute | solution.py:291
  17.1 1.3 collective-permute-start.1
  18.4 0.6 constant_dynamic-update-slice_fusion.3
  19.3 1.4 collective-permute-done.1
  21.0 0.6 constant_dynamic-update-slice_fusion.2
  21.7 2.4 %collective-permute-done.6 = bf16[32,2176]{1,0:T(8,128)(2,1)S(1)} collective-permute-done((bf16[32,2176]{1,0:T(8,128)(2,1)S(1)}, bf16[32,2176]{1,0:T(8,128)(2,1)S(1)}, u32[]{:S(2)}, u32[]{:S(2)}) %collective-permute-start.6) | collective-permute-done | bytes 139296 | tf_op jit(solution)/shard_map/ppermute | solution.py:291
  24.4 5.5 %collective-permute-done.7 = bf16[64,2176]{1,0:T(8,128)(2,1)S(1)} collective-permute-done((bf16[64,2176]{1,0:T(8,128)(2,1)S(1)}, bf16[64,2176]{1,0:T(8,128)(2,1)S(1)}, u32[]{:S(2)}, u32[]{:S(2)}) %collective-permute-start.7) | collective-permute-done | bytes 278560 | tf_op jit(solution)/shard_map/ppermute | solution.py:291
  30.0 1.3 collective-permute-start.8
  31.7 7.8 %collective-permute-done.8 = bf16[128,2176]{1,0:T(8,128)(2,1)S(1)} collective-permute-done((bf16[128,2176]{1,0:T(8,128)(2,1)S(1)}, bf16[128,2176]{1,0:T(8,128)(2,1)S(1)}, u32[]{:S(2)}, u32[]{:S(2)}) %collective-permute-start.8) | collective-permute-done | bytes 557088 | tf_op jit(solution)/shard_map/ppermute | solution.py:291
  39.5 4.8 %collective-permute-start.9 = (bf16[256,2176]{1,0:T(8,128)(2,1)S(1)}, bf16[256,2176]{1,0:T(8,128)(2,1)S(1)}, u32[]{:S(2)}, u32[]{:S(2)}) collective-permute-start(bf16[256,2176]{1,0:T(8,128)(2,1)S(1)} %constant_dynamic-update-slice_fusion.5.own_ref), channel_id=1, source_target_pairs={{0,2},{1,3},{2,0},{3,1},{4,6},{5,7},{6,4},{7,5},{8,10},{9,11},{10,... | collective-permute-start | bytes 3342344 | tf_op jit(solution)/shard_map/ppermute | solution.py:292
  44.3 0.7 constant_dynamic-update-slice_fusion.1
  45.0 0.7 constant_dynamic-update-slice_fusion.own_ref
  45.7 2.4 %collective-permute-start.4 = (bf16[256,1152]{1,0:T(8,128)(2,1)}, bf16[256,1152]{1,0:T(8,128)(2,1)}, u32[]{:S(2)}, u32[]{:S(2)}) collective-permute-start(bf16[256,1152]{1,0:T(8,128)(2,1)} %constant_dynamic-update-slice_fusion.own_ref), channel_id=1, source_target_pairs={{0,2},{1,3},{2,0},{3,1},{4,6},{5,7},{6,4},{7,5},{8,10},{9,11},{10,... | collective-permute-start | bytes 1769480 | tf_op jit(solution)/shard_map/ppermute | solution.py:292
  48.6 8.7 %first.1 = (bf16[1024,2048]{1,0:T(8,128)(2,1)}, bf16[1024,2048]{1,0:T(8,128)(2,1)}, f32[1024,128]{1,0:T(8,128)S(1)}, bf16[512,2176]{1,0:T(8,128)(2,1)}, f32[8,12...) custom-call(s32[34]{0:T(128)S(1)} %pad_add_fusion.tab, bf16[256,2176]{1,0:T(8,128)(2,1)S(1)} %constant_dynamic-update-slice_fusion.5.own_ref, ...), custom_call_target="tpu_custom_call" | custom-call | tf_op jit(solution)/shard_map/first/pallas_call | solution.py:415
  57.2 10.4 %second.1 = (bf16[2048,256]{1,0:T(8,128)(2,1)S(1)}, bf16[1024,256]{1,0:T(8,128)(2,1)S(1)}, f32[256,1152]{1,0:T(8,128)S(1)}, bf16[256,1152]{1,0:T(8,128)(2,1)S(1)}, f32[8,256]{1,0:T(8,128)S(1)}) custom-call(s32[34]{0:T(128)S(1)} %pad_add_fusion.tab, bf16[256,1152]{1,0:T(8,128)(2,1)} %constant_dynamic-update-slice_fusion.own_ref, ...), custom_call_target="tpu_custom_call" | custom-call | tf_op jit(solution)/shard_map/second/pallas_call | solution.py:451
  67.7 2.0 %collective-permute-done.22 = bf16[256,1152]{1,0:T(8,128)(2,1)S(1)} collective-permute-done((bf16[256,1152]{1,0:T(8,128)(2,1)S(1)}, bf16[256,1152]{1,0:T(8,128)(2,1)S(1)}, u32[]{:S(2)}, u32[]{:S(2)}) %collective-permute-start.22) | collective-permute-done | bytes 589856 | tf_op jit(solution)/shard_map/ppermute | solution.py:296
  69.9 1.3 collective-permute-start.23
  71.2 1.2 collective-permute-done.11
  72.3 3.4 %collective-permute-done.12 = f32[8,256]{1,0:T(8,128)S(1)} collective-permute-done((f32[8,256]{1,0:T(8,128)S(1)}, f32[8,256]{1,0:T(8,128)S(1)}, u32[]{:S(2)}, u32[]{:S(2)}) %collective-permute-start.12) | collective-permute-done | bytes 8224 | tf_op jit(solution)/shard_map/ppermute | solution.py:306
  75.7 2.5 %collective-permute-done.13 = f32[8,256]{1,0:T(8,128)S(1)} collective-permute-done((f32[8,256]{1,0:T(8,128)S(1)}, f32[8,256]{1,0:T(8,128)S(1)}, u32[]{:S(2)}, u32[]{:S(2)}) %collective-permute-start.13) | collective-permute-done | bytes 8224 | tf_op jit(solution)/shard_map/ppermute | solution.py:306
  78.6 2.2 %collective-permute-done.14 = f32[8,256]{1,0:T(8,128)S(1)} collective-permute-done((f32[8,256]{1,0:T(8,128)S(1)}, f32[8,256]{1,0:T(8,128)S(1)}, u32[]{:S(2)}, u32[]{:S(2)}) %collective-permute-start.14) | collective-permute-done | bytes 8224 | tf_op jit(solution)/shard_map/ppermute | solution.py:306
  81.5 12.8 %back.1 = (bf16[1024,2048]{1,0:T(8,128)(2,1)}, bf16[1024,128]{1,0:T(8,128)(2,1)S(1)}, f32[256,2176]{1,0:T(8,128)}, bf16[256,2176]{1,0:T(8,128)(2,1)S(1)}) custom-call(s32[34]{0:T(128)S(1)} %pad_add_fusion.tab, bf16[1024,256]{1,0:T(8,128)(2,1)S(1)} %get-tuple-element.49.dm_ref, bf16[2048,256]{1,0:T(8,128)(2,1)S(1)} %get-tuple-element.50.w_ref, ...), custom_call_target="tpu_custom_call" | custom-call | tf_op jit(solution)/shard_map/back/pallas_call | solution.py:488
  94.3 4.2 %collective-permute-start.17 = (bf16[256,2176]{1,0:T(8,128)(2,1)S(1)}, bf16[256,2176]{1,0:T(8,128)(2,1)S(1)}, u32[]{:S(2)}, u32[]{:S(2)}) collective-permute-start(bf16[256,2176]{1,0:T(8,128)(2,1)S(1)} %get-tuple-element.60), channel_id=1, source_target_pairs={{0,2},{1,3},{2,0},{3,1},{4,6},{5,7},{6,4},{7,5},{8,10},{9,11},{10,... | collective-permute-start | bytes 3342344 | tf_op jit(solution)/shard_map/ppermute | solution.py:296
  98.5 6.2 %input.1 = (f32[4,512,256]{2,1,0:T(8,128)}, bf16[1024,256]{1,0:T(8,128)(2,1)S(1)}) custom-call(s32[34]{0:T(128)S(1)} %pad_add_fusion.tab, bf16[1024,2048]{1,0:T(8,128)(2,1)} %get-tuple-element.54.dp_ref, bf16[1024,128]{1,0:T(8,128)(2,1)S(1)} %get-tuple-element.55.dg_ref, bf16[512,2176]{1,0:T(8,128)(2,1)S(1)} %copy-done.1), custom_call_target="tpu_custom_call" | custom-call | tf_op jit(solution)/shard_map/input/pallas_call | solution.py:522
  104.7 0.9 collective-permute-start.16
  105.7 0.5 slice.116
  107.6 0.6 collective-permute-start.24
  108.2 0.6 add_multiply_fusion.4
  108.8 12.6 %collective-permute-done.24 = bf16[64,1152]{1,0:T(8,128)(2,1)S(1)} collective-permute-done((bf16[64,1152]{1,0:T(8,128)(2,1)S(1)}, bf16[64,1152]{1,0:T(8,128)(2,1)S(1)}, u32[]{:S(2)}, u32[]{:S(2)}) %collective-permute-start.24) | collective-permute-done | bytes 147488 | tf_op jit(solution)/shard_map/ppermute | solution.py:299
  121.9 1.3 collective-permute-start.18
  123.3 1.8 %collective-permute-done.25 = bf16[32,1152]{1,0:T(8,128)(2,1)S(1)} collective-permute-done((bf16[32,1152]{1,0:T(8,128)(2,1)S(1)}, bf16[32,1152]{1,0:T(8,128)(2,1)S(1)}, u32[]{:S(2)}, u32[]{:S(2)}) %collective-permute-start.25) | collective-permute-done | bytes 73760 | tf_op jit(solution)/shard_map/ppermute | solution.py:299
  125.2 6.0 %collective-permute-done.18 = bf16[128,2176]{1,0:T(8,128)(2,1)S(1)} collective-permute-done((bf16[128,2176]{1,0:T(8,128)(2,1)S(1)}, bf16[128,2176]{1,0:T(8,128)(2,1)S(1)}, u32[]{:S(2)}, u32[]{:S(2)}) %collective-permute-start.18) | collective-permute-done | bytes 557088 | tf_op jit(solution)/shard_map/ppermute | solution.py:299
  131.4 1.0 collective-permute-start.19
  132.4 4.4 %collective-permute-done.19 = bf16[64,2176]{1,0:T(8,128)(2,1)S(1)} collective-permute-done((bf16[64,2176]{1,0:T(8,128)(2,1)S(1)}, bf16[64,2176]{1,0:T(8,128)(2,1)S(1)}, u32[]{:S(2)}, u32[]{:S(2)}) %collective-permute-start.19) | collective-permute-done | bytes 278560 | tf_op jit(solution)/shard_map/ppermute | solution.py:299
  137.0 3.3 %collective-permute-start.20 = (bf16[32,2176]{1,0:T(8,128)(2,1)S(1)}, bf16[32,2176]{1,0:T(8,128)(2,1)S(1)}, u32[]{:S(2)}, u32[]{:S(2)}) collective-permute-start(bf16[32,2176]{1,0:T(8,128)(2,1)S(1)} %slice.167), channel_id=1, source_target_pairs={{0,8},{1,9},{2,10},{3,11},{4,12},{5,13},{6,14},{7,15},{8,0},{9,1},... | collective-permute-start | bytes 417800 | tf_op jit(solution)/shard_map/ppermute | solution.py:299
  140.3 0.7 add_multiply_fusion.1
  141.0 1.7 %collective-permute-done.20 = bf16[32,2176]{1,0:T(8,128)(2,1)S(1)} collective-permute-done((bf16[32,2176]{1,0:T(8,128)(2,1)S(1)}, bf16[32,2176]{1,0:T(8,128)(2,1)S(1)}, u32[]{:S(2)}, u32[]{:S(2)}) %collective-permute-start.20) | collective-permute-done | bytes 139296 | tf_op jit(solution)/shard_map/ppermute | solution.py:299
  142.9 0.6 add_multiply_fusion.2
  143.5 3.4 %collective-permute-done.21 = bf16[16,2176]{1,0:T(8,128)(2,1)S(1)} collective-permute-done((bf16[16,2176]{1,0:T(8,128)(2,1)S(1)}, bf16[16,2176]{1,0:T(8,128)(2,1)S(1)}, u32[]{:S(2)}, u32[]{:S(2)}) %collective-permute-start.21) | collective-permute-done | bytes 69664 | tf_op jit(solution)/shard_map/ppermute | solution.py:299
  147.0 0.8 add_multiply_fusion
  147.8 0.6 add_multiply_fusion.3
  (127 shorter events, 4.6 us)
Async XLA Ops:
  0.7 12.1 %copy-start.4 = (f32[8,8,256]{2,1,0:T(8,128)S(1)}, f32[8,8,256]{2,1,0:T(8,128)}, u32[]{:S(2)}) copy-start(f32[8,8,256]{2,1,0:T(8,128)} %param.27) | copy-start | bytes 196612
  0.7 12.1 %copy-start.9 = (f32[2,8,128]{2,1,0:T(8,128)S(1)}, f32[2,8,128]{2,1,0:T(8,128)}, u32[]{:S(2)}) copy-start(f32[2,8,128]{2,1,0:T(8,128)} %param.28) | copy-start | bytes 24580
  6.5 12.6 %collective-permute-start.5 = (bf16[16,2176]{1,0:T(8,128)(2,1)S(1)}, bf16[16,2176]{1,0:T(8,128)(2,1)S(1)}, u32[]{:S(2)}, u32[]{:S(2)}) collective-permute-start(bf16[16,2176]{1,0:T(8,128)(2,1)S(1)} %concatenate.53), channel_id=1, source_target_pairs={{0,16},{1,17},{2,18},{3,19},{4,20},{5,21},{6,22},{7,23},{8,24},{9,... | collective-permute-start | bytes 208904 | tf_op jit(solution)/shard_map/ppermute | solution.py:291
  11.5 37.0 %collective-permute-start.10 = (bf16[1024,256]{1,0:T(8,128)(2,1)}, bf16[1024,256]{1,0:T(8,128)(2,1)}, u32[]{:S(2)}, u32[]{:S(2)}) collective-permute-start(bf16[1024,256]{1,0:T(8,128)(2,1)} %bitcast.9), channel_id=1, source_target_pairs={{0,1},{1,0},{2,3},{3,2},{4,5},{5,4},{6,7},{7,6},{8,9},{9,8},{10,11... | collective-permute-start | bytes 1572872 | tf_op jit(solution)/shard_map/ppermute | solution.py:383
  13.4 3.7 %collective-permute-start = (bf16[16,1152]{1,0:T(8,128)(2,1)S(1)}, bf16[16,1152]{1,0:T(8,128)(2,1)S(1)}, u32[]{:S(2)}, u32[]{:S(2)}) collective-permute-start(bf16[16,1152]{1,0:T(8,128)(2,1)S(1)} %get-tuple-element.78), channel_id=1, source_target_pairs={{0,16},{1,17},{2,18},{3,19},{4,20},{5,21},{6,22},{7,23},{8,24},{9,... | collective-permute-start | bytes 110600 | tf_op jit(solution)/shard_map/ppermute | solution.py:291
  17.1 3.6 %collective-permute-start.1 = (bf16[32,1152]{1,0:T(8,128)(2,1)S(1)}, bf16[32,1152]{1,0:T(8,128)(2,1)S(1)}, u32[]{:S(2)}, u32[]{:S(2)}) collective-permute-start(bf16[32,1152]{1,0:T(8,128)(2,1)S(1)} %pad_maximum_fusion.5), channel_id=1, source_target_pairs={{0,8},{1,9},{2,10},{3,11},{4,12},{5,13},{6,14},{7,15},{8,0},{9,1},... | collective-permute-start | bytes 221192 | tf_op jit(solution)/shard_map/ppermute | solution.py:291
  19.1 5.0 %collective-permute-start.6 = (bf16[32,2176]{1,0:T(8,128)(2,1)S(1)}, bf16[32,2176]{1,0:T(8,128)(2,1)S(1)}, u32[]{:S(2)}, u32[]{:S(2)}) collective-permute-start(bf16[32,2176]{1,0:T(8,128)(2,1)S(1)} %pad_maximum_fusion.4), channel_id=1, source_target_pairs={{0,8},{1,9},{2,10},{3,11},{4,12},{5,13},{6,14},{7,15},{8,0},{9,1},... | collective-permute-start | bytes 417800 | tf_op jit(solution)/shard_map/ppermute | solution.py:291
  20.7 10.5 %collective-permute-start.2 = (bf16[64,1152]{1,0:T(8,128)(2,1)S(1)}, bf16[64,1152]{1,0:T(8,128)(2,1)S(1)}, u32[]{:S(2)}, u32[]{:S(2)}) collective-permute-start(bf16[64,1152]{1,0:T(8,128)(2,1)S(1)} %pad_maximum_fusion.3), channel_id=1, source_target_pairs={{0,4},{1,5},{2,3},{3,2},{4,0},{5,1},{6,7},{7,6},{8,12},{9,13},{10,... | collective-permute-start | bytes 442376 | tf_op jit(solution)/shard_map/ppermute | solution.py:291
  24.1 5.8 %collective-permute-start.7 = (bf16[64,2176]{1,0:T(8,128)(2,1)S(1)}, bf16[64,2176]{1,0:T(8,128)(2,1)S(1)}, u32[]{:S(2)}, u32[]{:S(2)}) collective-permute-start(bf16[64,2176]{1,0:T(8,128)(2,1)S(1)} %pad_maximum_fusion.2), channel_id=1, source_target_pairs={{0,4},{1,5},{2,3},{3,2},{4,0},{5,1},{6,7},{7,6},{8,12},{9,13},{10,... | collective-permute-start | bytes 835592 | tf_op jit(solution)/shard_map/ppermute | solution.py:291
  30.0 9.5 %collective-permute-start.8 = (bf16[128,2176]{1,0:T(8,128)(2,1)S(1)}, bf16[128,2176]{1,0:T(8,128)(2,1)S(1)}, u32[]{:S(2)}, u32[]{:S(2)}) collective-permute-start(bf16[128,2176]{1,0:T(8,128)(2,1)S(1)} %pad_maximum_fusion), channel_id=1, source_target_pairs={{0,1},{1,0},{2,6},{3,7},{4,5},{5,4},{6,2},{7,3},{8,9},{9,8},{10,14... | collective-permute-start | bytes 1671176 | tf_op jit(solution)/shard_map/ppermute | solution.py:291
  31.3 13.7 %collective-permute-start.3 = (bf16[128,1152]{1,0:T(8,128)(2,1)S(1)}, bf16[128,1152]{1,0:T(8,128)(2,1)S(1)}, u32[]{:S(2)}, u32[]{:S(2)}) collective-permute-start(bf16[128,1152]{1,0:T(8,128)(2,1)S(1)} %pad_maximum_fusion.1), channel_id=1, source_target_pairs={{0,1},{1,0},{2,6},{3,7},{4,5},{5,4},{6,2},{7,3},{8,9},{9,8},{10,14... | collective-permute-start | bytes 884744 | tf_op jit(solution)/shard_map/ppermute | solution.py:291
  31.6 16.7 %copy-start.16 = (s32[4,512]{1,0:T(4,128)S(1)}, s32[4,512]{1,0:T(4,128)}, u32[]{:S(2)}) copy-start(s32[4,512]{1,0:T(4,128)} %param.24) | copy-start | bytes 24580
  31.7 16.6 %copy-start.17 = (s32[4,512]{1,0:T(4,128)S(1)}, s32[4,512]{1,0:T(4,128)}, u32[]{:S(2)}) copy-start(s32[4,512]{1,0:T(4,128)} %param.23) | copy-start | bytes 24580
  31.7 16.9 %copy-start.15 = (f32[2,128]{1,0:T(2,128)S(1)}, f32[2,128]{1,0:T(2,128)}, u32[]{:S(2)}) copy-start(f32[2,128]{1,0:T(2,128)} %param.29) | copy-start | bytes 3076
  31.7 16.9 %copy-start = (bf16[4,512,256]{2,1,0:T(8,128)(2,1)S(1)}, bf16[4,512,256]{2,1,0:T(8,128)(2,1)}, u32[]{:S(2)}) copy-start(bf16[4,512,256]{2,1,0:T(8,128)(2,1)} %xo_ref.1) | copy-start | bytes 3145732
  39.5 9.0 %collective-permute-start.9 = (bf16[256,2176]{1,0:T(8,128)(2,1)S(1)}, bf16[256,2176]{1,0:T(8,128)(2,1)S(1)}, u32[]{:S(2)}, u32[]{:S(2)}) collective-permute-start(bf16[256,2176]{1,0:T(8,128)(2,1)S(1)} %constant_dynamic-update-slice_fusion.5.own_ref), channel_id=1, source_target_pairs={{0,2},{1,3},{2,0},{3,1},{4,6},{5,7},{6,4},{7,5},{8,10},{9,11},{10,... | collective-permute-start | bytes 3342344 | tf_op jit(solution)/shard_map/ppermute | solution.py:292
  45.7 11.5 %collective-permute-start.4 = (bf16[256,1152]{1,0:T(8,128)(2,1)}, bf16[256,1152]{1,0:T(8,128)(2,1)}, u32[]{:S(2)}, u32[]{:S(2)}) collective-permute-start(bf16[256,1152]{1,0:T(8,128)(2,1)} %constant_dynamic-update-slice_fusion.own_ref), channel_id=1, source_target_pairs={{0,2},{1,3},{2,0},{3,1},{4,6},{5,7},{6,4},{7,5},{8,10},{9,11},{10,... | collective-permute-start | bytes 1769480 | tf_op jit(solution)/shard_map/ppermute | solution.py:292
  67.7 2.1 %collective-permute-start.22 = (bf16[256,1152]{1,0:T(8,128)(2,1)S(1)}, bf16[256,1152]{1,0:T(8,128)(2,1)S(1)}, u32[]{:S(2)}, u32[]{:S(2)}) collective-permute-start(bf16[256,1152]{1,0:T(8,128)(2,1)S(1)} %get-tuple-element.62), channel_id=1, source_target_pairs={{0,2},{1,3},{2,0},{3,1},{4,6},{5,7},{6,4},{7,5},{8,10},{9,11},{10,... | collective-permute-start | bytes 1769480 | tf_op jit(solution)/shard_map/ppermute | solution.py:296
  69.9 37.7 %collective-permute-start.23 = (bf16[128,1152]{1,0:T(8,128)(2,1)S(1)}, bf16[128,1152]{1,0:T(8,128)(2,1)S(1)}, u32[]{:S(2)}, u32[]{:S(2)}) collective-permute-start(bf16[128,1152]{1,0:T(8,128)(2,1)S(1)} %slice.164), channel_id=1, source_target_pairs={{0,1},{1,0},{2,6},{3,7},{4,5},{5,4},{6,2},{7,3},{8,9},{9,8},{10,14... | collective-permute-start | bytes 884744 | tf_op jit(solution)/shard_map/ppermute | solution.py:299
  71.2 1.2 collective-permute-start.11
  72.3 3.4 %collective-permute-start.12 = (f32[8,256]{1,0:T(8,128)S(1)}, f32[8,256]{1,0:T(8,128)S(1)}, u32[]{:S(2)}, u32[]{:S(2)}) collective-permute-start(f32[8,256]{1,0:T(8,128)S(1)} %add.209), channel_id=1, source_target_pairs={{0,16},{1,17},{2,18},{3,19},{4,20},{5,21},{6,22},{7,23},{8,24},{9,... | collective-permute-start | bytes 24584 | tf_op jit(solution)/shard_map/ppermute | solution.py:306
  75.7 2.5 %collective-permute-start.13 = (f32[8,256]{1,0:T(8,128)S(1)}, f32[8,256]{1,0:T(8,128)S(1)}, u32[]{:S(2)}, u32[]{:S(2)}) collective-permute-start(f32[8,256]{1,0:T(8,128)S(1)} %add.210), channel_id=1, source_target_pairs={{0,8},{1,9},{2,10},{3,11},{4,12},{5,13},{6,14},{7,15},{8,0},{9,1},... | collective-permute-start | bytes 24584 | tf_op jit(solution)/shard_map/ppermute | solution.py:306
  78.2 2.5 %collective-permute-start.14 = (f32[8,256]{1,0:T(8,128)S(1)}, f32[8,256]{1,0:T(8,128)S(1)}, u32[]{:S(2)}, u32[]{:S(2)}) collective-permute-start(f32[8,256]{1,0:T(8,128)S(1)} %add.211), channel_id=1, source_target_pairs={{0,4},{1,5},{2,3},{3,2},{4,0},{5,1},{6,7},{7,6},{8,12},{9,13},{10,... | collective-permute-start | bytes 24584 | tf_op jit(solution)/shard_map/ppermute | solution.py:306
  80.8 24.9 %collective-permute-start.15 = (f32[8,256]{1,0:T(8,128)S(1)}, f32[8,256]{1,0:T(8,128)S(1)}, u32[]{:S(2)}, u32[]{:S(2)}) collective-permute-start(f32[8,256]{1,0:T(8,128)S(1)} %add.212), channel_id=1, source_target_pairs={{0,1},{1,0},{2,6},{3,7},{4,5},{5,4},{6,2},{7,3},{8,9},{9,8},{10,14... | collective-permute-start | bytes 24584 | tf_op jit(solution)/shard_map/ppermute | solution.py:306
  81.5 17.0 %copy-start.1 = (bf16[512,2176]{1,0:T(8,128)(2,1)S(1)}, bf16[512,2176]{1,0:T(8,128)(2,1)}, u32[]{:S(2)}) copy-start(bf16[512,2176]{1,0:T(8,128)(2,1)} %get-tuple-element.56.w_ref) | copy-start | bytes 6684676
  94.3 27.2 %collective-permute-start.17 = (bf16[256,2176]{1,0:T(8,128)(2,1)S(1)}, bf16[256,2176]{1,0:T(8,128)(2,1)S(1)}, u32[]{:S(2)}, u32[]{:S(2)}) collective-permute-start(bf16[256,2176]{1,0:T(8,128)(2,1)S(1)} %get-tuple-element.60), channel_id=1, source_target_pairs={{0,2},{1,3},{2,0},{3,1},{4,6},{5,7},{6,4},{7,5},{8,10},{9,11},{10,... | collective-permute-start | bytes 3342344 | tf_op jit(solution)/shard_map/ppermute | solution.py:296
  104.7 3.5 %copy-start.18 = (f32[2,128]{1,0:T(2,128)S(1)}, f32[2,128]{1,0:T(2,128)}, u32[]{:S(2)}) copy-start(f32[2,128]{1,0:T(2,128)} %param.39) | copy-start | bytes 3076
  104.7 3.5 %copy-start.19 = (f32[2,128]{1,0:T(2,128)S(1)}, f32[2,128]{1,0:T(2,128)}, u32[]{:S(2)}) copy-start(f32[2,128]{1,0:T(2,128)} %param.34) | copy-start | bytes 3076
  104.7 18.5 %collective-permute-start.16 = (bf16[1024,256]{1,0:T(8,128)(2,1)S(1)}, bf16[1024,256]{1,0:T(8,128)(2,1)S(1)}, u32[]{:S(2)}, u32[]{:S(2)}) collective-permute-start(bf16[1024,256]{1,0:T(8,128)(2,1)S(1)} %get-tuple-element.58), channel_id=1, source_target_pairs={{0,1},{1,0},{2,3},{3,2},{4,5},{5,4},{6,7},{7,6},{8,9},{9,8},{10,11... | collective-permute-start | bytes 1572872 | tf_op jit(solution)/shard_map/ppermute | solution.py:544
  107.5 14.0 %copy-start.2 = (f32[256,2176]{1,0:T(8,128)S(1)}, f32[256,2176]{1,0:T(8,128)}, u32[]{:S(2)}) copy-start(f32[256,2176]{1,0:T(8,128)} %get-tuple-element.59) | copy-start | bytes 6684676
  107.6 13.8 %collective-permute-start.24 = (bf16[64,1152]{1,0:T(8,128)(2,1)S(1)}, bf16[64,1152]{1,0:T(8,128)(2,1)S(1)}, u32[]{:S(2)}, u32[]{:S(2)}) collective-permute-start(bf16[64,1152]{1,0:T(8,128)(2,1)S(1)} %slice.166), channel_id=1, source_target_pairs={{0,4},{1,5},{2,3},{3,2},{4,0},{5,1},{6,7},{7,6},{8,12},{9,13},{10,... | collective-permute-start | bytes 442376 | tf_op jit(solution)/shard_map/ppermute | solution.py:299
  121.5 3.6 %collective-permute-start.25 = (bf16[32,1152]{1,0:T(8,128)(2,1)S(1)}, bf16[32,1152]{1,0:T(8,128)(2,1)S(1)}, u32[]{:S(2)}, u32[]{:S(2)}) collective-permute-start(bf16[32,1152]{1,0:T(8,128)(2,1)S(1)} %slice.168), channel_id=1, source_target_pairs={{0,8},{1,9},{2,10},{3,11},{4,12},{5,13},{6,14},{7,15},{8,0},{9,1},... | collective-permute-start | bytes 221192 | tf_op jit(solution)/shard_map/ppermute | solution.py:299
  121.9 9.3 %collective-permute-start.18 = (bf16[128,2176]{1,0:T(8,128)(2,1)S(1)}, bf16[128,2176]{1,0:T(8,128)(2,1)S(1)}, u32[]{:S(2)}, u32[]{:S(2)}) collective-permute-start(bf16[128,2176]{1,0:T(8,128)(2,1)S(1)} %slice.163), channel_id=1, source_target_pairs={{0,1},{1,0},{2,6},{3,7},{4,5},{5,4},{6,2},{7,3},{8,9},{9,8},{10,14... | collective-permute-start | bytes 1671176 | tf_op jit(solution)/shard_map/ppermute | solution.py:299
  123.3 8.0 %copy-start.21 = (f32[4,512,256]{2,1,0:T(8,128)}, f32[4,512,256]{2,1,0:T(8,128)S(1)}, u32[]{:S(2)}) copy-start(f32[4,512,256]{2,1,0:T(8,128)S(1)} %convert_dynamic-update-slice_fusion) | copy-start | bytes 6291460
  125.1 7.3 %collective-permute-start.26 = (bf16[16,1152]{1,0:T(8,128)(2,1)S(1)}, bf16[16,1152]{1,0:T(8,128)(2,1)S(1)}, u32[]{:S(2)}, u32[]{:S(2)}) collective-permute-start(bf16[16,1152]{1,0:T(8,128)(2,1)S(1)} %slice.170), channel_id=1, source_target_pairs={{0,16},{1,17},{2,18},{3,19},{4,20},{5,21},{6,22},{7,23},{8,24},{9,... | collective-permute-start | bytes 110600 | tf_op jit(solution)/shard_map/ppermute | solution.py:299
  131.4 9.0 %copy-start.7 = (f32[8,8,256]{2,1,0:T(8,128)S(1)}, f32[8,8,256]{2,1,0:T(8,128)}, u32[]{:S(2)}) copy-start(f32[8,8,256]{2,1,0:T(8,128)} %param.37) | copy-start | bytes 196612
  131.4 9.0 %copy-start.8 = (f32[8,8,256]{2,1,0:T(8,128)S(1)}, f32[8,8,256]{2,1,0:T(8,128)}, u32[]{:S(2)}) copy-start(f32[8,8,256]{2,1,0:T(8,128)} %param.32) | copy-start | bytes 196612
  131.4 5.5 %collective-permute-start.19 = (bf16[64,2176]{1,0:T(8,128)(2,1)S(1)}, bf16[64,2176]{1,0:T(8,128)(2,1)S(1)}, u32[]{:S(2)}, u32[]{:S(2)}) collective-permute-start(bf16[64,2176]{1,0:T(8,128)(2,1)S(1)} %slice.165), channel_id=1, source_target_pairs={{0,4},{1,5},{2,3},{3,2},{4,0},{5,1},{6,7},{7,6},{8,12},{9,13},{10,... | collective-permute-start | bytes 835592 | tf_op jit(solution)/shard_map/ppermute | solution.py:299
  136.9 6.0 %copy-start.11 = (f32[2,8,128]{2,1,0:T(8,128)S(1)}, f32[2,8,128]{2,1,0:T(8,128)}, u32[]{:S(2)}) copy-start(f32[2,8,128]{2,1,0:T(8,128)} %param.38) | copy-start | bytes 24580
  136.9 6.0 %copy-start.12 = (f32[2,8,128]{2,1,0:T(8,128)S(1)}, f32[2,8,128]{2,1,0:T(8,128)}, u32[]{:S(2)}) copy-start(f32[2,8,128]{2,1,0:T(8,128)} %param.33) | copy-start | bytes 24580
  136.9 10.0 %copy-start.3 = (f32[16,2048]{1,0:T(8,128)S(1)}, f32[16,2048]{1,0:T(8,128)}, u32[]{:S(2)}) copy-start(f32[16,2048]{1,0:T(8,128)} %param.25) | copy-start | bytes 393220
  136.9 10.0 %copy-start.5 = (f32[16,2048]{1,0:T(8,128)S(1)}, f32[16,2048]{1,0:T(8,128)}, u32[]{:S(2)}) copy-start(f32[16,2048]{1,0:T(8,128)} %param.35) | copy-start | bytes 393220
  137.0 10.0 %copy-start.6 = (f32[16,2048]{1,0:T(8,128)S(1)}, f32[16,2048]{1,0:T(8,128)}, u32[]{:S(2)}) copy-start(f32[16,2048]{1,0:T(8,128)} %param.30) | copy-start | bytes 393220
  137.0 5.8 %collective-permute-start.20 = (bf16[32,2176]{1,0:T(8,128)(2,1)S(1)}, bf16[32,2176]{1,0:T(8,128)(2,1)S(1)}, u32[]{:S(2)}, u32[]{:S(2)}) collective-permute-start(bf16[32,2176]{1,0:T(8,128)(2,1)S(1)} %slice.167), channel_id=1, source_target_pairs={{0,8},{1,9},{2,10},{3,11},{4,12},{5,13},{6,14},{7,15},{8,0},{9,1},... | collective-permute-start | bytes 417800 | tf_op jit(solution)/shard_map/ppermute | solution.py:299
  141.0 6.8 %copy-start.10 = (f32[16,16]{1,0:T(8,128)S(1)}, f32[16,16]{1,0:T(8,128)}, u32[]{:S(2)}) copy-start(f32[16,16]{1,0:T(8,128)} %param.26) | copy-start | bytes 3076
  141.0 6.8 %copy-start.13 = (f32[16,16]{1,0:T(8,128)S(1)}, f32[16,16]{1,0:T(8,128)}, u32[]{:S(2)}) copy-start(f32[16,16]{1,0:T(8,128)} %param.36) | copy-start | bytes 3076
  141.0 6.8 %copy-start.14 = (f32[16,16]{1,0:T(8,128)S(1)}, f32[16,16]{1,0:T(8,128)}, u32[]{:S(2)}) copy-start(f32[16,16]{1,0:T(8,128)} %param.31) | copy-start | bytes 3076
  142.8 4.1 %collective-permute-start.21 = (bf16[16,2176]{1,0:T(8,128)(2,1)S(1)}, bf16[16,2176]{1,0:T(8,128)(2,1)S(1)}, u32[]{:S(2)}, u32[]{:S(2)}) collective-permute-start(bf16[16,2176]{1,0:T(8,128)(2,1)S(1)} %slice.169), channel_id=1, source_target_pairs={{0,16},{1,17},{2,18},{3,19},{4,20},{5,21},{6,22},{7,23},{8,24},{9,... | collective-permute-start | bytes 208904 | tf_op jit(solution)/shard_map/ppermute | solution.py:299
  (1 other events, 1.6 us)

commit v2 on v1

--- a/solution.py
+++ b/solution.py
@@ -49,7 +49,7 @@
 
 
 def first_kernel(
-    tab, own_ref, oth_ref, xo_ref, xr_ref, meta_ref, ga_ref, gs_ref, gate_ref, w_ref, cnt_ref, xt_ref
+    tab, own_ref, oth_ref, xo_ref, xr_ref, meta_ref, ga_ref, gs_ref, gate_ref, w_ref, xt_ref
 ):
     pairs = own_ref.shape[0] // BLOCK
     half = xo_ref.shape[-1]
@@ -65,14 +65,6 @@
             w_ref[rows16(row), :] = src[rows16(place * BLOCK), :]
 
         each_block(tab, pairs, put)
-        side_cols = w_ref[:, wide:].astype(f32)
-        lane = lax.broadcasted_iota(jnp.int32, side_cols.shape, 1)
-        base = 2 * experts
-        scale = jnp.where(
-            lane == base, 1.0, jnp.where(lane == base + 1, 256.0, jnp.where(lane == base + 2, 65536.0, 0.0))
-        )
-        total = jnp.sum(jnp.sum(side_cols * scale, axis=1, keepdims=True), axis=0, keepdims=True)
-        cnt_ref[...] = jnp.broadcast_to(total, cnt_ref.shape)
 
     x = jnp.concatenate([xo_ref[0], xr_ref[...]], axis=1)
     xt_ref[...] = x.T
@@ -89,11 +81,11 @@
     for k in range(experts):
         cols = pl.ds(k * hidden, hidden)
         pre = dot(x, w_ref[:, cols])
-        s = sigmoid(pre)
-        a = pre * s
-        g = gate[:, k : k + 1]
-        ga_ref[:, cols] = (g * a).astype(bf16)
-        gs_ref[:, cols] = (g * (s + a * (1.0 - s))).astype(bf16)
+        low = 0.5 * pre
+        up = 1.0 + jnp.tanh(low)
+        scaled = (0.5 * gate[:, k : k + 1]) * up
+        ga_ref[:, cols] = (scaled * pre).astype(bf16)
+        gs_ref[:, cols] = (scaled * (1.0 + pre - low * up)).astype(bf16)
 
 
 def tab_experts(wide, hidden):
@@ -101,28 +93,13 @@
 
 
 def second_kernel(
-    tab,
-    own_ref,
-    oth_ref,
-    ga_ref,
-    meta_ref,
-    cnt_ref,
-    to_ref,
-    w_ref,
-    dm_ref,
-    keep_ref,
-    send_ref,
-    side_ref,
-    ti_ref,
-    gwo_ref,
-    gti_ref,
+    tab, own_ref, oth_ref, ga_ref, meta_ref, to_ref, w_ref, dm_ref, gti_ref, side_ref, ti_ref, cnt_ref
 ):
     pairs = own_ref.shape[0] // BLOCK
     step = pl.program_id(0)
     out_cols = dm_ref.shape[1]
     hidden = pairs * BLOCK
-    experts = w_ref.shape[0] // hidden
-    part = experts // 2
+    part = w_ref.shape[0] // hidden // 2
 
     @pl.when(step == 0)
     def _():
@@ -134,17 +111,22 @@
             row = (2 * j + core) * BLOCK
             upper = jnp.concatenate([a0[:8], a1[:8]], axis=0).astype(bf16)
             lower = jnp.concatenate([a0[8:], a1[8:]], axis=0).astype(bf16)
+            at = part * out_cols
             for k in range(part):
                 cols = slice(k * out_cols, (k + 1) * out_cols)
                 w_ref[rows16(k * hidden + row), :] = upper[:, cols]
                 w_ref[rows16((k + part) * hidden + row), :] = lower[:, cols]
-            ti_ref[rows16(row), 0:LANES] = upper[:, part * out_cols :]
-            ti_ref[rows16(row), LANES : 2 * LANES] = lower[:, part * out_cols :]
-
+            ti_ref[rows16(row), 0:LANES] = upper[:, at : at + LANES]
+            ti_ref[rows16(row), LANES : 2 * LANES] = lower[:, at : at + LANES]
+            return (a0 + a1)[:, at + LANES :]
+
+        digits = jnp.zeros((BLOCK, LANES), f32)
         for j in range(pairs // 2):
-            put(0, j)
-            put(1, j)
-        gwo_ref[...] = jnp.zeros_like(gwo_ref)
+            digits = digits + put(0, j) + put(1, j)
+        lane = lax.broadcasted_iota(jnp.int32, digits.shape, 1)
+        scale = jnp.where(lane == 0, 1.0, jnp.where(lane == 1, 256.0, jnp.where(lane == 2, 65536.0, 0.0)))
+        total = jnp.sum(jnp.sum(digits * scale, axis=1, keepdims=True), axis=0, keepdims=True)
+        cnt_ref[...] = jnp.broadcast_to(total, cnt_ref.shape)
         gti_ref[...] = jnp.zeros_like(gti_ref)
         side_ref[...] = jnp.zeros_like(side_ref)
 
@@ -161,32 +143,47 @@
     act = jnp.where(picked, act, 0.0)
     chosen = jnp.sum(act * head, axis=1, keepdims=True)
     soft = jnp.maximum(chosen, 0.0) + jnp.log1p(jnp.exp(-jnp.abs(chosen)))
-    loss = jnp.sum(valid * (soft - label * chosen), axis=0, keepdims=True)
+    loss = jnp.sum(valid * (soft - label * chosen), axis=0, keepdims=True) / count
     dlogit = (valid * (sigmoid(chosen) - label) / count).astype(bf16).astype(f32)
     slope = s * (1.0 + tpre * (1.0 - s))
     dtpre = jnp.where(picked, dlogit * head * slope, 0.0).astype(bf16)
-    side_ref[0:1, :] += jnp.sum(dlogit * act, axis=0, keepdims=True)
-    side_ref[1:2, :] += jnp.broadcast_to(loss, (1, side_ref.shape[1]))
+    width = head.shape[1]
+    side_ref[0:1, 0:width] += jnp.sum(dlogit * act, axis=0, keepdims=True)
+    side_ref[0:1, width : width + LANES] += jnp.broadcast_to(loss, (1, LANES))
     gti_ref[...] += t_dot(mixed, dtpre)
-    dmixed = dot_t(dtpre, ti_ref[...]).astype(bf16)
-    dm_ref[...] = dmixed
-    for k in range(experts):
-        gwo_ref[k] += t_dot(ga_ref[:, pl.ds(k * hidden, hidden)], dmixed)
-
-    @pl.when(step == pl.num_programs(0) - 1)
-    def _():
+    dm_ref[...] = dot_t(dtpre, ti_ref[...]).astype(bf16)
+
+
+def outer_kernel(tab, dm_ref, ga_ref, gb_ref, gti_ref, side_ref, keep_ref, send_ref, gwo_ref):
+    pairs = keep_ref.shape[0] // BLOCK
+    step = pl.program_id(0)
+    out_cols = dm_ref.shape[1]
+    gwo_ref[0] = t_dot(ga_ref[...], dm_ref[...])
+    gwo_ref[1] = t_dot(gb_ref[...], dm_ref[...])
+
+    def pack(above, below, cols):
         def put(side, place, rr, ff):
             dst = keep_ref if side == 0 else send_ref
             row = pl.ds(pl.multiple_of(rr * BLOCK + ff * 8, 8), 8)
-            for k in range(part):
-                cols = slice(k * out_cols, (k + 1) * out_cols)
-                tile = jnp.concatenate([gwo_ref[k, row, :], gwo_ref[k + part, row, :]], axis=0)
-                dst[rows16(place * BLOCK), cols] = tile.astype(dst.dtype)
-            tile = gti_ref[row, :]
-            tile = jnp.concatenate([tile[:, :LANES], tile[:, LANES:]], axis=0)
-            dst[rows16(place * BLOCK), part * out_cols :] = tile.astype(dst.dtype)
+            tile = jnp.concatenate([above(row), below(row)], axis=0)
+            dst[rows16(place * BLOCK), cols] = tile.astype(dst.dtype)
 
         each_block(tab, pairs, put)
+
+    pack(
+        lambda row: gwo_ref[0, row, :],
+        lambda row: gwo_ref[1, row, :],
+        pl.ds(pl.multiple_of(step * out_cols, out_cols), out_cols),
+    )
+
+    @pl.when(step == 0)
+    def _():
+        at = keep_ref.shape[1] - LANES
+        pack(
+            lambda row: gti_ref[row, 0:LANES],
+            lambda row: gti_ref[row, LANES : 2 * LANES],
+            slice(at, at + LANES),
+        )
 
 
 def back_kernel(
@@ -286,25 +283,49 @@
         return out + (low << self.outer) + (high << (self.outer + 1))
 
 
-def gather(cube, block):
+def gather_two(cube, block_a, block_b):
     for pairs in cube.steps:
-        block = jnp.concatenate([block, lax.ppermute(block, both, pairs)], axis=0)
-    return block, lax.ppermute(block, both, cube.core)
-
-
-def scatter(cube, keep, send):
-    total = keep + lax.ppermute(send, both, cube.core).astype(f32)
-    for pairs in reversed(cube.steps):
-        half = total.shape[0] // 2
-        got = lax.ppermute(total[half:].astype(bf16), both, pairs)
-        total = total[:half] + got.astype(f32)
-    return total
-
-
-def sum_all(cube, part):
-    for pairs in [cube.core] + cube.steps:
-        part = part + lax.ppermute(part, both, pairs)
-    return part
+        got = lax.ppermute(block_a, both, pairs)
+        block_a = jnp.concatenate([block_a, got], axis=0)
+        got = lax.ppermute(after(block_b, got), both, pairs)
+        block_b = jnp.concatenate([block_b, got], axis=0)
+    oth_a = lax.ppermute(block_a, both, cube.core)
+    return block_a, oth_a, block_b, lax.ppermute(block_b, both, cube.core)
+
+
+def after(values, *earlier):
+    return lax.optimization_barrier((values,) + earlier)[0]
+
+
+def fold(total, got):
+    rows = got.shape[0]
+    total = total[:rows] + got.astype(f32)
+    half = rows // 2
+    return total, total[half:].astype(bf16)
+
+
+def split_two(values):
+    high = lax.reduce_precision(values, 8, 7)
+    low = lax.reduce_precision(values - high, 8, 7)
+    return jnp.concatenate([high, low], axis=0).astype(bf16)
+
+
+def join_two(rows):
+    rows = rows.astype(f32)
+    half = rows.shape[0] // 2
+    return rows[:half] + rows[half:]
+
+
+def beside(part, side):
+    mine = split_two(side)
+    return jnp.concatenate([part, mine], axis=0), join_two(mine)
+
+
+def fold_beside(total, side, got):
+    rows = got.shape[0] - 8
+    total, part = fold(total, got[:rows])
+    message, side = beside(part, side + join_two(got[rows:]))
+    return total, message, side
 
 
 def renew(weight, velocity, average, gradient, rate):
@@ -319,11 +340,19 @@
 
 
 def whole(dims):
+    return pl.BlockSpec(dims, lambda i, tab: (0,) * len(dims), pipeline_mode=pl.Buffered(1))
+
+
+def whole_out(dims):
     return pl.BlockSpec(dims, lambda i, tab: (0,) * len(dims))
 
 
-def params(limit=48):
+def params(limit):
     return pltpu.CompilerParams(vmem_limit_bytes=limit << 20)
+
+
+def cost(flops):
+    return pl.CostEstimate(flops=flops, bytes_accessed=8 << 20, transcendentals=0)
 
 
 def on_device(
@@ -367,8 +396,9 @@
     own_valid = own_half(valid_mask, f)
     ones = jnp.sum(own_valid)
     digits = jnp.stack([ones % 256, (ones // 256) % 256, ones // 65536]).astype(bf16)
-    extra = jnp.zeros((first_rows, LANES - tasks * experts), bf16).at[0, :3].set(digits)
-    block_a = jnp.concatenate([expert_in.astype(bf16), gate_in.astype(bf16), extra], axis=1)
+    extra = jnp.zeros((2 * second_rows, LANES), bf16).at[0, :3].set(digits)
+    empty = jnp.zeros((first_rows, LANES - tasks * experts), bf16)
+    block_a = jnp.concatenate([expert_in.astype(bf16), gate_in.astype(bf16), empty], axis=1)
     block_b = jnp.concatenate(
         [
             expert_out.astype(bf16)
@@ -376,13 +406,13 @@
             .transpose(0, 2, 1, 3)
             .reshape(2 * second_rows, part * out_cols),
             tower_in.astype(bf16).reshape(2 * second_rows, tower_cols),
+            extra,
         ],
         axis=1,
     )
-    x_send = own_half(inputs, 1 - f).reshape(rows_own, width)
+    x_send = own_half(after(inputs, block_a), 1 - f).reshape(rows_own, width)
     x_got = lax.ppermute(x_send, "field", [(0, 1), (1, 0)])
-    own_a, oth_a = gather(cube, block_a)
-    own_b, oth_b = gather(cube, block_b)
+    own_a, oth_a, own_b, oth_b = gather_two(cube, block_a, block_b)
 
     pairs = 2 * width // BLOCK // 2
     fit = first_rows == BLOCK
@@ -411,8 +441,9 @@
     )
     a_cols, b_cols = wide + LANES, part * out_cols + LANES
     half = width
-
-    ga, gs, gate, first_w, count, x_t = pl.pallas_call(
+    heads = tasks * tower_cols
+
+    ga, gs, gate, first_w, x_t = pl.pallas_call(
         first_kernel,
         grid_spec=pltpu.PrefetchScalarGridSpec(
             num_scalar_prefetch=1,
@@ -428,8 +459,7 @@
                 pl.BlockSpec((tile, wide), lambda i, tab: (i, 0)),
                 pl.BlockSpec((tile, wide), lambda i, tab: (i, 0)),
                 pl.BlockSpec((tile, LANES), lambda i, tab: (i, 0)),
-                whole((2 * half, a_cols)),
-                whole((8, LANES)),
+                whole_out((2 * half, a_cols)),
                 pl.BlockSpec((2 * width, tile), lambda i, tab: (0, i)),
             ],
         ),
@@ -438,52 +468,47 @@
             shape((rows_own, wide), bf16),
             shape((rows_own, LANES), f32),
             shape((2 * half, a_cols), bf16),
-            shape((8, LANES), f32),
             shape((2 * width, rows_own), bf16),
         ],
-        compiler_params=params(),
+        compiler_params=params(24),
+        cost_estimate=cost(4 * rows_own * 2 * width * a_cols),
         name="first",
     )(tab, own_a, oth_a, inputs, x_got, meta)
 
-    head = jnp.broadcast_to(
-        tower_out.astype(bf16).astype(f32).reshape(1, tasks * tower_cols), (8, tasks * tower_cols)
-    )
-    second_w, dmixed, keep_b, send_b, side = pl.pallas_call(
+    head = jnp.broadcast_to(tower_out.astype(bf16).astype(f32).reshape(1, heads), (8, heads))
+    second_w, dmixed, grad_ti, side = pl.pallas_call(
         second_kernel,
         grid_spec=pltpu.PrefetchScalarGridSpec(
             num_scalar_prefetch=1,
             grid=(micro,),
             in_specs=[
-                whole((half, b_cols)),
-                whole((half, b_cols)),
+                whole((half, b_cols + LANES)),
+                whole((half, b_cols + LANES)),
                 pl.BlockSpec((tile, wide), lambda i, tab: (i, 0)),
                 pl.BlockSpec((1, 8, tile), lambda i, tab: (i, 0, 0)),
-                whole((8, LANES)),
-                whole((8, tasks * tower_cols)),
+                whole((8, heads)),
             ],
             out_specs=[
-                whole((wide, out_cols)),
+                whole_out((wide, out_cols)),
                 pl.BlockSpec((tile, out_cols), lambda i, tab: (i, 0)),
-                whole((half, b_cols)),
-                whole((half, b_cols)),
-                whole((8, tasks * tower_cols)),
+                whole_out((out_cols, heads)),
+                whole_out((8, b_cols)),
             ],
             scratch_shapes=[
-                pltpu.VMEM((out_cols, tasks * tower_cols), bf16),
-                pltpu.VMEM((experts, hidden, out_cols), f32),
-                pltpu.VMEM((out_cols, tasks * tower_cols), f32),
+                pltpu.VMEM((out_cols, heads), bf16),
+                pltpu.VMEM((8, LANES), f32),
             ],
         ),
         out_shape=[
             shape((wide, out_cols), bf16),
             shape((rows_own, out_cols), bf16),
-            shape((half, b_cols), f32),
-            shape((half, b_cols), sent),
-            shape((8, tasks * tower_cols), f32),
+            shape((out_cols, heads), f32),
+            shape((8, b_cols), f32),
         ],
-        compiler_params=params(),
+        compiler_params=params(24),
+        cost_estimate=cost(4 * rows_own * wide * out_cols),
         name="second",
-    )(tab, own_b, oth_b, ga, meta, count, head)
+    )(tab, own_b, oth_b, ga, meta, head)
 
     dpre, dgate, keep_a, send_a = pl.pallas_call(
         back_kernel,
@@ -500,9 +525,9 @@
             ],
             out_specs=[
                 pl.BlockSpec((rows_own, hidden), lambda i, tab: (0, i)),
-                whole((rows_own, LANES)),
-                whole((half, a_cols)),
-                whole((half, a_cols)),
+                whole_out((rows_own, LANES)),
+                whole_out((half, a_cols)),
+                whole_out((half, a_cols)),
             ],
             scratch_shapes=[
                 pltpu.VMEM((rows_own, LANES), f32),
@@ -515,10 +540,43 @@
             shape((half, a_cols), f32),
             shape((half, a_cols), sent),
         ],
-        compiler_params=params(),
+        compiler_params=params(24),
+        cost_estimate=cost(6 * rows_own * 2 * width * a_cols),
         name="back",
     )(tab, dmixed, second_w, ga, gs, x_t, gate)
 
+    order = [cube.core] + cube.steps[::-1]
+    if not fit:
+        keep_a, send_a = unsorted(keep_a, send_a, rows_a)
+    got_a = lax.ppermute(send_a, both, order[0])
+    keep_b, send_b = pl.pallas_call(
+        outer_kernel,
+        grid_spec=pltpu.PrefetchScalarGridSpec(
+            num_scalar_prefetch=1,
+            grid=(part,),
+            in_specs=[
+                whole((rows_own, out_cols)),
+                pl.BlockSpec((rows_own, hidden), lambda i, tab: (0, i)),
+                pl.BlockSpec((rows_own, hidden), lambda i, tab: (0, i + part)),
+                whole((out_cols, heads)),
+                whole((8, b_cols)),
+            ],
+            out_specs=[whole_out((half, b_cols)), whole_out((half, b_cols))],
+            scratch_shapes=[pltpu.VMEM((2, hidden, out_cols), f32)],
+        ),
+        out_shape=[shape((half, b_cols), f32), shape((half, b_cols), sent)],
+        compiler_params=params(16),
+        cost_estimate=cost(4 * rows_own * wide * out_cols),
+        name="outer",
+    )(tab, after(dmixed, dgate), ga, ga, grad_ti, side)
+
+    if not fit:
+        keep_b, send_b = unsorted(keep_b, send_b, rows_b)
+    side = side[:4]
+    message, side = beside(after(send_b, got_a), side)
+    sum_a, next_a = fold(keep_a, after(got_a, keep_b))
+    got_a = lax.ppermute(next_a, both, order[1])
+    got_b = lax.ppermute(message, both, order[0])
     grad_keep, grad_send = pl.pallas_call(
         input_kernel,
         grid_spec=pltpu.PrefetchScalarGridSpec(
@@ -538,20 +596,25 @@
             shape((micro, rows_dev, width), f32),
             shape((rows_own, width), bf16),
         ],
-        compiler_params=params(),
+        compiler_params=params(16),
+        cost_estimate=cost(4 * rows_own * 2 * width * a_cols),
         name="input",
-    )(tab, dpre, dgate, first_w)
-    grad_got = lax.ppermute(grad_send, "field", [(0, 1), (1, 0)])
+    )(tab, dpre, after(dgate, next_a), first_w)
+    sum_b, message, side = fold_beside(keep_b, side, after(got_b, grad_send))
+    for at in range(1, len(order)):
+        if at == 2:
+            grad_got = lax.ppermute(after(grad_send, got_a), "field", [(0, 1), (1, 0)])
+        sum_a, next_a = fold(sum_a, got_a)
+        got_b = lax.ppermute(after(message, got_a), both, order[at])
+        if at + 1 < len(order):
+            got_a = lax.ppermute(next_a, both, order[at + 1])
+            sum_b, message, side = fold_beside(sum_b, side, got_b)
+    rows = got_b.shape[0] - 8
+    sum_b = sum_b[:rows] + got_b[:rows].astype(f32)
+    side = side + join_two(got_b[rows:])
     input_grad = lax.dynamic_update_slice_in_dim(
         grad_keep, grad_got.astype(f32).reshape(micro, tile, width), (1 - f) * tile, 1
     )
-
-    if not fit:
-        keep_b, send_b = unsorted(keep_b, send_b, rows_b)
-        keep_a, send_a = unsorted(keep_a, send_a, rows_a)
-    sum_b = scatter(cube, keep_b, send_b)
-    sum_a = scatter(cube, keep_a, send_a)
-    side = sum_all(cube, side)
 
     second_sum = (
         sum_b[:, : part * out_cols]
@@ -564,7 +627,7 @@
         sum_a[:, wide : wide + tasks * experts],
         second_sum,
         sum_b[:, part * out_cols :].reshape(tasks, second_rows, tower_cols),
-        side[0].reshape(tasks, tower_cols),
+        side[0, :heads].reshape(tasks, tower_cols),
     )
     weights = (expert_in, gate_in, expert_out, tower_in, tower_out)
     velocities = (
@@ -582,7 +645,7 @@
         average_tower_out,
     )
     scale_root = math.sqrt(total_rows)
-    results = [side[1, 0] / count[0, 0], input_grad]
+    results = [side[0, heads], input_grad]
     for at in range(5):
         results.extend(
             renew(weights[at], velocities[at], averages[at], gradients[at], rate_bases[at] * scale_root)

time: 150 us -> 120 us (0.80)
  the two profiles are of different devices: /device:TPU:1 before, /device:TPU:0 now
where the time goes in v2:
time: 120 us
  waiting for transfers between devices  50 us (42%)
  Pallas kernels  31.6 us (26%)
  starting transfers between devices  22.5 us (19%)
  other arithmetic  7.14 us (6%)
  local copies, waits for them, and re-layouts  4.49 us (4%)
  between operations  4.07 us (3%)
    ppermute x3, waiting for transfers between devices, on_device(): got_a = lax.ppermute(next_a, both, order[at + 1])  14.1 us
    ppermute x4, waiting for transfers between devices, gather_two(): got = lax.ppermute(block_a, both, pairs)  12.3 us
    ppermute x4, waiting for transfers between devices, gather_two(): got = lax.ppermute(after(block_b, got), both, pairs)  10.5 us
    pallas_call x1, Pallas kernels, on_device(): pl.pallas_call(back_kernel, grid_spec=pltpu.PrefetchScalarGridSpec(num_sc...  9.95 us
    ppermute x4, waiting for transfers between devices, on_device(): got_b = lax.ppermute(after(message, got_a), both, order[at])  9.56 us
    pallas_call x1, Pallas kernels, on_device(): pl.pallas_call(first_kernel, grid_spec=pltpu.PrefetchScalarGridSpec(num_s...  7.9 us
    ppermute x4, starting transfers between devices, gather_two(): got = lax.ppermute(block_a, both, pairs)  7.81 us
    pallas_call x1, Pallas kernels, on_device(): pl.pallas_call(second_kernel, grid_spec=pltpu.PrefetchScalarGridSpec(num_...  5.84 us
  transfers between devices with their start and end apart: 22, of which 10 were waited for; matrix products, arithmetic and copies ran while one was open for 7% of the time, Pallas kernels for 13%

profile of v2, /device:TPU:0, one launch (start us, length us, event | category | flops | bytes accessed | tf_op | source)
XLA Modules:
  0.0 119.8 jit_solution(4078707614981954347)
XLA Ops:
  0.7 1.0 convert_element_type.107
  1.7 0.7 convert_element_type.108
  2.4 0.1 concatenate.89
  2.5 4.0 %collective-permute-start = (bf16[16,2176]{1,0:T(8,128)(2,1)S(1)}, bf16[16,2176]{1,0:T(8,128)(2,1)S(1)}, u32[]{:S(2)}, u32[]{:S(2)}) collective-permute-start(bf16[16,2176]{1,0:T(8,128)(2,1)S(1)} %concatenate.89), channel_id=1, source_target_pairs={{0,16},{1,17},{2,18},{3,19},{4,20},{5,21},{6,22},{7,23},{8,24},{9,... | collective-permute-start | bytes 208904 | tf_op jit(solution)/shard_map/ppermute | solution.py:288
  6.5 1.9 %constant_dynamic-slice_fusion = bf16[4,256,256]{2,1,0:T(8,128)(2,1)} fusion(bf16[4,512,256]{2,1,0:T(8,128)(2,1)} %xo_ref.1, s32[]{:T(128)S(6)} %select_n.70), kind=kLoop, calls=%fused_computation.117 | loop fusion | bytes 1048580 | tf_op jit(solution)/shard_map/dynamic_slice | solution.py:394
  8.4 1.5 %collective-permute-start.10 = (bf16[1024,256]{1,0:T(8,128)(2,1)}, bf16[1024,256]{1,0:T(8,128)(2,1)}, u32[]{:S(2)}, u32[]{:S(2)}) collective-permute-start(bf16[1024,256]{1,0:T(8,128)(2,1)} %bitcast.9), channel_id=1, source_target_pairs={{0,1},{1,0},{2,3},{3,2},{4,5},{5,4},{6,7},{7,6},{8,9},{9,8},{10,11... | collective-permute-start | bytes 1572872 | tf_op jit(solution)/shard_map/ppermute | solution.py:414
  9.9 0.6 dynamic-slice_convert_fusion.2
  13.7 1.6 %collective-permute-start.2 = (bf16[32,2176]{1,0:T(8,128)(2,1)S(1)}, bf16[32,2176]{1,0:T(8,128)(2,1)S(1)}, u32[]{:S(2)}, u32[]{:S(2)}) collective-permute-start(bf16[32,2176]{1,0:T(8,128)(2,1)S(1)} %pad_maximum_fusion.7), channel_id=1, source_target_pairs={{0,8},{1,9},{2,10},{3,11},{4,12},{5,13},{6,14},{7,15},{8,0},{9,1},... | collective-permute-start | bytes 417800 | tf_op jit(solution)/shard_map/ppermute | solution.py:288
  15.3 0.3 collective-permute-start.1
  15.6 4.9 %collective-permute-done.1 = bf16[16,1280]{1,0:T(8,128)(2,1)S(1)} collective-permute-done((bf16[16,1280]{1,0:T(8,128)(2,1)S(1)}, bf16[16,1280]{1,0:T(8,128)(2,1)S(1)}, u32[]{:S(2)}, u32[]{:S(2)}) %collective-permute-start.1) | collective-permute-done | bytes 40992 | tf_op jit(solution)/shard_map/ppermute | solution.py:290
  20.6 1.6 %collective-permute-start.4 = (bf16[64,2176]{1,0:T(8,128)(2,1)S(1)}, bf16[64,2176]{1,0:T(8,128)(2,1)S(1)}, u32[]{:S(2)}, u32[]{:S(2)}) collective-permute-start(bf16[64,2176]{1,0:T(8,128)(2,1)S(1)} %pad_maximum_fusion.4), channel_id=1, source_target_pairs={{0,4},{1,5},{2,3},{3,2},{4,0},{5,1},{6,7},{7,6},{8,12},{9,13},{10,... | collective-permute-start | bytes 835592 | tf_op jit(solution)/shard_map/ppermute | solution.py:288
  22.1 0.2 collective-permute-start.3
  22.3 4.9 %collective-permute-done.4 = bf16[64,2176]{1,0:T(8,128)(2,1)S(1)} collective-permute-done((bf16[64,2176]{1,0:T(8,128)(2,1)S(1)}, bf16[64,2176]{1,0:T(8,128)(2,1)S(1)}, u32[]{:S(2)}, u32[]{:S(2)}) %collective-permute-start.4) | collective-permute-done | bytes 278560 | tf_op jit(solution)/shard_map/ppermute | solution.py:288
  27.2 0.6 collective-permute-start.6
  27.8 1.6 %collective-permute-start.5 = (bf16[64,1280]{1,0:T(8,128)(2,1)S(1)}, bf16[64,1280]{1,0:T(8,128)(2,1)S(1)}, u32[]{:S(2)}, u32[]{:S(2)}) collective-permute-start(bf16[64,1280]{1,0:T(8,128)(2,1)S(1)} %pad_maximum_fusion.6), channel_id=1, source_target_pairs={{0,4},{1,5},{2,3},{3,2},{4,0},{5,1},{6,7},{7,6},{8,12},{9,13},{10,... | collective-permute-start | bytes 491528 | tf_op jit(solution)/shard_map/ppermute | solution.py:290
  29.4 7.4 %collective-permute-done.6 = bf16[128,2176]{1,0:T(8,128)(2,1)S(1)} collective-permute-done((bf16[128,2176]{1,0:T(8,128)(2,1)S(1)}, bf16[128,2176]{1,0:T(8,128)(2,1)S(1)}, u32[]{:S(2)}, u32[]{:S(2)}) %collective-permute-start.6) | collective-permute-done | bytes 557088 | tf_op jit(solution)/shard_map/ppermute | solution.py:288
  37.1 1.5 %collective-permute-start.7 = (bf16[128,1280]{1,0:T(8,128)(2,1)S(1)}, bf16[128,1280]{1,0:T(8,128)(2,1)S(1)}, u32[]{:S(2)}, u32[]{:S(2)}) collective-permute-start(bf16[128,1280]{1,0:T(8,128)(2,1)S(1)} %pad_maximum_fusion.2), channel_id=1, source_target_pairs={{0,1},{1,0},{2,6},{3,7},{4,5},{5,4},{6,2},{7,3},{8,9},{9,8},{10,14... | collective-permute-start | bytes 983048 | tf_op jit(solution)/shard_map/ppermute | solution.py:290
  38.6 5.6 %collective-permute-done.7 = bf16[128,1280]{1,0:T(8,128)(2,1)S(1)} collective-permute-done((bf16[128,1280]{1,0:T(8,128)(2,1)S(1)}, bf16[128,1280]{1,0:T(8,128)(2,1)S(1)}, u32[]{:S(2)}, u32[]{:S(2)}) %collective-permute-start.7) | collective-permute-done | bytes 327712 | tf_op jit(solution)/shard_map/ppermute | solution.py:290
  44.5 7.9 %first.1 = (bf16[1024,2048]{1,0:T(8,128)(2,1)S(1)}, bf16[1024,2048]{1,0:T(8,128)(2,1)S(1)}, f32[1024,128]{1,0:T(8,128)S(1)}, bf16[512,2176]{1,0:T(8,128)(2,1)S(1)}, bf16[512,1024]{1,0:T(8,128)(2,1)S(1)}) custom-call(s32[34]{0:T(128)S(1)} %pad_add_fusion.tab, bf16[256,2176]{1,0:T(8,128)(2,1)S(1)} %constant_dynamic-update-slice_fusion.5.own_ref, ...), custom_call_target="tpu_custom_call" | custom-call | flops 4563402752 | bytes 8388608 | tf_op jit(solution)/shard_map/first/pallas_call | solution.py:446
  52.5 5.8 %second.1 = (bf16[2048,256]{1,0:T(8,128)(2,1)S(1)}, bf16[1024,256]{1,0:T(8,128)(2,1)S(1)}, f32[256,256]{1,0:T(8,128)S(1)}, f32[8,1152]{1,0:T(8,128)S(1)}) custom-call(s32[34]{0:T(128)S(1)} %pad_add_fusion.tab, bf16[256,1280]{1,0:T(8,128)(2,1)S(1)} %constant_dynamic-update-slice_fusion.own_ref, bf16[256,1280]{1,0:T(8,128)(2,1)S(1)} %collective-permute-done.8.oth_ref, ...), custom_call_target="tpu_custom_call" | custom-call | flops 2147483648 | bytes 8388608 | tf_op jit(solution)/shard_map/second/pallas_call | solution.py:479
  58.3 10.0 %back.1 = (bf16[1024,2048]{1,0:T(8,128)(2,1)S(1)}, bf16[1024,128]{1,0:T(8,128)(2,1)S(1)}, f32[256,2176]{1,0:T(8,128)S(1)}, bf16[256,2176]{1,0:T(8,128)(2,1)S(1)}) custom-call(s32[34]{0:T(128)S(1)} %pad_add_fusion.tab, bf16[1024,256]{1,0:T(8,128)(2,1)S(1)} %get-tuple-element.74.dm_ref, bf16[2048,256]{1,0:T(8,128)(2,1)S(1)} %get-tuple-element.69.w_ref, ...), custom_call_target="tpu_custom_call" | custom-call | flops 6845104128 | bytes 8388608 | tf_op jit(solution)/shard_map/back/pallas_call | solution.py:513
  68.3 0.6 collective-permute-start.11
  68.8 3.5 %outer.1 = (f32[256,1152]{1,0:T(8,128)S(1)}, bf16[256,1152]{1,0:T(8,128)(2,1)S(1)}) custom-call(s32[34]{0:T(128)S(1)} %pad_add_fusion.tab, bf16[1024,256]{1,0:T(8,128)(2,1)S(1)} %get-tuple-element.74.dm_ref, bf16[1024,2048]{1,0:T(8,128)(2,1)S(1)} %get-tuple-element.66.ga_ref.gb_ref, bf16[1024,2048]{1,0:T(8,128)(2,1)S(1)} %get-tuple-element.66.ga_ref.gb_ref, ...), custom_call_target="tpu_custom_call" | custom-call | flops 2147483648 | bytes 8388608 | tf_op jit(solution)/shard_map/outer/pallas_call | solution.py:552
  72.4 0.2 convert_add_fusion
  72.7 1.5 %collective-permute-start.13 = (bf16[128,2176]{1,0:T(8,128)(2,1)S(1)}, bf16[128,2176]{1,0:T(8,128)(2,1)S(1)}, u32[]{:S(2)}, u32[]{:S(2)}) collective-permute-start(bf16[128,2176]{1,0:T(8,128)(2,1)S(1)} %slice.363), channel_id=1, source_target_pairs={{0,1},{1,0},{2,6},{3,7},{4,5},{5,4},{6,2},{7,3},{8,9},{9,8},{10,14... | collective-permute-start | bytes 1671176 | tf_op jit(solution)/shard_map/ppermute | solution.py:578
  74.3 4.4 %input.1 = (f32[4,512,256]{2,1,0:T(8,128)}, bf16[1024,256]{1,0:T(8,128)(2,1)S(1)}) custom-call(s32[34]{0:T(128)S(1)} %pad_add_fusion.tab, bf16[1024,2048]{1,0:T(8,128)(2,1)S(1)} %get-tuple-element.79.dp_ref, bf16[1024,128]{1,0:T(8,128)(2,1)S(1)} %get-tuple-element.83.dg_ref, bf16[512,2176]{1,0:T(8,128)(2,1)S(1)} %get-tuple-element.84.w_ref), custom_call_target="tpu_custom_call" | custom-call | flops 4563402752 | bytes 8388608 | tf_op jit(solution)/shard_map/input/pallas_call | solution.py:580
  78.7 3.5 %collective-permute-done.13 = bf16[128,2176]{1,0:T(8,128)(2,1)S(1)} collective-permute-done((bf16[128,2176]{1,0:T(8,128)(2,1)S(1)}, bf16[128,2176]{1,0:T(8,128)(2,1)S(1)}, u32[]{:S(2)}, u32[]{:S(2)}) %collective-permute-start.13) | collective-permute-done | bytes 557088 | tf_op jit(solution)/shard_map/ppermute | solution.py:578
  82.3 0.1 slice_add_fusion
  82.4 1.6 %collective-permute-start.15 = (bf16[64,2176]{1,0:T(8,128)(2,1)S(1)}, bf16[64,2176]{1,0:T(8,128)(2,1)S(1)}, u32[]{:S(2)}, u32[]{:S(2)}) collective-permute-start(bf16[64,2176]{1,0:T(8,128)(2,1)S(1)} %slice.365), channel_id=1, source_target_pairs={{0,4},{1,5},{2,3},{3,2},{4,0},{5,1},{6,7},{7,6},{8,12},{9,13},{10,... | collective-permute-start | bytes 835592 | tf_op jit(solution)/shard_map/ppermute | solution.py:610
  84.0 0.1 convert_add_fusion.1
  84.3 0.6 collective-permute-start.14
  84.9 7.2 %collective-permute-done.15 = bf16[64,2176]{1,0:T(8,128)(2,1)S(1)} collective-permute-done((bf16[64,2176]{1,0:T(8,128)(2,1)S(1)}, bf16[64,2176]{1,0:T(8,128)(2,1)S(1)}, u32[]{:S(2)}, u32[]{:S(2)}) %collective-permute-start.15) | collective-permute-done | bytes 278560 | tf_op jit(solution)/shard_map/ppermute | solution.py:610
  92.1 1.1 collective-permute-start.17
  93.2 1.1 collective-permute-start.21
  94.6 3.4 %collective-permute-done.17 = bf16[32,2176]{1,0:T(8,128)(2,1)S(1)} collective-permute-done((bf16[32,2176]{1,0:T(8,128)(2,1)S(1)}, bf16[32,2176]{1,0:T(8,128)(2,1)S(1)}, u32[]{:S(2)}, u32[]{:S(2)}) %collective-permute-start.17) | collective-permute-done | bytes 139296 | tf_op jit(solution)/shard_map/ppermute | solution.py:610
  98.0 0.6 collective-permute-start.19
  98.7 1.6 %collective-permute-start.16 = (bf16[72,1152]{1,0:T(8,128)(2,1)S(1)}, bf16[72,1152]{1,0:T(8,128)(2,1)S(1)}, u32[]{:S(2)}, u32[]{:S(2)}) collective-permute-start(bf16[72,1152]{1,0:T(8,128)(2,1)S(1)} %pad_maximum_fusion.5), channel_id=1, source_target_pairs={{0,4},{1,5},{2,3},{3,2},{4,0},{5,1},{6,7},{7,6},{8,12},{9,13},{10,... | collective-permute-start | bytes 497672 | tf_op jit(solution)/shard_map/ppermute | solution.py:608
  100.2 3.6 %collective-permute-done.19 = bf16[16,2176]{1,0:T(8,128)(2,1)S(1)} collective-permute-done((bf16[16,2176]{1,0:T(8,128)(2,1)S(1)}, bf16[16,2176]{1,0:T(8,128)(2,1)S(1)}, u32[]{:S(2)}, u32[]{:S(2)}) %collective-permute-start.19) | collective-permute-done | bytes 69664 | tf_op jit(solution)/shard_map/ppermute | solution.py:610
  103.8 0.8 add_multiply_fusion
  104.6 0.6 add_multiply_fusion.3
  105.5 5.1 %collective-permute-done.18 = bf16[40,1152]{1,0:T(8,128)(2,1)S(1)} collective-permute-done((bf16[40,1152]{1,0:T(8,128)(2,1)S(1)}, bf16[40,1152]{1,0:T(8,128)(2,1)S(1)}, u32[]{:S(2)}, u32[]{:S(2)}) %collective-permute-start.18) | collective-permute-done | bytes 92192 | tf_op jit(solution)/shard_map/ppermute | solution.py:608
  110.7 0.7 collective-permute-start.20
  111.4 4.5 %collective-permute-done.20 = bf16[24,1152]{1,0:T(8,128)(2,1)S(1)} collective-permute-done((bf16[24,1152]{1,0:T(8,128)(2,1)S(1)}, bf16[24,1152]{1,0:T(8,128)(2,1)S(1)}, u32[]{:S(2)}, u32[]{:S(2)}) %collective-permute-start.20) | collective-permute-done | bytes 55328 | tf_op jit(solution)/shard_map/ppermute | solution.py:608
  116.0 0.6 add_multiply_fusion.4
  116.6 0.5 slice.277
  117.1 0.6 add_multiply_fusion.2
  117.7 0.7 add_multiply_fusion.1
  118.5 1.3 %copy-done.21 = f32[4,512,256]{2,1,0:T(8,128)} copy-done((f32[4,512,256]{2,1,0:T(8,128)}, f32[4,512,256]{2,1,0:T(8,128)S(1)}, u32[]{:S(2)}) %copy-start.21) | copy-done | bytes 2097176
  (138 shorter events, 2.1 us)
Async XLA Ops:
  0.7 9.3 %copy-start.15 = (s32[4,512]{1,0:T(4,128)S(1)}, s32[4,512]{1,0:T(4,128)}, u32[]{:S(2)}) copy-start(s32[4,512]{1,0:T(4,128)} %param.22) | copy-start | bytes 24580
  0.7 12.8 %copy-start.2 = (f32[8,8,256]{2,1,0:T(8,128)S(1)}, f32[8,8,256]{2,1,0:T(8,128)}, u32[]{:S(2)}) copy-start(f32[8,8,256]{2,1,0:T(8,128)} %param.27) | copy-start | bytes 196612
  0.7 12.8 %copy-start.9 = (f32[2,8,128]{2,1,0:T(8,128)S(1)}, f32[2,8,128]{2,1,0:T(8,128)}, u32[]{:S(2)}) copy-start(f32[2,8,128]{2,1,0:T(8,128)} %param.28) | copy-start | bytes 24580
  0.7 12.9 %copy-start.17 = (s32[4,512]{1,0:T(4,128)S(1)}, s32[4,512]{1,0:T(4,128)}, u32[]{:S(2)}) copy-start(s32[4,512]{1,0:T(4,128)} %param.23) | copy-start | bytes 24580
  0.7 12.9 %copy-start.16 = (s32[4,512]{1,0:T(4,128)S(1)}, s32[4,512]{1,0:T(4,128)}, u32[]{:S(2)}) copy-start(s32[4,512]{1,0:T(4,128)} %param.24) | copy-start | bytes 24580
  2.5 11.2 %collective-permute-start = (bf16[16,2176]{1,0:T(8,128)(2,1)S(1)}, bf16[16,2176]{1,0:T(8,128)(2,1)S(1)}, u32[]{:S(2)}, u32[]{:S(2)}) collective-permute-start(bf16[16,2176]{1,0:T(8,128)(2,1)S(1)} %concatenate.89), channel_id=1, source_target_pairs={{0,16},{1,17},{2,18},{3,19},{4,20},{5,21},{6,22},{7,23},{8,24},{9,... | collective-permute-start | bytes 208904 | tf_op jit(solution)/shard_map/ppermute | solution.py:288
  8.4 36.1 %collective-permute-start.10 = (bf16[1024,256]{1,0:T(8,128)(2,1)}, bf16[1024,256]{1,0:T(8,128)(2,1)}, u32[]{:S(2)}, u32[]{:S(2)}) collective-permute-start(bf16[1024,256]{1,0:T(8,128)(2,1)} %bitcast.9), channel_id=1, source_target_pairs={{0,1},{1,0},{2,3},{3,2},{4,5},{5,4},{6,7},{7,6},{8,9},{9,8},{10,11... | collective-permute-start | bytes 1572872 | tf_op jit(solution)/shard_map/ppermute | solution.py:414
  13.7 6.9 %collective-permute-start.2 = (bf16[32,2176]{1,0:T(8,128)(2,1)S(1)}, bf16[32,2176]{1,0:T(8,128)(2,1)S(1)}, u32[]{:S(2)}, u32[]{:S(2)}) collective-permute-start(bf16[32,2176]{1,0:T(8,128)(2,1)S(1)} %pad_maximum_fusion.7), channel_id=1, source_target_pairs={{0,8},{1,9},{2,10},{3,11},{4,12},{5,13},{6,14},{7,15},{8,0},{9,1},... | collective-permute-start | bytes 417800 | tf_op jit(solution)/shard_map/ppermute | solution.py:288
  15.3 5.2 %collective-permute-start.1 = (bf16[16,1280]{1,0:T(8,128)(2,1)S(1)}, bf16[16,1280]{1,0:T(8,128)(2,1)S(1)}, u32[]{:S(2)}, u32[]{:S(2)}) collective-permute-start(bf16[16,1280]{1,0:T(8,128)(2,1)S(1)} %get-tuple-element.61), channel_id=1, source_target_pairs={{0,16},{1,17},{2,18},{3,19},{4,20},{5,21},{6,22},{7,23},{8,24},{9,... | collective-permute-start | bytes 122888 | tf_op jit(solution)/shard_map/ppermute | solution.py:290
  20.6 6.6 %collective-permute-start.4 = (bf16[64,2176]{1,0:T(8,128)(2,1)S(1)}, bf16[64,2176]{1,0:T(8,128)(2,1)S(1)}, u32[]{:S(2)}, u32[]{:S(2)}) collective-permute-start(bf16[64,2176]{1,0:T(8,128)(2,1)S(1)} %pad_maximum_fusion.4), channel_id=1, source_target_pairs={{0,4},{1,5},{2,3},{3,2},{4,0},{5,1},{6,7},{7,6},{8,12},{9,13},{10,... | collective-permute-start | bytes 835592 | tf_op jit(solution)/shard_map/ppermute | solution.py:288
  22.1 5.7 %collective-permute-start.3 = (bf16[32,1280]{1,0:T(8,128)(2,1)S(1)}, bf16[32,1280]{1,0:T(8,128)(2,1)S(1)}, u32[]{:S(2)}, u32[]{:S(2)}) collective-permute-start(bf16[32,1280]{1,0:T(8,128)(2,1)S(1)} %pad_maximum_fusion.9), channel_id=1, source_target_pairs={{0,8},{1,9},{2,10},{3,11},{4,12},{5,13},{6,14},{7,15},{8,0},{9,1},... | collective-permute-start | bytes 245768 | tf_op jit(solution)/shard_map/ppermute | solution.py:290
  27.2 9.6 %collective-permute-start.6 = (bf16[128,2176]{1,0:T(8,128)(2,1)S(1)}, bf16[128,2176]{1,0:T(8,128)(2,1)S(1)}, u32[]{:S(2)}, u32[]{:S(2)}) collective-permute-start(bf16[128,2176]{1,0:T(8,128)(2,1)S(1)} %pad_maximum_fusion.1), channel_id=1, source_target_pairs={{0,1},{1,0},{2,6},{3,7},{4,5},{5,4},{6,2},{7,3},{8,9},{9,8},{10,14... | collective-permute-start | bytes 1671176 | tf_op jit(solution)/shard_map/ppermute | solution.py:288
  27.8 9.2 %collective-permute-start.5 = (bf16[64,1280]{1,0:T(8,128)(2,1)S(1)}, bf16[64,1280]{1,0:T(8,128)(2,1)S(1)}, u32[]{:S(2)}, u32[]{:S(2)}) collective-permute-start(bf16[64,1280]{1,0:T(8,128)(2,1)S(1)} %pad_maximum_fusion.6), channel_id=1, source_target_pairs={{0,4},{1,5},{2,3},{3,2},{4,0},{5,1},{6,7},{7,6},{8,12},{9,13},{10,... | collective-permute-start | bytes 491528 | tf_op jit(solution)/shard_map/ppermute | solution.py:290
  36.9 7.6 %copy-start.14 = (f32[2,128]{1,0:T(2,128)S(1)}, f32[2,128]{1,0:T(2,128)}, u32[]{:S(2)}) copy-start(f32[2,128]{1,0:T(2,128)} %param.29) | copy-start | bytes 3076
  36.9 7.6 %copy-start = (bf16[4,512,256]{2,1,0:T(8,128)(2,1)S(1)}, bf16[4,512,256]{2,1,0:T(8,128)(2,1)}, u32[]{:S(2)}) copy-start(bf16[4,512,256]{2,1,0:T(8,128)(2,1)} %xo_ref.1) | copy-start | bytes 3145732
  36.9 7.6 %collective-permute-start.9 = (bf16[256,2176]{1,0:T(8,128)(2,1)S(1)}, bf16[256,2176]{1,0:T(8,128)(2,1)}, u32[]{:S(2)}, u32[]{:S(2)}) collective-permute-start(bf16[256,2176]{1,0:T(8,128)(2,1)S(1)} %constant_dynamic-update-slice_fusion.5.own_ref), channel_id=1, source_target_pairs={{0,2},{1,3},{2,0},{3,1},{4,6},{5,7},{6,4},{7,5},{8,10},{9,11},{10,... | collective-permute-start | bytes 3342344 | tf_op jit(solution)/shard_map/ppermute | solution.py:292
  37.1 7.1 %collective-permute-start.7 = (bf16[128,1280]{1,0:T(8,128)(2,1)S(1)}, bf16[128,1280]{1,0:T(8,128)(2,1)S(1)}, u32[]{:S(2)}, u32[]{:S(2)}) collective-permute-start(bf16[128,1280]{1,0:T(8,128)(2,1)S(1)} %pad_maximum_fusion.2), channel_id=1, source_target_pairs={{0,1},{1,0},{2,6},{3,7},{4,5},{5,4},{6,2},{7,3},{8,9},{9,8},{10,14... | collective-permute-start | bytes 983048 | tf_op jit(solution)/shard_map/ppermute | solution.py:290
  44.2 8.2 %collective-permute-start.8 = (bf16[256,1280]{1,0:T(8,128)(2,1)S(1)}, bf16[256,1280]{1,0:T(8,128)(2,1)S(1)}, u32[]{:S(2)}, u32[]{:S(2)}) collective-permute-start(bf16[256,1280]{1,0:T(8,128)(2,1)S(1)} %constant_dynamic-update-slice_fusion.own_ref), channel_id=1, source_target_pairs={{0,2},{1,3},{2,0},{3,1},{4,6},{5,7},{6,4},{7,5},{8,10},{9,11},{10,... | collective-permute-start | bytes 1966088 | tf_op jit(solution)/shard_map/ppermute | solution.py:293
  68.3 4.1 %collective-permute-start.11 = (bf16[256,2176]{1,0:T(8,128)(2,1)S(1)}, bf16[256,2176]{1,0:T(8,128)(2,1)S(1)}, u32[]{:S(2)}, u32[]{:S(2)}) collective-permute-start(bf16[256,2176]{1,0:T(8,128)(2,1)S(1)} %get-tuple-element.77), channel_id=1, source_target_pairs={{0,2},{1,3},{2,0},{3,1},{4,6},{5,7},{6,4},{7,5},{8,10},{9,11},{10,... | collective-permute-start | bytes 3342344 | tf_op jit(solution)/shard_map/ppermute | solution.py:551
  72.7 9.6 %collective-permute-start.13 = (bf16[128,2176]{1,0:T(8,128)(2,1)S(1)}, bf16[128,2176]{1,0:T(8,128)(2,1)S(1)}, u32[]{:S(2)}, u32[]{:S(2)}) collective-permute-start(bf16[128,2176]{1,0:T(8,128)(2,1)S(1)} %slice.363), channel_id=1, source_target_pairs={{0,1},{1,0},{2,6},{3,7},{4,5},{5,4},{6,2},{7,3},{8,9},{9,8},{10,14... | collective-permute-start | bytes 1671176 | tf_op jit(solution)/shard_map/ppermute | solution.py:578
  74.3 9.7 %collective-permute-start.12 = (bf16[264,1152]{1,0:T(8,128)(2,1)S(1)}, bf16[264,1152]{1,0:T(8,128)(2,1)S(1)}, u32[]{:S(2)}, u32[]{:S(2)}) collective-permute-start(bf16[264,1152]{1,0:T(8,128)(2,1)S(1)} %pad_maximum_fusion), channel_id=1, source_target_pairs={{0,2},{1,3},{2,0},{3,1},{4,6},{5,7},{6,4},{7,5},{8,10},{9,11},{10,... | collective-permute-start | bytes 1824776 | tf_op jit(solution)/shard_map/ppermute | solution.py:579
  82.4 9.6 %collective-permute-start.15 = (bf16[64,2176]{1,0:T(8,128)(2,1)S(1)}, bf16[64,2176]{1,0:T(8,128)(2,1)S(1)}, u32[]{:S(2)}, u32[]{:S(2)}) collective-permute-start(bf16[64,2176]{1,0:T(8,128)(2,1)S(1)} %slice.365), channel_id=1, source_target_pairs={{0,4},{1,5},{2,3},{3,2},{4,0},{5,1},{6,7},{7,6},{8,12},{9,13},{10,... | collective-permute-start | bytes 835592 | tf_op jit(solution)/shard_map/ppermute | solution.py:610
  84.3 10.1 %collective-permute-start.14 = (bf16[136,1152]{1,0:T(8,128)(2,1)S(1)}, bf16[136,1152]{1,0:T(8,128)(2,1)S(1)}, u32[]{:S(2)}, u32[]{:S(2)}) collective-permute-start(bf16[136,1152]{1,0:T(8,128)(2,1)S(1)} %pad_maximum_fusion.3), channel_id=1, source_target_pairs={{0,1},{1,0},{2,6},{3,7},{4,5},{5,4},{6,2},{7,3},{8,9},{9,8},{10,14... | collective-permute-start | bytes 940040 | tf_op jit(solution)/shard_map/ppermute | solution.py:608
  92.1 5.9 %collective-permute-start.17 = (bf16[32,2176]{1,0:T(8,128)(2,1)S(1)}, bf16[32,2176]{1,0:T(8,128)(2,1)S(1)}, u32[]{:S(2)}, u32[]{:S(2)}) collective-permute-start(bf16[32,2176]{1,0:T(8,128)(2,1)S(1)} %slice.367), channel_id=1, source_target_pairs={{0,8},{1,9},{2,10},{3,11},{4,12},{5,13},{6,14},{7,15},{8,0},{9,1},... | collective-permute-start | bytes 417800 | tf_op jit(solution)/shard_map/ppermute | solution.py:610
  93.2 25.2 %collective-permute-start.21 = (bf16[1024,256]{1,0:T(8,128)(2,1)S(1)}, bf16[1024,256]{1,0:T(8,128)(2,1)S(1)}, u32[]{:S(2)}, u32[]{:S(2)}) collective-permute-start(bf16[1024,256]{1,0:T(8,128)(2,1)S(1)} %get-tuple-element.92), channel_id=1, source_target_pairs={{0,1},{1,0},{2,3},{3,2},{4,5},{5,4},{6,7},{7,6},{8,9},{9,8},{10,11... | collective-permute-start | bytes 1572872 | tf_op jit(solution)/shard_map/ppermute | solution.py:606
  94.4 9.4 %copy-start.1 = (f32[16,2048]{1,0:T(8,128)S(1)}, f32[16,2048]{1,0:T(8,128)}, u32[]{:S(2)}) copy-start(f32[16,2048]{1,0:T(8,128)} %param.25) | copy-start | bytes 393220
  94.4 9.4 %copy-start.4 = (f32[16,2048]{1,0:T(8,128)S(1)}, f32[16,2048]{1,0:T(8,128)}, u32[]{:S(2)}) copy-start(f32[16,2048]{1,0:T(8,128)} %param.35) | copy-start | bytes 393220
  94.4 9.4 %copy-start.5 = (f32[16,2048]{1,0:T(8,128)S(1)}, f32[16,2048]{1,0:T(8,128)}, u32[]{:S(2)}) copy-start(f32[16,2048]{1,0:T(8,128)} %param.30) | copy-start | bytes 393220
  94.6 10.1 %copy-start.8 = (f32[16,16]{1,0:T(8,128)S(1)}, f32[16,16]{1,0:T(8,128)}, u32[]{:S(2)}) copy-start(f32[16,16]{1,0:T(8,128)} %param.26) | copy-start | bytes 3076
  94.6 10.0 %copy-start.10 = (f32[16,16]{1,0:T(8,128)S(1)}, f32[16,16]{1,0:T(8,128)}, u32[]{:S(2)}) copy-start(f32[16,16]{1,0:T(8,128)} %param.36) | copy-start | bytes 3076
  94.6 10.0 %copy-start.11 = (f32[16,16]{1,0:T(8,128)S(1)}, f32[16,16]{1,0:T(8,128)}, u32[]{:S(2)}) copy-start(f32[16,16]{1,0:T(8,128)} %param.31) | copy-start | bytes 3076
  98.0 5.8 %collective-permute-start.19 = (bf16[16,2176]{1,0:T(8,128)(2,1)S(1)}, bf16[16,2176]{1,0:T(8,128)(2,1)S(1)}, u32[]{:S(2)}, u32[]{:S(2)}) collective-permute-start(bf16[16,2176]{1,0:T(8,128)(2,1)S(1)} %slice.369), channel_id=1, source_target_pairs={{0,16},{1,17},{2,18},{3,19},{4,20},{5,21},{6,22},{7,23},{8,24},{9,... | collective-permute-start | bytes 208904 | tf_op jit(solution)/shard_map/ppermute | solution.py:610
  98.7 6.6 %collective-permute-start.16 = (bf16[72,1152]{1,0:T(8,128)(2,1)S(1)}, bf16[72,1152]{1,0:T(8,128)(2,1)S(1)}, u32[]{:S(2)}, u32[]{:S(2)}) collective-permute-start(bf16[72,1152]{1,0:T(8,128)(2,1)S(1)} %pad_maximum_fusion.5), channel_id=1, source_target_pairs={{0,4},{1,5},{2,3},{3,2},{4,0},{5,1},{6,7},{7,6},{8,12},{9,13},{10,... | collective-permute-start | bytes 497672 | tf_op jit(solution)/shard_map/ppermute | solution.py:608
  105.2 10.7 %copy-start.18 = (f32[2,128]{1,0:T(2,128)S(1)}, f32[2,128]{1,0:T(2,128)}, u32[]{:S(2)}) copy-start(f32[2,128]{1,0:T(2,128)} %param.39) | copy-start | bytes 3076
  105.2 10.8 %copy-start.19 = (f32[2,128]{1,0:T(2,128)S(1)}, f32[2,128]{1,0:T(2,128)}, u32[]{:S(2)}) copy-start(f32[2,128]{1,0:T(2,128)} %param.34) | copy-start | bytes 3076
  105.2 11.9 %copy-start.12 = (f32[2,8,128]{2,1,0:T(8,128)S(1)}, f32[2,8,128]{2,1,0:T(8,128)}, u32[]{:S(2)}) copy-start(f32[2,8,128]{2,1,0:T(8,128)} %param.38) | copy-start | bytes 24580
  105.2 11.9 %copy-start.13 = (f32[2,8,128]{2,1,0:T(8,128)S(1)}, f32[2,8,128]{2,1,0:T(8,128)}, u32[]{:S(2)}) copy-start(f32[2,8,128]{2,1,0:T(8,128)} %param.33) | copy-start | bytes 24580
  105.3 12.4 %copy-start.3 = (f32[8,8,256]{2,1,0:T(8,128)S(1)}, f32[8,8,256]{2,1,0:T(8,128)}, u32[]{:S(2)}) copy-start(f32[8,8,256]{2,1,0:T(8,128)} %param.27) | copy-start | bytes 196612
  105.3 12.4 %copy-start.6 = (f32[8,8,256]{2,1,0:T(8,128)S(1)}, f32[8,8,256]{2,1,0:T(8,128)}, u32[]{:S(2)}) copy-start(f32[8,8,256]{2,1,0:T(8,128)} %param.37) | copy-start | bytes 196612
  105.3 12.4 %copy-start.7 = (f32[8,8,256]{2,1,0:T(8,128)S(1)}, f32[8,8,256]{2,1,0:T(8,128)}, u32[]{:S(2)}) copy-start(f32[8,8,256]{2,1,0:T(8,128)} %param.32) | copy-start | bytes 196612
  105.4 13.1 %copy-start.20 = (f32[4,512,256]{2,1,0:T(8,128)S(1)}, f32[4,512,256]{2,1,0:T(8,128)}, u32[]{:S(2)}) copy-start(f32[4,512,256]{2,1,0:T(8,128)} %get-tuple-element.91) | copy-start | bytes 6291460
  105.4 5.2 %collective-permute-start.18 = (bf16[40,1152]{1,0:T(8,128)(2,1)S(1)}, bf16[40,1152]{1,0:T(8,128)(2,1)S(1)}, u32[]{:S(2)}, u32[]{:S(2)}) collective-permute-start(bf16[40,1152]{1,0:T(8,128)(2,1)S(1)} %pad_maximum_fusion.8), channel_id=1, source_target_pairs={{0,8},{1,9},{2,10},{3,11},{4,12},{5,13},{6,14},{7,15},{8,0},{9,1},... | collective-permute-start | bytes 276488 | tf_op jit(solution)/shard_map/ppermute | solution.py:608
  110.7 5.2 %collective-permute-start.20 = (bf16[24,1152]{1,0:T(8,128)(2,1)S(1)}, bf16[24,1152]{1,0:T(8,128)(2,1)S(1)}, u32[]{:S(2)}, u32[]{:S(2)}) collective-permute-start(bf16[24,1152]{1,0:T(8,128)(2,1)S(1)} %pad_maximum_fusion.10), channel_id=1, source_target_pairs={{0,16},{1,17},{2,18},{3,19},{4,20},{5,21},{6,22},{7,23},{8,24},{9,... | collective-permute-start | bytes 165896 | tf_op jit(solution)/shard_map/ppermute | solution.py:608
  118.5 1.3 %copy-start.21 = (f32[4,512,256]{2,1,0:T(8,128)}, f32[4,512,256]{2,1,0:T(8,128)S(1)}, u32[]{:S(2)}) copy-start(f32[4,512,256]{2,1,0:T(8,128)S(1)} %convert_dynamic-update-slice_fusion) | copy-start | bytes 6291460

commit v3 on v0

v3 whole, which is shorter than its diff:
```python
import functools
import math

import jax
import jax.numpy as jnp
import numpy as np
from jax import lax
from jax.experimental import pallas as pl
from jax.experimental.pallas import tpu as pltpu
from jax.sharding import PartitionSpec as P

momentum_mu = 0.5
average_keep = 0.5
rate_bases = (17.0, 1.0, 24.0, 4.0, 0.25)
both = ("rows", "field")
f32 = jnp.float32
bf16 = jnp.bfloat16
BLOCK = 16
LANES = 128


def dot(a, b):
    return lax.dot_general(a, b, (((1,), (0,)), ((), ())), preferred_element_type=f32)


def dot_t(a, b):
    return lax.dot_general(a, b, (((1,), (1,)), ((), ())), preferred_element_type=f32)


def t_dot(a, b):
    return lax.dot_general(a, b, (((0,), (0,)), ((), ())), preferred_element_type=f32)


def sigmoid(v):
    return 0.5 + 0.5 * jnp.tanh(0.5 * v)


def rows16(start):
    return pl.ds(pl.multiple_of(start, BLOCK), BLOCK)


def each_block(tab, pairs, body):
    for j in range(pairs):
        for side in range(2):
            core = tab[2 * pairs] if side == 0 else 1 - tab[2 * pairs]
            body(side, tab[side * pairs + j], 2 * (j // 2) + core, j % 2)


def pack_a_kernel(expert_ref, gate_ref, out_ref):
    wide, gates = expert_ref.shape[1], gate_ref.shape[1]
    out_ref[:, 0:wide] = expert_ref[...].astype(bf16)
    out_ref[:, wide:] = jnp.zeros((out_ref.shape[0], LANES), bf16)
    out_ref[:, wide : wide + gates] = gate_ref[...].astype(bf16)


def pack_b_kernel(expert_ref, tower_ref, digits_ref, out_ref):
    experts, rows, out_cols = expert_ref.shape
    part = experts // 2
    for k in range(part):
        both_k = jnp.concatenate([expert_ref[k], expert_ref[k + part]], axis=0)
        out_ref[:, k * out_cols : (k + 1) * out_cols] = both_k.astype(bf16)
    at = part * out_cols
    towers = jnp.concatenate([tower_ref[0], tower_ref[1]], axis=0)
    out_ref[:, at : at + LANES] = towers.astype(bf16)
    out_ref[:, at + LANES :] = digits_ref[0 : 2 * rows, :].astype(bf16)


def rows_kernel(tab, in_ref, got_ref, meta_ref, x_ref, xt_ref, by_row_ref):
    micro, rows_dev, width = in_ref.shape
    tile = rows_dev // 2
    start = pl.multiple_of(tab[tab.shape[0] - 1] * tile, tile)
    for m in range(micro):
        rows = slice(m * tile, (m + 1) * tile)
        x = jnp.concatenate([in_ref[m, pl.ds(start, tile), :], got_ref[rows, :]], axis=1)
        x_ref[rows, :] = x
        xt_ref[:, rows] = x.T
        by_row_ref[rows, :] = meta_ref[m].T


def first_kernel(tab, own_ref, oth_ref, x_ref, by_row_ref, ga_ref, gs_ref, gate_ref, w_ref):
    half = own_ref.shape[0]
    pairs = half // BLOCK
    count, wide = ga_ref.shape
    experts = wide // half
    tile = count // 2

    def put(side, place, rr, ff):
        src = own_ref if side == 0 else oth_ref
        row = (ff ^ tab[2 * pairs + 1]) * half + rr * BLOCK
        w_ref[rows16(row), :] = src[rows16(place * BLOCK), :]

    each_block(tab, pairs, put)

    def step(i, carry):
        rows = pl.ds(pl.multiple_of(i * tile, tile), tile)
        x = x_ref[rows, :]
        domain = by_row_ref[rows, 2:3]
        logits = dot(x, w_ref[:, wide:])
        lane = lax.broadcasted_iota(jnp.int32, logits.shape, 1)
        picked = (lane // experts).astype(f32) == domain
        masked = jnp.where(picked, logits, -jnp.inf)
        raised = jnp.exp(masked - jnp.max(masked, axis=1, keepdims=True))
        gate = raised / jnp.sum(raised, axis=1, keepdims=True)
        gate_ref[rows, :] = gate
        gate = 0.5 * (gate + pltpu.roll(gate, LANES - experts, axis=1))
        for k in range(experts):
            cols = slice(k * half, (k + 1) * half)
            pre = dot(x, w_ref[:, cols])
            low = 0.5 * pre
            up = 1.0 + jnp.tanh(low)
            scaled = gate[:, k : k + 1] * up
            ga_ref[rows, cols] = (scaled * pre).astype(bf16)
            gs_ref[rows, cols] = (scaled * (1.0 + pre - low * up)).astype(bf16)
        return carry

    lax.fori_loop(0, 2, step, 0)


def rest_kernel(
    tab,
    own_ref,
    oth_ref,
    ga_ref,
    gs_ref,
    gate_ref,
    by_row_ref,
    to_ref,
    xt_ref,
    dm_ref,
    gti_ref,
    side_ref,
    dp_ref,
    dg_ref,
    keep_ref,
    send_ref,
    w_ref,
    ti_ref,
    q_ref,
    g_ref,
):
    half = own_ref.shape[0]
    pairs = half // BLOCK
    count, out_cols = dm_ref.shape
    hidden = half
    wide = ga_ref.shape[1]
    experts = wide // hidden
    part = experts // 2

    digits = jnp.zeros((BLOCK, LANES), f32)
    for side in range(2):
        for j in range(pairs // 2):
            src = own_ref if side == 0 else oth_ref
            core = tab[2 * pairs] if side == 0 else 1 - tab[2 * pairs]
            a0 = src[rows16(tab[side * pairs + 2 * j] * BLOCK), :].astype(f32)
            a1 = src[rows16(tab[side * pairs + 2 * j + 1] * BLOCK), :].astype(f32)
            row = (2 * j + core) * BLOCK
            upper = jnp.concatenate([a0[:8], a1[:8]], axis=0).astype(bf16)
            lower = jnp.concatenate([a0[8:], a1[8:]], axis=0).astype(bf16)
            at = part * out_cols
            for k in range(part):
                cols = slice(k * out_cols, (k + 1) * out_cols)
                w_ref[rows16(k * hidden + row), :] = upper[:, cols]
                w_ref[rows16((k + part) * hidden + row), :] = lower[:, cols]
            ti_ref[rows16(row), 0:LANES] = upper[:, at : at + LANES]
            ti_ref[rows16(row), LANES : 2 * LANES] = lower[:, at : at + LANES]
            digits = digits + (a0 + a1)[:, at + LANES :]
    lane = lax.broadcasted_iota(jnp.int32, digits.shape, 1)
    scale = jnp.where(lane == 0, 1.0, jnp.where(lane == 1, 256.0, jnp.where(lane == 2, 65536.0, 0.0)))
    real = jnp.sum(jnp.sum(digits * scale, axis=1, keepdims=True), axis=0, keepdims=True)

    valid, label, domain = by_row_ref[:, 0:1], by_row_ref[:, 1:2], by_row_ref[:, 2:3]
    head = to_ref[0:1, :]
    mixed = dot(ga_ref[...], w_ref[...]).astype(bf16)
    tpre = dot(mixed, ti_ref[...])
    lane = lax.broadcasted_iota(jnp.int32, tpre.shape, 1)
    picked = (lane // LANES).astype(f32) == domain
    s = sigmoid(tpre)
    act = (tpre * s).astype(bf16).astype(f32)
    act = jnp.where(picked, act, 0.0)
    chosen = jnp.sum(act * head, axis=1, keepdims=True)
    soft = jnp.maximum(chosen, 0.0) + jnp.log1p(jnp.exp(-jnp.abs(chosen)))
    loss = jnp.sum(valid * (soft - label * chosen), axis=0, keepdims=True) / real
    dlogit = (valid * (sigmoid(chosen) - label) / real).astype(bf16).astype(f32)
    slope = s * (1.0 + tpre * (1.0 - s))
    dtpre = jnp.where(picked, dlogit * head * slope, 0.0).astype(bf16)
    heads = head.shape[1]
    side_ref[...] = jnp.zeros_like(side_ref)
    side_ref[0:1, 0:heads] = jnp.sum(dlogit * act, axis=0, keepdims=True)
    side_ref[0:1, heads : heads + LANES] = jnp.broadcast_to(loss, (1, LANES))
    dm_ref[...] = dot_t(dtpre, ti_ref[...]).astype(bf16)

    def pack(start, width):
        def put(side, place, rr, ff):
            dst = keep_ref if side == 0 else send_ref
            row = (ff ^ tab[2 * pairs + 1]) * half + rr * BLOCK
            tile = g_ref[rows16(row), start : start + width]
            dst[rows16(place * BLOCK), start : start + width] = tile.astype(dst.dtype)

        each_block(tab, pairs, put)

    tile = count // 4
    lane = lax.broadcasted_iota(jnp.int32, (tile, LANES), 1)
    q_ref[...] = jnp.zeros_like(q_ref)
    for k in range(experts):
        cols = slice(k * hidden, (k + 1) * hidden)
        for i in range(4):
            rows = slice(i * tile, (i + 1) * tile)
            u = dot_t(dm_ref[rows, :], w_ref[cols, :])
            dp_ref[rows, cols] = (u * gs_ref[rows, cols].astype(f32)).astype(bf16)
            q = jnp.sum(u * ga_ref[rows, cols].astype(f32), axis=1, keepdims=True)
            q_ref[rows, :] = jnp.where((lane == k) | (lane == k + experts), q, q_ref[rows, :])
        g_ref[:, cols] = dot(xt_ref[...], dp_ref[:, cols])
        pack(k * hidden, hidden)
    q = q_ref[...]
    lane = lax.broadcasted_iota(jnp.int32, q.shape, 1)
    total = jnp.sum(jnp.where(lane < experts, q, 0.0), axis=1, keepdims=True)
    mine = (lane // experts).astype(f32) == domain
    dg_ref[...] = (jnp.where(mine, q, 0.0) - gate_ref[...] * total).astype(bf16)
    g_ref[:, wide:] = dot(xt_ref[...], dg_ref[...])
    pack(wide, LANES)
    gti_ref[...] = t_dot(mixed, dtpre)


def outer_kernel(tab, dm_ref, ga_ref, gti_ref, keep_ref, send_ref, g_ref):
    half = keep_ref.shape[0]
    pairs = half // BLOCK
    out_cols = dm_ref.shape[1]
    part = ga_ref.shape[1] // half // 2

    def pack(above, below, cols):
        def put(side, place, rr, ff):
            dst = keep_ref if side == 0 else send_ref
            row = pl.ds(pl.multiple_of(rr * BLOCK + ff * 8, 8), 8)
            tile = jnp.concatenate([above(row), below(row)], axis=0)
            dst[rows16(place * BLOCK), cols] = tile.astype(dst.dtype)

        each_block(tab, pairs, put)

    for k in range(part):
        g_ref[k] = t_dot(ga_ref[:, k * half : (k + 1) * half], dm_ref[...])
        g_ref[k + part] = t_dot(ga_ref[:, (k + part) * half : (k + part + 1) * half], dm_ref[...])
        pack(
            lambda row: g_ref[k, row, :],
            lambda row: g_ref[k + part, row, :],
            slice(k * out_cols, (k + 1) * out_cols),
        )
    at = part * out_cols
    pack(lambda row: gti_ref[row, 0:LANES], lambda row: gti_ref[row, LANES : 2 * LANES], slice(at, at + LANES))


def input_kernel(tab, dp_ref, dg_ref, w_ref, keep_ref, send_ref):
    wide = dp_ref.shape[1]
    grad = dot_t(dp_ref[...], w_ref[:, 0:wide]) + dot_t(dg_ref[...], w_ref[:, wide:])
    half = grad.shape[1] // 2
    keep_ref[0] = grad[:, :half]
    send_ref[...] = grad[:, half:].astype(bf16)


def place_kernel(tab, got_ref, held_ref, out_ref):
    out_ref[0] = got_ref[...].astype(f32)


def update_kernel(rates, sum_a, got_a, sum_b, got_b, side, *refs):
    weights, velocities, averages, outs = refs[0:5], refs[5:10], refs[10:15], refs[15:]
    wide = weights[0].shape[1]
    gates = weights[1].shape[1]
    experts, rows, out_cols = weights[2].shape
    tasks = weights[3].shape[0]
    part = experts // 2

    def renew(at, place, gradient):
        velocity = momentum_mu * velocities[at][place] + gradient
        weight = weights[at][place] - rates[at] * (gradient + momentum_mu * velocity)
        outs[3 * at][place] = weight
        outs[3 * at + 1][place] = velocity
        outs[3 * at + 2][place] = average_keep * averages[at][place] + (1.0 - average_keep) * weight

    first = sum_a[0 : got_a.shape[0], :] + got_a[...].astype(f32)
    renew(0, (slice(None), slice(None)), first[:, :wide])
    renew(1, (slice(None), slice(None)), first[:, wide : wide + gates])
    second = sum_b[0 : got_b.shape[0], :] + got_b[...].astype(f32)
    for k in range(experts):
        top = (k // part) * rows
        renew(2, k, second[top : top + rows, (k % part) * out_cols : (k % part + 1) * out_cols])
    for t in range(tasks):
        renew(3, t, second[t * rows : (t + 1) * rows, part * out_cols :])
        renew(4, (slice(t, t + 1), slice(None)), side[0:1, t * LANES : (t + 1) * LANES])


class Cube:
    def __init__(self):
        self.rows = lax.axis_size("rows")
        self.fields = lax.axis_size("field")
        bits = int(math.log2(self.rows))
        assert 1 << bits == self.rows and self.fields == 2
        outer = [("row", b) for b in range(bits - 1, 1, -1)]
        mixed = [("mixed", 0), ("mixed", 1)]
        self.order = outer + mixed
        self.core = ("row", 0)

    def pairs(self, step):
        kind, which = step
        pairs = []
        for r in range(self.rows):
            for f in range(self.fields):
                if kind == "row":
                    to = (r ^ (1 << which), f)
                else:
                    to = (r ^ 2, f) if (r & 1) == which else (r, f ^ 1)
                pairs.append((r * self.fields + f, to[0] * self.fields + to[1]))
        return pairs

    def swap(self, values, step):
        return lax.ppermute(values, both, self.pairs(step))

    def place(self, order, rr, ff, r, f):
        dr, df, core = rr ^ r, ff ^ f, r & 1
        out = jnp.zeros_like(dr + df)
        for s, (kind, which) in enumerate(order):
            if kind == "row":
                bit = (dr >> which) & 1
            else:
                bit = jnp.where(core == which, (dr >> 1) & 1, df)
            out = out + (bit << s)
        return out


def gather_two(cube, block_a, block_b, x):
    got_b = None
    for at, step in enumerate(cube.order):
        got_a = cube.swap(block_a, step)
        if at:
            block_b = jnp.concatenate([block_b, after(got_b, block_a)], axis=0)
        else:
            block_b = after(block_b, block_a)
        got_b = cube.swap(block_b, step)
        if at + 1 == len(cube.order):
            got_a = after(got_a, x)
        block_a = jnp.concatenate([block_a, after(got_a, block_b)], axis=0)
    return block_a, cube.swap(block_a, cube.core), block_b, got_b


def after(values, *earlier):
    return lax.optimization_barrier((values,) + earlier)[0]


def fold(total, got):
    rows = got.shape[0]
    total = total[:rows] + got.astype(f32)
    half = rows // 2
    return total, total[half:].astype(bf16)


def split_two(values):
    high = lax.reduce_precision(values, 8, 7)
    low = lax.reduce_precision(values - high, 8, 7)
    return jnp.concatenate([high, low], axis=0).astype(bf16)


def join_two(rows):
    rows = rows.astype(f32)
    half = rows.shape[0] // 2
    return rows[:half] + rows[half:]


def beside(part, side):
    mine = split_two(side)
    return jnp.concatenate([part, mine], axis=0), join_two(mine)


def fold_beside(total, side, got):
    rows = got.shape[0] - 8
    total, part = fold(total, got[:rows])
    message, side = beside(part, side + join_two(got[rows:]))
    return total, message, side


def shape(dims, dtype):
    return jax.ShapeDtypeStruct(dims, dtype)


def params(limit):
    return pltpu.CompilerParams(vmem_limit_bytes=limit << 20)


vmem = pl.BlockSpec()
smem = pl.BlockSpec(memory_space=pltpu.SMEM)


def cost(flops):
    return pl.CostEstimate(flops=flops, bytes_accessed=8 << 20, transcendentals=0)


def on_device(
    inputs,
    valid_mask,
    labels,
    domains,
    expert_in,
    gate_in,
    expert_out,
    tower_in,
    tower_out,
    velocity_expert_in,
    velocity_gate_in,
    velocity_expert_out,
    velocity_tower_in,
    velocity_tower_out,
    average_expert_in,
    average_gate_in,
    average_expert_out,
    average_tower_in,
    average_tower_out,
):
    cube = Cube()
    micro, rows_dev, width = inputs.shape
    fields = cube.fields
    tile = rows_dev // fields
    rows_own = micro * tile
    experts, second_rows, out_cols = expert_out.shape
    tasks, tower_cols = tower_out.shape
    wide = expert_in.shape[1]
    hidden = wide // experts
    first_rows = expert_in.shape[0]
    part = experts // 2
    total_rows = micro * rows_dev * cube.rows
    r, f = lax.axis_index("rows"), lax.axis_index("field")

    def own_half(values, which):
        return lax.dynamic_slice_in_dim(values, which * tile, tile, 1)

    block_a = pl.pallas_call(
        pack_a_kernel,
        out_shape=shape((first_rows, wide + LANES), bf16),
        compiler_params=params(4),
        name="pack_a",
    )(expert_in, gate_in)
    own_valid = own_half(after(valid_mask, block_a), f)
    ones = jnp.broadcast_to(jnp.sum(own_valid), (2 * second_rows, LANES))
    row, lane = (lax.broadcasted_iota(jnp.int32, ones.shape, d) for d in range(2))
    digits = jnp.where(lane == 2, ones >> 16, jnp.where(lane == 1, ones >> 8, ones) & 255)
    digits = jnp.where((row == 0) & (lane < 3), digits, 0).astype(f32)
    block_b = pl.pallas_call(
        pack_b_kernel,
        out_shape=shape((2 * second_rows, part * out_cols + 2 * LANES), bf16),
        compiler_params=params(4),
        name="pack_b",
    )(expert_out, tower_in, digits)
    x_send = own_half(after(inputs, block_a), 1 - f).reshape(rows_own, width)
    x_got = lax.ppermute(x_send, "field", [(0, 1), (1, 0)])

    pairs = width // BLOCK
    fit = first_rows == BLOCK
    j = jnp.arange(pairs // 2, dtype=jnp.int32)[:, None]
    ff = jnp.arange(2, dtype=jnp.int32)[None, :]
    if fit:
        core = r & 1
        places = [
            cube.place(cube.order, 2 * j + core, ff, r, f).reshape(-1),
            cube.place(cube.order, 2 * j + 1 - core, ff, r ^ 1, f).reshape(-1),
        ]
    else:
        core = jnp.int32(0)
        places = [(2 * j + ff).reshape(-1)] * 2
    tab = jnp.concatenate(places + [jnp.stack([core, f])]).astype(jnp.int32)
    sent = bf16 if fit else f32

    meta = jnp.stack(
        [own_valid.astype(f32), own_half(labels, f).astype(f32), own_half(domains, f).astype(f32)]
        + [jnp.zeros((micro, tile), f32)] * 5,
        axis=1,
    )
    a_cols, b_cols = wide + LANES, part * out_cols + LANES
    heads = tasks * tower_cols

    x, x_t, by_row = pl.pallas_call(
        rows_kernel,
        in_specs=[smem, vmem, vmem, vmem],
        out_specs=[vmem] * 3,
        out_shape=[
            shape((rows_own, 2 * width), bf16),
            shape((2 * width, rows_own), bf16),
            shape((rows_own, 8), f32),
        ],
        compiler_params=params(8),
        cost_estimate=cost(1 << 20),
        name="rows",
    )(tab, inputs, x_got, meta)

    own_a, oth_a, own_b, got_b = gather_two(cube, block_a, block_b, x)
    if not fit:
        rows_a = first_sorted(cube, cube.order, r, f, width, first_rows)
        own_a, oth_a = jnp.split(jnp.take(jnp.concatenate([own_a, oth_a]), rows_a, axis=0), 2)
    ga, gs, gate, first_w = pl.pallas_call(
        first_kernel,
        in_specs=[smem] + [vmem] * 4,
        out_specs=[vmem] * 4,
        out_shape=[
            shape((rows_own, wide), bf16),
            shape((rows_own, wide), bf16),
            shape((rows_own, LANES), f32),
            shape((2 * width, a_cols), bf16),
        ],
        compiler_params=params(12),
        cost_estimate=cost(4 * rows_own * 2 * width * a_cols),
        name="first",
    )(tab, own_a, oth_a, x, by_row)

    own_b = jnp.concatenate([own_b, after(got_b, gate)], axis=0)
    oth_b = cube.swap(own_b, cube.core)
    if not fit:
        rows_b = second_sorted(cube, cube.order, r, f, width, second_rows)
        own_b, oth_b = jnp.split(jnp.take(jnp.concatenate([own_b, oth_b]), rows_b, axis=0), 2)
    head = jnp.broadcast_to(tower_out.astype(bf16).astype(f32).reshape(1, heads), (8, heads))
    dmixed, grad_ti, side, dpre, dgate, keep_a, send_a = pl.pallas_call(
        rest_kernel,
        in_specs=[smem] + [vmem] * 8,
        out_specs=[vmem] * 7,
        out_shape=[
            shape((rows_own, out_cols), bf16),
            shape((out_cols, heads), f32),
            shape((8, b_cols), f32),
            shape((rows_own, wide), bf16),
            shape((rows_own, LANES), bf16),
            shape((width, a_cols), f32),
            shape((width, a_cols), sent),
        ],
        scratch_shapes=[
            pltpu.VMEM((wide, out_cols), bf16),
            pltpu.VMEM((out_cols, heads), bf16),
            pltpu.VMEM((rows_own, LANES), f32),
            pltpu.VMEM((2 * width, a_cols), f32),
        ],
        compiler_params=params(24),
        cost_estimate=cost(6 * rows_own * 2 * width * a_cols),
        name="rest",
    )(tab, own_b, oth_b, ga, gs, gate, by_row, head, x_t)

    steps = [cube.core] + cube.order[::-1]
    if not fit:
        keep_a, send_a = unsorted(keep_a, send_a, rows_a)
    got_a = cube.swap(send_a, steps[0])
    keep_b, send_b = pl.pallas_call(
        outer_kernel,
        in_specs=[smem] + [vmem] * 3,
        out_specs=[vmem] * 2,
        out_shape=[shape((width, b_cols), f32), shape((width, b_cols), sent)],
        scratch_shapes=[pltpu.VMEM((experts, hidden, out_cols), f32)],
        compiler_params=params(8),
        cost_estimate=cost(4 * rows_own * wide * out_cols),
        name="outer",
    )(tab, dmixed, ga, grad_ti)
    if not fit:
        keep_b, send_b = unsorted(keep_b, send_b, rows_b)

    message, side = beside(send_b, side[:4])
    got_b = cube.swap(message, steps[0])
    sum_a, next_a = fold(keep_a, after(got_a, message))
    sum_b = keep_b
    for at in range(1, len(steps)):
        got_a = cube.swap(next_a, steps[at])
        sum_b, message, side = fold_beside(sum_b, side, after(got_b, next_a))
        got_b = cube.swap(message, steps[at])
        if at == 1:
            grad_keep, grad_send = pl.pallas_call(
                input_kernel,
                grid_spec=pltpu.PrefetchScalarGridSpec(
                    num_scalar_prefetch=1,
                    grid=(micro,),
                    in_specs=[
                        pl.BlockSpec((tile, wide), lambda i, tab: (i, 0)),
                        pl.BlockSpec((tile, LANES), lambda i, tab: (i, 0)),
                        pl.BlockSpec((2 * width, a_cols), lambda i, tab: (0, 0)),
                    ],
                    out_specs=[
                        pl.BlockSpec((1, tile, width), lambda i, tab: (i, tab[2 * pairs + 1], 0)),
                        pl.BlockSpec((tile, width), lambda i, tab: (i, 0)),
                    ],
                ),
                out_shape=[
                    shape((micro, rows_dev, width), f32),
                    shape((rows_own, width), bf16),
                ],
                compiler_params=params(12),
                cost_estimate=cost(4 * rows_own * 2 * width * a_cols),
                name="input",
            )(tab, dpre, after(dgate, message), first_w)
        if at == 3:
            grad_got = lax.ppermute(after(grad_send, next_a), "field", [(0, 1), (1, 0)])
        if at + 1 < len(steps):
            sum_a, next_a = fold(sum_a, after(got_a, message))
    side = side + join_two(got_b[got_b.shape[0] - 8 :])
    input_grad = pl.pallas_call(
        place_kernel,
        grid_spec=pltpu.PrefetchScalarGridSpec(
            num_scalar_prefetch=1,
            grid=(micro,),
            in_specs=[
                pl.BlockSpec((tile, width), lambda i, tab: (i, 0)),
                pl.BlockSpec(memory_space=pl.ANY),
            ],
            out_specs=pl.BlockSpec((1, tile, width), lambda i, tab: (i, 1 - tab[2 * pairs + 1], 0)),
        ),
        out_shape=shape((micro, rows_dev, width), f32),
        input_output_aliases={2: 0},
        compiler_params=params(8),
        cost_estimate=cost(1 << 20),
        name="place",
    )(tab, grad_got, grad_keep)

    weights = (expert_in, gate_in, expert_out, tower_in, tower_out)
    velocities = (
        velocity_expert_in,
        velocity_gate_in,
        velocity_expert_out,
        velocity_tower_in,
        velocity_tower_out,
    )
    averages = (
        average_expert_in,
        average_gate_in,
        average_expert_out,
        average_tower_in,
        average_tower_out,
    )
    rates = [base * math.sqrt(total_rows) for base in rate_bases]
    updated = pl.pallas_call(
        functools.partial(update_kernel, rates),
        out_shape=[shape(w.shape, f32) for w in weights for _ in range(3)],
        compiler_params=params(8),
        cost_estimate=cost(1 << 20),
        name="update",
    )(
        sum_a,
        after(got_a, input_grad),
        sum_b,
        got_b[: got_b.shape[0] - 8],
        side,
        *weights,
        *velocities,
        *averages,
    )
    return (side[0, heads], input_grad, *updated)


def owner_rows(cube, order, r, f, rr, ff, inner, size):
    held = cube.rows * cube.fields // 2
    same = (rr & 1) == (r & 1)
    here = cube.place(order, rr, ff, r, f)
    there = cube.place(order, rr, ff, r ^ 1, f)
    return (jnp.where(same, here, held + there) * size + inner).reshape(-1)


def block_grid(width):
    side = np.arange(2)[:, None, None, None]
    j = np.arange(width // (2 * BLOCK))[None, :, None, None]
    ff = np.arange(2)[None, None, :, None]
    inner = np.arange(BLOCK)[None, None, None, :]
    ahead = (2 * j + side) * BLOCK + 0 * ff + 0 * inner
    full = np.zeros(ahead.shape, np.int32)
    return ahead.astype(np.int32), full + ff.astype(np.int32), full + inner.astype(np.int32)


def first_sorted(cube, order, r, f, width, size):
    ahead, ff, inner = block_grid(width)
    at = ahead + inner
    return owner_rows(
        cube, order, r, f, jnp.asarray(at // size), jnp.asarray(ff), jnp.asarray(at % size), size
    )


def second_sorted(cube, order, r, f, width, size):
    ahead, ff, inner = block_grid(width)
    at = ahead + ff * 8 + inner % 8
    owner = at // size
    held = at % size + size * (inner // 8)
    return owner_rows(
        cube, order, r, f, jnp.asarray(owner // 2), jnp.asarray(owner % 2), jnp.asarray(held), 2 * size
    )


def unsorted(keep, send, rows):
    every = jnp.concatenate([keep, send])
    back = jnp.zeros_like(rows).at[rows].set(jnp.arange(rows.shape[0], dtype=rows.dtype))
    keep, send = jnp.split(jnp.take(every, back, axis=0), 2)
    return keep, send.astype(bf16)


def solution(mesh):
    first = P(("field", "rows"), None)
    second = P(None, ("rows", "field"), None)
    by_row = P(None, "rows")
    inputs = P(None, "rows", "field")
    weights = (first, first, second, second, P())
    return jax.shard_map(
        on_device,
        mesh=mesh,
        in_specs=(inputs, by_row, by_row, by_row) + weights * 3,
        out_specs=(P(), inputs) + tuple(spec for spec in weights for _ in range(3)),
        check_vma=False,
    )
```

time: 728 us -> 102 us (0.14)
  waiting for transfers between devices: 324 us -> 38.3 us
  blocking collectives: 167 us -> 0 us
  matrix products: 111 us -> 0 us
  other arithmetic: 49.4 us -> 3.29 us
  local copies, waits for them, and re-layouts: 46.6 us -> 7.32 us
  Pallas kernels: 0 us -> 27.1 us
  starting transfers between devices: 0.97 us -> 22.5 us
  between operations: 22.8 us -> 2.7 us
    psum x2 -> x0, waiting for transfers between devices: 253 us -> none  [the longest x1 164 us: on_device(): lax.psum((grad_second, grad_tower, grad_head, loss_total), ('rows', 'fiel...]
    dot_general x56 -> x0, matrix products: 111 us -> none  [the longest x4 19.1 us: local_pass(): dgate = jnp.einsum('rto,rko->rtk', dmixed, expert_res, precision=highest)]
    all_gather x2 -> x0, blocking collectives: 94.7 us -> none  [the longest x1 71.4 us: on_device(): lax.all_gather(tower_in.astype(jnp.bfloat16), ('rows', 'field'), axis=1,...]
    psum x2 -> x0, blocking collectives: 72.1 us -> none  [the longest x1 40 us: on_device(): lax.psum((grad_second, grad_tower, grad_head, loss_total), ('rows', 'fiel...]
    reduce_scatter x4 -> x0, waiting for transfers between devices: 52.1 us -> none  [on_device(): lax.psum_scatter(jnp.dot(rows_x, first_both, preferred_element_type=jnp.f...]
    ppermute x0 -> x22, waiting for transfers between devices: none -> 38.3 us  [the longest x20 37 us: swap(): return lax.ppermute(values, both, self.pairs(step))]
    pallas_call x0 -> x9, Pallas kernels: none -> 27.1 us  [the longest x1 10.4 us: on_device(): pl.pallas_call(rest_kernel, in_specs=[smem] + [vmem] * 8, out_specs=[vmem...]
    ppermute x0 -> x22, starting transfers between devices: none -> 22.5 us  [the longest x20 20 us: swap(): return lax.ppermute(values, both, self.pairs(step))]
  transfers between devices with their start and end apart: 12 -> 22, of which waited for: 5 -> 15; matrix products, arithmetic and copies ran while one was open for 17% -> 7% of each run, Pallas kernels for 0% -> 16%
where the time goes in v3:
time: 102 us; the launch traced here: 101 us
  waiting for transfers between devices  38.3 us (38%)
  Pallas kernels  27.1 us (27%)
  starting transfers between devices  22.5 us (22%)
  local copies, waits for them, and re-layouts  7.32 us (7%)
  other arithmetic  3.29 us (3%)
  between operations  2.7 us (3%)
    ppermute x20, waiting for transfers between devices, swap(): return lax.ppermute(values, both, self.pairs(step))  37 us
    ppermute x20, starting transfers between devices, swap(): return lax.ppermute(values, both, self.pairs(step))  20 us
    pallas_call x1, Pallas kernels, on_device(): pl.pallas_call(rest_kernel, in_specs=[smem] + [vmem] * 8, out_specs=[vmem...  10.4 us
    pallas_call x1, Pallas kernels, on_device(): pl.pallas_call(first_kernel, in_specs=[smem] + [vmem] * 4, out_specs=[vme...  5.84 us
    unnamed x53, local copies, waits for them, and re-layouts  5.21 us
    pallas_call x1, Pallas kernels, on_device(): pl.pallas_call(input_kernel, grid_spec=pltpu.PrefetchScalarGridSpec(num_s...  4.38 us
    pallas_call x1, Pallas kernels, on_device(): pl.pallas_call(outer_kernel, in_specs=[smem] + [vmem] * 3, out_specs=[vme...  2.28 us
    pallas_call x1, Pallas kernels, on_device(): pl.pallas_call(place_kernel, grid_spec=pltpu.PrefetchScalarGridSpec(num_s...  2.1 us
  transfers between devices with their start and end apart: 22, of which 15 were waited for; matrix products, arithmetic and copies ran while one was open for 7% of the time, Pallas kernels for 16%

profile of v3, /device:TPU:0, one launch (start us, length us, event | category | flops | bytes accessed | tf_op | source)
XLA Modules:
  0.0 101.2 jit_solution(16652102275134646481)
XLA Ops:
  0.7 0.9 copy-done.1
  1.6 0.7 copy-done.9
  2.3 4.1 %collective-permute-start.1 = (bf16[16,2176]{1,0:T(8,128)(2,1)S(1)}, bf16[16,2176]{1,0:T(8,128)(2,1)S(1)}, u32[]{:S(2)}, u32[]{:S(2)}) collective-permute-start(bf16[16,2176]{1,0:T(8,128)(2,1)S(1)} %pack_a.1), channel_id=1, source_target_pairs={{0,16},{1,17},{2,18},{3,19},{4,20},{5,21},{6,22},{7,23},{8,24},{9,... | collective-permute-start | bytes 208904 | tf_op jit(solution)/shard_map/ppermute | solution.py:314
  6.4 1.3 %dynamic-slice_convert_fusion.2 = (f32[4,256]{1,0:T(4,128)S(1)}, s32[]{:T(128)}) fusion(s32[4,512]{1,0:T(4,128)} %param.20, s32[]{:T(128)S(6)} %select_n.62), kind=kLoop, calls=%fused_computation.93 | loop fusion | flops 2047 | bytes 8200 | tf_op jit(solution)/shard_map/convert_element_type | solution.py:469
  9.0 0.6 fusion.15
  9.8 0.8 copy-done.3
  10.6 0.7 copy-done.11
  11.3 1.1 %constant_dynamic-slice_fusion = bf16[4,256,256]{2,1,0:T(8,128)(2,1)S(1)} fusion(bf16[4,512,256]{2,1,0:T(8,128)(2,1)} %in_ref.1, s32[]{:T(128)S(6)} %select_n.66), kind=kLoop, calls=%fused_computation.96 | loop fusion | bytes 1048580 | tf_op jit(solution)/shard_map/dynamic_slice | solution.py:430
  12.4 1.9 %collective-permute-start.8 = (bf16[1024,256]{1,0:T(8,128)(2,1)S(1)}, bf16[1024,256]{1,0:T(8,128)(2,1)S(1)}, u32[]{:S(2)}, u32[]{:S(2)}) collective-permute-start(bf16[1024,256]{1,0:T(8,128)(2,1)S(1)} %bitcast.7), channel_id=1, source_target_pairs={{0,1},{1,0},{2,3},{3,2},{4,5},{5,4},{6,7},{7,6},{8,9},{9,8},{10,11... | collective-permute-start | bytes 1572872 | tf_op jit(solution)/shard_map/ppermute | solution.py:450
  14.3 0.6 constant_dynamic-update-slice_fusion.8
  15.4 1.6 %collective-permute-start.3 = (bf16[32,2176]{1,0:T(8,128)(2,1)S(1)}, bf16[32,2176]{1,0:T(8,128)(2,1)S(1)}, u32[]{:S(2)}, u32[]{:S(2)}) collective-permute-start(bf16[32,2176]{1,0:T(8,128)(2,1)S(1)} %pad_maximum_fusion.5), channel_id=1, source_target_pairs={{0,8},{1,9},{2,10},{3,11},{4,12},{5,13},{6,14},{7,15},{8,0},{9,1},... | collective-permute-start | bytes 417800 | tf_op jit(solution)/shard_map/ppermute | solution.py:314
  17.1 0.6 constant_dynamic-update-slice_fusion.7
  17.7 0.7 collective-permute-start.2
  18.4 3.0 %collective-permute-done.3 = bf16[32,2176]{1,0:T(8,128)(2,1)S(1)} collective-permute-done((bf16[32,2176]{1,0:T(8,128)(2,1)S(1)}, bf16[32,2176]{1,0:T(8,128)(2,1)S(1)}, u32[]{:S(2)}, u32[]{:S(2)}) %collective-permute-start.3) | collective-permute-done | bytes 139296 | tf_op jit(solution)/shard_map/ppermute | solution.py:314
  21.4 1.6 %collective-permute-start.5 = (bf16[64,2176]{1,0:T(8,128)(2,1)S(1)}, bf16[64,2176]{1,0:T(8,128)(2,1)S(1)}, u32[]{:S(2)}, u32[]{:S(2)}) collective-permute-start(bf16[64,2176]{1,0:T(8,128)(2,1)S(1)} %pad_maximum_fusion.3), channel_id=1, source_target_pairs={{0,4},{1,5},{2,3},{3,2},{4,0},{5,1},{6,7},{7,6},{8,12},{9,13},{10,... | collective-permute-start | bytes 835592 | tf_op jit(solution)/shard_map/ppermute | solution.py:314
  23.0 0.7 constant_dynamic-update-slice_fusion.6
  23.7 0.8 collective-permute-start.4
  24.5 3.6 %collective-permute-done.5 = bf16[64,2176]{1,0:T(8,128)(2,1)S(1)} collective-permute-done((bf16[64,2176]{1,0:T(8,128)(2,1)S(1)}, bf16[64,2176]{1,0:T(8,128)(2,1)S(1)}, u32[]{:S(2)}, u32[]{:S(2)}) %collective-permute-start.5) | collective-permute-done | bytes 278560 | tf_op jit(solution)/shard_map/ppermute | solution.py:314
  28.4 1.4 %collective-permute-done.4 = bf16[64,1280]{1,0:T(8,128)(2,1)S(1)} collective-permute-done((bf16[64,1280]{1,0:T(8,128)(2,1)S(1)}, bf16[64,1280]{1,0:T(8,128)(2,1)S(1)}, u32[]{:S(2)}, u32[]{:S(2)}) %collective-permute-start.4) | collective-permute-done | bytes 163872 | tf_op jit(solution)/shard_map/ppermute | solution.py:314
  29.9 1.1 %rows.1 = (bf16[1024,512]{1,0:T(8,128)(2,1)S(1)}, bf16[512,1024]{1,0:T(8,128)(2,1)S(1)}, f32[1024,8]{1,0:T(8,128)S(1)}) custom-call(s32[34]{0:T(128)S(1)} %pad_add_fusion.tab, bf16[4,512,256]{2,1,0:T(8,128)(2,1)S(1)} %copy-done, bf16[1024,256]{1,0:T(8,128)(2,1)S(1)} %collective-permute-done.8.got_ref, f32[4,8,256]{2,1,0:T(8,128)S(1)} %stack.27.meta_ref), custom_call_target="tpu_custom_call" | custom-call | flops 1048576 | bytes 8388608 | tf_op jit(solution)/shard_map/rows/pallas_call | solution.py:476
  31.0 6.7 %collective-permute-done.7 = bf16[128,2176]{1,0:T(8,128)(2,1)S(1)} collective-permute-done((bf16[128,2176]{1,0:T(8,128)(2,1)S(1)}, bf16[128,2176]{1,0:T(8,128)(2,1)S(1)}, u32[]{:S(2)}, u32[]{:S(2)}) %collective-permute-start.7) | collective-permute-done | bytes 557088 | tf_op jit(solution)/shard_map/ppermute | solution.py:314
  37.9 1.0 collective-permute-start.6
  38.8 1.8 %collective-permute-done.9.oth_ref = bf16[256,2176]{1,0:T(8,128)(2,1)S(1)} collective-permute-done((bf16[256,2176]{1,0:T(8,128)(2,1)S(1)}, bf16[256,2176]{1,0:T(8,128)(2,1)S(1)}, u32[]{:S(2)}, u32[]{:S(2)}) %collective-permute-start.9) | collective-permute-done | bytes 1114144 | tf_op jit(solution)/shard_map/ppermute | solution.py:314
  40.6 5.8 %first.1 = (bf16[1024,2048]{1,0:T(8,128)(2,1)S(1)}, bf16[1024,2048]{1,0:T(8,128)(2,1)S(1)}, f32[1024,128]{1,0:T(8,128)S(1)}, bf16[512,2176]{1,0:T(8,128)(2,1)S(1)}) custom-call(s32[34]{0:T(128)S(1)} %pad_add_fusion.tab, bf16[256,2176]{1,0:T(8,128)(2,1)S(1)} %constant_dynamic-update-slice_fusion.9.own_ref, ...), custom_call_target="tpu_custom_call" | custom-call | flops 4563402752 | bytes 8388608 | tf_op jit(solution)/shard_map/first/pallas_call | solution.py:494
  46.7 2.0 %collective-permute-done.10.oth_ref = bf16[256,1280]{1,0:T(8,128)(2,1)S(1)} collective-permute-done((bf16[256,1280]{1,0:T(8,128)(2,1)S(1)}, bf16[256,1280]{1,0:T(8,128)(2,1)S(1)}, u32[]{:S(2)}, u32[]{:S(2)}) %collective-permute-start.10) | collective-permute-done | bytes 655392 | tf_op jit(solution)/shard_map/ppermute | solution.py:314
  48.7 10.4 %rest.1 = (bf16[1024,256]{1,0:T(8,128)(2,1)S(1)}, f32[256,256]{1,0:T(8,128)S(1)}, f32[8,1152]{1,0:T(8,128)S(1)}, bf16[1024,2048]{1,0:T(8,128)(2,1)S(1)}, bf16[10...) custom-call(s32[34]{0:T(128)S(1)} %pad_add_fusion.tab, ...), custom_call_target="tpu_custom_call" | custom-call | flops 6845104128 | bytes 8388608 | tf_op jit(solution)/shard_map/rest/pallas_call | solution.py:515
  59.3 2.3 %outer.1 = (f32[256,1152]{1,0:T(8,128)S(1)}, bf16[256,1152]{1,0:T(8,128)(2,1)S(1)}) custom-call(s32[34]{0:T(128)S(1)} %pad_add_fusion.tab, bf16[1024,256]{1,0:T(8,128)(2,1)S(1)} %get-tuple-element.92.dm_ref, bf16[1024,2048]{1,0:T(8,128)(2,1)S(1)} %get-tuple-element.88.ga_ref, f32[256,256]{1,0:T(8,128)S(1)} %get-tuple-element.93.gti_ref), custom_call_target="tpu_custom_call" | custom-call | flops 2147483648 | bytes 8388608 | tf_op jit(solution)/shard_map/outer/pallas_call | solution.py:543
  62.4 0.7 collective-permute-start.14
  63.1 0.7 collective-permute-done.11
  64.0 0.9 collective-permute-start.13
  64.9 4.4 %input.1 = (f32[4,512,256]{2,1,0:T(8,128)}, bf16[1024,256]{1,0:T(8,128)(2,1)S(1)}) custom-call(s32[34]{0:T(128)S(1)} %pad_add_fusion.tab, bf16[1024,2048]{1,0:T(8,128)(2,1)S(1)} %get-tuple-element.106.dp_ref, bf16[1024,128]{1,0:T(8,128)(2,1)S(1)} %get-tuple-element.108.dg_ref, bf16[512,2176]{1,0:T(8,128)(2,1)S(1)} %get-tuple-element.109.w_ref), custom_call_target="tpu_custom_call" | custom-call | flops 4563402752 | bytes 8388608 | tf_op jit(solution)/shard_map/input/pallas_call | solution.py:565
  69.3 2.7 %collective-permute-done.14 = bf16[128,2176]{1,0:T(8,128)(2,1)S(1)} collective-permute-done((bf16[128,2176]{1,0:T(8,128)(2,1)S(1)}, bf16[128,2176]{1,0:T(8,128)(2,1)S(1)}, u32[]{:S(2)}, u32[]{:S(2)}) %collective-permute-start.14) | collective-permute-done | bytes 557088 | tf_op jit(solution)/shard_map/ppermute | solution.py:314
  72.1 3.2 %collective-permute-done.13 = bf16[136,1152]{1,0:T(8,128)(2,1)S(1)} collective-permute-done((bf16[136,1152]{1,0:T(8,128)(2,1)S(1)}, bf16[136,1152]{1,0:T(8,128)(2,1)S(1)}, u32[]{:S(2)}, u32[]{:S(2)}) %collective-permute-start.13) | collective-permute-done | bytes 313376 | tf_op jit(solution)/shard_map/ppermute | solution.py:314
  75.4 1.6 %collective-permute-start.16 = (bf16[64,2176]{1,0:T(8,128)(2,1)S(1)}, bf16[64,2176]{1,0:T(8,128)(2,1)S(1)}, u32[]{:S(2)}, u32[]{:S(2)}) collective-permute-start(bf16[64,2176]{1,0:T(8,128)(2,1)S(1)} %slice.296), channel_id=1, source_target_pairs={{0,4},{1,5},{2,3},{3,2},{4,0},{5,1},{6,7},{7,6},{8,12},{9,13},{10,... | collective-permute-start | bytes 835592 | tf_op jit(solution)/shard_map/ppermute | solution.py:314
  77.1 0.6 collective-permute-start.15
  77.7 4.4 %collective-permute-done.16 = bf16[64,2176]{1,0:T(8,128)(2,1)S(1)} collective-permute-done((bf16[64,2176]{1,0:T(8,128)(2,1)S(1)}, bf16[64,2176]{1,0:T(8,128)(2,1)S(1)}, u32[]{:S(2)}, u32[]{:S(2)}) %collective-permute-start.16) | collective-permute-done | bytes 278560 | tf_op jit(solution)/shard_map/ppermute | solution.py:314
  82.1 1.7 %collective-permute-done.15 = bf16[72,1152]{1,0:T(8,128)(2,1)S(1)} collective-permute-done((bf16[72,1152]{1,0:T(8,128)(2,1)S(1)}, bf16[72,1152]{1,0:T(8,128)(2,1)S(1)}, u32[]{:S(2)}, u32[]{:S(2)}) %collective-permute-start.15) | collective-permute-done | bytes 165920 | tf_op jit(solution)/shard_map/ppermute | solution.py:314
  83.9 1.2 %collective-permute-start.18 = (bf16[32,2176]{1,0:T(8,128)(2,1)S(1)}, bf16[32,2176]{1,0:T(8,128)(2,1)S(1)}, u32[]{:S(2)}, u32[]{:S(2)}) collective-permute-start(bf16[32,2176]{1,0:T(8,128)(2,1)S(1)} %slice.298), channel_id=1, source_target_pairs={{0,8},{1,9},{2,10},{3,11},{4,12},{5,13},{6,14},{7,15},{8,0},{9,1},... | collective-permute-start | bytes 417800 | tf_op jit(solution)/shard_map/ppermute | solution.py:314
  85.1 1.0 collective-permute-start.17
  86.1 0.6 collective-permute-start.20
  86.7 2.2 %collective-permute-done.18 = bf16[32,2176]{1,0:T(8,128)(2,1)S(1)} collective-permute-done((bf16[32,2176]{1,0:T(8,128)(2,1)S(1)}, bf16[32,2176]{1,0:T(8,128)(2,1)S(1)}, u32[]{:S(2)}, u32[]{:S(2)}) %collective-permute-start.18) | collective-permute-done | bytes 139296 | tf_op jit(solution)/shard_map/ppermute | solution.py:314
  89.0 0.9 collective-permute-done.17
  90.1 3.0 %collective-permute-start.19 = (bf16[24,1152]{1,0:T(8,128)(2,1)S(1)}, bf16[24,1152]{1,0:T(8,128)(2,1)S(1)}, u32[]{:S(2)}, u32[]{:S(2)}) collective-permute-start(bf16[24,1152]{1,0:T(8,128)(2,1)S(1)} %pad_maximum_fusion.7), channel_id=1, source_target_pairs={{0,16},{1,17},{2,18},{3,19},{4,20},{5,21},{6,22},{7,23},{8,24},{9,... | collective-permute-start | bytes 165896 | tf_op jit(solution)/shard_map/ppermute | solution.py:314
  93.2 2.8 %collective-permute-done.19 = bf16[24,1152]{1,0:T(8,128)(2,1)S(1)} collective-permute-done((bf16[24,1152]{1,0:T(8,128)(2,1)S(1)}, bf16[24,1152]{1,0:T(8,128)(2,1)S(1)}, u32[]{:S(2)}, u32[]{:S(2)}) %collective-permute-start.19) | collective-permute-done | bytes 55328 | tf_op jit(solution)/shard_map/ppermute | solution.py:314
  96.0 0.5 slice.227
  96.5 1.3 %collective-permute-done.20.got_ref = bf16[1024,256]{1,0:T(8,128)(2,1)S(1)} collective-permute-done((bf16[1024,256]{1,0:T(8,128)(2,1)S(1)}, bf16[1024,256]{1,0:T(8,128)(2,1)S(1)}, u32[]{:S(2)}, u32[]{:S(2)}) %collective-permute-start.20) | collective-permute-done | bytes 524320 | tf_op jit(solution)/shard_map/ppermute | solution.py:589
  97.9 2.1 %place.1 = f32[4,512,256]{2,1,0:T(8,128)} custom-call(s32[34]{0:T(128)S(1)} %pad_add_fusion.tab, bf16[1024,256]{1,0:T(8,128)(2,1)S(1)} %collective-permute-done.20.got_ref, f32[4,512,256]{2,1,0:T(8,128)} %get-tuple-element.112.held_ref), custom_call_target="tpu_custom_call", output_to_operand_aliasing={{}: (2, {})} | custom-call | flops 1048576 | bytes 8388608 | tf_op jit(solution)/shard_map/place/pallas_call | solution.py:593
  100.1 0.9 update.1
  (129 shorter events, 3.4 us)
Async XLA Ops:
  0.7 0.9 copy-start.1
  1.6 0.7 copy-start.9
  2.3 13.0 %copy-start.21 = (s32[4,512]{1,0:T(4,128)S(1)}, s32[4,512]{1,0:T(4,128)}, u32[]{:S(2)}) copy-start(s32[4,512]{1,0:T(4,128)} %param.22) | copy-start | bytes 24580
  2.3 13.0 %copy-start.22 = (s32[4,512]{1,0:T(4,128)S(1)}, s32[4,512]{1,0:T(4,128)}, u32[]{:S(2)}) copy-start(s32[4,512]{1,0:T(4,128)} %param.21) | copy-start | bytes 24580
  2.3 13.2 %collective-permute-start.1 = (bf16[16,2176]{1,0:T(8,128)(2,1)S(1)}, bf16[16,2176]{1,0:T(8,128)(2,1)S(1)}, u32[]{:S(2)}, u32[]{:S(2)}) collective-permute-start(bf16[16,2176]{1,0:T(8,128)(2,1)S(1)} %pack_a.1), channel_id=1, source_target_pairs={{0,16},{1,17},{2,18},{3,19},{4,20},{5,21},{6,22},{7,23},{8,24},{9,... | collective-permute-start | bytes 208904 | tf_op jit(solution)/shard_map/ppermute | solution.py:314
  9.8 0.8 copy-start.3
  10.6 0.7 copy-start.11
  11.3 5.8 %collective-permute-start = (bf16[16,1280]{1,0:T(8,128)(2,1)S(1)}, bf16[16,1280]{1,0:T(8,128)(2,1)S(1)}, u32[]{:S(2)}, u32[]{:S(2)}) collective-permute-start(bf16[16,1280]{1,0:T(8,128)(2,1)S(1)} %pack_b.1), channel_id=1, source_target_pairs={{0,16},{1,17},{2,18},{3,19},{4,20},{5,21},{6,22},{7,23},{8,24},{9,... | collective-permute-start | bytes 122888 | tf_op jit(solution)/shard_map/ppermute | solution.py:314
  12.4 17.5 %collective-permute-start.8 = (bf16[1024,256]{1,0:T(8,128)(2,1)S(1)}, bf16[1024,256]{1,0:T(8,128)(2,1)S(1)}, u32[]{:S(2)}, u32[]{:S(2)}) collective-permute-start(bf16[1024,256]{1,0:T(8,128)(2,1)S(1)} %bitcast.7), channel_id=1, source_target_pairs={{0,1},{1,0},{2,3},{3,2},{4,5},{5,4},{6,7},{7,6},{8,9},{9,8},{10,11... | collective-permute-start | bytes 1572872 | tf_op jit(solution)/shard_map/ppermute | solution.py:450
  15.4 6.0 %collective-permute-start.3 = (bf16[32,2176]{1,0:T(8,128)(2,1)S(1)}, bf16[32,2176]{1,0:T(8,128)(2,1)S(1)}, u32[]{:S(2)}, u32[]{:S(2)}) collective-permute-start(bf16[32,2176]{1,0:T(8,128)(2,1)S(1)} %pad_maximum_fusion.5), channel_id=1, source_target_pairs={{0,8},{1,9},{2,10},{3,11},{4,12},{5,13},{6,14},{7,15},{8,0},{9,1},... | collective-permute-start | bytes 417800 | tf_op jit(solution)/shard_map/ppermute | solution.py:314
  17.7 5.3 %collective-permute-start.2 = (bf16[32,1280]{1,0:T(8,128)(2,1)S(1)}, bf16[32,1280]{1,0:T(8,128)(2,1)S(1)}, u32[]{:S(2)}, u32[]{:S(2)}) collective-permute-start(bf16[32,1280]{1,0:T(8,128)(2,1)S(1)} %get-tuple-element.145), channel_id=1, source_target_pairs={{0,8},{1,9},{2,10},{3,11},{4,12},{5,13},{6,14},{7,15},{8,0},{9,1},... | collective-permute-start | bytes 245768 | tf_op jit(solution)/shard_map/ppermute | solution.py:314
  21.4 6.6 %collective-permute-start.5 = (bf16[64,2176]{1,0:T(8,128)(2,1)S(1)}, bf16[64,2176]{1,0:T(8,128)(2,1)S(1)}, u32[]{:S(2)}, u32[]{:S(2)}) collective-permute-start(bf16[64,2176]{1,0:T(8,128)(2,1)S(1)} %pad_maximum_fusion.3), channel_id=1, source_target_pairs={{0,4},{1,5},{2,3},{3,2},{4,0},{5,1},{6,7},{7,6},{8,12},{9,13},{10,... | collective-permute-start | bytes 835592 | tf_op jit(solution)/shard_map/ppermute | solution.py:314
  23.7 6.2 %copy-start.20 = (bf16[128,1280]{1,0:T(8,128)(2,1)S(1)}, bf16[128,1280]{1,0:T(8,128)(2,1)}, u32[]{:S(2)}) copy-start(bf16[128,1280]{1,0:T(8,128)(2,1)} %get-tuple-element.139) | copy-start | bytes 983044
  23.7 6.2 %collective-permute-start.4 = (bf16[64,1280]{1,0:T(8,128)(2,1)S(1)}, bf16[64,1280]{1,0:T(8,128)(2,1)S(1)}, u32[]{:S(2)}, u32[]{:S(2)}) collective-permute-start(bf16[64,1280]{1,0:T(8,128)(2,1)S(1)} %get-tuple-element.141), channel_id=1, source_target_pairs={{0,4},{1,5},{2,3},{3,2},{4,0},{5,1},{6,7},{7,6},{8,12},{9,13},{10,... | collective-permute-start | bytes 491528 | tf_op jit(solution)/shard_map/ppermute | solution.py:314
  24.5 5.4 %copy-start = (bf16[4,512,256]{2,1,0:T(8,128)(2,1)S(1)}, bf16[4,512,256]{2,1,0:T(8,128)(2,1)}, u32[]{:S(2)}) copy-start(bf16[4,512,256]{2,1,0:T(8,128)(2,1)} %in_ref.1) | copy-start | bytes 3145732
  28.1 9.6 %collective-permute-start.7 = (bf16[128,2176]{1,0:T(8,128)(2,1)S(1)}, bf16[128,2176]{1,0:T(8,128)(2,1)S(1)}, u32[]{:S(2)}, u32[]{:S(2)}) collective-permute-start(bf16[128,2176]{1,0:T(8,128)(2,1)S(1)} %pad_maximum_fusion.1), channel_id=1, source_target_pairs={{0,1},{1,0},{2,6},{3,7},{4,5},{5,4},{6,2},{7,3},{8,9},{9,8},{10,14... | collective-permute-start | bytes 1671176 | tf_op jit(solution)/shard_map/ppermute | solution.py:314
  37.8 2.8 %collective-permute-start.9 = (bf16[256,2176]{1,0:T(8,128)(2,1)S(1)}, bf16[256,2176]{1,0:T(8,128)(2,1)S(1)}, u32[]{:S(2)}, u32[]{:S(2)}) collective-permute-start(bf16[256,2176]{1,0:T(8,128)(2,1)S(1)} %constant_dynamic-update-slice_fusion.9.own_ref), channel_id=1, source_target_pairs={{0,2},{1,3},{2,0},{3,1},{4,6},{5,7},{6,4},{7,5},{8,10},{9,11},{10,... | collective-permute-start | bytes 3342344 | tf_op jit(solution)/shard_map/ppermute | solution.py:314
  37.9 8.6 %collective-permute-start.6 = (bf16[128,1280]{1,0:T(8,128)(2,1)S(1)}, bf16[128,1280]{1,0:T(8,128)(2,1)S(1)}, u32[]{:S(2)}, u32[]{:S(2)}) collective-permute-start(bf16[128,1280]{1,0:T(8,128)(2,1)S(1)} %get-tuple-element.137), channel_id=1, source_target_pairs={{0,1},{1,0},{2,6},{3,7},{4,5},{5,4},{6,2},{7,3},{8,9},{9,8},{10,14... | collective-permute-start | bytes 983048 | tf_op jit(solution)/shard_map/ppermute | solution.py:314
  40.6 6.1 %copy-start.17 = (f32[2,128]{1,0:T(2,128)S(1)}, f32[2,128]{1,0:T(2,128)}, u32[]{:S(2)}) copy-start(f32[2,128]{1,0:T(2,128)} %refs_4_.1) | copy-start | bytes 3076
  46.5 2.2 %collective-permute-start.10 = (bf16[256,1280]{1,0:T(8,128)(2,1)S(1)}, bf16[256,1280]{1,0:T(8,128)(2,1)S(1)}, u32[]{:S(2)}, u32[]{:S(2)}) collective-permute-start(bf16[256,1280]{1,0:T(8,128)(2,1)S(1)} %constant_dynamic-update-slice_fusion.14.own_ref), channel_id=1, source_target_pairs={{0,2},{1,3},{2,0},{3,1},{4,6},{5,7},{6,4},{7,5},{8,10},{9,11},{10,... | collective-permute-start | bytes 1966088 | tf_op jit(solution)/shard_map/ppermute | solution.py:314
  59.1 3.0 %collective-permute-start.12 = (bf16[256,2176]{1,0:T(8,128)(2,1)S(1)}, bf16[256,2176]{1,0:T(8,128)(2,1)S(1)}, u32[]{:S(2)}, u32[]{:S(2)}) collective-permute-start(bf16[256,2176]{1,0:T(8,128)(2,1)S(1)} %get-tuple-element.96), channel_id=1, source_target_pairs={{0,2},{1,3},{2,0},{3,1},{4,6},{5,7},{6,4},{7,5},{8,10},{9,11},{10,... | collective-permute-start | bytes 3342344 | tf_op jit(solution)/shard_map/ppermute | solution.py:314
  61.6 2.1 %collective-permute-start.11 = (bf16[264,1152]{1,0:T(8,128)(2,1)S(1)}, bf16[264,1152]{1,0:T(8,128)(2,1)S(1)}, u32[]{:S(2)}, u32[]{:S(2)}) collective-permute-start(bf16[264,1152]{1,0:T(8,128)(2,1)S(1)} %pad_maximum_fusion), channel_id=1, source_target_pairs={{0,2},{1,3},{2,0},{3,1},{4,6},{5,7},{6,4},{7,5},{8,10},{9,11},{10,... | collective-permute-start | bytes 1824776 | tf_op jit(solution)/shard_map/ppermute | solution.py:314
  62.4 9.6 %collective-permute-start.14 = (bf16[128,2176]{1,0:T(8,128)(2,1)S(1)}, bf16[128,2176]{1,0:T(8,128)(2,1)S(1)}, u32[]{:S(2)}, u32[]{:S(2)}) collective-permute-start(bf16[128,2176]{1,0:T(8,128)(2,1)S(1)} %slice.294), channel_id=1, source_target_pairs={{0,1},{1,0},{2,6},{3,7},{4,5},{5,4},{6,2},{7,3},{8,9},{9,8},{10,14... | collective-permute-start | bytes 1671176 | tf_op jit(solution)/shard_map/ppermute | solution.py:314
  64.0 11.4 %collective-permute-start.13 = (bf16[136,1152]{1,0:T(8,128)(2,1)S(1)}, bf16[136,1152]{1,0:T(8,128)(2,1)S(1)}, u32[]{:S(2)}, u32[]{:S(2)}) collective-permute-start(bf16[136,1152]{1,0:T(8,128)(2,1)S(1)} %pad_maximum_fusion.2), channel_id=1, source_target_pairs={{0,1},{1,0},{2,6},{3,7},{4,5},{5,4},{6,2},{7,3},{8,9},{9,8},{10,14... | collective-permute-start | bytes 940040 | tf_op jit(solution)/shard_map/ppermute | solution.py:314
  75.4 6.6 %collective-permute-start.16 = (bf16[64,2176]{1,0:T(8,128)(2,1)S(1)}, bf16[64,2176]{1,0:T(8,128)(2,1)S(1)}, u32[]{:S(2)}, u32[]{:S(2)}) collective-permute-start(bf16[64,2176]{1,0:T(8,128)(2,1)S(1)} %slice.296), channel_id=1, source_target_pairs={{0,4},{1,5},{2,3},{3,2},{4,0},{5,1},{6,7},{7,6},{8,12},{9,13},{10,... | collective-permute-start | bytes 835592 | tf_op jit(solution)/shard_map/ppermute | solution.py:314
  77.1 6.7 %collective-permute-start.15 = (bf16[72,1152]{1,0:T(8,128)(2,1)S(1)}, bf16[72,1152]{1,0:T(8,128)(2,1)S(1)}, u32[]{:S(2)}, u32[]{:S(2)}) collective-permute-start(bf16[72,1152]{1,0:T(8,128)(2,1)S(1)} %pad_maximum_fusion.4), channel_id=1, source_target_pairs={{0,4},{1,5},{2,3},{3,2},{4,0},{5,1},{6,7},{7,6},{8,12},{9,13},{10,... | collective-permute-start | bytes 497672 | tf_op jit(solution)/shard_map/ppermute | solution.py:314
  83.9 5.1 %collective-permute-start.18 = (bf16[32,2176]{1,0:T(8,128)(2,1)S(1)}, bf16[32,2176]{1,0:T(8,128)(2,1)S(1)}, u32[]{:S(2)}, u32[]{:S(2)}) collective-permute-start(bf16[32,2176]{1,0:T(8,128)(2,1)S(1)} %slice.298), channel_id=1, source_target_pairs={{0,8},{1,9},{2,10},{3,11},{4,12},{5,13},{6,14},{7,15},{8,0},{9,1},... | collective-permute-start | bytes 417800 | tf_op jit(solution)/shard_map/ppermute | solution.py:314
  85.1 4.8 %collective-permute-start.17 = (bf16[40,1152]{1,0:T(8,128)(2,1)S(1)}, bf16[40,1152]{1,0:T(8,128)(2,1)S(1)}, u32[]{:S(2)}, u32[]{:S(2)}) collective-permute-start(bf16[40,1152]{1,0:T(8,128)(2,1)S(1)} %pad_maximum_fusion.6), channel_id=1, source_target_pairs={{0,8},{1,9},{2,10},{3,11},{4,12},{5,13},{6,14},{7,15},{8,0},{9,1},... | collective-permute-start | bytes 276488 | tf_op jit(solution)/shard_map/ppermute | solution.py:314
  86.1 11.7 %collective-permute-start.20 = (bf16[1024,256]{1,0:T(8,128)(2,1)S(1)}, bf16[1024,256]{1,0:T(8,128)(2,1)S(1)}, u32[]{:S(2)}, u32[]{:S(2)}) collective-permute-start(bf16[1024,256]{1,0:T(8,128)(2,1)S(1)} %get-tuple-element.111), channel_id=1, source_target_pairs={{0,1},{1,0},{2,3},{3,2},{4,5},{5,4},{6,7},{7,6},{8,9},{9,8},{10,11... | collective-permute-start | bytes 1572872 | tf_op jit(solution)/shard_map/ppermute | solution.py:589
  90.1 5.9 %collective-permute-start.19 = (bf16[24,1152]{1,0:T(8,128)(2,1)S(1)}, bf16[24,1152]{1,0:T(8,128)(2,1)S(1)}, u32[]{:S(2)}, u32[]{:S(2)}) collective-permute-start(bf16[24,1152]{1,0:T(8,128)(2,1)S(1)} %pad_maximum_fusion.7), channel_id=1, source_target_pairs={{0,16},{1,17},{2,18},{3,19},{4,20},{5,21},{6,22},{7,23},{8,24},{9,... | collective-permute-start | bytes 165896 | tf_op jit(solution)/shard_map/ppermute | solution.py:314
  93.1 6.9 %collective-permute-start.21 = (bf16[16,2176]{1,0:T(8,128)(2,1)S(1)}, bf16[16,2176]{1,0:T(8,128)(2,1)S(1)}, u32[]{:S(2)}, u32[]{:S(2)}) collective-permute-start(bf16[16,2176]{1,0:T(8,128)(2,1)S(1)} %slice.300), channel_id=1, source_target_pairs={{0,16},{1,17},{2,18},{3,19},{4,20},{5,21},{6,22},{7,23},{8,24},{9,... | collective-permute-start | bytes 208904 | tf_op jit(solution)/shard_map/ppermute | solution.py:314
  97.8 2.2 %copy-start.2 = (f32[16,2048]{1,0:T(8,128)S(1)}, f32[16,2048]{1,0:T(8,128)}, u32[]{:S(2)}) copy-start(f32[16,2048]{1,0:T(8,128)} %refs_0_.1) | copy-start | bytes 393220
  97.8 2.2 %copy-start.4 = (f32[8,8,256]{2,1,0:T(8,128)S(1)}, f32[8,8,256]{2,1,0:T(8,128)}, u32[]{:S(2)}) copy-start(f32[8,8,256]{2,1,0:T(8,128)} %refs_2_.1) | copy-start | bytes 196612
  97.8 2.2 %copy-start.5 = (f32[16,2048]{1,0:T(8,128)S(1)}, f32[16,2048]{1,0:T(8,128)}, u32[]{:S(2)}) copy-start(f32[16,2048]{1,0:T(8,128)} %refs_5_.1) | copy-start | bytes 393220
  97.8 2.2 %copy-start.6 = (f32[16,2048]{1,0:T(8,128)S(1)}, f32[16,2048]{1,0:T(8,128)}, u32[]{:S(2)}) copy-start(f32[16,2048]{1,0:T(8,128)} %refs_10_.1) | copy-start | bytes 393220
  97.8 2.3 %copy-start.7 = (f32[8,8,256]{2,1,0:T(8,128)S(1)}, f32[8,8,256]{2,1,0:T(8,128)}, u32[]{:S(2)}) copy-start(f32[8,8,256]{2,1,0:T(8,128)} %refs_7_.1) | copy-start | bytes 196612
  97.8 2.2 %copy-start.8 = (f32[8,8,256]{2,1,0:T(8,128)S(1)}, f32[8,8,256]{2,1,0:T(8,128)}, u32[]{:S(2)}) copy-start(f32[8,8,256]{2,1,0:T(8,128)} %refs_12_.1) | copy-start | bytes 196612
  97.8 2.2 %copy-start.10 = (f32[16,16]{1,0:T(8,128)S(1)}, f32[16,16]{1,0:T(8,128)}, u32[]{:S(2)}) copy-start(f32[16,16]{1,0:T(8,128)} %refs_1_.1) | copy-start | bytes 3076
  97.8 2.2 %copy-start.12 = (f32[2,8,128]{2,1,0:T(8,128)S(1)}, f32[2,8,128]{2,1,0:T(8,128)}, u32[]{:S(2)}) copy-start(f32[2,8,128]{2,1,0:T(8,128)} %refs_3_.1) | copy-start | bytes 24580
  97.8 2.2 %copy-start.13 = (f32[16,16]{1,0:T(8,128)S(1)}, f32[16,16]{1,0:T(8,128)}, u32[]{:S(2)}) copy-start(f32[16,16]{1,0:T(8,128)} %refs_6_.1) | copy-start | bytes 3076
  97.8 2.2 %copy-start.14 = (f32[2,8,128]{2,1,0:T(8,128)S(1)}, f32[2,8,128]{2,1,0:T(8,128)}, u32[]{:S(2)}) copy-start(f32[2,8,128]{2,1,0:T(8,128)} %refs_8_.1) | copy-start | bytes 24580
  97.9 2.2 %copy-start.15 = (f32[16,16]{1,0:T(8,128)S(1)}, f32[16,16]{1,0:T(8,128)}, u32[]{:S(2)}) copy-start(f32[16,16]{1,0:T(8,128)} %refs_11_.1) | copy-start | bytes 3076
  97.9 2.2 %copy-start.16 = (f32[2,8,128]{2,1,0:T(8,128)S(1)}, f32[2,8,128]{2,1,0:T(8,128)}, u32[]{:S(2)}) copy-start(f32[2,8,128]{2,1,0:T(8,128)} %refs_13_.1) | copy-start | bytes 24580
  97.9 2.2 %copy-start.18 = (f32[2,128]{1,0:T(2,128)S(1)}, f32[2,128]{1,0:T(2,128)}, u32[]{:S(2)}) copy-start(f32[2,128]{1,0:T(2,128)} %refs_9_.1) | copy-start | bytes 3076
  97.9 2.2 %copy-start.19 = (f32[2,128]{1,0:T(2,128)S(1)}, f32[2,128]{1,0:T(2,128)}, u32[]{:S(2)}) copy-start(f32[2,128]{1,0:T(2,128)} %refs_14_.1) | copy-start | bytes 3076

commit v4 on v3

v4 whole, which is shorter than its diff:
```python
import functools
import math

import jax
import jax.numpy as jnp
import numpy as np
from jax import lax
from jax.experimental import pallas as pl
from jax.experimental.pallas import tpu as pltpu
from jax.sharding import PartitionSpec as P

momentum_mu = 0.5
average_keep = 0.5
rate_bases = (17.0, 1.0, 24.0, 4.0, 0.25)
both = ("rows", "field")
f32 = jnp.float32
bf16 = jnp.bfloat16
BLOCK = 16
LANES = 128


def dot(a, b):
    return lax.dot_general(a, b, (((1,), (0,)), ((), ())), preferred_element_type=f32)


def dot_t(a, b):
    return lax.dot_general(a, b, (((1,), (1,)), ((), ())), preferred_element_type=f32)


def t_dot(a, b):
    return lax.dot_general(a, b, (((0,), (0,)), ((), ())), preferred_element_type=f32)


def sigmoid(v):
    return 0.5 + 0.5 * jnp.tanh(0.5 * v)


def rows16(start):
    return pl.ds(pl.multiple_of(start, BLOCK), BLOCK)


class Places:
    def __init__(self, fit, order):
        self.fit, self.order = fit, order

    def bits(self, core, rr, ff):
        out = 0
        for s, (kind, which) in enumerate(self.order):
            if kind == "row":
                bit = (rr >> which) & 1
            else:
                bit = (rr >> 1) & 1 if core == which else ff
            out = out | (bit << s)
        return out

    def start(self):
        r, self.field = lax.axis_index("rows"), lax.axis_index("field")
        self.core = r & 1 if self.fit else jnp.int32(0)
        self.bases = [self.bits(core, r, self.field) for core in range(2)]

    def block(self, side, j):
        core = self.core if side == 0 else 1 - self.core
        pair, ff = j // 2, j % 2
        if not self.fit:
            return j, 2 * pair + side, ff
        ways = [base ^ self.bits(c, 2 * pair, ff) for c, base in enumerate(self.bases)]
        return jnp.where(core == 0, ways[0], ways[1]), 2 * pair + core, ff

    def each(self, pairs, body):
        for j in range(pairs):
            for side in range(2):
                body(side, *self.block(side, j))


def pack_a_kernel(expert_ref, gate_ref, out_ref):
    wide, gates = expert_ref.shape[1], gate_ref.shape[1]
    out_ref[:, 0:wide] = expert_ref[...].astype(bf16)
    out_ref[:, wide:] = jnp.zeros((out_ref.shape[0], LANES), bf16)
    out_ref[:, wide : wide + gates] = gate_ref[...].astype(bf16)


def pack_b_kernel(expert_ref, tower_ref, valid_ref, out_ref):
    experts, rows, out_cols = expert_ref.shape
    part = experts // 2
    for k in range(part):
        both_k = jnp.concatenate([expert_ref[k], expert_ref[k + part]], axis=0)
        out_ref[:, k * out_cols : (k + 1) * out_cols] = both_k.astype(bf16)
    at = part * out_cols
    towers = jnp.concatenate([tower_ref[0], tower_ref[1]], axis=0)
    out_ref[:, at : at + LANES] = towers.astype(bf16)
    tile = valid_ref.shape[1] // 2
    own = valid_ref[:, pl.ds(pl.multiple_of(lax.axis_index("field") * tile, tile), tile)].astype(f32)
    ones = jnp.sum(jnp.sum(own, axis=1, keepdims=True), axis=0, keepdims=True).astype(jnp.int32)
    ones = jnp.broadcast_to(ones, (2 * rows, LANES))
    row, lane = (lax.broadcasted_iota(jnp.int32, ones.shape, d) for d in range(2))
    digits = jnp.where(lane == 2, ones >> 16, jnp.where(lane == 1, ones >> 8, ones) & 255)
    digits = jnp.where((row == 0) & (lane < 3), digits, 0).astype(f32)
    out_ref[:, at + LANES :] = digits.astype(bf16)


def rows_kernel(in_ref, got_ref, valid_ref, label_ref, domain_ref, x_ref, xt_ref, flags_ref, by_row_ref):
    micro, rows_dev, width = in_ref.shape
    tile = rows_dev // 2
    start = pl.multiple_of(lax.axis_index("field") * tile, tile)
    for m in range(micro):
        rows = slice(m * tile, (m + 1) * tile)
        x = jnp.concatenate([in_ref[m, pl.ds(start, tile), :], got_ref[rows, :]], axis=1)
        x_ref[rows, :] = x
        xt_ref[:, rows] = x.T
        kinds = [ref[m : m + 1, pl.ds(start, tile)].astype(f32) for ref in (valid_ref, label_ref, domain_ref)]
        flags = jnp.concatenate(kinds + [jnp.zeros((5, tile), f32)], axis=0)
        flags_ref[:, rows] = flags
        by_row_ref[rows, :] = flags.T


def first_kernel(places, own_ref, oth_ref, x_ref, xt_ref, flags_ref, ga_ref, gs_ref, gate_ref, w_ref):
    half = own_ref.shape[0]
    count, wide = ga_ref.shape
    experts = wide // half
    tile = count // 2
    places.start()

    def put(side, place, rr, ff):
        src = own_ref if side == 0 else oth_ref
        row = (ff ^ places.field) * half + rr * BLOCK
        w_ref[rows16(row), :] = src[rows16(place * BLOCK), :]

    places.each(half // BLOCK, put)
    logits = dot(w_ref[:, wide:].T, xt_ref[...])
    logits = jnp.where(flags_ref[2:3, :] == 0.0, logits[0:experts], logits[experts : 2 * experts])
    raised = jnp.exp(logits - jnp.max(logits, axis=0, keepdims=True))
    gate = raised / jnp.sum(raised, axis=0, keepdims=True)
    gate_ref[...] = jnp.concatenate([gate, gate], axis=0).T

    def step(i, carry):
        rows = pl.ds(pl.multiple_of(i * tile, tile), tile)
        x = x_ref[rows, :]
        gate = 0.5 * gate_ref[rows, :]
        for k in range(experts):
            cols = slice(k * half, (k + 1) * half)
            pre = dot(x, w_ref[:, cols])
            low = 0.5 * pre
            up = 1.0 + jnp.tanh(low)
            scaled = gate[:, k : k + 1] * up
            ga_ref[rows, cols] = (scaled * pre).astype(bf16)
            gs_ref[rows, cols] = (scaled * (1.0 + pre - low * up)).astype(bf16)
        return carry

    lax.fori_loop(0, 2, step, 0)


def second_kernel(
    places,
    own_ref,
    oth_ref,
    ga_ref,
    flags_ref,
    by_row_ref,
    to_ref,
    w_ref,
    dm_ref,
    side_ref,
    keep_ref,
    send_ref,
    ti_ref,
    mix_ref,
    g_ref,
    gti_ref,
):
    half = own_ref.shape[0]
    pairs = half // BLOCK
    count, out_cols = dm_ref.shape
    hidden = half
    wide = ga_ref.shape[1]
    experts = wide // hidden
    part = experts // 2

    places.start()

    digits = jnp.zeros((BLOCK, LANES), f32)
    for side in range(2):
        for j in range(pairs // 2):
            src = own_ref if side == 0 else oth_ref
            (place0, rr, _), (place1, _, _) = places.block(side, 2 * j), places.block(side, 2 * j + 1)
            a0 = src[rows16(place0 * BLOCK), :].astype(f32)
            a1 = src[rows16(place1 * BLOCK), :].astype(f32)
            row = rr * BLOCK
            upper = jnp.concatenate([a0[:8], a1[:8]], axis=0).astype(bf16)
            lower = jnp.concatenate([a0[8:], a1[8:]], axis=0).astype(bf16)
            at = part * out_cols
            for k in range(part):
                cols = slice(k * out_cols, (k + 1) * out_cols)
                w_ref[rows16(k * hidden + row), :] = upper[:, cols]
                w_ref[rows16((k + part) * hidden + row), :] = lower[:, cols]
            ti_ref[rows16(row), 0:LANES] = upper[:, at : at + LANES]
            ti_ref[rows16(row), LANES : 2 * LANES] = lower[:, at : at + LANES]
            digits = digits + (a0 + a1)[:, at + LANES :]
    lane = lax.broadcasted_iota(jnp.int32, digits.shape, 1)
    scale = jnp.where(lane == 0, 1.0, jnp.where(lane == 1, 256.0, jnp.where(lane == 2, 65536.0, 0.0)))
    real = jnp.sum(jnp.sum(digits * scale, axis=1, keepdims=True), axis=0, keepdims=True)

    domain = by_row_ref[:, 2:3]
    heads = to_ref[...].astype(bf16).astype(f32)
    empty = jnp.zeros((6, LANES), f32)
    tile = count // 4
    for i in range(4):
        rows = slice(i * tile, (i + 1) * tile)
        mix_ref[rows, :] = dot(ga_ref[rows, :], w_ref[...]).astype(bf16)
    mixed = mix_ref[...]
    tpre = dot(mixed, ti_ref[...])
    tpre = jnp.where(domain == 0.0, tpre[:, :LANES], tpre[:, LANES:])
    s = sigmoid(tpre)
    act = (tpre * s).astype(bf16)
    logits = dot_t(jnp.concatenate([heads, empty], axis=0).astype(bf16), act)
    valid, label, first = flags_ref[0:1, :], flags_ref[1:2, :], flags_ref[2:3, :] == 0.0
    chosen = jnp.where(first, logits[0:1, :], logits[1:2, :])
    soft = jnp.maximum(chosen, 0.0) + jnp.log1p(jnp.exp(-jnp.abs(chosen)))
    loss = jnp.sum(valid * (soft - label * chosen), axis=1, keepdims=True) / real
    dlogit = valid * (sigmoid(chosen) - label) / real
    dlogit = jnp.concatenate(
        [jnp.where(first, dlogit, 0.0), jnp.where(first, 0.0, dlogit), jnp.zeros((6, count), f32)], axis=0
    ).astype(bf16)
    apart = jnp.concatenate(
        [
            jnp.concatenate([heads[0:1], jnp.zeros((1, LANES), f32)], axis=1),
            jnp.concatenate([jnp.zeros((1, LANES), f32), heads[1:2]], axis=1),
            jnp.concatenate([empty, empty], axis=1),
        ],
        axis=0,
    ).astype(bf16)
    slope = s * (1.0 + tpre * (1.0 - s))
    dtpre = (t_dot(dlogit, apart) * jnp.concatenate([slope, slope], axis=1)).astype(bf16)
    dm_ref[...] = dot_t(dtpre, ti_ref[...]).astype(bf16)
    head_grad = dot(dlogit, act)
    side_ref[...] = jnp.zeros_like(side_ref)
    side_ref[0:1, 0:LANES] = head_grad[0:1]
    side_ref[0:1, LANES : 2 * LANES] = head_grad[1:2]
    side_ref[0:1, 2 * LANES : 3 * LANES] = jnp.broadcast_to(loss, (1, LANES))
    gti_ref[...] = t_dot(mixed, dtpre)

    def pack(above, below, cols):
        def put(side, place, rr, ff):
            dst = keep_ref if side == 0 else send_ref
            row = pl.ds(pl.multiple_of(rr * BLOCK + ff * 8, 8), 8)
            tile = jnp.concatenate([above(row), below(row)], axis=0)
            dst[rows16(place * BLOCK), cols] = tile.astype(dst.dtype)

        places.each(pairs, put)

    for k in range(part):
        g_ref[k] = t_dot(ga_ref[:, k * hidden : (k + 1) * hidden], dm_ref[...])
        g_ref[k + part] = t_dot(ga_ref[:, (k + part) * hidden : (k + part + 1) * hidden], dm_ref[...])
        pack(
            lambda row: g_ref[k, row, :],
            lambda row: g_ref[k + part, row, :],
            slice(k * out_cols, (k + 1) * out_cols),
        )
    at = part * out_cols
    pack(lambda row: gti_ref[row, 0:LANES], lambda row: gti_ref[row, LANES : 2 * LANES], slice(at, at + LANES))


def back_part(places, ks, w_ref, dm_ref, ga_ref, gs_ref, xt_ref, dp_ref, keep_ref, send_ref, g_ref):
    half = keep_ref.shape[0]
    tile = dm_ref.shape[0] // 4
    places.start()
    terms = []
    for at, k in enumerate(ks):
        cols, here = slice(k * half, (k + 1) * half), slice(at * half, (at + 1) * half)
        sums = []
        for i in range(4):
            rows = slice(i * tile, (i + 1) * tile)
            u = dot_t(dm_ref[rows, :], w_ref[cols, :])
            dp_ref[rows, here] = (u * gs_ref[rows, cols].astype(f32)).astype(bf16)
            sums.append(jnp.sum(u * ga_ref[rows, cols].astype(f32), axis=1, keepdims=True))
        terms.append(sums)
        g_ref[:, here] = dot(xt_ref[...], dp_ref[:, here])
        back_pack(places, here, keep_ref, send_ref, g_ref)
    return terms


def back_pack(places, cols, keep_ref, send_ref, g_ref):
    half = keep_ref.shape[0]

    def put(side, place, rr, ff):
        dst = keep_ref if side == 0 else send_ref
        row = (ff ^ places.field) * half + rr * BLOCK
        dst[rows16(place * BLOCK), cols] = g_ref[rows16(row), cols].astype(dst.dtype)

    places.each(half // BLOCK, put)


def set_terms(q_ref, terms, ks):
    tile = q_ref.shape[0] // 4
    experts = q_ref.shape[1] // 2
    lane = lax.broadcasted_iota(jnp.int32, (tile, 2 * experts), 1)
    for i in range(4):
        rows = slice(i * tile, (i + 1) * tile)
        q = q_ref[rows, :]
        for k, sums in zip(ks, terms):
            q = jnp.where((lane == k) | (lane == k + experts), sums[i], q)
        q_ref[rows, :] = q


def back_first_kernel(
    places, ks, w_ref, dm_ref, ga_ref, gs_ref, xt_ref, dp_ref, keep_ref, send_ref, q_ref, g_ref
):
    terms = back_part(places, ks, w_ref, dm_ref, ga_ref, gs_ref, xt_ref, dp_ref, keep_ref, send_ref, g_ref)
    q_ref[...] = jnp.zeros_like(q_ref)
    set_terms(q_ref, terms, ks)


def back_last_kernel(
    places,
    ks,
    w_ref,
    dm_ref,
    ga_ref,
    gs_ref,
    xt_ref,
    before_ref,
    gate_ref,
    by_row_ref,
    dp_ref,
    keep_ref,
    send_ref,
    dg_ref,
    g_ref,
    q_ref,
):
    terms = back_part(places, ks, w_ref, dm_ref, ga_ref, gs_ref, xt_ref, dp_ref, keep_ref, send_ref, g_ref)
    q_ref[...] = before_ref[...]
    set_terms(q_ref, terms, ks)
    q = q_ref[...]
    experts = q.shape[1] // 2
    lane = lax.broadcasted_iota(jnp.int32, q.shape, 1)
    total = 0.5 * jnp.sum(q, axis=1, keepdims=True)
    mine = (lane // experts).astype(f32) == by_row_ref[:, 2:3]
    dg_ref[...] = jnp.zeros_like(dg_ref)
    dg_ref[:, 0 : 2 * experts] = jnp.where(mine, q - gate_ref[...] * total, 0.0).astype(bf16)
    cols = slice(dp_ref.shape[1], dp_ref.shape[1] + LANES)
    g_ref[:, cols] = dot(xt_ref[...], dg_ref[...])
    back_pack(places, cols, keep_ref, send_ref, g_ref)


def input_kernel(at, low_ref, high_ref, dg_ref, w_ref, keep_ref, send_ref):
    part = low_ref.shape[1]
    wide = part + high_ref.shape[1]
    grad = dot_t(low_ref[...], w_ref[:, 0:part]) + dot_t(high_ref[...], w_ref[:, part:wide])
    grad = grad + dot_t(dg_ref[...], w_ref[:, wide:])
    half = grad.shape[1] // 2
    keep_ref[0] = grad[:, :half]
    send_ref[...] = grad[:, half:].astype(bf16)


def update_kernel(rates, sum_a, got_a, sum_b, got_b, side, dx_ref, held_ref, *refs):
    weights, velocities, averages = refs[0:5], refs[5:10], refs[10:15]
    grad_ref, outs, (wide_ref, sems) = refs[15], refs[16:31], refs[31:]
    micro, tile, _ = wide_ref.shape
    start = pl.multiple_of((1 - lax.axis_index("field")) * tile, tile)
    copies = []
    for m in range(micro):
        wide_ref[m] = dx_ref[m * tile : (m + 1) * tile, :].astype(f32)
        copy = pltpu.make_async_copy(wide_ref.at[m], grad_ref.at[m, pl.ds(start, tile), :], sems.at[m])
        copy.start()
        copies.append(copy)
    wide = weights[0].shape[1]
    gates = weights[1].shape[1]
    experts, rows, out_cols = weights[2].shape
    tasks = weights[3].shape[0]
    part = experts // 2

    def renew(at, place, gradient):
        velocity = momentum_mu * velocities[at][place] + gradient
        weight = weights[at][place] - rates[at] * (gradient + momentum_mu * velocity)
        outs[3 * at][place] = weight
        outs[3 * at + 1][place] = velocity
        outs[3 * at + 2][place] = average_keep * averages[at][place] + (1.0 - average_keep) * weight

    first = sum_a[0 : got_a.shape[0], :] + got_a[...].astype(f32)
    renew(0, (slice(None), slice(None)), first[:, :wide])
    renew(1, (slice(None), slice(None)), first[:, wide : wide + gates])
    count = got_b.shape[0] - 8
    second = sum_b[0:count, :] + got_b[0:count, :].astype(f32)
    for k in range(experts):
        top = (k // part) * rows
        renew(2, k, second[top : top + rows, (k % part) * out_cols : (k % part + 1) * out_cols])
    for t in range(tasks):
        renew(3, t, second[t * rows : (t + 1) * rows, part * out_cols :])
        renew(4, (slice(t, t + 1), slice(None)), side[0:1, t * LANES : (t + 1) * LANES])
    for copy in copies:
        copy.wait()


class Cube:
    def __init__(self):
        self.rows = lax.axis_size("rows")
        self.fields = lax.axis_size("field")
        bits = int(math.log2(self.rows))
        assert 1 << bits == self.rows and self.fields == 2
        outer = [("row", b) for b in range(bits - 1, 1, -1)]
        self.order = outer + [("mixed", 0), ("mixed", 1)]
        self.other_order = outer + [("mixed", 1), ("mixed", 0)]
        self.core = ("row", 0)

    def pairs(self, step):
        kind, which = step
        pairs = []
        for r in range(self.rows):
            for f in range(self.fields):
                if kind == "row":
                    to = (r ^ (1 << which), f)
                else:
                    to = (r ^ 2, f) if (r & 1) == which else (r, f ^ 1)
                pairs.append((r * self.fields + f, to[0] * self.fields + to[1]))
        return pairs

    def swap(self, values, step):
        return lax.ppermute(values, both, self.pairs(step))

    def place(self, order, rr, ff, r, f):
        dr, df, core = rr ^ r, ff ^ f, r & 1
        out = jnp.zeros_like(dr + df)
        for s, (kind, which) in enumerate(order):
            if kind == "row":
                bit = (dr >> which) & 1
            else:
                bit = jnp.where(core == which, (dr >> 1) & 1, df)
            out = out + (bit << s)
        return out


def gather_two(cube, block_a, make_b, x):
    got_a = cube.swap(block_a, cube.order[0])
    block_a = jnp.concatenate([block_a, got_a], axis=0)
    block_b = make_b(block_a)
    for at in range(1, len(cube.order)):
        got_a = cube.swap(block_a, cube.order[at])
        got_b = cube.swap(block_b, cube.order[at - 1])
        if at + 1 == len(cube.order):
            got_a = after(got_a, x)
        block_a = jnp.concatenate([block_a, after(got_a, got_b)], axis=0)
        block_b = jnp.concatenate([block_b, after(got_b, block_a)], axis=0)
    oth_a = cube.swap(block_a, cube.core)
    return block_a, oth_a, block_b, cube.swap(block_b, cube.order[-1])


def after(values, *earlier):
    return lax.optimization_barrier((values,) + earlier)[0]


def fold(total, got):
    rows = got.shape[0]
    total = total[:rows] + got.astype(f32)
    half = rows // 2
    return total, total[half:].astype(bf16)


def split_two(values):
    high = lax.reduce_precision(values, 8, 7)
    low = lax.reduce_precision(values - high, 8, 7)
    return jnp.concatenate([high, low], axis=0).astype(bf16)


def join_two(rows):
    rows = rows.astype(f32)
    half = rows.shape[0] // 2
    return rows[:half] + rows[half:]


def beside(part, side):
    mine = split_two(side)
    return jnp.concatenate([part, mine], axis=0), join_two(mine)


def fold_beside(total, side, got):
    rows = got.shape[0] - 8
    total, part = fold(total, got[:rows])
    message, side = beside(part, side + join_two(got[rows:]))
    return total, message, side


def shape(dims, dtype):
    return jax.ShapeDtypeStruct(dims, dtype)


def params(limit):
    return pltpu.CompilerParams(vmem_limit_bytes=limit << 20)


vmem = pl.BlockSpec()


def cost(flops):
    return pl.CostEstimate(flops=flops, bytes_accessed=8 << 20, transcendentals=0)


def on_device(
    inputs,
    valid_mask,
    labels,
    domains,
    expert_in,
    gate_in,
    expert_out,
    tower_in,
    tower_out,
    velocity_expert_in,
    velocity_gate_in,
    velocity_expert_out,
    velocity_tower_in,
    velocity_tower_out,
    average_expert_in,
    average_gate_in,
    average_expert_out,
    average_tower_in,
    average_tower_out,
):
    cube = Cube()
    micro, rows_dev, width = inputs.shape
    fields = cube.fields
    tile = rows_dev // fields
    rows_own = micro * tile
    experts, second_rows, out_cols = expert_out.shape
    tasks, tower_cols = tower_out.shape
    wide = expert_in.shape[1]
    hidden = wide // experts
    first_rows = expert_in.shape[0]
    part = experts // 2
    total_rows = micro * rows_dev * cube.rows
    r, f = lax.axis_index("rows"), lax.axis_index("field")

    def own_half(values, which):
        return lax.dynamic_slice_in_dim(values, which * tile, tile, 1)

    block_a = pl.pallas_call(
        pack_a_kernel,
        out_shape=shape((first_rows, wide + LANES), bf16),
        compiler_params=params(4),
        name="pack_a",
    )(expert_in, gate_in)

    def make_b(earlier):
        return pl.pallas_call(
            pack_b_kernel,
            out_shape=shape((2 * second_rows, part * out_cols + 2 * LANES), bf16),
            compiler_params=params(4),
            name="pack_b",
        )(expert_out, tower_in, after(valid_mask, earlier))

    x_send = own_half(after(inputs, block_a), 1 - f).reshape(rows_own, width)
    x_got = lax.ppermute(x_send, "field", [(0, 1), (1, 0)])

    pairs = width // BLOCK
    fit = first_rows == BLOCK
    places = Places(fit, cube.order)
    sent = bf16 if fit else f32

    a_cols, b_cols = wide + LANES, part * out_cols + LANES
    heads = tasks * tower_cols

    x, x_t, flags, by_row = pl.pallas_call(
        rows_kernel,
        out_shape=[
            shape((rows_own, 2 * width), bf16),
            shape((2 * width, rows_own), bf16),
            shape((8, rows_own), f32),
            shape((rows_own, 8), f32),
        ],
        compiler_params=params(8),
        cost_estimate=cost(1 << 20),
        name="rows",
    )(inputs, x_got, valid_mask, labels, domains)

    own_a, oth_a, own_b, got_b = gather_two(cube, block_a, make_b, x)
    if not fit:
        rows_a = first_sorted(cube, cube.order, r, f, width, first_rows)
        own_a, oth_a = jnp.split(jnp.take(jnp.concatenate([own_a, oth_a]), rows_a, axis=0), 2)
    ga, gs, gate, first_w = pl.pallas_call(
        functools.partial(first_kernel, places),
        out_shape=[
            shape((rows_own, wide), bf16),
            shape((rows_own, wide), bf16),
            shape((rows_own, tasks * experts), f32),
            shape((2 * width, a_cols), bf16),
        ],
        compiler_params=params(12),
        cost_estimate=cost(4 * rows_own * 2 * width * a_cols),
        name="first",
    )(own_a, oth_a, x, x_t, flags)

    own_b = jnp.concatenate([own_b, after(got_b, gate)], axis=0)
    oth_b = cube.swap(own_b, cube.core)
    if not fit:
        rows_b = second_sorted(cube, cube.order, r, f, width, second_rows)
        own_b, oth_b = jnp.split(jnp.take(jnp.concatenate([own_b, oth_b]), rows_b, axis=0), 2)
    second_w, dmixed, side, keep_b, send_b = pl.pallas_call(
        functools.partial(second_kernel, places),
        out_shape=[
            shape((wide, out_cols), bf16),
            shape((rows_own, out_cols), bf16),
            shape((8, b_cols), f32),
            shape((width, b_cols), f32),
            shape((width, b_cols), sent),
        ],
        scratch_shapes=[
            pltpu.VMEM((out_cols, heads), bf16),
            pltpu.VMEM((rows_own, out_cols), bf16),
            pltpu.VMEM((experts, hidden, out_cols), f32),
            pltpu.VMEM((out_cols, heads), f32),
        ],
        compiler_params=params(20),
        name="second",
    )(own_b, oth_b, ga, flags, by_row, tower_out)
    if not fit:
        keep_b, send_b = unsorted(keep_b, send_b, rows_b)
    message, side = beside(send_b, side[:4])
    steps = [cube.core] + cube.order[::-1]
    got_b = cube.swap(message, steps[0])

    cut = 7
    low_cols, high_cols = cut * hidden, (experts - cut) * hidden + LANES
    dpre_low, keep_low, send_low, terms = pl.pallas_call(
        functools.partial(back_first_kernel, places, range(cut)),
        out_shape=[
            shape((rows_own, low_cols), bf16),
            shape((width, low_cols), f32),
            shape((width, low_cols), sent),
            shape((rows_own, tasks * experts), f32),
        ],
        scratch_shapes=[pltpu.VMEM((2 * width, low_cols), f32)],
        compiler_params=params(16),
        name="back_first",
    )(after(second_w, message), dmixed, ga, gs, x_t)
    if not fit:
        keep_low, send_low = unsorted(keep_low, send_low, rows_a)
    got_low = cube.swap(send_low, steps[0])
    sum_b, message, side = fold_beside(keep_b, side, after(got_b, send_low))
    got_b = cube.swap(message, steps[1])
    dpre_high, keep_high, send_high, dgate = pl.pallas_call(
        functools.partial(back_last_kernel, places, range(cut, experts)),
        out_shape=[
            shape((rows_own, high_cols - LANES), bf16),
            shape((width, high_cols), f32),
            shape((width, high_cols), sent),
            shape((rows_own, LANES), bf16),
        ],
        scratch_shapes=[
            pltpu.VMEM((2 * width, high_cols), f32),
            pltpu.VMEM((rows_own, tasks * experts), f32),
        ],
        compiler_params=params(16),
        name="back_last",
    )(second_w, dmixed, ga, gs, x_t, after(terms, message), gate, by_row)
    if not fit:
        keep_high, send_high = unsorted(keep_high, send_high, rows_a)
    got_high = cube.swap(send_high, steps[0])
    keep_a = jnp.concatenate([keep_low, keep_high], axis=1)
    got_a = jnp.concatenate([after(got_low, send_high), got_high], axis=1)
    sum_a, next_a = fold(keep_a, got_a)
    grad_keep, grad_send = pl.pallas_call(
        input_kernel,
        grid_spec=pltpu.PrefetchScalarGridSpec(
            num_scalar_prefetch=1,
            grid=(micro,),
            in_specs=[
                pl.BlockSpec((tile, low_cols), lambda i, at: (i, 0)),
            pl.BlockSpec((tile, high_cols - LANES), lambda i, at: (i, 0)),
                pl.BlockSpec((tile, LANES), lambda i, at: (i, 0)),
                pl.BlockSpec((2 * width, a_cols), lambda i, at: (0, 0)),
            ],
            out_specs=[
                pl.BlockSpec((1, tile, width), lambda i, at: (i, at[0], 0)),
                pl.BlockSpec((tile, width), lambda i, at: (i, 0)),
            ],
        ),
        out_shape=[
            shape((micro, rows_dev, width), f32),
            shape((rows_own, width), bf16),
        ],
        compiler_params=params(12),
        cost_estimate=cost(4 * rows_own * 2 * width * a_cols),
        name="input",
    )(f.astype(jnp.int32).reshape(1), dpre_low, dpre_high, after(dgate, next_a), first_w)
    for at in range(1, len(steps)):
        got_a = cube.swap(next_a, steps[at])
        if at + 1 < len(steps):
            sum_b, message, side = fold_beside(sum_b, side, after(got_b, next_a))
            got_b = cube.swap(message, steps[at + 1])
            sum_a, next_a = fold(sum_a, after(got_a, got_b, grad_send))
        if at == 1:
            grad_got = lax.ppermute(after(grad_send, next_a), "field", [(0, 1), (1, 0)])
    side = side + join_two(got_b[got_b.shape[0] - 8 :])
    weights = (expert_in, gate_in, expert_out, tower_in, tower_out)
    velocities = (
        velocity_expert_in,
        velocity_gate_in,
        velocity_expert_out,
        velocity_tower_in,
        velocity_tower_out,
    )
    averages = (
        average_expert_in,
        average_gate_in,
        average_expert_out,
        average_tower_in,
        average_tower_out,
    )
    rates = [base * math.sqrt(total_rows) for base in rate_bases]
    hbm = pl.BlockSpec(memory_space=pl.ANY)
    input_grad, *updated = pl.pallas_call(
        functools.partial(update_kernel, rates),
        in_specs=[vmem] * 6 + [hbm] + [vmem] * 15,
        out_specs=[hbm] + [vmem] * 15,
        out_shape=[shape((micro, rows_dev, width), f32)]
        + [shape(w.shape, f32) for w in weights for _ in range(3)],
        scratch_shapes=[pltpu.VMEM((micro, tile, width), f32), pltpu.SemaphoreType.DMA((micro,))],
        input_output_aliases={6: 0},
        compiler_params=params(8),
        cost_estimate=cost(1 << 20),
        name="update",
    )(sum_a, got_a, sum_b, got_b, side, grad_got, grad_keep, *weights, *velocities, *averages)
    return (side[0, heads], input_grad, *updated)


def owner_rows(cube, order, r, f, rr, ff, inner, size):
    held = cube.rows * cube.fields // 2
    same = (rr & 1) == (r & 1)
    here = cube.place(order, rr, ff, r, f)
    there = cube.place(order, rr, ff, r ^ 1, f)
    return (jnp.where(same, here, held + there) * size + inner).reshape(-1)


def block_grid(width):
    side = np.arange(2)[:, None, None, None]
    j = np.arange(width // (2 * BLOCK))[None, :, None, None]
    ff = np.arange(2)[None, None, :, None]
    inner = np.arange(BLOCK)[None, None, None, :]
    ahead = (2 * j + side) * BLOCK + 0 * ff + 0 * inner
    full = np.zeros(ahead.shape, np.int32)
    return ahead.astype(np.int32), full + ff.astype(np.int32), full + inner.astype(np.int32)


def first_sorted(cube, order, r, f, width, size):
    ahead, ff, inner = block_grid(width)
    at = ahead + inner
    return owner_rows(
        cube, order, r, f, jnp.asarray(at // size), jnp.asarray(ff), jnp.asarray(at % size), size
    )


def second_sorted(cube, order, r, f, width, size):
    ahead, ff, inner = block_grid(width)
    at = ahead + ff * 8 + inner % 8
    owner = at // size
    held = at % size + size * (inner // 8)
    return owner_rows(
        cube, order, r, f, jnp.asarray(owner // 2), jnp.asarray(owner % 2), jnp.asarray(held), 2 * size
    )


def unsorted(keep, send, rows):
    every = jnp.concatenate([keep, send])
    back = jnp.zeros_like(rows).at[rows].set(jnp.arange(rows.shape[0], dtype=rows.dtype))
    keep, send = jnp.split(jnp.take(every, back, axis=0), 2)
    return keep, send.astype(bf16)


def solution(mesh):
    first = P(("field", "rows"), None)
    second = P(None, ("rows", "field"), None)
    by_row = P(None, "rows")
    inputs = P(None, "rows", "field")
    weights = (first, first, second, second, P())
    return jax.shard_map(
        on_device,
        mesh=mesh,
        in_specs=(inputs, by_row, by_row, by_row) + weights * 3,
        out_specs=(P(), inputs) + tuple(spec for spec in weights for _ in range(3)),
        check_vma=False,
    )
```

time: 102 us -> 93.3 us (0.915)
  starting transfers between devices: 22.5 us -> 32.3 us
  Pallas kernels: 27.1 us -> 21.4 us
  waiting for transfers between devices: 38.3 us -> 33.2 us
  local copies, waits for them, and re-layouts: 7.32 us -> 3.65 us
  other arithmetic: 3.29 us -> 1.1 us
  between operations: 2.7 us -> 1.45 us
    ppermute x20 -> x21, starting transfers between devices: 20 us -> 30.3 us  [swap(): return lax.ppermute(values, both, self.pairs(step))]
    pallas_call x7, Pallas kernels: 22.7 us -> 17.4 us  [the longest x1 5.24 us: on_device(): pl.pallas_call(functools.partial(first_kernel, places), out_shape=[shape(...]
    ppermute x20 -> x21, waiting for transfers between devices: 37 us -> 33.2 us  [swap(): return lax.ppermute(values, both, self.pairs(step))]
    unnamed x53 -> x50, local copies, waits for them, and re-layouts: 5.21 us -> 1.79 us
    convert_element_type x3 -> x0, other arithmetic: 1.42 us -> none  [the longest x1 1.33 us: on_device(): own_valid.astype(f32)]
    ppermute x1, waiting for transfers between devices: 1.26 us -> 0.01 us  [on_device(): grad_got = lax.ppermute(after(grad_send, next_a), 'field', [(0, 1), (1, 0)])]
  transfers between devices with their start and end apart: 22 -> 23, of which waited for: 15 -> 14; matrix products, arithmetic and copies ran while one was open for 7% -> 3% of each run, Pallas kernels for 16% -> 17%
where the time goes in v4:
time: 93.3 us; the launch traced here: 93.1 us
  waiting for transfers between devices  33.2 us (36%)
  starting transfers between devices  32.3 us (35%)
  Pallas kernels  21.4 us (23%)
  local copies, waits for them, and re-layouts  3.65 us (4%)
  between operations  1.45 us (2%)
  other arithmetic  1.1 us (1%)
    ppermute x21, waiting for transfers between devices, swap(): return lax.ppermute(values, both, self.pairs(step))  33.2 us
    ppermute x21, starting transfers between devices, swap(): return lax.ppermute(values, both, self.pairs(step))  30.3 us
    pallas_call x1, Pallas kernels, on_device(): pl.pallas_call(functools.partial(first_kernel, places), out_shape=[shape(...  5.24 us
    pallas_call x1, Pallas kernels, on_device(): pl.pallas_call(functools.partial(second_kernel, places), out_shape=[shape...  4.09 us
    pallas_call x1, Pallas kernels, on_device(): pl.pallas_call(functools.partial(back_first_kernel, places, range(cut)),...  4.07 us
    pallas_call x1, Pallas kernels, on_device(): pl.pallas_call(input_kernel, grid_spec=pltpu.PrefetchScalarGridSpec(num_s...  3.96 us
    pallas_call x1, Pallas kernels, on_device(): pl.pallas_call(functools.partial(update_kernel, rates), in_specs=[vmem] *...  1.9 us
  transfers between devices with their start and end apart: 23, of which 14 were waited for; matrix products, arithmetic and copies ran while one was open for 3% of the time, Pallas kernels for 17%

profile of v4, /device:TPU:0, one launch (start us, length us, event | category | flops | bytes accessed | tf_op | source)
XLA Modules:
  0.0 93.1 jit_solution(2521281883361414492)
XLA Ops:
  0.7 0.9 copy-done.1
  1.6 0.7 copy-done.8
  2.3 4.1 %collective-permute-start = (bf16[16,2176]{1,0:T(8,128)(2,1)S(1)}, bf16[16,2176]{1,0:T(8,128)(2,1)S(1)}, u32[]{:S(2)}, u32[]{:S(2)}) collective-permute-start(bf16[16,2176]{1,0:T(8,128)(2,1)S(1)} %pack_a.1), channel_id=1, source_target_pairs={{0,16},{1,17},{2,18},{3,19},{4,20},{5,21},{6,22},{7,23},{8,24},{9,... | collective-permute-start | bytes 208904 | tf_op jit(solution)/shard_map/ppermute | solution.py:418
  6.4 1.1 %constant_dynamic-slice_fusion = bf16[4,256,256]{2,1,0:T(8,128)(2,1)S(1)} fusion(bf16[4,512,256]{2,1,0:T(8,128)(2,1)} %in_ref.1, s32[]{:T(128)S(6)} %select_n.3), kind=kLoop, calls=%fused_computation.82 | loop fusion | bytes 1048580 | tf_op jit(solution)/shard_map/dynamic_slice | solution.py:533
  7.5 1.6 %collective-permute-start.7 = (bf16[1024,256]{1,0:T(8,128)(2,1)S(1)}, bf16[1024,256]{1,0:T(8,128)(2,1)S(1)}, u32[]{:S(2)}, u32[]{:S(2)}) collective-permute-start(bf16[1024,256]{1,0:T(8,128)(2,1)S(1)} %bitcast.3), channel_id=1, source_target_pairs={{0,1},{1,0},{2,3},{3,2},{4,5},{5,4},{6,7},{7,6},{8,9},{9,8},{10,11... | collective-permute-start | bytes 1572872 | tf_op jit(solution)/shard_map/ppermute | solution.py:551
  9.1 1.1 %collective-permute-done = bf16[16,2176]{1,0:T(8,128)(2,1)S(1)} collective-permute-done((bf16[16,2176]{1,0:T(8,128)(2,1)S(1)}, bf16[16,2176]{1,0:T(8,128)(2,1)S(1)}, u32[]{:S(2)}, u32[]{:S(2)}) %collective-permute-start) | collective-permute-done | bytes 69664 | tf_op jit(solution)/shard_map/ppermute | solution.py:418
  10.2 0.7 collective-permute-start.2
  10.9 0.1 pack_b.1
  11.0 3.4 %collective-permute-start.1 = (bf16[16,1280]{1,0:T(8,128)(2,1)S(1)}, bf16[16,1280]{1,0:T(8,128)(2,1)S(1)}, u32[]{:S(2)}, u32[]{:S(2)}) collective-permute-start(bf16[16,1280]{1,0:T(8,128)(2,1)S(1)} %pack_b.1), channel_id=1, source_target_pairs={{0,16},{1,17},{2,18},{3,19},{4,20},{5,21},{6,22},{7,23},{8,24},{9,... | collective-permute-start | bytes 122888 | tf_op jit(solution)/shard_map/ppermute | solution.py:418
  14.4 2.1 %collective-permute-done.1 = bf16[16,1280]{1,0:T(8,128)(2,1)S(1)} collective-permute-done((bf16[16,1280]{1,0:T(8,128)(2,1)S(1)}, bf16[16,1280]{1,0:T(8,128)(2,1)S(1)}, u32[]{:S(2)}, u32[]{:S(2)}) %collective-permute-start.1) | collective-permute-done | bytes 40992 | tf_op jit(solution)/shard_map/ppermute | solution.py:418
  16.6 1.6 %collective-permute-start.4 = (bf16[64,2176]{1,0:T(8,128)(2,1)S(1)}, bf16[64,2176]{1,0:T(8,128)(2,1)S(1)}, u32[]{:S(2)}, u32[]{:S(2)}) collective-permute-start(bf16[64,2176]{1,0:T(8,128)(2,1)S(1)} %pad_maximum_fusion.4), channel_id=1, source_target_pairs={{0,4},{1,5},{2,3},{3,2},{4,0},{5,1},{6,7},{7,6},{8,12},{9,13},{10,... | collective-permute-start | bytes 835592 | tf_op jit(solution)/shard_map/ppermute | solution.py:418
  18.2 2.2 %collective-permute-start.3 = (bf16[32,1280]{1,0:T(8,128)(2,1)S(1)}, bf16[32,1280]{1,0:T(8,128)(2,1)S(1)}, u32[]{:S(2)}, u32[]{:S(2)}) collective-permute-start(bf16[32,1280]{1,0:T(8,128)(2,1)S(1)} %pad_maximum_fusion.9), channel_id=1, source_target_pairs={{0,8},{1,9},{2,10},{3,11},{4,12},{5,13},{6,14},{7,15},{8,0},{9,1},... | collective-permute-start | bytes 245768 | tf_op jit(solution)/shard_map/ppermute | solution.py:418
  20.4 2.4 %collective-permute-done.3 = bf16[32,1280]{1,0:T(8,128)(2,1)S(1)} collective-permute-done((bf16[32,1280]{1,0:T(8,128)(2,1)S(1)}, bf16[32,1280]{1,0:T(8,128)(2,1)S(1)}, u32[]{:S(2)}, u32[]{:S(2)}) %collective-permute-start.3) | collective-permute-done | bytes 81952 | tf_op jit(solution)/shard_map/ppermute | solution.py:418
  22.8 0.4 collective-permute-done.4
  23.2 1.6 %collective-permute-start.6 = (bf16[128,2176]{1,0:T(8,128)(2,1)S(1)}, bf16[128,2176]{1,0:T(8,128)(2,1)S(1)}, u32[]{:S(2)}, u32[]{:S(2)}) collective-permute-start(bf16[128,2176]{1,0:T(8,128)(2,1)S(1)} %pad_maximum_fusion.1), channel_id=1, source_target_pairs={{0,1},{1,0},{2,6},{3,7},{4,5},{5,4},{6,2},{7,3},{8,9},{9,8},{10,14... | collective-permute-start | bytes 1671176 | tf_op jit(solution)/shard_map/ppermute | solution.py:418
  24.8 1.6 %collective-permute-start.5 = (bf16[64,1280]{1,0:T(8,128)(2,1)S(1)}, bf16[64,1280]{1,0:T(8,128)(2,1)S(1)}, u32[]{:S(2)}, u32[]{:S(2)}) collective-permute-start(bf16[64,1280]{1,0:T(8,128)(2,1)S(1)} %pad_maximum_fusion.6), channel_id=1, source_target_pairs={{0,4},{1,5},{2,3},{3,2},{4,0},{5,1},{6,7},{7,6},{8,12},{9,13},{10,... | collective-permute-start | bytes 491528 | tf_op jit(solution)/shard_map/ppermute | solution.py:418
  26.5 0.6 rows.1
  27.0 7.6 %collective-permute-done.6 = bf16[128,2176]{1,0:T(8,128)(2,1)S(1)} collective-permute-done((bf16[128,2176]{1,0:T(8,128)(2,1)S(1)}, bf16[128,2176]{1,0:T(8,128)(2,1)S(1)}, u32[]{:S(2)}, u32[]{:S(2)}) %collective-permute-start.6) | collective-permute-done | bytes 557088 | tf_op jit(solution)/shard_map/ppermute | solution.py:418
  34.8 1.6 %collective-permute-start.8 = (bf16[128,1280]{1,0:T(8,128)(2,1)S(1)}, bf16[128,1280]{1,0:T(8,128)(2,1)S(1)}, u32[]{:S(2)}, u32[]{:S(2)}) collective-permute-start(bf16[128,1280]{1,0:T(8,128)(2,1)S(1)} %pad_maximum_fusion.2), channel_id=1, source_target_pairs={{0,1},{1,0},{2,6},{3,7},{4,5},{5,4},{6,2},{7,3},{8,9},{9,8},{10,14... | collective-permute-start | bytes 983048 | tf_op jit(solution)/shard_map/ppermute | solution.py:418
  36.4 1.1 %collective-permute-done.9.oth_ref = bf16[256,2176]{1,0:T(8,128)(2,1)S(1)} collective-permute-done((bf16[256,2176]{1,0:T(8,128)(2,1)S(1)}, bf16[256,2176]{1,0:T(8,128)(2,1)S(1)}, u32[]{:S(2)}, u32[]{:S(2)}) %collective-permute-start.9) | collective-permute-done | bytes 1114144 | tf_op jit(solution)/shard_map/ppermute | solution.py:418
  37.5 5.2 %first.1 = (bf16[1024,2048]{1,0:T(8,128)(2,1)S(1)}, bf16[1024,2048]{1,0:T(8,128)(2,1)S(1)}, f32[1024,16]{1,0:T(8,128)S(1)}, bf16[512,2176]{1,0:T(8,128)(2,1)S(1)}) custom-call(bf16[256,2176]{1,0:T(8,128)(2,1)S(1)} %constant_dynamic-update-slice_fusion.own_ref, bf16[256,2176]{1,0:T(8,128)(2,1)S(1)} %collective-permute-done.9.oth_ref, ...), custom_call_target="tpu_custom_call" | custom-call | flops 4563402752 | bytes 8388608 | tf_op jit(solution)/shard_map/first/pallas_call | solution.py:578
  42.8 0.2 collective-permute-start.10
  43.0 2.0 %collective-permute-done.10.oth_ref = bf16[256,1280]{1,0:T(8,128)(2,1)S(1)} collective-permute-done((bf16[256,1280]{1,0:T(8,128)(2,1)S(1)}, bf16[256,1280]{1,0:T(8,128)(2,1)S(1)}, u32[]{:S(2)}, u32[]{:S(2)}) %collective-permute-start.10) | collective-permute-done | bytes 655392 | tf_op jit(solution)/shard_map/ppermute | solution.py:418
  44.9 4.1 %second.1 = (bf16[2048,256]{1,0:T(8,128)(2,1)S(1)}, bf16[1024,256]{1,0:T(8,128)(2,1)S(1)}, f32[8,1152]{1,0:T(8,128)S(1)}, f32[256,1152]{1,0:T(8,128)S(1)}, bf16[256,1152]{1,0:T(8,128)(2,1)S(1)}) custom-call(bf16[256,1280]{1,0:T(8,128)(2,1)S(1)} %constant_dynamic-update-slice_fusion.5.own_ref, bf16[256,1280]{1,0:T(8,128)(2,1)S(1)} %collective-permute-done.10.oth_ref, ...), custom_call_target="tpu_custom_call" | custom-call | tf_op jit(solution)/shard_map/second/pallas_call | solution.py:596
  49.1 0.2 collective-permute-start.11
  49.3 4.1 %back_first.1 = (bf16[1024,1792]{1,0:T(8,128)(2,1)S(1)}, f32[256,1792]{1,0:T(8,128)S(1)}, bf16[256,1792]{1,0:T(8,128)(2,1)S(1)}, f32[1024,16]{1,0:T(8,128)S(1)}) custom-call(bf16[2048,256]{1,0:T(8,128)(2,1)S(1)} %get-tuple-element.97.w_ref, bf16[1024,256]{1,0:T(8,128)(2,1)S(1)} %get-tuple-element.98.dm_ref, bf16[1024,2048]{1,0:T(8,128)(2,1)S(1)} %get-tuple-element.92.ga_ref, ...), custom_call_target="tpu_custom_call" | custom-call | tf_op jit(solution)/shard_map/back_first/pallas_call | solution.py:622
  53.4 0.4 collective-permute-start.13
  54.1 1.6 %collective-permute-start.12 = (bf16[136,1152]{1,0:T(8,128)(2,1)S(1)}, bf16[136,1152]{1,0:T(8,128)(2,1)S(1)}, u32[]{:S(2)}, u32[]{:S(2)}) collective-permute-start(bf16[136,1152]{1,0:T(8,128)(2,1)S(1)} %pad_maximum_fusion.3), channel_id=1, source_target_pairs={{0,1},{1,0},{2,6},{3,7},{4,5},{5,4},{6,2},{7,3},{8,9},{9,8},{10,14... | collective-permute-start | bytes 940040 | tf_op jit(solution)/shard_map/ppermute | solution.py:418
  55.7 1.4 %back_last.1 = (bf16[1024,256]{1,0:T(8,128)(2,1)S(1)}, f32[256,384]{1,0:T(8,128)S(1)}, bf16[256,384]{1,0:T(8,128)(2,1)S(1)}, bf16[1024,128]{1,0:T(8,128)(2,1)S(1)}) custom-call(bf16[2048,256]{1,0:T(8,128)(2,1)S(1)} %get-tuple-element.97.w_ref, bf16[1024,256]{1,0:T(8,128)(2,1)S(1)} %get-tuple-element.98.dm_ref, ...), custom_call_target="tpu_custom_call" | custom-call | tf_op jit(solution)/shard_map/back_last/pallas_call | solution.py:639
  57.2 1.4 %collective-permute-done.14 = bf16[256,384]{1,0:T(8,128)(2,1)S(1)} collective-permute-done((bf16[256,384]{1,0:T(8,128)(2,1)S(1)}, bf16[256,384]{1,0:T(8,128)(2,1)S(1)}, u32[]{:S(2)}, u32[]{:S(2)}) %collective-permute-start.14) | collective-permute-done | bytes 196640 | tf_op jit(solution)/shard_map/ppermute | solution.py:418
  58.6 0.2 maximum_add_fusion
  58.9 0.9 %collective-permute-start.16 = (bf16[128,2176]{1,0:T(8,128)(2,1)S(1)}, bf16[128,2176]{1,0:T(8,128)(2,1)S(1)}, u32[]{:S(2)}, u32[]{:S(2)}) collective-permute-start(bf16[128,2176]{1,0:T(8,128)(2,1)S(1)} %slice.289), channel_id=1, source_target_pairs={{0,1},{1,0},{2,6},{3,7},{4,5},{5,4},{6,2},{7,3},{8,9},{9,8},{10,14... | collective-permute-start | bytes 1671176 | tf_op jit(solution)/shard_map/ppermute | solution.py:418
  59.8 4.0 %input.1 = (f32[4,512,256]{2,1,0:T(8,128)}, bf16[1024,256]{1,0:T(8,128)(2,1)S(1)}) custom-call(s32[1]{0:T(128)} %bitcast.1.at, bf16[1024,1792]{1,0:T(8,128)(2,1)S(1)} %get-tuple-element.110.low_ref, bf16[1024,256]{1,0:T(8,128)(2,1)S(1)} %get-tuple-element.111.high_ref, bf16[1024,128]{1,0:T(8,128)(2,1)S(1)} %get-tuple-element.113.dg_ref, ...), custom_call_target="tpu_custom_call" | custom-call | flops 4563402752 | bytes 8388608 | tf_op jit(solution)/shard_map/input/pallas_call | solution.py:660
  64.0 1.1 %collective-permute-start.15 = (bf16[72,1152]{1,0:T(8,128)(2,1)S(1)}, bf16[72,1152]{1,0:T(8,128)(2,1)S(1)}, u32[]{:S(2)}, u32[]{:S(2)}) collective-permute-start(bf16[72,1152]{1,0:T(8,128)(2,1)S(1)} %pad_maximum_fusion.5), channel_id=1, source_target_pairs={{0,4},{1,5},{2,3},{3,2},{4,0},{5,1},{6,7},{7,6},{8,12},{9,13},{10,... | collective-permute-start | bytes 497672 | tf_op jit(solution)/shard_map/ppermute | solution.py:418
  65.1 4.4 %collective-permute-done.15 = bf16[72,1152]{1,0:T(8,128)(2,1)S(1)} collective-permute-done((bf16[72,1152]{1,0:T(8,128)(2,1)S(1)}, bf16[72,1152]{1,0:T(8,128)(2,1)S(1)}, u32[]{:S(2)}, u32[]{:S(2)}) %collective-permute-start.15) | collective-permute-done | bytes 165920 | tf_op jit(solution)/shard_map/ppermute | solution.py:418
  69.4 0.5 collective-permute-done.16
  70.1 1.8 %collective-permute-start.18 = (bf16[64,2176]{1,0:T(8,128)(2,1)S(1)}, bf16[64,2176]{1,0:T(8,128)(2,1)S(1)}, u32[]{:S(2)}, u32[]{:S(2)}) collective-permute-start(bf16[64,2176]{1,0:T(8,128)(2,1)S(1)} %slice.291), channel_id=1, source_target_pairs={{0,4},{1,5},{2,3},{3,2},{4,0},{5,1},{6,7},{7,6},{8,12},{9,13},{10,... | collective-permute-start | bytes 835592 | tf_op jit(solution)/shard_map/ppermute | solution.py:418
  72.0 1.7 %collective-permute-start.17 = (bf16[40,1152]{1,0:T(8,128)(2,1)S(1)}, bf16[40,1152]{1,0:T(8,128)(2,1)S(1)}, u32[]{:S(2)}, u32[]{:S(2)}) collective-permute-start(bf16[40,1152]{1,0:T(8,128)(2,1)S(1)} %pad_maximum_fusion.8), channel_id=1, source_target_pairs={{0,8},{1,9},{2,10},{3,11},{4,12},{5,13},{6,14},{7,15},{8,0},{9,1},... | collective-permute-start | bytes 276488 | tf_op jit(solution)/shard_map/ppermute | solution.py:418
  73.7 0.5 collective-permute-start.22
  74.2 2.4 %collective-permute-done.17 = bf16[40,1152]{1,0:T(8,128)(2,1)S(1)} collective-permute-done((bf16[40,1152]{1,0:T(8,128)(2,1)S(1)}, bf16[40,1152]{1,0:T(8,128)(2,1)S(1)}, u32[]{:S(2)}, u32[]{:S(2)}) %collective-permute-start.17) | collective-permute-done | bytes 92192 | tf_op jit(solution)/shard_map/ppermute | solution.py:418
  76.6 0.1 collective-permute-done.18
  77.0 2.5 %collective-permute-start.20 = (bf16[32,2176]{1,0:T(8,128)(2,1)S(1)}, bf16[32,2176]{1,0:T(8,128)(2,1)S(1)}, u32[]{:S(2)}, u32[]{:S(2)}) collective-permute-start(bf16[32,2176]{1,0:T(8,128)(2,1)S(1)} %slice.293), channel_id=1, source_target_pairs={{0,8},{1,9},{2,10},{3,11},{4,12},{5,13},{6,14},{7,15},{8,0},{9,1},... | collective-permute-start | bytes 417800 | tf_op jit(solution)/shard_map/ppermute | solution.py:418
  79.6 1.0 %collective-permute-start.19 = (bf16[24,1152]{1,0:T(8,128)(2,1)S(1)}, bf16[24,1152]{1,0:T(8,128)(2,1)S(1)}, u32[]{:S(2)}, u32[]{:S(2)}) collective-permute-start(bf16[24,1152]{1,0:T(8,128)(2,1)S(1)} %pad_maximum_fusion.10), channel_id=1, source_target_pairs={{0,16},{1,17},{2,18},{3,19},{4,20},{5,21},{6,22},{7,23},{8,24},{9,... | collective-permute-start | bytes 165896 | tf_op jit(solution)/shard_map/ppermute | solution.py:418
  80.6 4.5 %collective-permute-done.19.got_b = bf16[24,1152]{1,0:T(8,128)(2,1)S(1)} collective-permute-done((bf16[24,1152]{1,0:T(8,128)(2,1)S(1)}, bf16[24,1152]{1,0:T(8,128)(2,1)S(1)}, u32[]{:S(2)}, u32[]{:S(2)}) %collective-permute-start.19) | collective-permute-done | bytes 55328 | tf_op jit(solution)/shard_map/ppermute | solution.py:418
  85.2 1.9 %collective-permute-start.21 = (bf16[16,2176]{1,0:T(8,128)(2,1)S(1)}, bf16[16,2176]{1,0:T(8,128)(2,1)S(1)}, u32[]{:S(2)}, u32[]{:S(2)}) collective-permute-start(bf16[16,2176]{1,0:T(8,128)(2,1)S(1)} %slice.295), channel_id=1, source_target_pairs={{0,16},{1,17},{2,18},{3,19},{4,20},{5,21},{6,22},{7,23},{8,24},{9,... | collective-permute-start | bytes 208904 | tf_op jit(solution)/shard_map/ppermute | solution.py:418
  87.1 0.5 slice.221
  87.6 3.2 %collective-permute-done.21.got_a = bf16[16,2176]{1,0:T(8,128)(2,1)S(1)} collective-permute-done((bf16[16,2176]{1,0:T(8,128)(2,1)S(1)}, bf16[16,2176]{1,0:T(8,128)(2,1)S(1)}, u32[]{:S(2)}, u32[]{:S(2)}) %collective-permute-start.21) | collective-permute-done | bytes 69664 | tf_op jit(solution)/shard_map/ppermute | solution.py:418
  91.0 1.9 %update.1 = (f32[4,512,256]{2,1,0:T(8,128)}, f32[16,2048]{1,0:T(8,128)}, f32[16,2048]{1,0:T(8,128)}, f32[16,2048]{1,0:T(8,128)}, f32[16,16]{1,0:T(8,128)}, /*ind...) custom-call(f32[32,2176]{1,0:T(8,128)S(1)} %slice_add_fusion.4.sum_a, ...), custom_call_target="tpu_custom_call", output_to_operand_aliasing={{0}: (6, {})} | custom-call | flops 1048576 | bytes 8388608 | tf_op jit(solution)/shard_map/update/pallas_call | solution.py:710
  (108 shorter events, 1.5 us)
Async XLA Ops:
  0.7 0.9 copy-start.1
  1.6 0.7 copy-start.8
  2.3 8.6 %copy-start.3 = (f32[8,8,256]{2,1,0:T(8,128)S(1)}, f32[8,8,256]{2,1,0:T(8,128)}, u32[]{:S(2)}) copy-start(f32[8,8,256]{2,1,0:T(8,128)} %refs_2_.1) | copy-start | bytes 196612
  2.3 8.6 %copy-start.10 = (s32[4,512]{1,0:T(4,128)S(1)}, s32[4,512]{1,0:T(4,128)}, u32[]{:S(2)}) copy-start(s32[4,512]{1,0:T(4,128)} %valid_ref.2) | copy-start | bytes 24580
  2.3 8.6 %copy-start.11 = (f32[2,8,128]{2,1,0:T(8,128)S(1)}, f32[2,8,128]{2,1,0:T(8,128)}, u32[]{:S(2)}) copy-start(f32[2,8,128]{2,1,0:T(8,128)} %refs_3_.1) | copy-start | bytes 24580
  2.3 7.9 %collective-permute-start = (bf16[16,2176]{1,0:T(8,128)(2,1)S(1)}, bf16[16,2176]{1,0:T(8,128)(2,1)S(1)}, u32[]{:S(2)}, u32[]{:S(2)}) collective-permute-start(bf16[16,2176]{1,0:T(8,128)(2,1)S(1)} %pack_a.1), channel_id=1, source_target_pairs={{0,16},{1,17},{2,18},{3,19},{4,20},{5,21},{6,22},{7,23},{8,24},{9,... | collective-permute-start | bytes 208904 | tf_op jit(solution)/shard_map/ppermute | solution.py:418
  7.5 19.0 %collective-permute-start.7 = (bf16[1024,256]{1,0:T(8,128)(2,1)S(1)}, bf16[1024,256]{1,0:T(8,128)(2,1)S(1)}, u32[]{:S(2)}, u32[]{:S(2)}) collective-permute-start(bf16[1024,256]{1,0:T(8,128)(2,1)S(1)} %bitcast.3), channel_id=1, source_target_pairs={{0,1},{1,0},{2,3},{3,2},{4,5},{5,4},{6,7},{7,6},{8,9},{9,8},{10,11... | collective-permute-start | bytes 1572872 | tf_op jit(solution)/shard_map/ppermute | solution.py:551
  10.2 6.4 %collective-permute-start.2 = (bf16[32,2176]{1,0:T(8,128)(2,1)S(1)}, bf16[32,2176]{1,0:T(8,128)(2,1)S(1)}, u32[]{:S(2)}, u32[]{:S(2)}) collective-permute-start(bf16[32,2176]{1,0:T(8,128)(2,1)S(1)} %pad_maximum_fusion.7), channel_id=1, source_target_pairs={{0,8},{1,9},{2,10},{3,11},{4,12},{5,13},{6,14},{7,15},{8,0},{9,1},... | collective-permute-start | bytes 417800 | tf_op jit(solution)/shard_map/ppermute | solution.py:418
  11.0 5.6 %collective-permute-start.1 = (bf16[16,1280]{1,0:T(8,128)(2,1)S(1)}, bf16[16,1280]{1,0:T(8,128)(2,1)S(1)}, u32[]{:S(2)}, u32[]{:S(2)}) collective-permute-start(bf16[16,1280]{1,0:T(8,128)(2,1)S(1)} %pack_b.1), channel_id=1, source_target_pairs={{0,16},{1,17},{2,18},{3,19},{4,20},{5,21},{6,22},{7,23},{8,24},{9,... | collective-permute-start | bytes 122888 | tf_op jit(solution)/shard_map/ppermute | solution.py:418
  16.6 6.6 %collective-permute-start.4 = (bf16[64,2176]{1,0:T(8,128)(2,1)S(1)}, bf16[64,2176]{1,0:T(8,128)(2,1)S(1)}, u32[]{:S(2)}, u32[]{:S(2)}) collective-permute-start(bf16[64,2176]{1,0:T(8,128)(2,1)S(1)} %pad_maximum_fusion.4), channel_id=1, source_target_pairs={{0,4},{1,5},{2,3},{3,2},{4,0},{5,1},{6,7},{7,6},{8,12},{9,13},{10,... | collective-permute-start | bytes 835592 | tf_op jit(solution)/shard_map/ppermute | solution.py:418
  18.1 8.3 %copy-start = (bf16[4,512,256]{2,1,0:T(8,128)(2,1)S(1)}, bf16[4,512,256]{2,1,0:T(8,128)(2,1)}, u32[]{:S(2)}) copy-start(bf16[4,512,256]{2,1,0:T(8,128)(2,1)} %in_ref.1) | copy-start | bytes 3145732
  18.1 8.3 %copy-start.12 = (s32[4,512]{1,0:T(4,128)S(1)}, s32[4,512]{1,0:T(4,128)}, u32[]{:S(2)}) copy-start(s32[4,512]{1,0:T(4,128)} %label_ref.1) | copy-start | bytes 24580
  18.1 8.3 %copy-start.13 = (s32[4,512]{1,0:T(4,128)S(1)}, s32[4,512]{1,0:T(4,128)}, u32[]{:S(2)}) copy-start(s32[4,512]{1,0:T(4,128)} %domain_ref.1) | copy-start | bytes 24580
  18.2 4.6 %collective-permute-start.3 = (bf16[32,1280]{1,0:T(8,128)(2,1)S(1)}, bf16[32,1280]{1,0:T(8,128)(2,1)S(1)}, u32[]{:S(2)}, u32[]{:S(2)}) collective-permute-start(bf16[32,1280]{1,0:T(8,128)(2,1)S(1)} %pad_maximum_fusion.9), channel_id=1, source_target_pairs={{0,8},{1,9},{2,10},{3,11},{4,12},{5,13},{6,14},{7,15},{8,0},{9,1},... | collective-permute-start | bytes 245768 | tf_op jit(solution)/shard_map/ppermute | solution.py:418
  23.2 11.4 %collective-permute-start.6 = (bf16[128,2176]{1,0:T(8,128)(2,1)S(1)}, bf16[128,2176]{1,0:T(8,128)(2,1)S(1)}, u32[]{:S(2)}, u32[]{:S(2)}) collective-permute-start(bf16[128,2176]{1,0:T(8,128)(2,1)S(1)} %pad_maximum_fusion.1), channel_id=1, source_target_pairs={{0,1},{1,0},{2,6},{3,7},{4,5},{5,4},{6,2},{7,3},{8,9},{9,8},{10,14... | collective-permute-start | bytes 1671176 | tf_op jit(solution)/shard_map/ppermute | solution.py:418
  24.8 9.8 %collective-permute-start.5 = (bf16[64,1280]{1,0:T(8,128)(2,1)S(1)}, bf16[64,1280]{1,0:T(8,128)(2,1)S(1)}, u32[]{:S(2)}, u32[]{:S(2)}) collective-permute-start(bf16[64,1280]{1,0:T(8,128)(2,1)S(1)} %pad_maximum_fusion.6), channel_id=1, source_target_pairs={{0,4},{1,5},{2,3},{3,2},{4,0},{5,1},{6,7},{7,6},{8,12},{9,13},{10,... | collective-permute-start | bytes 491528 | tf_op jit(solution)/shard_map/ppermute | solution.py:418
  34.6 2.8 %collective-permute-start.9 = (bf16[256,2176]{1,0:T(8,128)(2,1)S(1)}, bf16[256,2176]{1,0:T(8,128)(2,1)S(1)}, u32[]{:S(2)}, u32[]{:S(2)}) collective-permute-start(bf16[256,2176]{1,0:T(8,128)(2,1)S(1)} %constant_dynamic-update-slice_fusion.own_ref), channel_id=1, source_target_pairs={{0,2},{1,3},{2,0},{3,1},{4,6},{5,7},{6,4},{7,5},{8,10},{9,11},{10,... | collective-permute-start | bytes 3342344 | tf_op jit(solution)/shard_map/ppermute | solution.py:418
  34.8 7.9 %collective-permute-start.8 = (bf16[128,1280]{1,0:T(8,128)(2,1)S(1)}, bf16[128,1280]{1,0:T(8,128)(2,1)S(1)}, u32[]{:S(2)}, u32[]{:S(2)}) collective-permute-start(bf16[128,1280]{1,0:T(8,128)(2,1)S(1)} %pad_maximum_fusion.2), channel_id=1, source_target_pairs={{0,1},{1,0},{2,6},{3,7},{4,5},{5,4},{6,2},{7,3},{8,9},{9,8},{10,14... | collective-permute-start | bytes 983048 | tf_op jit(solution)/shard_map/ppermute | solution.py:418
  37.5 7.5 %copy-start.18 = (f32[2,128]{1,0:T(2,128)S(1)}, f32[2,128]{1,0:T(2,128)}, u32[]{:S(2)}) copy-start(f32[2,128]{1,0:T(2,128)} %refs_4_.1) | copy-start | bytes 3076
  42.8 2.2 %collective-permute-start.10 = (bf16[256,1280]{1,0:T(8,128)(2,1)S(1)}, bf16[256,1280]{1,0:T(8,128)(2,1)S(1)}, u32[]{:S(2)}, u32[]{:S(2)}) collective-permute-start(bf16[256,1280]{1,0:T(8,128)(2,1)S(1)} %constant_dynamic-update-slice_fusion.5.own_ref), channel_id=1, source_target_pairs={{0,2},{1,3},{2,0},{3,1},{4,6},{5,7},{6,4},{7,5},{8,10},{9,11},{10,... | collective-permute-start | bytes 1966088 | tf_op jit(solution)/shard_map/ppermute | solution.py:418
  49.1 4.7 %collective-permute-start.11 = (bf16[264,1152]{1,0:T(8,128)(2,1)S(1)}, bf16[264,1152]{1,0:T(8,128)(2,1)S(1)}, u32[]{:S(2)}, u32[]{:S(2)}) collective-permute-start(bf16[264,1152]{1,0:T(8,128)(2,1)S(1)} %pad_maximum_fusion), channel_id=1, source_target_pairs={{0,2},{1,3},{2,0},{3,1},{4,6},{5,7},{6,4},{7,5},{8,10},{9,11},{10,... | collective-permute-start | bytes 1824776 | tf_op jit(solution)/shard_map/ppermute | solution.py:418
  53.4 3.8 %collective-permute-start.13 = (bf16[256,1792]{1,0:T(8,128)(2,1)S(1)}, bf16[256,1792]{1,0:T(8,128)(2,1)S(1)}, u32[]{:S(2)}, u32[]{:S(2)}) collective-permute-start(bf16[256,1792]{1,0:T(8,128)(2,1)S(1)} %get-tuple-element.100), channel_id=1, source_target_pairs={{0,2},{1,3},{2,0},{3,1},{4,6},{5,7},{6,4},{7,5},{8,10},{9,11},{10,... | collective-permute-start | bytes 2752520 | tf_op jit(solution)/shard_map/ppermute | solution.py:418
  54.1 9.7 %collective-permute-start.12 = (bf16[136,1152]{1,0:T(8,128)(2,1)S(1)}, bf16[136,1152]{1,0:T(8,128)(2,1)S(1)}, u32[]{:S(2)}, u32[]{:S(2)}) collective-permute-start(bf16[136,1152]{1,0:T(8,128)(2,1)S(1)} %pad_maximum_fusion.3), channel_id=1, source_target_pairs={{0,1},{1,0},{2,6},{3,7},{4,5},{5,4},{6,2},{7,3},{8,9},{9,8},{10,14... | collective-permute-start | bytes 940040 | tf_op jit(solution)/shard_map/ppermute | solution.py:418
  57.1 1.5 %collective-permute-start.14 = (bf16[256,384]{1,0:T(8,128)(2,1)S(1)}, bf16[256,384]{1,0:T(8,128)(2,1)S(1)}, u32[]{:S(2)}, u32[]{:S(2)}) collective-permute-start(bf16[256,384]{1,0:T(8,128)(2,1)S(1)} %get-tuple-element.107), channel_id=1, source_target_pairs={{0,2},{1,3},{2,0},{3,1},{4,6},{5,7},{6,4},{7,5},{8,10},{9,11},{10,... | collective-permute-start | bytes 589832 | tf_op jit(solution)/shard_map/ppermute | solution.py:418
  58.9 11.0 %collective-permute-start.16 = (bf16[128,2176]{1,0:T(8,128)(2,1)S(1)}, bf16[128,2176]{1,0:T(8,128)(2,1)S(1)}, u32[]{:S(2)}, u32[]{:S(2)}) collective-permute-start(bf16[128,2176]{1,0:T(8,128)(2,1)S(1)} %slice.289), channel_id=1, source_target_pairs={{0,1},{1,0},{2,6},{3,7},{4,5},{5,4},{6,2},{7,3},{8,9},{9,8},{10,14... | collective-permute-start | bytes 1671176 | tf_op jit(solution)/shard_map/ppermute | solution.py:418
  64.0 5.5 %collective-permute-start.15 = (bf16[72,1152]{1,0:T(8,128)(2,1)S(1)}, bf16[72,1152]{1,0:T(8,128)(2,1)S(1)}, u32[]{:S(2)}, u32[]{:S(2)}) collective-permute-start(bf16[72,1152]{1,0:T(8,128)(2,1)S(1)} %pad_maximum_fusion.5), channel_id=1, source_target_pairs={{0,4},{1,5},{2,3},{3,2},{4,0},{5,1},{6,7},{7,6},{8,12},{9,13},{10,... | collective-permute-start | bytes 497672 | tf_op jit(solution)/shard_map/ppermute | solution.py:418
  70.1 6.6 %collective-permute-start.18 = (bf16[64,2176]{1,0:T(8,128)(2,1)S(1)}, bf16[64,2176]{1,0:T(8,128)(2,1)S(1)}, u32[]{:S(2)}, u32[]{:S(2)}) collective-permute-start(bf16[64,2176]{1,0:T(8,128)(2,1)S(1)} %slice.291), channel_id=1, source_target_pairs={{0,4},{1,5},{2,3},{3,2},{4,0},{5,1},{6,7},{7,6},{8,12},{9,13},{10,... | collective-permute-start | bytes 835592 | tf_op jit(solution)/shard_map/ppermute | solution.py:418
  72.0 4.6 %collective-permute-start.17 = (bf16[40,1152]{1,0:T(8,128)(2,1)S(1)}, bf16[40,1152]{1,0:T(8,128)(2,1)S(1)}, u32[]{:S(2)}, u32[]{:S(2)}) collective-permute-start(bf16[40,1152]{1,0:T(8,128)(2,1)S(1)} %pad_maximum_fusion.8), channel_id=1, source_target_pairs={{0,8},{1,9},{2,10},{3,11},{4,12},{5,13},{6,14},{7,15},{8,0},{9,1},... | collective-permute-start | bytes 276488 | tf_op jit(solution)/shard_map/ppermute | solution.py:418
  73.7 17.1 %collective-permute-start.22 = (bf16[1024,256]{1,0:T(8,128)(2,1)S(1)}, bf16[1024,256]{1,0:T(8,128)(2,1)S(1)}, u32[]{:S(2)}, u32[]{:S(2)}) collective-permute-start(bf16[1024,256]{1,0:T(8,128)(2,1)S(1)} %get-tuple-element.121), channel_id=1, source_target_pairs={{0,1},{1,0},{2,3},{3,2},{4,5},{5,4},{6,7},{7,6},{8,9},{9,8},{10,11... | collective-permute-start | bytes 1572872 | tf_op jit(solution)/shard_map/ppermute | solution.py:691
  76.8 14.1 %copy-start.2 = (f32[16,2048]{1,0:T(8,128)S(1)}, f32[16,2048]{1,0:T(8,128)}, u32[]{:S(2)}) copy-start(f32[16,2048]{1,0:T(8,128)} %refs_0_.1) | copy-start | bytes 393220
  76.8 14.1 %copy-start.4 = (f32[16,2048]{1,0:T(8,128)S(1)}, f32[16,2048]{1,0:T(8,128)}, u32[]{:S(2)}) copy-start(f32[16,2048]{1,0:T(8,128)} %refs_5_.1) | copy-start | bytes 393220
  76.8 14.1 %copy-start.5 = (f32[16,2048]{1,0:T(8,128)S(1)}, f32[16,2048]{1,0:T(8,128)}, u32[]{:S(2)}) copy-start(f32[16,2048]{1,0:T(8,128)} %refs_10_.1) | copy-start | bytes 393220
  76.8 14.1 %copy-start.6 = (f32[8,8,256]{2,1,0:T(8,128)S(1)}, f32[8,8,256]{2,1,0:T(8,128)}, u32[]{:S(2)}) copy-start(f32[8,8,256]{2,1,0:T(8,128)} %refs_7_.1) | copy-start | bytes 196612
  76.8 14.1 %copy-start.7 = (f32[8,8,256]{2,1,0:T(8,128)S(1)}, f32[8,8,256]{2,1,0:T(8,128)}, u32[]{:S(2)}) copy-start(f32[8,8,256]{2,1,0:T(8,128)} %refs_12_.1) | copy-start | bytes 196612
  76.9 14.1 %copy-start.9 = (f32[16,16]{1,0:T(8,128)S(1)}, f32[16,16]{1,0:T(8,128)}, u32[]{:S(2)}) copy-start(f32[16,16]{1,0:T(8,128)} %refs_1_.1) | copy-start | bytes 3076
  76.9 14.1 %copy-start.14 = (f32[16,16]{1,0:T(8,128)S(1)}, f32[16,16]{1,0:T(8,128)}, u32[]{:S(2)}) copy-start(f32[16,16]{1,0:T(8,128)} %refs_6_.1) | copy-start | bytes 3076
  76.9 14.1 %copy-start.15 = (f32[2,8,128]{2,1,0:T(8,128)S(1)}, f32[2,8,128]{2,1,0:T(8,128)}, u32[]{:S(2)}) copy-start(f32[2,8,128]{2,1,0:T(8,128)} %refs_8_.1) | copy-start | bytes 24580
  76.9 14.1 %copy-start.16 = (f32[16,16]{1,0:T(8,128)S(1)}, f32[16,16]{1,0:T(8,128)}, u32[]{:S(2)}) copy-start(f32[16,16]{1,0:T(8,128)} %refs_11_.1) | copy-start | bytes 3076
  76.9 14.1 %copy-start.17 = (f32[2,8,128]{2,1,0:T(8,128)S(1)}, f32[2,8,128]{2,1,0:T(8,128)}, u32[]{:S(2)}) copy-start(f32[2,8,128]{2,1,0:T(8,128)} %refs_13_.1) | copy-start | bytes 24580
  76.9 14.1 %copy-start.19 = (f32[2,128]{1,0:T(2,128)S(1)}, f32[2,128]{1,0:T(2,128)}, u32[]{:S(2)}) copy-start(f32[2,128]{1,0:T(2,128)} %refs_9_.1) | copy-start | bytes 3076
  76.9 14.1 %copy-start.20 = (f32[2,128]{1,0:T(2,128)S(1)}, f32[2,128]{1,0:T(2,128)}, u32[]{:S(2)}) copy-start(f32[2,128]{1,0:T(2,128)} %refs_14_.1) | copy-start | bytes 3076
  77.0 8.2 %collective-permute-start.20 = (bf16[32,2176]{1,0:T(8,128)(2,1)S(1)}, bf16[32,2176]{1,0:T(8,128)(2,1)S(1)}, u32[]{:S(2)}, u32[]{:S(2)}) collective-permute-start(bf16[32,2176]{1,0:T(8,128)(2,1)S(1)} %slice.293), channel_id=1, source_target_pairs={{0,8},{1,9},{2,10},{3,11},{4,12},{5,13},{6,14},{7,15},{8,0},{9,1},... | collective-permute-start | bytes 417800 | tf_op jit(solution)/shard_map/ppermute | solution.py:418
  79.6 5.6 %collective-permute-start.19 = (bf16[24,1152]{1,0:T(8,128)(2,1)S(1)}, bf16[24,1152]{1,0:T(8,128)(2,1)S(1)}, u32[]{:S(2)}, u32[]{:S(2)}) collective-permute-start(bf16[24,1152]{1,0:T(8,128)(2,1)S(1)} %pad_maximum_fusion.10), channel_id=1, source_target_pairs={{0,16},{1,17},{2,18},{3,19},{4,20},{5,21},{6,22},{7,23},{8,24},{9,... | collective-permute-start | bytes 165896 | tf_op jit(solution)/shard_map/ppermute | solution.py:418
  85.2 5.7 %collective-permute-start.21 = (bf16[16,2176]{1,0:T(8,128)(2,1)S(1)}, bf16[16,2176]{1,0:T(8,128)(2,1)S(1)}, u32[]{:S(2)}, u32[]{:S(2)}) collective-permute-start(bf16[16,2176]{1,0:T(8,128)(2,1)S(1)} %slice.295), channel_id=1, source_target_pairs={{0,16},{1,17},{2,18},{3,19},{4,20},{5,21},{6,22},{7,23},{8,24},{9,... | collective-permute-start | bytes 208904 | tf_op jit(solution)/shard_map/ppermute | solution.py:418

commit v5 on v4

--- a/solution.py
+++ b/solution.py
@@ -117,7 +117,7 @@
     half = own_ref.shape[0]
     count, wide = ga_ref.shape
     experts = wide // half
-    tile = count // 2
+    tile = count // 4
     places.start()
 
     def put(side, place, rr, ff):
@@ -132,8 +132,8 @@
     gate = raised / jnp.sum(raised, axis=0, keepdims=True)
     gate_ref[...] = jnp.concatenate([gate, gate], axis=0).T
 
-    def step(i, carry):
-        rows = pl.ds(pl.multiple_of(i * tile, tile), tile)
+    for i in range(4):
+        rows = slice(i * tile, (i + 1) * tile)
         x = x_ref[rows, :]
         gate = 0.5 * gate_ref[rows, :]
         for k in range(experts):
@@ -144,9 +144,6 @@
             scaled = gate[:, k : k + 1] * up
             ga_ref[rows, cols] = (scaled * pre).astype(bf16)
             gs_ref[rows, cols] = (scaled * (1.0 + pre - low * up)).astype(bf16)
-        return carry
-
-    lax.fori_loop(0, 2, step, 0)
 
 
 def second_kernel(
@@ -261,20 +258,27 @@
 
 def back_part(places, ks, w_ref, dm_ref, ga_ref, gs_ref, xt_ref, dp_ref, keep_ref, send_ref, g_ref):
     half = keep_ref.shape[0]
-    tile = dm_ref.shape[0] // 4
+    tile = dm_ref.shape[0] // 2
     places.start()
+
+    def weights(at):
+        here = slice(at * half, (at + 1) * half)
+        g_ref[:, here] = dot(xt_ref[...], dp_ref[:, here])
+        back_pack(places, here, keep_ref, send_ref, g_ref)
+
     terms = []
     for at, k in enumerate(ks):
         cols, here = slice(k * half, (k + 1) * half), slice(at * half, (at + 1) * half)
         sums = []
-        for i in range(4):
+        for i in range(2):
             rows = slice(i * tile, (i + 1) * tile)
             u = dot_t(dm_ref[rows, :], w_ref[cols, :])
             dp_ref[rows, here] = (u * gs_ref[rows, cols].astype(f32)).astype(bf16)
             sums.append(jnp.sum(u * ga_ref[rows, cols].astype(f32), axis=1, keepdims=True))
         terms.append(sums)
-        g_ref[:, here] = dot(xt_ref[...], dp_ref[:, here])
-        back_pack(places, here, keep_ref, send_ref, g_ref)
+        if at:
+            weights(at - 1)
+    weights(len(ks) - 1)
     return terms
 
 
@@ -290,10 +294,10 @@
 
 
 def set_terms(q_ref, terms, ks):
-    tile = q_ref.shape[0] // 4
+    tile = q_ref.shape[0] // 2
     experts = q_ref.shape[1] // 2
     lane = lax.broadcasted_iota(jnp.int32, (tile, 2 * experts), 1)
-    for i in range(4):
+    for i in range(2):
         rows = slice(i * tile, (i + 1) * tile)
         q = q_ref[rows, :]
         for k, sums in zip(ks, terms):
@@ -342,7 +346,8 @@
     back_pack(places, cols, keep_ref, send_ref, g_ref)
 
 
-def input_kernel(at, low_ref, high_ref, dg_ref, w_ref, keep_ref, send_ref):
+def input_kernel(at, low_ref, high_ref, dg_ref, w_ref, *refs):
+    keep_ref, send_ref = refs[-2:]
     part = low_ref.shape[1]
     wide = part + high_ref.shape[1]
     grad = dot_t(low_ref[...], w_ref[:, 0:part]) + dot_t(high_ref[...], w_ref[:, part:wide])
@@ -352,19 +357,23 @@
     send_ref[...] = grad[:, half:].astype(bf16)
 
 
-def update_kernel(rates, sum_a, got_a, sum_b, got_b, side, dx_ref, held_ref, *refs):
-    weights, velocities, averages = refs[0:5], refs[5:10], refs[10:15]
-    grad_ref, outs, (wide_ref, sems) = refs[15], refs[16:31], refs[31:]
-    micro, tile, _ = wide_ref.shape
-    start = pl.multiple_of((1 - lax.axis_index("field")) * tile, tile)
-    copies = []
-    for m in range(micro):
-        wide_ref[m] = dx_ref[m * tile : (m + 1) * tile, :].astype(f32)
-        copy = pltpu.make_async_copy(wide_ref.at[m], grad_ref.at[m, pl.ds(start, tile), :], sems.at[m])
-        copy.start()
-        copies.append(copy)
-    wide = weights[0].shape[1]
-    gates = weights[1].shape[1]
+def place_kernel(at, early_ref, late_ref, held_ref, out_ref):
+    tile = out_ref.shape[1]
+    half = pl.num_programs(0) // 2
+    m = pl.program_id(0)
+
+    @pl.when(m < half)
+    def _():
+        out_ref[0] = early_ref[pl.ds(pl.multiple_of(m * tile, tile), tile), :].astype(f32)
+
+    @pl.when(m >= half)
+    def _():
+        out_ref[0] = late_ref[pl.ds(pl.multiple_of((m - half) * tile, tile), tile), :].astype(f32)
+
+
+def update_kernel(rates, sum_a, got_a, sum_b, got_b, side, *refs):
+    weights, velocities, averages, outs = refs[0:5], refs[5:10], refs[10:15], refs[15:30]
+    wide, gates = weights[0].shape[1], weights[1].shape[1]
     experts, rows, out_cols = weights[2].shape
     tasks = weights[3].shape[0]
     part = experts // 2
@@ -387,8 +396,6 @@
     for t in range(tasks):
         renew(3, t, second[t * rows : (t + 1) * rows, part * out_cols :])
         renew(4, (slice(t, t + 1), slice(None)), side[0:1, t * LANES : (t + 1) * LANES])
-    for copy in copies:
-        copy.wait()
 
 
 class Cube:
@@ -429,19 +436,20 @@
         return out
 
 
-def gather_two(cube, block_a, make_b, x):
+def gather_two(cube, block_a, make_b, make_x):
     got_a = cube.swap(block_a, cube.order[0])
+    x = make_x(block_a)
     block_a = jnp.concatenate([block_a, got_a], axis=0)
     block_b = make_b(block_a)
     for at in range(1, len(cube.order)):
         got_a = cube.swap(block_a, cube.order[at])
         got_b = cube.swap(block_b, cube.order[at - 1])
         if at + 1 == len(cube.order):
-            got_a = after(got_a, x)
+            got_a = after(got_a, x[0])
         block_a = jnp.concatenate([block_a, after(got_a, got_b)], axis=0)
         block_b = jnp.concatenate([block_b, after(got_b, block_a)], axis=0)
     oth_a = cube.swap(block_a, cube.core)
-    return block_a, oth_a, block_b, cube.swap(block_b, cube.order[-1])
+    return block_a, oth_a, block_b, cube.swap(block_b, cube.order[-1]), x
 
 
 def after(values, *earlier):
@@ -529,6 +537,9 @@
     total_rows = micro * rows_dev * cube.rows
     r, f = lax.axis_index("rows"), lax.axis_index("field")
 
+    def swap_field(values):
+        return lax.ppermute(values, "field", [(0, 1), (1, 0)])
+
     def own_half(values, which):
         return lax.dynamic_slice_in_dim(values, which * tile, tile, 1)
 
@@ -547,8 +558,10 @@
             name="pack_b",
         )(expert_out, tower_in, after(valid_mask, earlier))
 
-    x_send = own_half(after(inputs, block_a), 1 - f).reshape(rows_own, width)
-    x_got = lax.ppermute(x_send, "field", [(0, 1), (1, 0)])
+
+    def send_x(earlier):
+        return swap_field(own_half(after(inputs, earlier), 1 - f).reshape(rows_own, width))
+
 
     pairs = width // BLOCK
     fit = first_rows == BLOCK
@@ -558,20 +571,22 @@
     a_cols, b_cols = wide + LANES, part * out_cols + LANES
     heads = tasks * tower_cols
 
-    x, x_t, flags, by_row = pl.pallas_call(
-        rows_kernel,
-        out_shape=[
-            shape((rows_own, 2 * width), bf16),
-            shape((2 * width, rows_own), bf16),
-            shape((8, rows_own), f32),
-            shape((rows_own, 8), f32),
-        ],
-        compiler_params=params(8),
-        cost_estimate=cost(1 << 20),
-        name="rows",
-    )(inputs, x_got, valid_mask, labels, domains)
-
-    own_a, oth_a, own_b, got_b = gather_two(cube, block_a, make_b, x)
+    def make_x(earlier):
+        x_got = send_x(earlier)
+        return pl.pallas_call(
+            rows_kernel,
+            out_shape=[
+                shape((rows_own, 2 * width), bf16),
+                shape((2 * width, rows_own), bf16),
+                shape((8, rows_own), f32),
+                shape((rows_own, 8), f32),
+            ],
+            compiler_params=params(8),
+            cost_estimate=cost(1 << 20),
+            name="rows",
+        )(inputs, x_got, valid_mask, labels, domains)
+
+    own_a, oth_a, own_b, got_b, (x, x_t, flags, by_row) = gather_two(cube, block_a, make_b, make_x)
     if not fit:
         rows_a = first_sorted(cube, cube.order, r, f, width, first_rows)
         own_a, oth_a = jnp.split(jnp.take(jnp.concatenate([own_a, oth_a]), rows_a, axis=0), 2)
@@ -654,41 +669,54 @@
     if not fit:
         keep_high, send_high = unsorted(keep_high, send_high, rows_a)
     got_high = cube.swap(send_high, steps[0])
-    keep_a = jnp.concatenate([keep_low, keep_high], axis=1)
-    got_a = jnp.concatenate([after(got_low, send_high), got_high], axis=1)
-    sum_a, next_a = fold(keep_a, got_a)
-    grad_keep, grad_send = pl.pallas_call(
-        input_kernel,
-        grid_spec=pltpu.PrefetchScalarGridSpec(
-            num_scalar_prefetch=1,
-            grid=(micro,),
-            in_specs=[
-                pl.BlockSpec((tile, low_cols), lambda i, at: (i, 0)),
-            pl.BlockSpec((tile, high_cols - LANES), lambda i, at: (i, 0)),
-                pl.BlockSpec((tile, LANES), lambda i, at: (i, 0)),
-                pl.BlockSpec((2 * width, a_cols), lambda i, at: (0, 0)),
+    sum_low, next_low = fold(keep_low, after(got_low, send_high))
+    got_low = cube.swap(next_low, steps[1])
+    sum_high, next_a = fold(keep_high, after(got_high, next_low))
+    got_high = cube.swap(next_a, steps[1])
+    def input_part(first, held, gates):
+        half = micro // 2
+        return pl.pallas_call(
+            input_kernel,
+            grid_spec=pltpu.PrefetchScalarGridSpec(
+                num_scalar_prefetch=1,
+                grid=(half,),
+                in_specs=[
+                    pl.BlockSpec((tile, low_cols), lambda i, at: (i + first, 0)),
+                    pl.BlockSpec((tile, high_cols - LANES), lambda i, at: (i + first, 0)),
+                    pl.BlockSpec((tile, LANES), lambda i, at: (i + first, 0)),
+                    pl.BlockSpec((2 * width, a_cols), lambda i, at: (0, 0)),
+                ]
+                + [pl.BlockSpec(memory_space=pl.ANY)] * len(held),
+                out_specs=[
+                    pl.BlockSpec((1, tile, width), lambda i, at: (i + first, at[0], 0)),
+                    pl.BlockSpec((tile, width), lambda i, at: (i, 0)),
+                ],
+            ),
+            out_shape=[
+                shape((micro, rows_dev, width), f32),
+                shape((half * tile, width), bf16),
             ],
-            out_specs=[
-                pl.BlockSpec((1, tile, width), lambda i, at: (i, at[0], 0)),
-                pl.BlockSpec((tile, width), lambda i, at: (i, 0)),
-            ],
-        ),
-        out_shape=[
-            shape((micro, rows_dev, width), f32),
-            shape((rows_own, width), bf16),
-        ],
-        compiler_params=params(12),
-        cost_estimate=cost(4 * rows_own * 2 * width * a_cols),
-        name="input",
-    )(f.astype(jnp.int32).reshape(1), dpre_low, dpre_high, after(dgate, next_a), first_w)
+            input_output_aliases={5: 0} if held else {},
+            compiler_params=params(12),
+            name="input",
+        )(f.astype(jnp.int32).reshape(1), dpre_low, dpre_high, gates, first_w, *held)
+
+    grad_keep, grad_send = input_part(0, (), after(dgate, next_a))
+    grad_got = []
+    got_a = jnp.concatenate([got_low, got_high], axis=1)
+    sum_a = jnp.concatenate([sum_low, sum_high], axis=1)
     for at in range(1, len(steps)):
-        got_a = cube.swap(next_a, steps[at])
+        if at > 1:
+            got_a = cube.swap(next_a, steps[at])
         if at + 1 < len(steps):
             sum_b, message, side = fold_beside(sum_b, side, after(got_b, next_a))
             got_b = cube.swap(message, steps[at + 1])
+            if at == 1:
+                early = grad_send
+                grad_keep, grad_send = input_part(micro // 2, (grad_keep,), after(dgate, message))
+            elif at <= 3:
+                grad_got.append(swap_field(after(early if at == 2 else grad_send, message)))
             sum_a, next_a = fold(sum_a, after(got_a, got_b, grad_send))
-        if at == 1:
-            grad_got = lax.ppermute(after(grad_send, next_a), "field", [(0, 1), (1, 0)])
     side = side + join_two(got_b[got_b.shape[0] - 8 :])
     weights = (expert_in, gate_in, expert_out, tower_in, tower_out)
     velocities = (
@@ -706,19 +734,26 @@
         average_tower_out,
     )
     rates = [base * math.sqrt(total_rows) for base in rate_bases]
-    hbm = pl.BlockSpec(memory_space=pl.ANY)
-    input_grad, *updated = pl.pallas_call(
+    input_grad = pl.pallas_call(
+        place_kernel,
+        grid_spec=pltpu.PrefetchScalarGridSpec(
+            num_scalar_prefetch=1,
+            grid=(micro,),
+            in_specs=[pl.BlockSpec((rows_own // 2, width), lambda i, at: (0, 0))] * 2
+            + [pl.BlockSpec(memory_space=pl.ANY)],
+            out_specs=pl.BlockSpec((1, tile, width), lambda i, at: (i, 1 - at[0], 0)),
+        ),
+        out_shape=shape((micro, rows_dev, width), f32),
+        input_output_aliases={3: 0},
+        compiler_params=params(8),
+        name="place",
+    )(f.astype(jnp.int32).reshape(1), *grad_got, after(grad_keep, next_a))
+    updated = pl.pallas_call(
         functools.partial(update_kernel, rates),
-        in_specs=[vmem] * 6 + [hbm] + [vmem] * 15,
-        out_specs=[hbm] + [vmem] * 15,
-        out_shape=[shape((micro, rows_dev, width), f32)]
-        + [shape(w.shape, f32) for w in weights for _ in range(3)],
-        scratch_shapes=[pltpu.VMEM((micro, tile, width), f32), pltpu.SemaphoreType.DMA((micro,))],
-        input_output_aliases={6: 0},
+        out_shape=[shape(w.shape, f32) for w in weights for _ in range(3)],
         compiler_params=params(8),
-        cost_estimate=cost(1 << 20),
         name="update",
-    )(sum_a, got_a, sum_b, got_b, side, grad_got, grad_keep, *weights, *velocities, *averages)
+    )(sum_a, after(got_a, input_grad), sum_b, got_b, side, *weights, *velocities, *averages)
     return (side[0, heads], input_grad, *updated)
 
 

time: 93.3 us -> 89.2 us (0.956)
  waiting for transfers between devices: 33.2 us -> 25.9 us
  starting transfers between devices: 32.3 us -> 35.3 us
    ppermute x21 -> x22, waiting for transfers between devices: 33.2 us -> 25.2 us  [swap(): return lax.ppermute(values, both, self.pairs(step))]
    ppermute x2 -> x3, starting transfers between devices: 2.04 us -> 4.7 us  [swap_field(): return lax.ppermute(values, 'field', [(0, 1), (1, 0)])]
    pallas_call x3 -> x5, Pallas kernels: 6.43 us -> 7.7 us  [the longest x2 4.65 us: input_part(): pl.pallas_call(input_kernel, grid_spec=pltpu.PrefetchScalarGridSpec(num_s...]
    ppermute x21 -> x22, starting transfers between devices: 30.3 us -> 30.6 us  [swap(): return lax.ppermute(values, both, self.pairs(step))]
  transfers between devices with their start and end apart: 23 -> 25, of which waited for: 14 -> 14; matrix products, arithmetic and copies ran while one was open for 3% -> 3% of each run, Pallas kernels for 17% -> 19%
where the time goes in v5:
time: 89.2 us; the launch traced here: 89 us
  starting transfers between devices  35.3 us (40%)
  waiting for transfers between devices  25.9 us (29%)
  Pallas kernels  21.6 us (24%)
  local copies, waits for them, and re-layouts  3.64 us (4%)
  between operations  1.42 us (2%)
  other arithmetic  1.21 us (1%)
    ppermute x22, starting transfers between devices, swap(): return lax.ppermute(values, both, self.pairs(step))  30.6 us
    ppermute x22, waiting for transfers between devices, swap(): return lax.ppermute(values, both, self.pairs(step))  25.2 us
    ppermute x3, starting transfers between devices, swap_field(): return lax.ppermute(values, 'field', [(0, 1), (1, 0)])  4.7 us
    pallas_call x2, Pallas kernels, input_part(): pl.pallas_call(input_kernel, grid_spec=pltpu.PrefetchScalarGridSpec(num_s...  4.65 us
    pallas_call x1, Pallas kernels, on_device(): pl.pallas_call(functools.partial(first_kernel, places), out_shape=[shape(...  4.41 us
    pallas_call x1, Pallas kernels, on_device(): pl.pallas_call(functools.partial(second_kernel, places), out_shape=[shape...  4.12 us
    pallas_call x1, Pallas kernels, on_device(): pl.pallas_call(functools.partial(back_first_kernel, places, range(cut)),...  3.77 us
  transfers between devices with their start and end apart: 25, of which 14 were waited for; matrix products, arithmetic and copies ran while one was open for 3% of the time, Pallas kernels for 19%

profile of v5, /device:TPU:0, one launch (start us, length us, event | category | flops | bytes accessed | tf_op | source)
XLA Modules:
  0.0 89.0 jit_solution(3706988601341931975)
XLA Ops:
  0.7 0.9 %copy-done.1 = f32[16,2048]{1,0:T(8,128)S(1)} copy-done((f32[16,2048]{1,0:T(8,128)S(1)}, f32[16,2048]{1,0:T(8,128)}, u32[]{:S(2)}) %copy-start.1) | copy-done | bytes 131096
  1.6 0.7 copy-done.8
  2.3 4.1 %collective-permute-start = (bf16[16,2176]{1,0:T(8,128)(2,1)S(1)}, bf16[16,2176]{1,0:T(8,128)(2,1)S(1)}, u32[]{:S(2)}, u32[]{:S(2)}) collective-permute-start(bf16[16,2176]{1,0:T(8,128)(2,1)S(1)} %pack_a.1), channel_id=1, source_target_pairs={{0,16},{1,17},{2,18},{3,19},{4,20},{5,21},{6,22},{7,23},{8,24},{9,... | collective-permute-start | bytes 208904 | tf_op jit(solution)/shard_map/ppermute | solution.py:425
  6.4 1.1 %constant_dynamic-slice_fusion = bf16[4,256,256]{2,1,0:T(8,128)(2,1)S(1)} fusion(bf16[4,512,256]{2,1,0:T(8,128)(2,1)} %in_ref.1, s32[]{:T(128)S(6)} %select_n.3), kind=kLoop, calls=%fused_computation.86 | loop fusion | bytes 1048580 | tf_op jit(solution)/shard_map/dynamic_slice | solution.py:544
  7.5 1.6 %collective-permute-start.7 = (bf16[1024,256]{1,0:T(8,128)(2,1)S(1)}, bf16[1024,256]{1,0:T(8,128)(2,1)S(1)}, u32[]{:S(2)}, u32[]{:S(2)}) collective-permute-start(bf16[1024,256]{1,0:T(8,128)(2,1)S(1)} %bitcast.3), channel_id=1, source_target_pairs={{0,1},{1,0},{2,3},{3,2},{4,5},{5,4},{6,7},{7,6},{8,9},{9,8},{10,11... | collective-permute-start | bytes 1572872 | tf_op jit(solution)/shard_map/ppermute | solution.py:541
  9.1 1.1 %collective-permute-done = bf16[16,2176]{1,0:T(8,128)(2,1)S(1)} collective-permute-done((bf16[16,2176]{1,0:T(8,128)(2,1)S(1)}, bf16[16,2176]{1,0:T(8,128)(2,1)S(1)}, u32[]{:S(2)}, u32[]{:S(2)}) %collective-permute-start) | collective-permute-done | bytes 69664 | tf_op jit(solution)/shard_map/ppermute | solution.py:425
  10.2 0.7 collective-permute-start.2
  11.0 3.4 %collective-permute-start.1 = (bf16[16,1280]{1,0:T(8,128)(2,1)S(1)}, bf16[16,1280]{1,0:T(8,128)(2,1)S(1)}, u32[]{:S(2)}, u32[]{:S(2)}) collective-permute-start(bf16[16,1280]{1,0:T(8,128)(2,1)S(1)} %pack_b.1), channel_id=1, source_target_pairs={{0,16},{1,17},{2,18},{3,19},{4,20},{5,21},{6,22},{7,23},{8,24},{9,... | collective-permute-start | bytes 122888 | tf_op jit(solution)/shard_map/ppermute | solution.py:425
  14.4 2.1 %collective-permute-done.1 = bf16[16,1280]{1,0:T(8,128)(2,1)S(1)} collective-permute-done((bf16[16,1280]{1,0:T(8,128)(2,1)S(1)}, bf16[16,1280]{1,0:T(8,128)(2,1)S(1)}, u32[]{:S(2)}, u32[]{:S(2)}) %collective-permute-start.1) | collective-permute-done | bytes 40992 | tf_op jit(solution)/shard_map/ppermute | solution.py:425
  16.6 1.6 %collective-permute-start.4 = (bf16[64,2176]{1,0:T(8,128)(2,1)S(1)}, bf16[64,2176]{1,0:T(8,128)(2,1)S(1)}, u32[]{:S(2)}, u32[]{:S(2)}) collective-permute-start(bf16[64,2176]{1,0:T(8,128)(2,1)S(1)} %pad_maximum_fusion.6), channel_id=1, source_target_pairs={{0,4},{1,5},{2,3},{3,2},{4,0},{5,1},{6,7},{7,6},{8,12},{9,13},{10,... | collective-permute-start | bytes 835592 | tf_op jit(solution)/shard_map/ppermute | solution.py:425
  18.2 2.2 %collective-permute-start.3 = (bf16[32,1280]{1,0:T(8,128)(2,1)S(1)}, bf16[32,1280]{1,0:T(8,128)(2,1)S(1)}, u32[]{:S(2)}, u32[]{:S(2)}) collective-permute-start(bf16[32,1280]{1,0:T(8,128)(2,1)S(1)} %pad_maximum_fusion.11), channel_id=1, source_target_pairs={{0,8},{1,9},{2,10},{3,11},{4,12},{5,13},{6,14},{7,15},{8,0},{9,1},... | collective-permute-start | bytes 245768 | tf_op jit(solution)/shard_map/ppermute | solution.py:425
  20.4 2.4 %collective-permute-done.3 = bf16[32,1280]{1,0:T(8,128)(2,1)S(1)} collective-permute-done((bf16[32,1280]{1,0:T(8,128)(2,1)S(1)}, bf16[32,1280]{1,0:T(8,128)(2,1)S(1)}, u32[]{:S(2)}, u32[]{:S(2)}) %collective-permute-start.3) | collective-permute-done | bytes 81952 | tf_op jit(solution)/shard_map/ppermute | solution.py:425
  22.8 0.4 collective-permute-done.4
  23.2 1.6 %collective-permute-start.6 = (bf16[128,2176]{1,0:T(8,128)(2,1)S(1)}, bf16[128,2176]{1,0:T(8,128)(2,1)S(1)}, u32[]{:S(2)}, u32[]{:S(2)}) collective-permute-start(bf16[128,2176]{1,0:T(8,128)(2,1)S(1)} %pad_maximum_fusion.2), channel_id=1, source_target_pairs={{0,1},{1,0},{2,6},{3,7},{4,5},{5,4},{6,2},{7,3},{8,9},{9,8},{10,14... | collective-permute-start | bytes 1671176 | tf_op jit(solution)/shard_map/ppermute | solution.py:425
  24.8 1.6 %collective-permute-start.5 = (bf16[64,1280]{1,0:T(8,128)(2,1)S(1)}, bf16[64,1280]{1,0:T(8,128)(2,1)S(1)}, u32[]{:S(2)}, u32[]{:S(2)}) collective-permute-start(bf16[64,1280]{1,0:T(8,128)(2,1)S(1)} %pad_maximum_fusion.8), channel_id=1, source_target_pairs={{0,4},{1,5},{2,3},{3,2},{4,0},{5,1},{6,7},{7,6},{8,12},{9,13},{10,... | collective-permute-start | bytes 491528 | tf_op jit(solution)/shard_map/ppermute | solution.py:425
  26.5 0.6 rows.1
  27.0 7.6 %collective-permute-done.6 = bf16[128,2176]{1,0:T(8,128)(2,1)S(1)} collective-permute-done((bf16[128,2176]{1,0:T(8,128)(2,1)S(1)}, bf16[128,2176]{1,0:T(8,128)(2,1)S(1)}, u32[]{:S(2)}, u32[]{:S(2)}) %collective-permute-start.6) | collective-permute-done | bytes 557088 | tf_op jit(solution)/shard_map/ppermute | solution.py:425
  34.8 1.6 %collective-permute-start.8 = (bf16[128,1280]{1,0:T(8,128)(2,1)S(1)}, bf16[128,1280]{1,0:T(8,128)(2,1)S(1)}, u32[]{:S(2)}, u32[]{:S(2)}) collective-permute-start(bf16[128,1280]{1,0:T(8,128)(2,1)S(1)} %pad_maximum_fusion.4), channel_id=1, source_target_pairs={{0,1},{1,0},{2,6},{3,7},{4,5},{5,4},{6,2},{7,3},{8,9},{9,8},{10,14... | collective-permute-start | bytes 983048 | tf_op jit(solution)/shard_map/ppermute | solution.py:425
  36.4 1.1 %collective-permute-done.9.oth_ref = bf16[256,2176]{1,0:T(8,128)(2,1)S(1)} collective-permute-done((bf16[256,2176]{1,0:T(8,128)(2,1)S(1)}, bf16[256,2176]{1,0:T(8,128)(2,1)S(1)}, u32[]{:S(2)}, u32[]{:S(2)}) %collective-permute-start.9) | collective-permute-done | bytes 1114144 | tf_op jit(solution)/shard_map/ppermute | solution.py:425
  37.5 4.4 %first.1 = (bf16[1024,2048]{1,0:T(8,128)(2,1)S(1)}, bf16[1024,2048]{1,0:T(8,128)(2,1)S(1)}, f32[1024,16]{1,0:T(8,128)S(1)}, bf16[512,2176]{1,0:T(8,128)(2,1)S(1)}) custom-call(bf16[256,2176]{1,0:T(8,128)(2,1)S(1)} %constant_dynamic-update-slice_fusion.own_ref, bf16[256,2176]{1,0:T(8,128)(2,1)S(1)} %collective-permute-done.9.oth_ref, ...), custom_call_target="tpu_custom_call" | custom-call | flops 4563402752 | bytes 8388608 | tf_op jit(solution)/shard_map/first/pallas_call | solution.py:593
  42.1 2.0 %collective-permute-done.10.oth_ref = bf16[256,1280]{1,0:T(8,128)(2,1)S(1)} collective-permute-done((bf16[256,1280]{1,0:T(8,128)(2,1)S(1)}, bf16[256,1280]{1,0:T(8,128)(2,1)S(1)}, u32[]{:S(2)}, u32[]{:S(2)}) %collective-permute-start.10) | collective-permute-done | bytes 655392 | tf_op jit(solution)/shard_map/ppermute | solution.py:425
  44.1 4.1 %second.1 = (bf16[2048,256]{1,0:T(8,128)(2,1)S(1)}, bf16[1024,256]{1,0:T(8,128)(2,1)S(1)}, f32[8,1152]{1,0:T(8,128)S(1)}, f32[256,1152]{1,0:T(8,128)S(1)}, bf16[256,1152]{1,0:T(8,128)(2,1)S(1)}) custom-call(bf16[256,1280]{1,0:T(8,128)(2,1)S(1)} %constant_dynamic-update-slice_fusion.5.own_ref, bf16[256,1280]{1,0:T(8,128)(2,1)S(1)} %collective-permute-done.10.oth_ref, ...), custom_call_target="tpu_custom_call" | custom-call | tf_op jit(solution)/shard_map/second/pallas_call | solution.py:611
  48.3 0.2 collective-permute-start.11
  48.5 3.8 %back_first.1 = (bf16[1024,1792]{1,0:T(8,128)(2,1)S(1)}, f32[256,1792]{1,0:T(8,128)S(1)}, bf16[256,1792]{1,0:T(8,128)(2,1)S(1)}, f32[1024,16]{1,0:T(8,128)S(1)}) custom-call(bf16[2048,256]{1,0:T(8,128)(2,1)S(1)} %get-tuple-element.103.w_ref, bf16[1024,256]{1,0:T(8,128)(2,1)S(1)} %get-tuple-element.104.dm_ref, ...), custom_call_target="tpu_custom_call" | custom-call | tf_op jit(solution)/shard_map/back_first/pallas_call | solution.py:637
  52.3 0.4 collective-permute-start.14
  53.1 1.6 %collective-permute-start.12 = (bf16[136,1152]{1,0:T(8,128)(2,1)S(1)}, bf16[136,1152]{1,0:T(8,128)(2,1)S(1)}, u32[]{:S(2)}, u32[]{:S(2)}) collective-permute-start(bf16[136,1152]{1,0:T(8,128)(2,1)S(1)} %pad_maximum_fusion.5), channel_id=1, source_target_pairs={{0,1},{1,0},{2,6},{3,7},{4,5},{5,4},{6,2},{7,3},{8,9},{9,8},{10,14... | collective-permute-start | bytes 940040 | tf_op jit(solution)/shard_map/ppermute | solution.py:425
  54.7 1.5 %back_last.1 = (bf16[1024,256]{1,0:T(8,128)(2,1)S(1)}, f32[256,384]{1,0:T(8,128)S(1)}, bf16[256,384]{1,0:T(8,128)(2,1)S(1)}, bf16[1024,128]{1,0:T(8,128)(2,1)S(1)}) custom-call(bf16[2048,256]{1,0:T(8,128)(2,1)S(1)} %get-tuple-element.103.w_ref, bf16[1024,256]{1,0:T(8,128)(2,1)S(1)} %get-tuple-element.104.dm_ref, ...), custom_call_target="tpu_custom_call" | custom-call | tf_op jit(solution)/shard_map/back_last/pallas_call | solution.py:654
  56.5 1.3 %collective-permute-start.16 = (bf16[128,1792]{1,0:T(8,128)(2,1)S(1)}, bf16[128,1792]{1,0:T(8,128)(2,1)S(1)}, u32[]{:S(2)}, u32[]{:S(2)}) collective-permute-start(bf16[128,1792]{1,0:T(8,128)(2,1)S(1)} %slice.294), channel_id=1, source_target_pairs={{0,1},{1,0},{2,6},{3,7},{4,5},{5,4},{6,2},{7,3},{8,9},{9,8},{10,14... | collective-permute-start | bytes 1376264 | tf_op jit(solution)/shard_map/ppermute | solution.py:425
  57.8 0.9 collective-permute-start.17
  58.7 2.3 %input.2 = (f32[4,512,256]{2,1,0:T(8,128)}, bf16[512,256]{1,0:T(8,128)(2,1)S(1)}) custom-call(s32[1]{0:T(128)} %bitcast.1.at, bf16[1024,1792]{1,0:T(8,128)(2,1)S(1)} %get-tuple-element.117.low_ref, bf16[1024,256]{1,0:T(8,128)(2,1)S(1)} %get-tuple-element.118.high_ref, bf16[1024,128]{1,0:T(8,128)(2,1)S(1)} %get-tuple-element.122.dg_ref, ...), custom_call_target="tpu_custom_call" | custom-call | tf_op jit(solution)/shard_map/input/pallas_call | solution.py:678
  61.2 1.4 %collective-permute-start.15 = (bf16[72,1152]{1,0:T(8,128)(2,1)S(1)}, bf16[72,1152]{1,0:T(8,128)(2,1)S(1)}, u32[]{:S(2)}, u32[]{:S(2)}) collective-permute-start(bf16[72,1152]{1,0:T(8,128)(2,1)S(1)} %pad_maximum_fusion.7), channel_id=1, source_target_pairs={{0,4},{1,5},{2,3},{3,2},{4,0},{5,1},{6,7},{7,6},{8,12},{9,13},{10,... | collective-permute-start | bytes 497672 | tf_op jit(solution)/shard_map/ppermute | solution.py:425
  62.7 2.3 %input.3 = (f32[4,512,256]{2,1,0:T(8,128)}, bf16[512,256]{1,0:T(8,128)(2,1)S(1)}) custom-call(s32[1]{0:T(128)} %bitcast.1.at, bf16[1024,1792]{1,0:T(8,128)(2,1)S(1)} %get-tuple-element.117.low_ref, bf16[1024,256]{1,0:T(8,128)(2,1)S(1)} %get-tuple-element.118.high_ref, ...), custom_call_target="tpu_custom_call", output_to_operand_aliasing={{0}: (5, {})} | custom-call | tf_op jit(solution)/shard_map/input/pallas_call | solution.py:678
  65.0 2.9 %collective-permute-done.17 = bf16[128,384]{1,0:T(8,128)(2,1)S(1)} collective-permute-done((bf16[128,384]{1,0:T(8,128)(2,1)S(1)}, bf16[128,384]{1,0:T(8,128)(2,1)S(1)}, u32[]{:S(2)}, u32[]{:S(2)}) %collective-permute-start.17) | collective-permute-done | bytes 98336 | tf_op jit(solution)/shard_map/ppermute | solution.py:425
  68.1 1.4 %collective-permute-start.19 = (bf16[64,2176]{1,0:T(8,128)(2,1)S(1)}, bf16[64,2176]{1,0:T(8,128)(2,1)S(1)}, u32[]{:S(2)}, u32[]{:S(2)}) collective-permute-start(bf16[64,2176]{1,0:T(8,128)(2,1)S(1)} %slice.296), channel_id=1, source_target_pairs={{0,4},{1,5},{2,3},{3,2},{4,0},{5,1},{6,7},{7,6},{8,12},{9,13},{10,... | collective-permute-start | bytes 835592 | tf_op jit(solution)/shard_map/ppermute | solution.py:425
  69.6 1.8 %collective-permute-start.18 = (bf16[40,1152]{1,0:T(8,128)(2,1)S(1)}, bf16[40,1152]{1,0:T(8,128)(2,1)S(1)}, u32[]{:S(2)}, u32[]{:S(2)}) collective-permute-start(bf16[40,1152]{1,0:T(8,128)(2,1)S(1)} %pad_maximum_fusion.10), channel_id=1, source_target_pairs={{0,8},{1,9},{2,10},{3,11},{4,12},{5,13},{6,14},{7,15},{8,0},{9,1},... | collective-permute-start | bytes 276488 | tf_op jit(solution)/shard_map/ppermute | solution.py:425
  71.4 1.6 %collective-permute-start.21 = (bf16[512,256]{1,0:T(8,128)(2,1)S(1)}, bf16[512,256]{1,0:T(8,128)(2,1)S(1)}, u32[]{:S(2)}, u32[]{:S(2)}) collective-permute-start(bf16[512,256]{1,0:T(8,128)(2,1)S(1)} %get-tuple-element.130), channel_id=1, source_target_pairs={{0,1},{1,0},{2,3},{3,2},{4,5},{5,4},{6,7},{7,6},{8,9},{9,8},{10,11... | collective-permute-start | bytes 786440 | tf_op jit(solution)/shard_map/ppermute | solution.py:541
  73.0 1.3 %collective-permute-done.18 = bf16[40,1152]{1,0:T(8,128)(2,1)S(1)} collective-permute-done((bf16[40,1152]{1,0:T(8,128)(2,1)S(1)}, bf16[40,1152]{1,0:T(8,128)(2,1)S(1)}, u32[]{:S(2)}, u32[]{:S(2)}) %collective-permute-start.18) | collective-permute-done | bytes 92192 | tf_op jit(solution)/shard_map/ppermute | solution.py:425
  74.2 0.5 collective-permute-done.19
  74.9 2.2 %collective-permute-start.23 = (bf16[32,2176]{1,0:T(8,128)(2,1)S(1)}, bf16[32,2176]{1,0:T(8,128)(2,1)S(1)}, u32[]{:S(2)}, u32[]{:S(2)}) collective-permute-start(bf16[32,2176]{1,0:T(8,128)(2,1)S(1)} %slice.298), channel_id=1, source_target_pairs={{0,8},{1,9},{2,10},{3,11},{4,12},{5,13},{6,14},{7,15},{8,0},{9,1},... | collective-permute-start | bytes 417800 | tf_op jit(solution)/shard_map/ppermute | solution.py:425
  77.1 1.0 %collective-permute-start.20 = (bf16[24,1152]{1,0:T(8,128)(2,1)S(1)}, bf16[24,1152]{1,0:T(8,128)(2,1)S(1)}, u32[]{:S(2)}, u32[]{:S(2)}) collective-permute-start(bf16[24,1152]{1,0:T(8,128)(2,1)S(1)} %pad_maximum_fusion.12), channel_id=1, source_target_pairs={{0,16},{1,17},{2,18},{3,19},{4,20},{5,21},{6,22},{7,23},{8,24},{9,... | collective-permute-start | bytes 165896 | tf_op jit(solution)/shard_map/ppermute | solution.py:425
  78.1 1.6 %collective-permute-start.22 = (bf16[512,256]{1,0:T(8,128)(2,1)S(1)}, bf16[512,256]{1,0:T(8,128)(2,1)S(1)}, u32[]{:S(2)}, u32[]{:S(2)}) collective-permute-start(bf16[512,256]{1,0:T(8,128)(2,1)S(1)} %get-tuple-element.131), channel_id=1, source_target_pairs={{0,1},{1,0},{2,3},{3,2},{4,5},{5,4},{6,7},{7,6},{8,9},{9,8},{10,11... | collective-permute-start | bytes 786440 | tf_op jit(solution)/shard_map/ppermute | solution.py:541
  79.7 2.6 %collective-permute-done.20.got_b = bf16[24,1152]{1,0:T(8,128)(2,1)S(1)} collective-permute-done((bf16[24,1152]{1,0:T(8,128)(2,1)S(1)}, bf16[24,1152]{1,0:T(8,128)(2,1)S(1)}, u32[]{:S(2)}, u32[]{:S(2)}) %collective-permute-start.20) | collective-permute-done | bytes 55328 | tf_op jit(solution)/shard_map/ppermute | solution.py:425
  82.4 1.4 %collective-permute-start.24 = (bf16[16,2176]{1,0:T(8,128)(2,1)S(1)}, bf16[16,2176]{1,0:T(8,128)(2,1)S(1)}, u32[]{:S(2)}, u32[]{:S(2)}) collective-permute-start(bf16[16,2176]{1,0:T(8,128)(2,1)S(1)} %slice.301), channel_id=1, source_target_pairs={{0,16},{1,17},{2,18},{3,19},{4,20},{5,21},{6,22},{7,23},{8,24},{9,... | collective-permute-start | bytes 208904 | tf_op jit(solution)/shard_map/ppermute | solution.py:425
  83.7 0.5 slice.226
  84.4 0.6 collective-permute-done.22.late_ref
  85.0 1.5 %place.1 = f32[4,512,256]{2,1,0:T(8,128)} custom-call(s32[1]{0:T(128)} %bitcast.1.at, bf16[512,256]{1,0:T(8,128)(2,1)S(1)} %collective-permute-done.21.early_ref, bf16[512,256]{1,0:T(8,128)(2,1)S(1)} %collective-permute-done.22.late_ref, f32[4,512,256]{2,1,0:T(8,128)} %get-tuple-element.134.held_ref), custom_call_target="tpu_custom_call", output_to_operand_aliasing={{}: (3, {})} | custom-call | tf_op jit(solution)/shard_map/place/pallas_call | solution.py:737
  86.6 1.2 %collective-permute-done.24.got_a = bf16[16,2176]{1,0:T(8,128)(2,1)S(1)} collective-permute-done((bf16[16,2176]{1,0:T(8,128)(2,1)S(1)}, bf16[16,2176]{1,0:T(8,128)(2,1)S(1)}, u32[]{:S(2)}, u32[]{:S(2)}) %collective-permute-start.24) | collective-permute-done | bytes 69664 | tf_op jit(solution)/shard_map/ppermute | solution.py:425
  87.9 0.9 %update.1 = (f32[16,2048]{1,0:T(8,128)}, f32[16,2048]{1,0:T(8,128)}, f32[16,2048]{1,0:T(8,128)}, f32[16,16]{1,0:T(8,128)}, f32[16,16]{1,0:T(8,128)}, /*index=5*/...) custom-call(f32[32,2176]{1,0:T(8,128)S(1)} %slice_add_fusion.3.sum_a, ...), custom_call_target="tpu_custom_call" | custom-call | tf_op jit(solution)/shard_map/update/pallas_call | solution.py:751
  (117 shorter events, 2.2 us)
Async XLA Ops:
  0.7 0.9 %copy-start.1 = (f32[16,2048]{1,0:T(8,128)S(1)}, f32[16,2048]{1,0:T(8,128)}, u32[]{:S(2)}) copy-start(f32[16,2048]{1,0:T(8,128)} %refs_0_.1) | copy-start | bytes 393220
  1.6 0.7 copy-start.8
  2.3 8.6 %copy-start.3 = (f32[8,8,256]{2,1,0:T(8,128)S(1)}, f32[8,8,256]{2,1,0:T(8,128)}, u32[]{:S(2)}) copy-start(f32[8,8,256]{2,1,0:T(8,128)} %refs_2_.1) | copy-start | bytes 196612
  2.3 8.6 %copy-start.10 = (s32[4,512]{1,0:T(4,128)S(1)}, s32[4,512]{1,0:T(4,128)}, u32[]{:S(2)}) copy-start(s32[4,512]{1,0:T(4,128)} %valid_ref.2) | copy-start | bytes 24580
  2.3 8.6 %copy-start.11 = (f32[2,8,128]{2,1,0:T(8,128)S(1)}, f32[2,8,128]{2,1,0:T(8,128)}, u32[]{:S(2)}) copy-start(f32[2,8,128]{2,1,0:T(8,128)} %refs_3_.1) | copy-start | bytes 24580
  2.3 7.9 %collective-permute-start = (bf16[16,2176]{1,0:T(8,128)(2,1)S(1)}, bf16[16,2176]{1,0:T(8,128)(2,1)S(1)}, u32[]{:S(2)}, u32[]{:S(2)}) collective-permute-start(bf16[16,2176]{1,0:T(8,128)(2,1)S(1)} %pack_a.1), channel_id=1, source_target_pairs={{0,16},{1,17},{2,18},{3,19},{4,20},{5,21},{6,22},{7,23},{8,24},{9,... | collective-permute-start | bytes 208904 | tf_op jit(solution)/shard_map/ppermute | solution.py:425
  7.5 19.0 %collective-permute-start.7 = (bf16[1024,256]{1,0:T(8,128)(2,1)S(1)}, bf16[1024,256]{1,0:T(8,128)(2,1)S(1)}, u32[]{:S(2)}, u32[]{:S(2)}) collective-permute-start(bf16[1024,256]{1,0:T(8,128)(2,1)S(1)} %bitcast.3), channel_id=1, source_target_pairs={{0,1},{1,0},{2,3},{3,2},{4,5},{5,4},{6,7},{7,6},{8,9},{9,8},{10,11... | collective-permute-start | bytes 1572872 | tf_op jit(solution)/shard_map/ppermute | solution.py:541
  10.2 6.4 %collective-permute-start.2 = (bf16[32,2176]{1,0:T(8,128)(2,1)S(1)}, bf16[32,2176]{1,0:T(8,128)(2,1)S(1)}, u32[]{:S(2)}, u32[]{:S(2)}) collective-permute-start(bf16[32,2176]{1,0:T(8,128)(2,1)S(1)} %pad_maximum_fusion.9), channel_id=1, source_target_pairs={{0,8},{1,9},{2,10},{3,11},{4,12},{5,13},{6,14},{7,15},{8,0},{9,1},... | collective-permute-start | bytes 417800 | tf_op jit(solution)/shard_map/ppermute | solution.py:425
  11.0 5.6 %collective-permute-start.1 = (bf16[16,1280]{1,0:T(8,128)(2,1)S(1)}, bf16[16,1280]{1,0:T(8,128)(2,1)S(1)}, u32[]{:S(2)}, u32[]{:S(2)}) collective-permute-start(bf16[16,1280]{1,0:T(8,128)(2,1)S(1)} %pack_b.1), channel_id=1, source_target_pairs={{0,16},{1,17},{2,18},{3,19},{4,20},{5,21},{6,22},{7,23},{8,24},{9,... | collective-permute-start | bytes 122888 | tf_op jit(solution)/shard_map/ppermute | solution.py:425
  16.6 6.6 %collective-permute-start.4 = (bf16[64,2176]{1,0:T(8,128)(2,1)S(1)}, bf16[64,2176]{1,0:T(8,128)(2,1)S(1)}, u32[]{:S(2)}, u32[]{:S(2)}) collective-permute-start(bf16[64,2176]{1,0:T(8,128)(2,1)S(1)} %pad_maximum_fusion.6), channel_id=1, source_target_pairs={{0,4},{1,5},{2,3},{3,2},{4,0},{5,1},{6,7},{7,6},{8,12},{9,13},{10,... | collective-permute-start | bytes 835592 | tf_op jit(solution)/shard_map/ppermute | solution.py:425
  18.1 8.3 %copy-start = (bf16[4,512,256]{2,1,0:T(8,128)(2,1)S(1)}, bf16[4,512,256]{2,1,0:T(8,128)(2,1)}, u32[]{:S(2)}) copy-start(bf16[4,512,256]{2,1,0:T(8,128)(2,1)} %in_ref.1) | copy-start | bytes 3145732
  18.1 8.3 %copy-start.12 = (s32[4,512]{1,0:T(4,128)S(1)}, s32[4,512]{1,0:T(4,128)}, u32[]{:S(2)}) copy-start(s32[4,512]{1,0:T(4,128)} %label_ref.1) | copy-start | bytes 24580
  18.1 8.3 %copy-start.13 = (s32[4,512]{1,0:T(4,128)S(1)}, s32[4,512]{1,0:T(4,128)}, u32[]{:S(2)}) copy-start(s32[4,512]{1,0:T(4,128)} %domain_ref.1) | copy-start | bytes 24580
  18.2 4.6 %collective-permute-start.3 = (bf16[32,1280]{1,0:T(8,128)(2,1)S(1)}, bf16[32,1280]{1,0:T(8,128)(2,1)S(1)}, u32[]{:S(2)}, u32[]{:S(2)}) collective-permute-start(bf16[32,1280]{1,0:T(8,128)(2,1)S(1)} %pad_maximum_fusion.11), channel_id=1, source_target_pairs={{0,8},{1,9},{2,10},{3,11},{4,12},{5,13},{6,14},{7,15},{8,0},{9,1},... | collective-permute-start | bytes 245768 | tf_op jit(solution)/shard_map/ppermute | solution.py:425
  23.2 11.4 %collective-permute-start.6 = (bf16[128,2176]{1,0:T(8,128)(2,1)S(1)}, bf16[128,2176]{1,0:T(8,128)(2,1)S(1)}, u32[]{:S(2)}, u32[]{:S(2)}) collective-permute-start(bf16[128,2176]{1,0:T(8,128)(2,1)S(1)} %pad_maximum_fusion.2), channel_id=1, source_target_pairs={{0,1},{1,0},{2,6},{3,7},{4,5},{5,4},{6,2},{7,3},{8,9},{9,8},{10,14... | collective-permute-start | bytes 1671176 | tf_op jit(solution)/shard_map/ppermute | solution.py:425
  24.8 9.8 %collective-permute-start.5 = (bf16[64,1280]{1,0:T(8,128)(2,1)S(1)}, bf16[64,1280]{1,0:T(8,128)(2,1)S(1)}, u32[]{:S(2)}, u32[]{:S(2)}) collective-permute-start(bf16[64,1280]{1,0:T(8,128)(2,1)S(1)} %pad_maximum_fusion.8), channel_id=1, source_target_pairs={{0,4},{1,5},{2,3},{3,2},{4,0},{5,1},{6,7},{7,6},{8,12},{9,13},{10,... | collective-permute-start | bytes 491528 | tf_op jit(solution)/shard_map/ppermute | solution.py:425
  34.7 2.8 %collective-permute-start.9 = (bf16[256,2176]{1,0:T(8,128)(2,1)S(1)}, bf16[256,2176]{1,0:T(8,128)(2,1)S(1)}, u32[]{:S(2)}, u32[]{:S(2)}) collective-permute-start(bf16[256,2176]{1,0:T(8,128)(2,1)S(1)} %constant_dynamic-update-slice_fusion.own_ref), channel_id=1, source_target_pairs={{0,2},{1,3},{2,0},{3,1},{4,6},{5,7},{6,4},{7,5},{8,10},{9,11},{10,... | collective-permute-start | bytes 3342344 | tf_op jit(solution)/shard_map/ppermute | solution.py:425
  34.8 7.1 %collective-permute-start.8 = (bf16[128,1280]{1,0:T(8,128)(2,1)S(1)}, bf16[128,1280]{1,0:T(8,128)(2,1)S(1)}, u32[]{:S(2)}, u32[]{:S(2)}) collective-permute-start(bf16[128,1280]{1,0:T(8,128)(2,1)S(1)} %pad_maximum_fusion.4), channel_id=1, source_target_pairs={{0,1},{1,0},{2,6},{3,7},{4,5},{5,4},{6,2},{7,3},{8,9},{9,8},{10,14... | collective-permute-start | bytes 983048 | tf_op jit(solution)/shard_map/ppermute | solution.py:425
  37.5 6.7 %copy-start.18 = (f32[2,128]{1,0:T(2,128)S(1)}, f32[2,128]{1,0:T(2,128)}, u32[]{:S(2)}) copy-start(f32[2,128]{1,0:T(2,128)} %refs_4_.1) | copy-start | bytes 3076
  42.0 2.2 %collective-permute-start.10 = (bf16[256,1280]{1,0:T(8,128)(2,1)S(1)}, bf16[256,1280]{1,0:T(8,128)(2,1)S(1)}, u32[]{:S(2)}, u32[]{:S(2)}) collective-permute-start(bf16[256,1280]{1,0:T(8,128)(2,1)S(1)} %constant_dynamic-update-slice_fusion.5.own_ref), channel_id=1, source_target_pairs={{0,2},{1,3},{2,0},{3,1},{4,6},{5,7},{6,4},{7,5},{8,10},{9,11},{10,... | collective-permute-start | bytes 1966088 | tf_op jit(solution)/shard_map/ppermute | solution.py:425
  48.3 4.4 %collective-permute-start.11 = (bf16[264,1152]{1,0:T(8,128)(2,1)S(1)}, bf16[264,1152]{1,0:T(8,128)(2,1)S(1)}, u32[]{:S(2)}, u32[]{:S(2)}) collective-permute-start(bf16[264,1152]{1,0:T(8,128)(2,1)S(1)} %pad_maximum_fusion.1), channel_id=1, source_target_pairs={{0,2},{1,3},{2,0},{3,1},{4,6},{5,7},{6,4},{7,5},{8,10},{9,11},{10,... | collective-permute-start | bytes 1824776 | tf_op jit(solution)/shard_map/ppermute | solution.py:425
  52.3 3.9 %collective-permute-start.14 = (bf16[256,1792]{1,0:T(8,128)(2,1)S(1)}, bf16[256,1792]{1,0:T(8,128)(2,1)S(1)}, u32[]{:S(2)}, u32[]{:S(2)}) collective-permute-start(bf16[256,1792]{1,0:T(8,128)(2,1)S(1)} %get-tuple-element.106), channel_id=1, source_target_pairs={{0,2},{1,3},{2,0},{3,1},{4,6},{5,7},{6,4},{7,5},{8,10},{9,11},{10,... | collective-permute-start | bytes 2752520 | tf_op jit(solution)/shard_map/ppermute | solution.py:425
  53.1 8.0 %collective-permute-start.12 = (bf16[136,1152]{1,0:T(8,128)(2,1)S(1)}, bf16[136,1152]{1,0:T(8,128)(2,1)S(1)}, u32[]{:S(2)}, u32[]{:S(2)}) collective-permute-start(bf16[136,1152]{1,0:T(8,128)(2,1)S(1)} %pad_maximum_fusion.5), channel_id=1, source_target_pairs={{0,1},{1,0},{2,6},{3,7},{4,5},{5,4},{6,2},{7,3},{8,9},{9,8},{10,14... | collective-permute-start | bytes 940040 | tf_op jit(solution)/shard_map/ppermute | solution.py:425
  56.1 1.6 %collective-permute-start.13 = (bf16[256,384]{1,0:T(8,128)(2,1)S(1)}, bf16[256,384]{1,0:T(8,128)(2,1)S(1)}, u32[]{:S(2)}, u32[]{:S(2)}) collective-permute-start(bf16[256,384]{1,0:T(8,128)(2,1)S(1)} %get-tuple-element.112), channel_id=1, source_target_pairs={{0,2},{1,3},{2,0},{3,1},{4,6},{5,7},{6,4},{7,5},{8,10},{9,11},{10,... | collective-permute-start | bytes 589832 | tf_op jit(solution)/shard_map/ppermute | solution.py:425
  56.5 11.4 %collective-permute-start.16 = (bf16[128,1792]{1,0:T(8,128)(2,1)S(1)}, bf16[128,1792]{1,0:T(8,128)(2,1)S(1)}, u32[]{:S(2)}, u32[]{:S(2)}) collective-permute-start(bf16[128,1792]{1,0:T(8,128)(2,1)S(1)} %slice.294), channel_id=1, source_target_pairs={{0,1},{1,0},{2,6},{3,7},{4,5},{5,4},{6,2},{7,3},{8,9},{9,8},{10,14... | collective-permute-start | bytes 1376264 | tf_op jit(solution)/shard_map/ppermute | solution.py:425
  57.8 10.0 %collective-permute-start.17 = (bf16[128,384]{1,0:T(8,128)(2,1)S(1)}, bf16[128,384]{1,0:T(8,128)(2,1)S(1)}, u32[]{:S(2)}, u32[]{:S(2)}) collective-permute-start(bf16[128,384]{1,0:T(8,128)(2,1)S(1)} %slice.299), channel_id=1, source_target_pairs={{0,1},{1,0},{2,6},{3,7},{4,5},{5,4},{6,2},{7,3},{8,9},{9,8},{10,14... | collective-permute-start | bytes 294920 | tf_op jit(solution)/shard_map/ppermute | solution.py:425
  61.2 6.7 %collective-permute-start.15 = (bf16[72,1152]{1,0:T(8,128)(2,1)S(1)}, bf16[72,1152]{1,0:T(8,128)(2,1)S(1)}, u32[]{:S(2)}, u32[]{:S(2)}) collective-permute-start(bf16[72,1152]{1,0:T(8,128)(2,1)S(1)} %pad_maximum_fusion.7), channel_id=1, source_target_pairs={{0,4},{1,5},{2,3},{3,2},{4,0},{5,1},{6,7},{7,6},{8,12},{9,13},{10,... | collective-permute-start | bytes 497672 | tf_op jit(solution)/shard_map/ppermute | solution.py:425
  68.1 6.6 %collective-permute-start.19 = (bf16[64,2176]{1,0:T(8,128)(2,1)S(1)}, bf16[64,2176]{1,0:T(8,128)(2,1)S(1)}, u32[]{:S(2)}, u32[]{:S(2)}) collective-permute-start(bf16[64,2176]{1,0:T(8,128)(2,1)S(1)} %slice.296), channel_id=1, source_target_pairs={{0,4},{1,5},{2,3},{3,2},{4,0},{5,1},{6,7},{7,6},{8,12},{9,13},{10,... | collective-permute-start | bytes 835592 | tf_op jit(solution)/shard_map/ppermute | solution.py:425
  69.6 4.6 %collective-permute-start.18 = (bf16[40,1152]{1,0:T(8,128)(2,1)S(1)}, bf16[40,1152]{1,0:T(8,128)(2,1)S(1)}, u32[]{:S(2)}, u32[]{:S(2)}) collective-permute-start(bf16[40,1152]{1,0:T(8,128)(2,1)S(1)} %pad_maximum_fusion.10), channel_id=1, source_target_pairs={{0,8},{1,9},{2,10},{3,11},{4,12},{5,13},{6,14},{7,15},{8,0},{9,1},... | collective-permute-start | bytes 276488 | tf_op jit(solution)/shard_map/ppermute | solution.py:425
  71.4 13.0 %collective-permute-start.21 = (bf16[512,256]{1,0:T(8,128)(2,1)S(1)}, bf16[512,256]{1,0:T(8,128)(2,1)S(1)}, u32[]{:S(2)}, u32[]{:S(2)}) collective-permute-start(bf16[512,256]{1,0:T(8,128)(2,1)S(1)} %get-tuple-element.130), channel_id=1, source_target_pairs={{0,1},{1,0},{2,3},{3,2},{4,5},{5,4},{6,7},{7,6},{8,9},{9,8},{10,11... | collective-permute-start | bytes 786440 | tf_op jit(solution)/shard_map/ppermute | solution.py:541
  74.9 7.4 %collective-permute-start.23 = (bf16[32,2176]{1,0:T(8,128)(2,1)S(1)}, bf16[32,2176]{1,0:T(8,128)(2,1)S(1)}, u32[]{:S(2)}, u32[]{:S(2)}) collective-permute-start(bf16[32,2176]{1,0:T(8,128)(2,1)S(1)} %slice.298), channel_id=1, source_target_pairs={{0,8},{1,9},{2,10},{3,11},{4,12},{5,13},{6,14},{7,15},{8,0},{9,1},... | collective-permute-start | bytes 417800 | tf_op jit(solution)/shard_map/ppermute | solution.py:425
  77.1 5.2 %collective-permute-start.20 = (bf16[24,1152]{1,0:T(8,128)(2,1)S(1)}, bf16[24,1152]{1,0:T(8,128)(2,1)S(1)}, u32[]{:S(2)}, u32[]{:S(2)}) collective-permute-start(bf16[24,1152]{1,0:T(8,128)(2,1)S(1)} %pad_maximum_fusion.12), channel_id=1, source_target_pairs={{0,16},{1,17},{2,18},{3,19},{4,20},{5,21},{6,22},{7,23},{8,24},{9,... | collective-permute-start | bytes 165896 | tf_op jit(solution)/shard_map/ppermute | solution.py:425
  78.1 6.9 %collective-permute-start.22 = (bf16[512,256]{1,0:T(8,128)(2,1)S(1)}, bf16[512,256]{1,0:T(8,128)(2,1)S(1)}, u32[]{:S(2)}, u32[]{:S(2)}) collective-permute-start(bf16[512,256]{1,0:T(8,128)(2,1)S(1)} %get-tuple-element.131), channel_id=1, source_target_pairs={{0,1},{1,0},{2,3},{3,2},{4,5},{5,4},{6,7},{7,6},{8,9},{9,8},{10,11... | collective-permute-start | bytes 786440 | tf_op jit(solution)/shard_map/ppermute | solution.py:541
  82.4 5.4 %collective-permute-start.24 = (bf16[16,2176]{1,0:T(8,128)(2,1)S(1)}, bf16[16,2176]{1,0:T(8,128)(2,1)S(1)}, u32[]{:S(2)}, u32[]{:S(2)}) collective-permute-start(bf16[16,2176]{1,0:T(8,128)(2,1)S(1)} %slice.301), channel_id=1, source_target_pairs={{0,16},{1,17},{2,18},{3,19},{4,20},{5,21},{6,22},{7,23},{8,24},{9,... | collective-permute-start | bytes 208904 | tf_op jit(solution)/shard_map/ppermute | solution.py:425
  84.3 3.5 %copy-start.2 = (f32[16,2048]{1,0:T(8,128)S(1)}, f32[16,2048]{1,0:T(8,128)}, u32[]{:S(2)}) copy-start(f32[16,2048]{1,0:T(8,128)} %refs_0_.1) | copy-start | bytes 393220
  84.3 3.5 %copy-start.4 = (f32[16,2048]{1,0:T(8,128)S(1)}, f32[16,2048]{1,0:T(8,128)}, u32[]{:S(2)}) copy-start(f32[16,2048]{1,0:T(8,128)} %refs_5_.1) | copy-start | bytes 393220
  84.3 3.5 %copy-start.5 = (f32[16,2048]{1,0:T(8,128)S(1)}, f32[16,2048]{1,0:T(8,128)}, u32[]{:S(2)}) copy-start(f32[16,2048]{1,0:T(8,128)} %refs_10_.1) | copy-start | bytes 393220
  84.3 3.5 %copy-start.6 = (f32[8,8,256]{2,1,0:T(8,128)S(1)}, f32[8,8,256]{2,1,0:T(8,128)}, u32[]{:S(2)}) copy-start(f32[8,8,256]{2,1,0:T(8,128)} %refs_7_.1) | copy-start | bytes 196612
  84.3 3.5 %copy-start.7 = (f32[8,8,256]{2,1,0:T(8,128)S(1)}, f32[8,8,256]{2,1,0:T(8,128)}, u32[]{:S(2)}) copy-start(f32[8,8,256]{2,1,0:T(8,128)} %refs_12_.1) | copy-start | bytes 196612
  84.3 3.5 %copy-start.9 = (f32[16,16]{1,0:T(8,128)S(1)}, f32[16,16]{1,0:T(8,128)}, u32[]{:S(2)}) copy-start(f32[16,16]{1,0:T(8,128)} %refs_1_.1) | copy-start | bytes 3076
  84.3 3.5 %copy-start.14 = (f32[16,16]{1,0:T(8,128)S(1)}, f32[16,16]{1,0:T(8,128)}, u32[]{:S(2)}) copy-start(f32[16,16]{1,0:T(8,128)} %refs_6_.1) | copy-start | bytes 3076
  84.3 3.5 %copy-start.15 = (f32[2,8,128]{2,1,0:T(8,128)S(1)}, f32[2,8,128]{2,1,0:T(8,128)}, u32[]{:S(2)}) copy-start(f32[2,8,128]{2,1,0:T(8,128)} %refs_8_.1) | copy-start | bytes 24580
  84.3 3.5 %copy-start.16 = (f32[16,16]{1,0:T(8,128)S(1)}, f32[16,16]{1,0:T(8,128)}, u32[]{:S(2)}) copy-start(f32[16,16]{1,0:T(8,128)} %refs_11_.1) | copy-start | bytes 3076
  84.3 3.5 %copy-start.17 = (f32[2,8,128]{2,1,0:T(8,128)S(1)}, f32[2,8,128]{2,1,0:T(8,128)}, u32[]{:S(2)}) copy-start(f32[2,8,128]{2,1,0:T(8,128)} %refs_13_.1) | copy-start | bytes 24580
  84.3 3.5 %copy-start.19 = (f32[2,128]{1,0:T(2,128)S(1)}, f32[2,128]{1,0:T(2,128)}, u32[]{:S(2)}) copy-start(f32[2,128]{1,0:T(2,128)} %refs_9_.1) | copy-start | bytes 3076
  84.4 3.5 %copy-start.20 = (f32[2,128]{1,0:T(2,128)S(1)}, f32[2,128]{1,0:T(2,128)}, u32[]{:S(2)}) copy-start(f32[2,128]{1,0:T(2,128)} %refs_14_.1) | copy-start | bytes 3076

commit v6 on v5

--- a/solution.py
+++ b/solution.py
@@ -446,7 +446,7 @@
         got_b = cube.swap(block_b, cube.order[at - 1])
         if at + 1 == len(cube.order):
             got_a = after(got_a, x[0])
-        block_a = jnp.concatenate([block_a, after(got_a, got_b)], axis=0)
+        block_a = jnp.concatenate([block_a, after(got_a, got_b if at > 1 else block_b)], axis=0)
         block_b = jnp.concatenate([block_b, after(got_b, block_a)], axis=0)
     oth_a = cube.swap(block_a, cube.core)
     return block_a, oth_a, block_b, cube.swap(block_b, cube.order[-1]), x

time: 89.2 us -> 88 us (0.987)
  waiting for transfers between devices: 25.9 us -> 24 us
    ppermute x22, waiting for transfers between devices: 25.2 us -> 22.9 us  [swap(): return lax.ppermute(values, both, self.pairs(step))]
    ppermute x22, starting transfers between devices: 30.6 us -> 31.7 us  [swap(): return lax.ppermute(values, both, self.pairs(step))]
  transfers between devices with their start and end apart: 25 -> 25, of which waited for: 14 -> 13; matrix products, arithmetic and copies ran while one was open for 3% -> 3% of each run, Pallas kernels for 19% -> 19%
where the time goes in v6:
time: 88 us; the launch traced here: 87.8 us
  starting transfers between devices  36 us (41%)
  waiting for transfers between devices  24 us (27%)
  Pallas kernels  21.6 us (25%)
  local copies, waits for them, and re-layouts  3.64 us (4%)
  between operations  1.42 us (2%)
  other arithmetic  1.21 us (1%)
    ppermute x22, starting transfers between devices, swap(): return lax.ppermute(values, both, self.pairs(step))  31.7 us
    ppermute x22, waiting for transfers between devices, swap(): return lax.ppermute(values, both, self.pairs(step))  22.9 us
    pallas_call x2, Pallas kernels, input_part(): pl.pallas_call(input_kernel, grid_spec=pltpu.PrefetchScalarGridSpec(num_s...  4.65 us
    pallas_call x1, Pallas kernels, on_device(): pl.pallas_call(functools.partial(first_kernel, places), out_shape=[shape(...  4.41 us
    ppermute x3, starting transfers between devices, swap_field(): return lax.ppermute(values, 'field', [(0, 1), (1, 0)])  4.2 us
    pallas_call x1, Pallas kernels, on_device(): pl.pallas_call(functools.partial(second_kernel, places), out_shape=[shape...  4.11 us
    pallas_call x1, Pallas kernels, on_device(): pl.pallas_call(functools.partial(back_first_kernel, places, range(cut)),...  3.76 us
    unnamed x50, local copies, waits for them, and re-layouts  1.78 us
  transfers between devices with their start and end apart: 25, of which 13 were waited for; matrix products, arithmetic and copies ran while one was open for 3% of the time, Pallas kernels for 19%

profile of v6, /device:TPU:0, one launch (start us, length us, event | category | flops | bytes accessed | tf_op | source)
XLA Modules:
  0.0 87.8 jit_solution(8601578979705548362)
XLA Ops:
  0.7 0.9 %copy-done.1 = f32[16,2048]{1,0:T(8,128)S(1)} copy-done((f32[16,2048]{1,0:T(8,128)S(1)}, f32[16,2048]{1,0:T(8,128)}, u32[]{:S(2)}) %copy-start.1) | copy-done | bytes 131096
  1.6 0.7 copy-done.8
  2.3 4.1 %collective-permute-start = (bf16[16,2176]{1,0:T(8,128)(2,1)S(1)}, bf16[16,2176]{1,0:T(8,128)(2,1)S(1)}, u32[]{:S(2)}, u32[]{:S(2)}) collective-permute-start(bf16[16,2176]{1,0:T(8,128)(2,1)S(1)} %pack_a.1), channel_id=1, source_target_pairs={{0,16},{1,17},{2,18},{3,19},{4,20},{5,21},{6,22},{7,23},{8,24},{9,... | collective-permute-start | bytes 208904 | tf_op jit(solution)/shard_map/ppermute | solution.py:425
  6.4 1.1 %constant_dynamic-slice_fusion = bf16[4,256,256]{2,1,0:T(8,128)(2,1)S(1)} fusion(bf16[4,512,256]{2,1,0:T(8,128)(2,1)} %in_ref.1, s32[]{:T(128)S(6)} %select_n.3), kind=kLoop, calls=%fused_computation.86 | loop fusion | bytes 1048580 | tf_op jit(solution)/shard_map/dynamic_slice | solution.py:544
  7.5 1.6 %collective-permute-start.7 = (bf16[1024,256]{1,0:T(8,128)(2,1)S(1)}, bf16[1024,256]{1,0:T(8,128)(2,1)S(1)}, u32[]{:S(2)}, u32[]{:S(2)}) collective-permute-start(bf16[1024,256]{1,0:T(8,128)(2,1)S(1)} %bitcast.3), channel_id=1, source_target_pairs={{0,1},{1,0},{2,3},{3,2},{4,5},{5,4},{6,7},{7,6},{8,9},{9,8},{10,11... | collective-permute-start | bytes 1572872 | tf_op jit(solution)/shard_map/ppermute | solution.py:541
  9.1 1.1 %collective-permute-done = bf16[16,2176]{1,0:T(8,128)(2,1)S(1)} collective-permute-done((bf16[16,2176]{1,0:T(8,128)(2,1)S(1)}, bf16[16,2176]{1,0:T(8,128)(2,1)S(1)}, u32[]{:S(2)}, u32[]{:S(2)}) %collective-permute-start) | collective-permute-done | bytes 69664 | tf_op jit(solution)/shard_map/ppermute | solution.py:425
  10.2 0.7 collective-permute-start.2
  11.0 3.4 %collective-permute-start.1 = (bf16[16,1280]{1,0:T(8,128)(2,1)S(1)}, bf16[16,1280]{1,0:T(8,128)(2,1)S(1)}, u32[]{:S(2)}, u32[]{:S(2)}) collective-permute-start(bf16[16,1280]{1,0:T(8,128)(2,1)S(1)} %pack_b.1), channel_id=1, source_target_pairs={{0,16},{1,17},{2,18},{3,19},{4,20},{5,21},{6,22},{7,23},{8,24},{9,... | collective-permute-start | bytes 122888 | tf_op jit(solution)/shard_map/ppermute | solution.py:425
  14.4 1.3 %collective-permute-done.2 = bf16[32,2176]{1,0:T(8,128)(2,1)S(1)} collective-permute-done((bf16[32,2176]{1,0:T(8,128)(2,1)S(1)}, bf16[32,2176]{1,0:T(8,128)(2,1)S(1)}, u32[]{:S(2)}, u32[]{:S(2)}) %collective-permute-start.2) | collective-permute-done | bytes 139296 | tf_op jit(solution)/shard_map/ppermute | solution.py:425
  15.8 1.8 %collective-permute-start.4 = (bf16[64,2176]{1,0:T(8,128)(2,1)S(1)}, bf16[64,2176]{1,0:T(8,128)(2,1)S(1)}, u32[]{:S(2)}, u32[]{:S(2)}) collective-permute-start(bf16[64,2176]{1,0:T(8,128)(2,1)S(1)} %pad_maximum_fusion.6), channel_id=1, source_target_pairs={{0,4},{1,5},{2,3},{3,2},{4,0},{5,1},{6,7},{7,6},{8,12},{9,13},{10,... | collective-permute-start | bytes 835592 | tf_op jit(solution)/shard_map/ppermute | solution.py:425
  17.6 1.2 %collective-permute-start.3 = (bf16[32,1280]{1,0:T(8,128)(2,1)S(1)}, bf16[32,1280]{1,0:T(8,128)(2,1)S(1)}, u32[]{:S(2)}, u32[]{:S(2)}) collective-permute-start(bf16[32,1280]{1,0:T(8,128)(2,1)S(1)} %pad_maximum_fusion.11), channel_id=1, source_target_pairs={{0,8},{1,9},{2,10},{3,11},{4,12},{5,13},{6,14},{7,15},{8,0},{9,1},... | collective-permute-start | bytes 245768 | tf_op jit(solution)/shard_map/ppermute | solution.py:425
  18.8 3.3 %collective-permute-done.3 = bf16[32,1280]{1,0:T(8,128)(2,1)S(1)} collective-permute-done((bf16[32,1280]{1,0:T(8,128)(2,1)S(1)}, bf16[32,1280]{1,0:T(8,128)(2,1)S(1)}, u32[]{:S(2)}, u32[]{:S(2)}) %collective-permute-start.3) | collective-permute-done | bytes 81952 | tf_op jit(solution)/shard_map/ppermute | solution.py:425
  22.1 0.3 collective-permute-done.4
  22.4 1.8 %collective-permute-start.6 = (bf16[128,2176]{1,0:T(8,128)(2,1)S(1)}, bf16[128,2176]{1,0:T(8,128)(2,1)S(1)}, u32[]{:S(2)}, u32[]{:S(2)}) collective-permute-start(bf16[128,2176]{1,0:T(8,128)(2,1)S(1)} %pad_maximum_fusion.2), channel_id=1, source_target_pairs={{0,1},{1,0},{2,6},{3,7},{4,5},{5,4},{6,2},{7,3},{8,9},{9,8},{10,14... | collective-permute-start | bytes 1671176 | tf_op jit(solution)/shard_map/ppermute | solution.py:425
  24.2 1.6 %collective-permute-start.5 = (bf16[64,1280]{1,0:T(8,128)(2,1)S(1)}, bf16[64,1280]{1,0:T(8,128)(2,1)S(1)}, u32[]{:S(2)}, u32[]{:S(2)}) collective-permute-start(bf16[64,1280]{1,0:T(8,128)(2,1)S(1)} %pad_maximum_fusion.8), channel_id=1, source_target_pairs={{0,4},{1,5},{2,3},{3,2},{4,0},{5,1},{6,7},{7,6},{8,12},{9,13},{10,... | collective-permute-start | bytes 491528 | tf_op jit(solution)/shard_map/ppermute | solution.py:425
  25.9 0.6 rows.1
  26.4 7.4 %collective-permute-done.6 = bf16[128,2176]{1,0:T(8,128)(2,1)S(1)} collective-permute-done((bf16[128,2176]{1,0:T(8,128)(2,1)S(1)}, bf16[128,2176]{1,0:T(8,128)(2,1)S(1)}, u32[]{:S(2)}, u32[]{:S(2)}) %collective-permute-start.6) | collective-permute-done | bytes 557088 | tf_op jit(solution)/shard_map/ppermute | solution.py:425
  33.9 0.2 collective-permute-start.9
  34.2 1.7 %collective-permute-start.8 = (bf16[128,1280]{1,0:T(8,128)(2,1)S(1)}, bf16[128,1280]{1,0:T(8,128)(2,1)S(1)}, u32[]{:S(2)}, u32[]{:S(2)}) collective-permute-start(bf16[128,1280]{1,0:T(8,128)(2,1)S(1)} %pad_maximum_fusion.4), channel_id=1, source_target_pairs={{0,1},{1,0},{2,6},{3,7},{4,5},{5,4},{6,2},{7,3},{8,9},{9,8},{10,14... | collective-permute-start | bytes 983048 | tf_op jit(solution)/shard_map/ppermute | solution.py:425
  35.9 0.8 collective-permute-done.9.oth_ref
  36.7 4.4 %first.1 = (bf16[1024,2048]{1,0:T(8,128)(2,1)S(1)}, bf16[1024,2048]{1,0:T(8,128)(2,1)S(1)}, f32[1024,16]{1,0:T(8,128)S(1)}, bf16[512,2176]{1,0:T(8,128)(2,1)S(1)}) custom-call(bf16[256,2176]{1,0:T(8,128)(2,1)S(1)} %constant_dynamic-update-slice_fusion.own_ref, bf16[256,2176]{1,0:T(8,128)(2,1)S(1)} %collective-permute-done.9.oth_ref, ...), custom_call_target="tpu_custom_call" | custom-call | flops 4563402752 | bytes 8388608 | tf_op jit(solution)/shard_map/first/pallas_call | solution.py:593
  41.4 2.1 %collective-permute-done.10.oth_ref = bf16[256,1280]{1,0:T(8,128)(2,1)S(1)} collective-permute-done((bf16[256,1280]{1,0:T(8,128)(2,1)S(1)}, bf16[256,1280]{1,0:T(8,128)(2,1)S(1)}, u32[]{:S(2)}, u32[]{:S(2)}) %collective-permute-start.10) | collective-permute-done | bytes 655392 | tf_op jit(solution)/shard_map/ppermute | solution.py:425
  43.5 4.1 %second.1 = (bf16[2048,256]{1,0:T(8,128)(2,1)S(1)}, bf16[1024,256]{1,0:T(8,128)(2,1)S(1)}, f32[8,1152]{1,0:T(8,128)S(1)}, f32[256,1152]{1,0:T(8,128)S(1)}, bf16[256,1152]{1,0:T(8,128)(2,1)S(1)}) custom-call(bf16[256,1280]{1,0:T(8,128)(2,1)S(1)} %constant_dynamic-update-slice_fusion.5.own_ref, bf16[256,1280]{1,0:T(8,128)(2,1)S(1)} %collective-permute-done.10.oth_ref, ...), custom_call_target="tpu_custom_call" | custom-call | tf_op jit(solution)/shard_map/second/pallas_call | solution.py:611
  47.7 0.2 collective-permute-start.11
  47.9 3.8 %back_first.1 = (bf16[1024,1792]{1,0:T(8,128)(2,1)S(1)}, f32[256,1792]{1,0:T(8,128)S(1)}, bf16[256,1792]{1,0:T(8,128)(2,1)S(1)}, f32[1024,16]{1,0:T(8,128)S(1)}) custom-call(bf16[2048,256]{1,0:T(8,128)(2,1)S(1)} %get-tuple-element.103.w_ref, bf16[1024,256]{1,0:T(8,128)(2,1)S(1)} %get-tuple-element.104.dm_ref, ...), custom_call_target="tpu_custom_call" | custom-call | tf_op jit(solution)/shard_map/back_first/pallas_call | solution.py:637
  51.7 0.4 collective-permute-start.14
  52.4 1.7 %collective-permute-start.12 = (bf16[136,1152]{1,0:T(8,128)(2,1)S(1)}, bf16[136,1152]{1,0:T(8,128)(2,1)S(1)}, u32[]{:S(2)}, u32[]{:S(2)}) collective-permute-start(bf16[136,1152]{1,0:T(8,128)(2,1)S(1)} %pad_maximum_fusion.5), channel_id=1, source_target_pairs={{0,1},{1,0},{2,6},{3,7},{4,5},{5,4},{6,2},{7,3},{8,9},{9,8},{10,14... | collective-permute-start | bytes 940040 | tf_op jit(solution)/shard_map/ppermute | solution.py:425
  54.2 1.5 %back_last.1 = (bf16[1024,256]{1,0:T(8,128)(2,1)S(1)}, f32[256,384]{1,0:T(8,128)S(1)}, bf16[256,384]{1,0:T(8,128)(2,1)S(1)}, bf16[1024,128]{1,0:T(8,128)(2,1)S(1)}) custom-call(bf16[2048,256]{1,0:T(8,128)(2,1)S(1)} %get-tuple-element.103.w_ref, bf16[1024,256]{1,0:T(8,128)(2,1)S(1)} %get-tuple-element.104.dm_ref, ...), custom_call_target="tpu_custom_call" | custom-call | tf_op jit(solution)/shard_map/back_last/pallas_call | solution.py:654
  56.0 1.4 %collective-permute-start.16 = (bf16[128,1792]{1,0:T(8,128)(2,1)S(1)}, bf16[128,1792]{1,0:T(8,128)(2,1)S(1)}, u32[]{:S(2)}, u32[]{:S(2)}) collective-permute-start(bf16[128,1792]{1,0:T(8,128)(2,1)S(1)} %slice.294), channel_id=1, source_target_pairs={{0,1},{1,0},{2,6},{3,7},{4,5},{5,4},{6,2},{7,3},{8,9},{9,8},{10,14... | collective-permute-start | bytes 1376264 | tf_op jit(solution)/shard_map/ppermute | solution.py:425
  57.4 0.8 collective-permute-start.17
  58.2 2.3 %input.2 = (f32[4,512,256]{2,1,0:T(8,128)}, bf16[512,256]{1,0:T(8,128)(2,1)S(1)}) custom-call(s32[1]{0:T(128)} %bitcast.1.at, bf16[1024,1792]{1,0:T(8,128)(2,1)S(1)} %get-tuple-element.117.low_ref, bf16[1024,256]{1,0:T(8,128)(2,1)S(1)} %get-tuple-element.118.high_ref, bf16[1024,128]{1,0:T(8,128)(2,1)S(1)} %get-tuple-element.122.dg_ref, ...), custom_call_target="tpu_custom_call" | custom-call | tf_op jit(solution)/shard_map/input/pallas_call | solution.py:678
  60.8 1.5 %collective-permute-start.15 = (bf16[72,1152]{1,0:T(8,128)(2,1)S(1)}, bf16[72,1152]{1,0:T(8,128)(2,1)S(1)}, u32[]{:S(2)}, u32[]{:S(2)}) collective-permute-start(bf16[72,1152]{1,0:T(8,128)(2,1)S(1)} %pad_maximum_fusion.7), channel_id=1, source_target_pairs={{0,4},{1,5},{2,3},{3,2},{4,0},{5,1},{6,7},{7,6},{8,12},{9,13},{10,... | collective-permute-start | bytes 497672 | tf_op jit(solution)/shard_map/ppermute | solution.py:425
  62.3 2.3 %input.3 = (f32[4,512,256]{2,1,0:T(8,128)}, bf16[512,256]{1,0:T(8,128)(2,1)S(1)}) custom-call(s32[1]{0:T(128)} %bitcast.1.at, bf16[1024,1792]{1,0:T(8,128)(2,1)S(1)} %get-tuple-element.117.low_ref, bf16[1024,256]{1,0:T(8,128)(2,1)S(1)} %get-tuple-element.118.high_ref, ...), custom_call_target="tpu_custom_call", output_to_operand_aliasing={{0}: (5, {})} | custom-call | tf_op jit(solution)/shard_map/input/pallas_call | solution.py:678
  64.6 2.7 %collective-permute-done.17 = bf16[128,384]{1,0:T(8,128)(2,1)S(1)} collective-permute-done((bf16[128,384]{1,0:T(8,128)(2,1)S(1)}, bf16[128,384]{1,0:T(8,128)(2,1)S(1)}, u32[]{:S(2)}, u32[]{:S(2)}) %collective-permute-start.17) | collective-permute-done | bytes 98336 | tf_op jit(solution)/shard_map/ppermute | solution.py:425
  67.5 1.6 %collective-permute-start.19 = (bf16[64,2176]{1,0:T(8,128)(2,1)S(1)}, bf16[64,2176]{1,0:T(8,128)(2,1)S(1)}, u32[]{:S(2)}, u32[]{:S(2)}) collective-permute-start(bf16[64,2176]{1,0:T(8,128)(2,1)S(1)} %slice.296), channel_id=1, source_target_pairs={{0,4},{1,5},{2,3},{3,2},{4,0},{5,1},{6,7},{7,6},{8,12},{9,13},{10,... | collective-permute-start | bytes 835592 | tf_op jit(solution)/shard_map/ppermute | solution.py:425
  69.2 1.5 %collective-permute-start.18 = (bf16[40,1152]{1,0:T(8,128)(2,1)S(1)}, bf16[40,1152]{1,0:T(8,128)(2,1)S(1)}, u32[]{:S(2)}, u32[]{:S(2)}) collective-permute-start(bf16[40,1152]{1,0:T(8,128)(2,1)S(1)} %pad_maximum_fusion.10), channel_id=1, source_target_pairs={{0,8},{1,9},{2,10},{3,11},{4,12},{5,13},{6,14},{7,15},{8,0},{9,1},... | collective-permute-start | bytes 276488 | tf_op jit(solution)/shard_map/ppermute | solution.py:425
  70.7 1.1 %collective-permute-start.21 = (bf16[512,256]{1,0:T(8,128)(2,1)S(1)}, bf16[512,256]{1,0:T(8,128)(2,1)S(1)}, u32[]{:S(2)}, u32[]{:S(2)}) collective-permute-start(bf16[512,256]{1,0:T(8,128)(2,1)S(1)} %get-tuple-element.130), channel_id=1, source_target_pairs={{0,1},{1,0},{2,3},{3,2},{4,5},{5,4},{6,7},{7,6},{8,9},{9,8},{10,11... | collective-permute-start | bytes 786440 | tf_op jit(solution)/shard_map/ppermute | solution.py:541
  71.8 2.1 %collective-permute-done.18 = bf16[40,1152]{1,0:T(8,128)(2,1)S(1)} collective-permute-done((bf16[40,1152]{1,0:T(8,128)(2,1)S(1)}, bf16[40,1152]{1,0:T(8,128)(2,1)S(1)}, u32[]{:S(2)}, u32[]{:S(2)}) %collective-permute-start.18) | collective-permute-done | bytes 92192 | tf_op jit(solution)/shard_map/ppermute | solution.py:425
  73.8 0.3 collective-permute-done.19
  74.3 1.6 %collective-permute-start.23 = (bf16[32,2176]{1,0:T(8,128)(2,1)S(1)}, bf16[32,2176]{1,0:T(8,128)(2,1)S(1)}, u32[]{:S(2)}, u32[]{:S(2)}) collective-permute-start(bf16[32,2176]{1,0:T(8,128)(2,1)S(1)} %slice.298), channel_id=1, source_target_pairs={{0,8},{1,9},{2,10},{3,11},{4,12},{5,13},{6,14},{7,15},{8,0},{9,1},... | collective-permute-start | bytes 417800 | tf_op jit(solution)/shard_map/ppermute | solution.py:425
  75.9 2.2 %collective-permute-start.20 = (bf16[24,1152]{1,0:T(8,128)(2,1)S(1)}, bf16[24,1152]{1,0:T(8,128)(2,1)S(1)}, u32[]{:S(2)}, u32[]{:S(2)}) collective-permute-start(bf16[24,1152]{1,0:T(8,128)(2,1)S(1)} %pad_maximum_fusion.12), channel_id=1, source_target_pairs={{0,16},{1,17},{2,18},{3,19},{4,20},{5,21},{6,22},{7,23},{8,24},{9,... | collective-permute-start | bytes 165896 | tf_op jit(solution)/shard_map/ppermute | solution.py:425
  78.1 1.6 %collective-permute-start.22 = (bf16[512,256]{1,0:T(8,128)(2,1)S(1)}, bf16[512,256]{1,0:T(8,128)(2,1)S(1)}, u32[]{:S(2)}, u32[]{:S(2)}) collective-permute-start(bf16[512,256]{1,0:T(8,128)(2,1)S(1)} %get-tuple-element.131), channel_id=1, source_target_pairs={{0,1},{1,0},{2,3},{3,2},{4,5},{5,4},{6,7},{7,6},{8,9},{9,8},{10,11... | collective-permute-start | bytes 786440 | tf_op jit(solution)/shard_map/ppermute | solution.py:541
  79.7 1.4 %collective-permute-done.20.got_b = bf16[24,1152]{1,0:T(8,128)(2,1)S(1)} collective-permute-done((bf16[24,1152]{1,0:T(8,128)(2,1)S(1)}, bf16[24,1152]{1,0:T(8,128)(2,1)S(1)}, u32[]{:S(2)}, u32[]{:S(2)}) %collective-permute-start.20) | collective-permute-done | bytes 55328 | tf_op jit(solution)/shard_map/ppermute | solution.py:425
  81.1 2.2 %collective-permute-start.24 = (bf16[16,2176]{1,0:T(8,128)(2,1)S(1)}, bf16[16,2176]{1,0:T(8,128)(2,1)S(1)}, u32[]{:S(2)}, u32[]{:S(2)}) collective-permute-start(bf16[16,2176]{1,0:T(8,128)(2,1)S(1)} %slice.301), channel_id=1, source_target_pairs={{0,16},{1,17},{2,18},{3,19},{4,20},{5,21},{6,22},{7,23},{8,24},{9,... | collective-permute-start | bytes 208904 | tf_op jit(solution)/shard_map/ppermute | solution.py:425
  83.3 0.5 slice.226
  83.9 1.1 %collective-permute-done.22.late_ref = bf16[512,256]{1,0:T(8,128)(2,1)S(1)} collective-permute-done((bf16[512,256]{1,0:T(8,128)(2,1)S(1)}, bf16[512,256]{1,0:T(8,128)(2,1)S(1)}, u32[]{:S(2)}, u32[]{:S(2)}) %collective-permute-start.22) | collective-permute-done | bytes 262176 | tf_op jit(solution)/shard_map/ppermute | solution.py:541
  85.1 1.5 %place.1 = f32[4,512,256]{2,1,0:T(8,128)} custom-call(s32[1]{0:T(128)} %bitcast.1.at, bf16[512,256]{1,0:T(8,128)(2,1)S(1)} %collective-permute-done.21.early_ref, bf16[512,256]{1,0:T(8,128)(2,1)S(1)} %collective-permute-done.22.late_ref, f32[4,512,256]{2,1,0:T(8,128)} %get-tuple-element.134.held_ref), custom_call_target="tpu_custom_call", output_to_operand_aliasing={{}: (3, {})} | custom-call | tf_op jit(solution)/shard_map/place/pallas_call | solution.py:737
  86.7 0.9 %update.1 = (f32[16,2048]{1,0:T(8,128)}, f32[16,2048]{1,0:T(8,128)}, f32[16,2048]{1,0:T(8,128)}, f32[16,16]{1,0:T(8,128)}, f32[16,16]{1,0:T(8,128)}, /*index=5*/...) custom-call(f32[32,2176]{1,0:T(8,128)S(1)} %slice_add_fusion.3.sum_a, ...), custom_call_target="tpu_custom_call" | custom-call | tf_op jit(solution)/shard_map/update/pallas_call | solution.py:751
  (117 shorter events, 2.2 us)
Async XLA Ops:
  0.7 0.9 %copy-start.1 = (f32[16,2048]{1,0:T(8,128)S(1)}, f32[16,2048]{1,0:T(8,128)}, u32[]{:S(2)}) copy-start(f32[16,2048]{1,0:T(8,128)} %refs_0_.1) | copy-start | bytes 393220
  1.6 0.7 copy-start.8
  2.3 8.6 %copy-start.3 = (f32[8,8,256]{2,1,0:T(8,128)S(1)}, f32[8,8,256]{2,1,0:T(8,128)}, u32[]{:S(2)}) copy-start(f32[8,8,256]{2,1,0:T(8,128)} %refs_2_.1) | copy-start | bytes 196612
  2.3 8.6 %copy-start.10 = (s32[4,512]{1,0:T(4,128)S(1)}, s32[4,512]{1,0:T(4,128)}, u32[]{:S(2)}) copy-start(s32[4,512]{1,0:T(4,128)} %valid_ref.2) | copy-start | bytes 24580
  2.3 8.6 %copy-start.11 = (f32[2,8,128]{2,1,0:T(8,128)S(1)}, f32[2,8,128]{2,1,0:T(8,128)}, u32[]{:S(2)}) copy-start(f32[2,8,128]{2,1,0:T(8,128)} %refs_3_.1) | copy-start | bytes 24580
  2.3 7.9 %collective-permute-start = (bf16[16,2176]{1,0:T(8,128)(2,1)S(1)}, bf16[16,2176]{1,0:T(8,128)(2,1)S(1)}, u32[]{:S(2)}, u32[]{:S(2)}) collective-permute-start(bf16[16,2176]{1,0:T(8,128)(2,1)S(1)} %pack_a.1), channel_id=1, source_target_pairs={{0,16},{1,17},{2,18},{3,19},{4,20},{5,21},{6,22},{7,23},{8,24},{9,... | collective-permute-start | bytes 208904 | tf_op jit(solution)/shard_map/ppermute | solution.py:425
  7.5 18.4 %collective-permute-start.7 = (bf16[1024,256]{1,0:T(8,128)(2,1)S(1)}, bf16[1024,256]{1,0:T(8,128)(2,1)S(1)}, u32[]{:S(2)}, u32[]{:S(2)}) collective-permute-start(bf16[1024,256]{1,0:T(8,128)(2,1)S(1)} %bitcast.3), channel_id=1, source_target_pairs={{0,1},{1,0},{2,3},{3,2},{4,5},{5,4},{6,7},{7,6},{8,9},{9,8},{10,11... | collective-permute-start | bytes 1572872 | tf_op jit(solution)/shard_map/ppermute | solution.py:541
  10.2 5.6 %collective-permute-start.2 = (bf16[32,2176]{1,0:T(8,128)(2,1)S(1)}, bf16[32,2176]{1,0:T(8,128)(2,1)S(1)}, u32[]{:S(2)}, u32[]{:S(2)}) collective-permute-start(bf16[32,2176]{1,0:T(8,128)(2,1)S(1)} %pad_maximum_fusion.9), channel_id=1, source_target_pairs={{0,8},{1,9},{2,10},{3,11},{4,12},{5,13},{6,14},{7,15},{8,0},{9,1},... | collective-permute-start | bytes 417800 | tf_op jit(solution)/shard_map/ppermute | solution.py:425
  11.0 6.6 %collective-permute-start.1 = (bf16[16,1280]{1,0:T(8,128)(2,1)S(1)}, bf16[16,1280]{1,0:T(8,128)(2,1)S(1)}, u32[]{:S(2)}, u32[]{:S(2)}) collective-permute-start(bf16[16,1280]{1,0:T(8,128)(2,1)S(1)} %pack_b.1), channel_id=1, source_target_pairs={{0,16},{1,17},{2,18},{3,19},{4,20},{5,21},{6,22},{7,23},{8,24},{9,... | collective-permute-start | bytes 122888 | tf_op jit(solution)/shard_map/ppermute | solution.py:425
  15.8 6.6 %collective-permute-start.4 = (bf16[64,2176]{1,0:T(8,128)(2,1)S(1)}, bf16[64,2176]{1,0:T(8,128)(2,1)S(1)}, u32[]{:S(2)}, u32[]{:S(2)}) collective-permute-start(bf16[64,2176]{1,0:T(8,128)(2,1)S(1)} %pad_maximum_fusion.6), channel_id=1, source_target_pairs={{0,4},{1,5},{2,3},{3,2},{4,0},{5,1},{6,7},{7,6},{8,12},{9,13},{10,... | collective-permute-start | bytes 835592 | tf_op jit(solution)/shard_map/ppermute | solution.py:425
  17.5 8.3 %copy-start = (bf16[4,512,256]{2,1,0:T(8,128)(2,1)S(1)}, bf16[4,512,256]{2,1,0:T(8,128)(2,1)}, u32[]{:S(2)}) copy-start(bf16[4,512,256]{2,1,0:T(8,128)(2,1)} %in_ref.1) | copy-start | bytes 3145732
  17.6 8.3 %copy-start.12 = (s32[4,512]{1,0:T(4,128)S(1)}, s32[4,512]{1,0:T(4,128)}, u32[]{:S(2)}) copy-start(s32[4,512]{1,0:T(4,128)} %label_ref.1) | copy-start | bytes 24580
  17.6 8.3 %copy-start.13 = (s32[4,512]{1,0:T(4,128)S(1)}, s32[4,512]{1,0:T(4,128)}, u32[]{:S(2)}) copy-start(s32[4,512]{1,0:T(4,128)} %domain_ref.1) | copy-start | bytes 24580
  17.6 4.5 %collective-permute-start.3 = (bf16[32,1280]{1,0:T(8,128)(2,1)S(1)}, bf16[32,1280]{1,0:T(8,128)(2,1)S(1)}, u32[]{:S(2)}, u32[]{:S(2)}) collective-permute-start(bf16[32,1280]{1,0:T(8,128)(2,1)S(1)} %pad_maximum_fusion.11), channel_id=1, source_target_pairs={{0,8},{1,9},{2,10},{3,11},{4,12},{5,13},{6,14},{7,15},{8,0},{9,1},... | collective-permute-start | bytes 245768 | tf_op jit(solution)/shard_map/ppermute | solution.py:425
  22.4 11.4 %collective-permute-start.6 = (bf16[128,2176]{1,0:T(8,128)(2,1)S(1)}, bf16[128,2176]{1,0:T(8,128)(2,1)S(1)}, u32[]{:S(2)}, u32[]{:S(2)}) collective-permute-start(bf16[128,2176]{1,0:T(8,128)(2,1)S(1)} %pad_maximum_fusion.2), channel_id=1, source_target_pairs={{0,1},{1,0},{2,6},{3,7},{4,5},{5,4},{6,2},{7,3},{8,9},{9,8},{10,14... | collective-permute-start | bytes 1671176 | tf_op jit(solution)/shard_map/ppermute | solution.py:425
  24.2 9.5 %collective-permute-start.5 = (bf16[64,1280]{1,0:T(8,128)(2,1)S(1)}, bf16[64,1280]{1,0:T(8,128)(2,1)S(1)}, u32[]{:S(2)}, u32[]{:S(2)}) collective-permute-start(bf16[64,1280]{1,0:T(8,128)(2,1)S(1)} %pad_maximum_fusion.8), channel_id=1, source_target_pairs={{0,4},{1,5},{2,3},{3,2},{4,0},{5,1},{6,7},{7,6},{8,12},{9,13},{10,... | collective-permute-start | bytes 491528 | tf_op jit(solution)/shard_map/ppermute | solution.py:425
  33.9 2.8 %collective-permute-start.9 = (bf16[256,2176]{1,0:T(8,128)(2,1)S(1)}, bf16[256,2176]{1,0:T(8,128)(2,1)S(1)}, u32[]{:S(2)}, u32[]{:S(2)}) collective-permute-start(bf16[256,2176]{1,0:T(8,128)(2,1)S(1)} %constant_dynamic-update-slice_fusion.own_ref), channel_id=1, source_target_pairs={{0,2},{1,3},{2,0},{3,1},{4,6},{5,7},{6,4},{7,5},{8,10},{9,11},{10,... | collective-permute-start | bytes 3342344 | tf_op jit(solution)/shard_map/ppermute | solution.py:425
  34.2 7.1 %collective-permute-start.8 = (bf16[128,1280]{1,0:T(8,128)(2,1)S(1)}, bf16[128,1280]{1,0:T(8,128)(2,1)S(1)}, u32[]{:S(2)}, u32[]{:S(2)}) collective-permute-start(bf16[128,1280]{1,0:T(8,128)(2,1)S(1)} %pad_maximum_fusion.4), channel_id=1, source_target_pairs={{0,1},{1,0},{2,6},{3,7},{4,5},{5,4},{6,2},{7,3},{8,9},{9,8},{10,14... | collective-permute-start | bytes 983048 | tf_op jit(solution)/shard_map/ppermute | solution.py:425
  36.7 6.8 %copy-start.18 = (f32[2,128]{1,0:T(2,128)S(1)}, f32[2,128]{1,0:T(2,128)}, u32[]{:S(2)}) copy-start(f32[2,128]{1,0:T(2,128)} %refs_4_.1) | copy-start | bytes 3076
  41.3 2.2 %collective-permute-start.10 = (bf16[256,1280]{1,0:T(8,128)(2,1)S(1)}, bf16[256,1280]{1,0:T(8,128)(2,1)S(1)}, u32[]{:S(2)}, u32[]{:S(2)}) collective-permute-start(bf16[256,1280]{1,0:T(8,128)(2,1)S(1)} %constant_dynamic-update-slice_fusion.5.own_ref), channel_id=1, source_target_pairs={{0,2},{1,3},{2,0},{3,1},{4,6},{5,7},{6,4},{7,5},{8,10},{9,11},{10,... | collective-permute-start | bytes 1966088 | tf_op jit(solution)/shard_map/ppermute | solution.py:425
  47.7 4.4 %collective-permute-start.11 = (bf16[264,1152]{1,0:T(8,128)(2,1)S(1)}, bf16[264,1152]{1,0:T(8,128)(2,1)S(1)}, u32[]{:S(2)}, u32[]{:S(2)}) collective-permute-start(bf16[264,1152]{1,0:T(8,128)(2,1)S(1)} %pad_maximum_fusion.1), channel_id=1, source_target_pairs={{0,2},{1,3},{2,0},{3,1},{4,6},{5,7},{6,4},{7,5},{8,10},{9,11},{10,... | collective-permute-start | bytes 1824776 | tf_op jit(solution)/shard_map/ppermute | solution.py:425
  51.7 4.0 %collective-permute-start.14 = (bf16[256,1792]{1,0:T(8,128)(2,1)S(1)}, bf16[256,1792]{1,0:T(8,128)(2,1)S(1)}, u32[]{:S(2)}, u32[]{:S(2)}) collective-permute-start(bf16[256,1792]{1,0:T(8,128)(2,1)S(1)} %get-tuple-element.106), channel_id=1, source_target_pairs={{0,2},{1,3},{2,0},{3,1},{4,6},{5,7},{6,4},{7,5},{8,10},{9,11},{10,... | collective-permute-start | bytes 2752520 | tf_op jit(solution)/shard_map/ppermute | solution.py:425
  52.4 8.2 %collective-permute-start.12 = (bf16[136,1152]{1,0:T(8,128)(2,1)S(1)}, bf16[136,1152]{1,0:T(8,128)(2,1)S(1)}, u32[]{:S(2)}, u32[]{:S(2)}) collective-permute-start(bf16[136,1152]{1,0:T(8,128)(2,1)S(1)} %pad_maximum_fusion.5), channel_id=1, source_target_pairs={{0,1},{1,0},{2,6},{3,7},{4,5},{5,4},{6,2},{7,3},{8,9},{9,8},{10,14... | collective-permute-start | bytes 940040 | tf_op jit(solution)/shard_map/ppermute | solution.py:425
  55.6 1.7 %collective-permute-start.13 = (bf16[256,384]{1,0:T(8,128)(2,1)S(1)}, bf16[256,384]{1,0:T(8,128)(2,1)S(1)}, u32[]{:S(2)}, u32[]{:S(2)}) collective-permute-start(bf16[256,384]{1,0:T(8,128)(2,1)S(1)} %get-tuple-element.112), channel_id=1, source_target_pairs={{0,2},{1,3},{2,0},{3,1},{4,6},{5,7},{6,4},{7,5},{8,10},{9,11},{10,... | collective-permute-start | bytes 589832 | tf_op jit(solution)/shard_map/ppermute | solution.py:425
  56.0 11.3 %collective-permute-start.16 = (bf16[128,1792]{1,0:T(8,128)(2,1)S(1)}, bf16[128,1792]{1,0:T(8,128)(2,1)S(1)}, u32[]{:S(2)}, u32[]{:S(2)}) collective-permute-start(bf16[128,1792]{1,0:T(8,128)(2,1)S(1)} %slice.294), channel_id=1, source_target_pairs={{0,1},{1,0},{2,6},{3,7},{4,5},{5,4},{6,2},{7,3},{8,9},{9,8},{10,14... | collective-permute-start | bytes 1376264 | tf_op jit(solution)/shard_map/ppermute | solution.py:425
  57.4 9.8 %collective-permute-start.17 = (bf16[128,384]{1,0:T(8,128)(2,1)S(1)}, bf16[128,384]{1,0:T(8,128)(2,1)S(1)}, u32[]{:S(2)}, u32[]{:S(2)}) collective-permute-start(bf16[128,384]{1,0:T(8,128)(2,1)S(1)} %slice.299), channel_id=1, source_target_pairs={{0,1},{1,0},{2,6},{3,7},{4,5},{5,4},{6,2},{7,3},{8,9},{9,8},{10,14... | collective-permute-start | bytes 294920 | tf_op jit(solution)/shard_map/ppermute | solution.py:425
  60.8 6.5 %collective-permute-start.15 = (bf16[72,1152]{1,0:T(8,128)(2,1)S(1)}, bf16[72,1152]{1,0:T(8,128)(2,1)S(1)}, u32[]{:S(2)}, u32[]{:S(2)}) collective-permute-start(bf16[72,1152]{1,0:T(8,128)(2,1)S(1)} %pad_maximum_fusion.7), channel_id=1, source_target_pairs={{0,4},{1,5},{2,3},{3,2},{4,0},{5,1},{6,7},{7,6},{8,12},{9,13},{10,... | collective-permute-start | bytes 497672 | tf_op jit(solution)/shard_map/ppermute | solution.py:425
  67.5 6.6 %collective-permute-start.19 = (bf16[64,2176]{1,0:T(8,128)(2,1)S(1)}, bf16[64,2176]{1,0:T(8,128)(2,1)S(1)}, u32[]{:S(2)}, u32[]{:S(2)}) collective-permute-start(bf16[64,2176]{1,0:T(8,128)(2,1)S(1)} %slice.296), channel_id=1, source_target_pairs={{0,4},{1,5},{2,3},{3,2},{4,0},{5,1},{6,7},{7,6},{8,12},{9,13},{10,... | collective-permute-start | bytes 835592 | tf_op jit(solution)/shard_map/ppermute | solution.py:425
  69.2 4.6 %collective-permute-start.18 = (bf16[40,1152]{1,0:T(8,128)(2,1)S(1)}, bf16[40,1152]{1,0:T(8,128)(2,1)S(1)}, u32[]{:S(2)}, u32[]{:S(2)}) collective-permute-start(bf16[40,1152]{1,0:T(8,128)(2,1)S(1)} %pad_maximum_fusion.10), channel_id=1, source_target_pairs={{0,8},{1,9},{2,10},{3,11},{4,12},{5,13},{6,14},{7,15},{8,0},{9,1},... | collective-permute-start | bytes 276488 | tf_op jit(solution)/shard_map/ppermute | solution.py:425
  70.7 13.2 %collective-permute-start.21 = (bf16[512,256]{1,0:T(8,128)(2,1)S(1)}, bf16[512,256]{1,0:T(8,128)(2,1)S(1)}, u32[]{:S(2)}, u32[]{:S(2)}) collective-permute-start(bf16[512,256]{1,0:T(8,128)(2,1)S(1)} %get-tuple-element.130), channel_id=1, source_target_pairs={{0,1},{1,0},{2,3},{3,2},{4,5},{5,4},{6,7},{7,6},{8,9},{9,8},{10,11... | collective-permute-start | bytes 786440 | tf_op jit(solution)/shard_map/ppermute | solution.py:541
  74.3 6.7 %collective-permute-start.23 = (bf16[32,2176]{1,0:T(8,128)(2,1)S(1)}, bf16[32,2176]{1,0:T(8,128)(2,1)S(1)}, u32[]{:S(2)}, u32[]{:S(2)}) collective-permute-start(bf16[32,2176]{1,0:T(8,128)(2,1)S(1)} %slice.298), channel_id=1, source_target_pairs={{0,8},{1,9},{2,10},{3,11},{4,12},{5,13},{6,14},{7,15},{8,0},{9,1},... | collective-permute-start | bytes 417800 | tf_op jit(solution)/shard_map/ppermute | solution.py:425
  75.9 5.1 %collective-permute-start.20 = (bf16[24,1152]{1,0:T(8,128)(2,1)S(1)}, bf16[24,1152]{1,0:T(8,128)(2,1)S(1)}, u32[]{:S(2)}, u32[]{:S(2)}) collective-permute-start(bf16[24,1152]{1,0:T(8,128)(2,1)S(1)} %pad_maximum_fusion.12), channel_id=1, source_target_pairs={{0,16},{1,17},{2,18},{3,19},{4,20},{5,21},{6,22},{7,23},{8,24},{9,... | collective-permute-start | bytes 165896 | tf_op jit(solution)/shard_map/ppermute | solution.py:425
  78.1 7.0 %collective-permute-start.22 = (bf16[512,256]{1,0:T(8,128)(2,1)S(1)}, bf16[512,256]{1,0:T(8,128)(2,1)S(1)}, u32[]{:S(2)}, u32[]{:S(2)}) collective-permute-start(bf16[512,256]{1,0:T(8,128)(2,1)S(1)} %get-tuple-element.131), channel_id=1, source_target_pairs={{0,1},{1,0},{2,3},{3,2},{4,5},{5,4},{6,7},{7,6},{8,9},{9,8},{10,11... | collective-permute-start | bytes 786440 | tf_op jit(solution)/shard_map/ppermute | solution.py:541
  81.1 5.5 %collective-permute-start.24 = (bf16[16,2176]{1,0:T(8,128)(2,1)S(1)}, bf16[16,2176]{1,0:T(8,128)(2,1)S(1)}, u32[]{:S(2)}, u32[]{:S(2)}) collective-permute-start(bf16[16,2176]{1,0:T(8,128)(2,1)S(1)} %slice.301), channel_id=1, source_target_pairs={{0,16},{1,17},{2,18},{3,19},{4,20},{5,21},{6,22},{7,23},{8,24},{9,... | collective-permute-start | bytes 208904 | tf_op jit(solution)/shard_map/ppermute | solution.py:425
  83.8 2.8 %copy-start.2 = (f32[16,2048]{1,0:T(8,128)S(1)}, f32[16,2048]{1,0:T(8,128)}, u32[]{:S(2)}) copy-start(f32[16,2048]{1,0:T(8,128)} %refs_0_.1) | copy-start | bytes 393220
  83.8 2.8 %copy-start.4 = (f32[16,2048]{1,0:T(8,128)S(1)}, f32[16,2048]{1,0:T(8,128)}, u32[]{:S(2)}) copy-start(f32[16,2048]{1,0:T(8,128)} %refs_5_.1) | copy-start | bytes 393220
  83.8 2.8 %copy-start.5 = (f32[16,2048]{1,0:T(8,128)S(1)}, f32[16,2048]{1,0:T(8,128)}, u32[]{:S(2)}) copy-start(f32[16,2048]{1,0:T(8,128)} %refs_10_.1) | copy-start | bytes 393220
  83.8 2.8 %copy-start.6 = (f32[8,8,256]{2,1,0:T(8,128)S(1)}, f32[8,8,256]{2,1,0:T(8,128)}, u32[]{:S(2)}) copy-start(f32[8,8,256]{2,1,0:T(8,128)} %refs_7_.1) | copy-start | bytes 196612
  83.8 2.8 %copy-start.7 = (f32[8,8,256]{2,1,0:T(8,128)S(1)}, f32[8,8,256]{2,1,0:T(8,128)}, u32[]{:S(2)}) copy-start(f32[8,8,256]{2,1,0:T(8,128)} %refs_12_.1) | copy-start | bytes 196612
  83.8 2.8 %copy-start.9 = (f32[16,16]{1,0:T(8,128)S(1)}, f32[16,16]{1,0:T(8,128)}, u32[]{:S(2)}) copy-start(f32[16,16]{1,0:T(8,128)} %refs_1_.1) | copy-start | bytes 3076
  83.8 2.8 %copy-start.14 = (f32[16,16]{1,0:T(8,128)S(1)}, f32[16,16]{1,0:T(8,128)}, u32[]{:S(2)}) copy-start(f32[16,16]{1,0:T(8,128)} %refs_6_.1) | copy-start | bytes 3076
  83.8 2.8 %copy-start.15 = (f32[2,8,128]{2,1,0:T(8,128)S(1)}, f32[2,8,128]{2,1,0:T(8,128)}, u32[]{:S(2)}) copy-start(f32[2,8,128]{2,1,0:T(8,128)} %refs_8_.1) | copy-start | bytes 24580
  83.9 2.8 %copy-start.16 = (f32[16,16]{1,0:T(8,128)S(1)}, f32[16,16]{1,0:T(8,128)}, u32[]{:S(2)}) copy-start(f32[16,16]{1,0:T(8,128)} %refs_11_.1) | copy-start | bytes 3076
  83.9 2.8 %copy-start.17 = (f32[2,8,128]{2,1,0:T(8,128)S(1)}, f32[2,8,128]{2,1,0:T(8,128)}, u32[]{:S(2)}) copy-start(f32[2,8,128]{2,1,0:T(8,128)} %refs_13_.1) | copy-start | bytes 24580
  83.9 2.8 %copy-start.19 = (f32[2,128]{1,0:T(2,128)S(1)}, f32[2,128]{1,0:T(2,128)}, u32[]{:S(2)}) copy-start(f32[2,128]{1,0:T(2,128)} %refs_9_.1) | copy-start | bytes 3076
  83.9 2.8 %copy-start.20 = (f32[2,128]{1,0:T(2,128)S(1)}, f32[2,128]{1,0:T(2,128)}, u32[]{:S(2)}) copy-start(f32[2,128]{1,0:T(2,128)} %refs_14_.1) | copy-start | bytes 3076

commit v7 on v6

--- a/solution.py
+++ b/solution.py
@@ -632,7 +632,7 @@
     steps = [cube.core] + cube.order[::-1]
     got_b = cube.swap(message, steps[0])
 
-    cut = 7
+    cut = 6
     low_cols, high_cols = cut * hidden, (experts - cut) * hidden + LANES
     dpre_low, keep_low, send_low, terms = pl.pallas_call(
         functools.partial(back_first_kernel, places, range(cut)),

time: 88 us -> 87.7 us (level)
  waiting for transfers between devices: 24 us -> 22.5 us
  starting transfers between devices: 36 us -> 36.9 us
    ppermute x22, starting transfers between devices: 31.7 us -> 33.1 us  [swap(): return lax.ppermute(values, both, self.pairs(step))]
    ppermute x3, waiting for transfers between devices: 1.15 us -> 0.26 us  [swap_field(): return lax.ppermute(values, 'field', [(0, 1), (1, 0)])]
  transfers between devices with their start and end apart: 25 -> 25, of which waited for: 13 -> 14; matrix products, arithmetic and copies ran while one was open for 3% -> 3% of each run, Pallas kernels for 19% -> 19%
where the time goes in v7:
time: 87.7 us; the launch traced here: 87.4 us
  starting transfers between devices  36.9 us (42%)
  waiting for transfers between devices  22.5 us (26%)
  Pallas kernels  21.8 us (25%)
  local copies, waits for them, and re-layouts  3.64 us (4%)
  between operations  1.38 us (2%)
  other arithmetic  1.25 us (1%)
    ppermute x22, starting transfers between devices, swap(): return lax.ppermute(values, both, self.pairs(step))  33.1 us
    ppermute x22, waiting for transfers between devices, swap(): return lax.ppermute(values, both, self.pairs(step))  22.2 us
    pallas_call x2, Pallas kernels, input_part(): pl.pallas_call(input_kernel, grid_spec=pltpu.PrefetchScalarGridSpec(num_s...  4.66 us
    pallas_call x1, Pallas kernels, on_device(): pl.pallas_call(functools.partial(first_kernel, places), out_shape=[shape(...  4.54 us
    pallas_call x1, Pallas kernels, on_device(): pl.pallas_call(functools.partial(second_kernel, places), out_shape=[shape...  4.18 us
    ppermute x3, starting transfers between devices, swap_field(): return lax.ppermute(values, 'field', [(0, 1), (1, 0)])  3.86 us
    pallas_call x1, Pallas kernels, on_device(): pl.pallas_call(functools.partial(back_first_kernel, places, range(cut)),...  3.49 us
    unnamed x50, local copies, waits for them, and re-layouts  1.78 us
  transfers between devices with their start and end apart: 25, of which 14 were waited for; matrix products, arithmetic and copies ran while one was open for 3% of the time, Pallas kernels for 19%

profile of v7, /device:TPU:0, one launch (start us, length us, event | category | flops | bytes accessed | tf_op | source)
XLA Modules:
  0.0 87.4 jit_solution(12095164380088194064)
XLA Ops:
  0.7 0.9 %copy-done.1 = f32[16,2048]{1,0:T(8,128)S(1)} copy-done((f32[16,2048]{1,0:T(8,128)S(1)}, f32[16,2048]{1,0:T(8,128)}, u32[]{:S(2)}) %copy-start.1) | copy-done | bytes 131096
  1.6 0.7 copy-done.8
  2.3 4.1 %collective-permute-start = (bf16[16,2176]{1,0:T(8,128)(2,1)S(1)}, bf16[16,2176]{1,0:T(8,128)(2,1)S(1)}, u32[]{:S(2)}, u32[]{:S(2)}) collective-permute-start(bf16[16,2176]{1,0:T(8,128)(2,1)S(1)} %pack_a.1), channel_id=1, source_target_pairs={{0,16},{1,17},{2,18},{3,19},{4,20},{5,21},{6,22},{7,23},{8,24},{9,... | collective-permute-start | bytes 208904 | tf_op jit(solution)/shard_map/ppermute | solution.py:425
  6.4 1.1 %constant_dynamic-slice_fusion = bf16[4,256,256]{2,1,0:T(8,128)(2,1)S(1)} fusion(bf16[4,512,256]{2,1,0:T(8,128)(2,1)} %in_ref.1, s32[]{:T(128)S(6)} %select_n.3), kind=kLoop, calls=%fused_computation.86 | loop fusion | bytes 1048580 | tf_op jit(solution)/shard_map/dynamic_slice | solution.py:544
  7.5 1.6 %collective-permute-start.7 = (bf16[1024,256]{1,0:T(8,128)(2,1)S(1)}, bf16[1024,256]{1,0:T(8,128)(2,1)S(1)}, u32[]{:S(2)}, u32[]{:S(2)}) collective-permute-start(bf16[1024,256]{1,0:T(8,128)(2,1)S(1)} %bitcast.3), channel_id=1, source_target_pairs={{0,1},{1,0},{2,3},{3,2},{4,5},{5,4},{6,7},{7,6},{8,9},{9,8},{10,11... | collective-permute-start | bytes 1572872 | tf_op jit(solution)/shard_map/ppermute | solution.py:541
  9.1 1.1 %collective-permute-done = bf16[16,2176]{1,0:T(8,128)(2,1)S(1)} collective-permute-done((bf16[16,2176]{1,0:T(8,128)(2,1)S(1)}, bf16[16,2176]{1,0:T(8,128)(2,1)S(1)}, u32[]{:S(2)}, u32[]{:S(2)}) %collective-permute-start) | collective-permute-done | bytes 69664 | tf_op jit(solution)/shard_map/ppermute | solution.py:425
  10.2 0.7 collective-permute-start.2
  11.0 3.4 %collective-permute-start.1 = (bf16[16,1280]{1,0:T(8,128)(2,1)S(1)}, bf16[16,1280]{1,0:T(8,128)(2,1)S(1)}, u32[]{:S(2)}, u32[]{:S(2)}) collective-permute-start(bf16[16,1280]{1,0:T(8,128)(2,1)S(1)} %pack_b.1), channel_id=1, source_target_pairs={{0,16},{1,17},{2,18},{3,19},{4,20},{5,21},{6,22},{7,23},{8,24},{9,... | collective-permute-start | bytes 122888 | tf_op jit(solution)/shard_map/ppermute | solution.py:425
  14.4 1.3 %collective-permute-done.2 = bf16[32,2176]{1,0:T(8,128)(2,1)S(1)} collective-permute-done((bf16[32,2176]{1,0:T(8,128)(2,1)S(1)}, bf16[32,2176]{1,0:T(8,128)(2,1)S(1)}, u32[]{:S(2)}, u32[]{:S(2)}) %collective-permute-start.2) | collective-permute-done | bytes 139296 | tf_op jit(solution)/shard_map/ppermute | solution.py:425
  15.8 1.8 %collective-permute-start.4 = (bf16[64,2176]{1,0:T(8,128)(2,1)S(1)}, bf16[64,2176]{1,0:T(8,128)(2,1)S(1)}, u32[]{:S(2)}, u32[]{:S(2)}) collective-permute-start(bf16[64,2176]{1,0:T(8,128)(2,1)S(1)} %pad_maximum_fusion.6), channel_id=1, source_target_pairs={{0,4},{1,5},{2,3},{3,2},{4,0},{5,1},{6,7},{7,6},{8,12},{9,13},{10,... | collective-permute-start | bytes 835592 | tf_op jit(solution)/shard_map/ppermute | solution.py:425
  17.6 1.2 %collective-permute-start.3 = (bf16[32,1280]{1,0:T(8,128)(2,1)S(1)}, bf16[32,1280]{1,0:T(8,128)(2,1)S(1)}, u32[]{:S(2)}, u32[]{:S(2)}) collective-permute-start(bf16[32,1280]{1,0:T(8,128)(2,1)S(1)} %pad_maximum_fusion.11), channel_id=1, source_target_pairs={{0,8},{1,9},{2,10},{3,11},{4,12},{5,13},{6,14},{7,15},{8,0},{9,1},... | collective-permute-start | bytes 245768 | tf_op jit(solution)/shard_map/ppermute | solution.py:425
  18.8 3.3 %collective-permute-done.3 = bf16[32,1280]{1,0:T(8,128)(2,1)S(1)} collective-permute-done((bf16[32,1280]{1,0:T(8,128)(2,1)S(1)}, bf16[32,1280]{1,0:T(8,128)(2,1)S(1)}, u32[]{:S(2)}, u32[]{:S(2)}) %collective-permute-start.3) | collective-permute-done | bytes 81952 | tf_op jit(solution)/shard_map/ppermute | solution.py:425
  22.1 0.3 collective-permute-done.4
  22.4 1.8 %collective-permute-start.6 = (bf16[128,2176]{1,0:T(8,128)(2,1)S(1)}, bf16[128,2176]{1,0:T(8,128)(2,1)S(1)}, u32[]{:S(2)}, u32[]{:S(2)}) collective-permute-start(bf16[128,2176]{1,0:T(8,128)(2,1)S(1)} %pad_maximum_fusion.2), channel_id=1, source_target_pairs={{0,1},{1,0},{2,6},{3,7},{4,5},{5,4},{6,2},{7,3},{8,9},{9,8},{10,14... | collective-permute-start | bytes 1671176 | tf_op jit(solution)/shard_map/ppermute | solution.py:425
  24.2 1.6 %collective-permute-start.5 = (bf16[64,1280]{1,0:T(8,128)(2,1)S(1)}, bf16[64,1280]{1,0:T(8,128)(2,1)S(1)}, u32[]{:S(2)}, u32[]{:S(2)}) collective-permute-start(bf16[64,1280]{1,0:T(8,128)(2,1)S(1)} %pad_maximum_fusion.8), channel_id=1, source_target_pairs={{0,4},{1,5},{2,3},{3,2},{4,0},{5,1},{6,7},{7,6},{8,12},{9,13},{10,... | collective-permute-start | bytes 491528 | tf_op jit(solution)/shard_map/ppermute | solution.py:425
  25.9 0.6 rows.1
  26.4 7.4 %collective-permute-done.6 = bf16[128,2176]{1,0:T(8,128)(2,1)S(1)} collective-permute-done((bf16[128,2176]{1,0:T(8,128)(2,1)S(1)}, bf16[128,2176]{1,0:T(8,128)(2,1)S(1)}, u32[]{:S(2)}, u32[]{:S(2)}) %collective-permute-start.6) | collective-permute-done | bytes 557088 | tf_op jit(solution)/shard_map/ppermute | solution.py:425
  33.8 0.3 collective-permute-start.9
  34.2 1.7 %collective-permute-start.8 = (bf16[128,1280]{1,0:T(8,128)(2,1)S(1)}, bf16[128,1280]{1,0:T(8,128)(2,1)S(1)}, u32[]{:S(2)}, u32[]{:S(2)}) collective-permute-start(bf16[128,1280]{1,0:T(8,128)(2,1)S(1)} %pad_maximum_fusion.4), channel_id=1, source_target_pairs={{0,1},{1,0},{2,6},{3,7},{4,5},{5,4},{6,2},{7,3},{8,9},{9,8},{10,14... | collective-permute-start | bytes 983048 | tf_op jit(solution)/shard_map/ppermute | solution.py:425
  35.9 0.8 collective-permute-done.9.oth_ref
  36.7 4.5 %first.1 = (bf16[1024,2048]{1,0:T(8,128)(2,1)S(1)}, bf16[1024,2048]{1,0:T(8,128)(2,1)S(1)}, f32[1024,16]{1,0:T(8,128)S(1)}, bf16[512,2176]{1,0:T(8,128)(2,1)S(1)}) custom-call(bf16[256,2176]{1,0:T(8,128)(2,1)S(1)} %constant_dynamic-update-slice_fusion.own_ref, bf16[256,2176]{1,0:T(8,128)(2,1)S(1)} %collective-permute-done.9.oth_ref, ...), custom_call_target="tpu_custom_call" | custom-call | flops 4563402752 | bytes 8388608 | tf_op jit(solution)/shard_map/first/pallas_call | solution.py:593
  41.5 2.0 %collective-permute-done.10.oth_ref = bf16[256,1280]{1,0:T(8,128)(2,1)S(1)} collective-permute-done((bf16[256,1280]{1,0:T(8,128)(2,1)S(1)}, bf16[256,1280]{1,0:T(8,128)(2,1)S(1)}, u32[]{:S(2)}, u32[]{:S(2)}) %collective-permute-start.10) | collective-permute-done | bytes 655392 | tf_op jit(solution)/shard_map/ppermute | solution.py:425
  43.5 4.2 %second.1 = (bf16[2048,256]{1,0:T(8,128)(2,1)S(1)}, bf16[1024,256]{1,0:T(8,128)(2,1)S(1)}, f32[8,1152]{1,0:T(8,128)S(1)}, f32[256,1152]{1,0:T(8,128)S(1)}, bf16[256,1152]{1,0:T(8,128)(2,1)S(1)}) custom-call(bf16[256,1280]{1,0:T(8,128)(2,1)S(1)} %constant_dynamic-update-slice_fusion.5.own_ref, bf16[256,1280]{1,0:T(8,128)(2,1)S(1)} %collective-permute-done.10.oth_ref, ...), custom_call_target="tpu_custom_call" | custom-call | tf_op jit(solution)/shard_map/second/pallas_call | solution.py:611
  47.8 0.2 collective-permute-start.11
  48.0 3.5 %back_first.1 = (bf16[1024,1536]{1,0:T(8,128)(2,1)S(1)}, f32[256,1536]{1,0:T(8,128)S(1)}, bf16[256,1536]{1,0:T(8,128)(2,1)S(1)}, f32[1024,16]{1,0:T(8,128)S(1)}) custom-call(bf16[2048,256]{1,0:T(8,128)(2,1)S(1)} %get-tuple-element.103.w_ref, bf16[1024,256]{1,0:T(8,128)(2,1)S(1)} %get-tuple-element.104.dm_ref, ...), custom_call_target="tpu_custom_call" | custom-call | tf_op jit(solution)/shard_map/back_first/pallas_call | solution.py:637
  51.5 0.4 collective-permute-start.14
  52.2 1.7 %collective-permute-start.12 = (bf16[136,1152]{1,0:T(8,128)(2,1)S(1)}, bf16[136,1152]{1,0:T(8,128)(2,1)S(1)}, u32[]{:S(2)}, u32[]{:S(2)}) collective-permute-start(bf16[136,1152]{1,0:T(8,128)(2,1)S(1)} %pad_maximum_fusion.5), channel_id=1, source_target_pairs={{0,1},{1,0},{2,6},{3,7},{4,5},{5,4},{6,2},{7,3},{8,9},{9,8},{10,14... | collective-permute-start | bytes 940040 | tf_op jit(solution)/shard_map/ppermute | solution.py:425
  53.9 1.8 %back_last.1 = (bf16[1024,512]{1,0:T(8,128)(2,1)S(1)}, f32[256,640]{1,0:T(8,128)S(1)}, bf16[256,640]{1,0:T(8,128)(2,1)S(1)}, bf16[1024,128]{1,0:T(8,128)(2,1)S(1)}) custom-call(bf16[2048,256]{1,0:T(8,128)(2,1)S(1)} %get-tuple-element.103.w_ref, bf16[1024,256]{1,0:T(8,128)(2,1)S(1)} %get-tuple-element.104.dm_ref, ...), custom_call_target="tpu_custom_call" | custom-call | tf_op jit(solution)/shard_map/back_last/pallas_call | solution.py:654
  56.1 1.4 %collective-permute-start.16 = (bf16[128,1536]{1,0:T(8,128)(2,1)S(1)}, bf16[128,1536]{1,0:T(8,128)(2,1)S(1)}, u32[]{:S(2)}, u32[]{:S(2)}) collective-permute-start(bf16[128,1536]{1,0:T(8,128)(2,1)S(1)} %slice.294), channel_id=1, source_target_pairs={{0,1},{1,0},{2,6},{3,7},{4,5},{5,4},{6,2},{7,3},{8,9},{9,8},{10,14... | collective-permute-start | bytes 1179656 | tf_op jit(solution)/shard_map/ppermute | solution.py:425
  57.6 1.6 %collective-permute-done.12 = bf16[136,1152]{1,0:T(8,128)(2,1)S(1)} collective-permute-done((bf16[136,1152]{1,0:T(8,128)(2,1)S(1)}, bf16[136,1152]{1,0:T(8,128)(2,1)S(1)}, u32[]{:S(2)}, u32[]{:S(2)}) %collective-permute-start.12) | collective-permute-done | bytes 313376 | tf_op jit(solution)/shard_map/ppermute | solution.py:425
  59.3 1.7 %collective-permute-start.17 = (bf16[128,640]{1,0:T(8,128)(2,1)S(1)}, bf16[128,640]{1,0:T(8,128)(2,1)S(1)}, u32[]{:S(2)}, u32[]{:S(2)}) collective-permute-start(bf16[128,640]{1,0:T(8,128)(2,1)S(1)} %slice.297), channel_id=1, source_target_pairs={{0,1},{1,0},{2,6},{3,7},{4,5},{5,4},{6,2},{7,3},{8,9},{9,8},{10,14... | collective-permute-start | bytes 491528 | tf_op jit(solution)/shard_map/ppermute | solution.py:425
  61.1 1.5 %collective-permute-start.15 = (bf16[72,1152]{1,0:T(8,128)(2,1)S(1)}, bf16[72,1152]{1,0:T(8,128)(2,1)S(1)}, u32[]{:S(2)}, u32[]{:S(2)}) collective-permute-start(bf16[72,1152]{1,0:T(8,128)(2,1)S(1)} %pad_maximum_fusion.7), channel_id=1, source_target_pairs={{0,4},{1,5},{2,3},{3,2},{4,0},{5,1},{6,7},{7,6},{8,12},{9,13},{10,... | collective-permute-start | bytes 497672 | tf_op jit(solution)/shard_map/ppermute | solution.py:425
  62.6 2.3 %input.2 = (f32[4,512,256]{2,1,0:T(8,128)}, bf16[512,256]{1,0:T(8,128)(2,1)S(1)}) custom-call(s32[1]{0:T(128)} %bitcast.1.at, bf16[1024,1536]{1,0:T(8,128)(2,1)S(1)} %get-tuple-element.117.low_ref, bf16[1024,512]{1,0:T(8,128)(2,1)S(1)} %get-tuple-element.118.high_ref, bf16[1024,128]{1,0:T(8,128)(2,1)S(1)} %get-tuple-element.122.dg_ref, ...), custom_call_target="tpu_custom_call" | custom-call | tf_op jit(solution)/shard_map/input/pallas_call | solution.py:678
  64.9 2.3 %input.3 = (f32[4,512,256]{2,1,0:T(8,128)}, bf16[512,256]{1,0:T(8,128)(2,1)S(1)}) custom-call(s32[1]{0:T(128)} %bitcast.1.at, bf16[1024,1536]{1,0:T(8,128)(2,1)S(1)} %get-tuple-element.117.low_ref, bf16[1024,512]{1,0:T(8,128)(2,1)S(1)} %get-tuple-element.118.high_ref, ...), custom_call_target="tpu_custom_call", output_to_operand_aliasing={{0}: (5, {})} | custom-call | tf_op jit(solution)/shard_map/input/pallas_call | solution.py:678
  67.7 1.5 %collective-permute-start.19 = (bf16[64,2176]{1,0:T(8,128)(2,1)S(1)}, bf16[64,2176]{1,0:T(8,128)(2,1)S(1)}, u32[]{:S(2)}, u32[]{:S(2)}) collective-permute-start(bf16[64,2176]{1,0:T(8,128)(2,1)S(1)} %slice.296), channel_id=1, source_target_pairs={{0,4},{1,5},{2,3},{3,2},{4,0},{5,1},{6,7},{7,6},{8,12},{9,13},{10,... | collective-permute-start | bytes 835592 | tf_op jit(solution)/shard_map/ppermute | solution.py:425
  69.3 1.1 %collective-permute-start.18 = (bf16[40,1152]{1,0:T(8,128)(2,1)S(1)}, bf16[40,1152]{1,0:T(8,128)(2,1)S(1)}, u32[]{:S(2)}, u32[]{:S(2)}) collective-permute-start(bf16[40,1152]{1,0:T(8,128)(2,1)S(1)} %pad_maximum_fusion.10), channel_id=1, source_target_pairs={{0,8},{1,9},{2,10},{3,11},{4,12},{5,13},{6,14},{7,15},{8,0},{9,1},... | collective-permute-start | bytes 276488 | tf_op jit(solution)/shard_map/ppermute | solution.py:425
  70.5 1.1 %collective-permute-start.21 = (bf16[512,256]{1,0:T(8,128)(2,1)S(1)}, bf16[512,256]{1,0:T(8,128)(2,1)S(1)}, u32[]{:S(2)}, u32[]{:S(2)}) collective-permute-start(bf16[512,256]{1,0:T(8,128)(2,1)S(1)} %get-tuple-element.130), channel_id=1, source_target_pairs={{0,1},{1,0},{2,3},{3,2},{4,5},{5,4},{6,7},{7,6},{8,9},{9,8},{10,11... | collective-permute-start | bytes 786440 | tf_op jit(solution)/shard_map/ppermute | solution.py:541
  71.5 2.4 %collective-permute-done.18 = bf16[40,1152]{1,0:T(8,128)(2,1)S(1)} collective-permute-done((bf16[40,1152]{1,0:T(8,128)(2,1)S(1)}, bf16[40,1152]{1,0:T(8,128)(2,1)S(1)}, u32[]{:S(2)}, u32[]{:S(2)}) %collective-permute-start.18) | collective-permute-done | bytes 92192 | tf_op jit(solution)/shard_map/ppermute | solution.py:425
  73.9 0.4 collective-permute-done.19
  74.4 1.3 %collective-permute-start.23 = (bf16[32,2176]{1,0:T(8,128)(2,1)S(1)}, bf16[32,2176]{1,0:T(8,128)(2,1)S(1)}, u32[]{:S(2)}, u32[]{:S(2)}) collective-permute-start(bf16[32,2176]{1,0:T(8,128)(2,1)S(1)} %slice.299), channel_id=1, source_target_pairs={{0,8},{1,9},{2,10},{3,11},{4,12},{5,13},{6,14},{7,15},{8,0},{9,1},... | collective-permute-start | bytes 417800 | tf_op jit(solution)/shard_map/ppermute | solution.py:425
  75.8 2.5 %collective-permute-start.20 = (bf16[24,1152]{1,0:T(8,128)(2,1)S(1)}, bf16[24,1152]{1,0:T(8,128)(2,1)S(1)}, u32[]{:S(2)}, u32[]{:S(2)}) collective-permute-start(bf16[24,1152]{1,0:T(8,128)(2,1)S(1)} %pad_maximum_fusion.12), channel_id=1, source_target_pairs={{0,16},{1,17},{2,18},{3,19},{4,20},{5,21},{6,22},{7,23},{8,24},{9,... | collective-permute-start | bytes 165896 | tf_op jit(solution)/shard_map/ppermute | solution.py:425
  78.3 1.2 %collective-permute-start.22 = (bf16[512,256]{1,0:T(8,128)(2,1)S(1)}, bf16[512,256]{1,0:T(8,128)(2,1)S(1)}, u32[]{:S(2)}, u32[]{:S(2)}) collective-permute-start(bf16[512,256]{1,0:T(8,128)(2,1)S(1)} %get-tuple-element.131), channel_id=1, source_target_pairs={{0,1},{1,0},{2,3},{3,2},{4,5},{5,4},{6,7},{7,6},{8,9},{9,8},{10,11... | collective-permute-start | bytes 786440 | tf_op jit(solution)/shard_map/ppermute | solution.py:541
  79.5 1.4 %collective-permute-done.20.got_b = bf16[24,1152]{1,0:T(8,128)(2,1)S(1)} collective-permute-done((bf16[24,1152]{1,0:T(8,128)(2,1)S(1)}, bf16[24,1152]{1,0:T(8,128)(2,1)S(1)}, u32[]{:S(2)}, u32[]{:S(2)}) %collective-permute-start.20) | collective-permute-done | bytes 55328 | tf_op jit(solution)/shard_map/ppermute | solution.py:425
  81.0 2.8 %collective-permute-start.24 = (bf16[16,2176]{1,0:T(8,128)(2,1)S(1)}, bf16[16,2176]{1,0:T(8,128)(2,1)S(1)}, u32[]{:S(2)}, u32[]{:S(2)}) collective-permute-start(bf16[16,2176]{1,0:T(8,128)(2,1)S(1)} %slice.301), channel_id=1, source_target_pairs={{0,16},{1,17},{2,18},{3,19},{4,20},{5,21},{6,22},{7,23},{8,24},{9,... | collective-permute-start | bytes 208904 | tf_op jit(solution)/shard_map/ppermute | solution.py:425
  83.8 0.5 slice.226
  84.4 0.3 collective-permute-done.22.late_ref
  84.7 1.5 %place.1 = f32[4,512,256]{2,1,0:T(8,128)} custom-call(s32[1]{0:T(128)} %bitcast.1.at, bf16[512,256]{1,0:T(8,128)(2,1)S(1)} %collective-permute-done.21.early_ref, bf16[512,256]{1,0:T(8,128)(2,1)S(1)} %collective-permute-done.22.late_ref, f32[4,512,256]{2,1,0:T(8,128)} %get-tuple-element.134.held_ref), custom_call_target="tpu_custom_call", output_to_operand_aliasing={{}: (3, {})} | custom-call | tf_op jit(solution)/shard_map/place/pallas_call | solution.py:737
  86.4 0.9 %update.1 = (f32[16,2048]{1,0:T(8,128)}, f32[16,2048]{1,0:T(8,128)}, f32[16,2048]{1,0:T(8,128)}, f32[16,16]{1,0:T(8,128)}, f32[16,16]{1,0:T(8,128)}, /*index=5*/...) custom-call(f32[32,2176]{1,0:T(8,128)S(1)} %slice_add_fusion.3.sum_a, ...), custom_call_target="tpu_custom_call" | custom-call | tf_op jit(solution)/shard_map/update/pallas_call | solution.py:751
  (117 shorter events, 2.3 us)
Async XLA Ops:
  0.7 0.9 %copy-start.1 = (f32[16,2048]{1,0:T(8,128)S(1)}, f32[16,2048]{1,0:T(8,128)}, u32[]{:S(2)}) copy-start(f32[16,2048]{1,0:T(8,128)} %refs_0_.1) | copy-start | bytes 393220
  1.6 0.7 copy-start.8
  2.3 8.6 %copy-start.3 = (f32[8,8,256]{2,1,0:T(8,128)S(1)}, f32[8,8,256]{2,1,0:T(8,128)}, u32[]{:S(2)}) copy-start(f32[8,8,256]{2,1,0:T(8,128)} %refs_2_.1) | copy-start | bytes 196612
  2.3 8.6 %copy-start.10 = (s32[4,512]{1,0:T(4,128)S(1)}, s32[4,512]{1,0:T(4,128)}, u32[]{:S(2)}) copy-start(s32[4,512]{1,0:T(4,128)} %valid_ref.2) | copy-start | bytes 24580
  2.3 8.6 %copy-start.11 = (f32[2,8,128]{2,1,0:T(8,128)S(1)}, f32[2,8,128]{2,1,0:T(8,128)}, u32[]{:S(2)}) copy-start(f32[2,8,128]{2,1,0:T(8,128)} %refs_3_.1) | copy-start | bytes 24580
  2.3 7.9 %collective-permute-start = (bf16[16,2176]{1,0:T(8,128)(2,1)S(1)}, bf16[16,2176]{1,0:T(8,128)(2,1)S(1)}, u32[]{:S(2)}, u32[]{:S(2)}) collective-permute-start(bf16[16,2176]{1,0:T(8,128)(2,1)S(1)} %pack_a.1), channel_id=1, source_target_pairs={{0,16},{1,17},{2,18},{3,19},{4,20},{5,21},{6,22},{7,23},{8,24},{9,... | collective-permute-start | bytes 208904 | tf_op jit(solution)/shard_map/ppermute | solution.py:425
  7.5 18.4 %collective-permute-start.7 = (bf16[1024,256]{1,0:T(8,128)(2,1)S(1)}, bf16[1024,256]{1,0:T(8,128)(2,1)S(1)}, u32[]{:S(2)}, u32[]{:S(2)}) collective-permute-start(bf16[1024,256]{1,0:T(8,128)(2,1)S(1)} %bitcast.3), channel_id=1, source_target_pairs={{0,1},{1,0},{2,3},{3,2},{4,5},{5,4},{6,7},{7,6},{8,9},{9,8},{10,11... | collective-permute-start | bytes 1572872 | tf_op jit(solution)/shard_map/ppermute | solution.py:541
  10.2 5.6 %collective-permute-start.2 = (bf16[32,2176]{1,0:T(8,128)(2,1)S(1)}, bf16[32,2176]{1,0:T(8,128)(2,1)S(1)}, u32[]{:S(2)}, u32[]{:S(2)}) collective-permute-start(bf16[32,2176]{1,0:T(8,128)(2,1)S(1)} %pad_maximum_fusion.9), channel_id=1, source_target_pairs={{0,8},{1,9},{2,10},{3,11},{4,12},{5,13},{6,14},{7,15},{8,0},{9,1},... | collective-permute-start | bytes 417800 | tf_op jit(solution)/shard_map/ppermute | solution.py:425
  11.0 6.6 %collective-permute-start.1 = (bf16[16,1280]{1,0:T(8,128)(2,1)S(1)}, bf16[16,1280]{1,0:T(8,128)(2,1)S(1)}, u32[]{:S(2)}, u32[]{:S(2)}) collective-permute-start(bf16[16,1280]{1,0:T(8,128)(2,1)S(1)} %pack_b.1), channel_id=1, source_target_pairs={{0,16},{1,17},{2,18},{3,19},{4,20},{5,21},{6,22},{7,23},{8,24},{9,... | collective-permute-start | bytes 122888 | tf_op jit(solution)/shard_map/ppermute | solution.py:425
  15.8 6.6 %collective-permute-start.4 = (bf16[64,2176]{1,0:T(8,128)(2,1)S(1)}, bf16[64,2176]{1,0:T(8,128)(2,1)S(1)}, u32[]{:S(2)}, u32[]{:S(2)}) collective-permute-start(bf16[64,2176]{1,0:T(8,128)(2,1)S(1)} %pad_maximum_fusion.6), channel_id=1, source_target_pairs={{0,4},{1,5},{2,3},{3,2},{4,0},{5,1},{6,7},{7,6},{8,12},{9,13},{10,... | collective-permute-start | bytes 835592 | tf_op jit(solution)/shard_map/ppermute | solution.py:425
  17.5 8.3 %copy-start = (bf16[4,512,256]{2,1,0:T(8,128)(2,1)S(1)}, bf16[4,512,256]{2,1,0:T(8,128)(2,1)}, u32[]{:S(2)}) copy-start(bf16[4,512,256]{2,1,0:T(8,128)(2,1)} %in_ref.1) | copy-start | bytes 3145732
  17.6 8.3 %copy-start.12 = (s32[4,512]{1,0:T(4,128)S(1)}, s32[4,512]{1,0:T(4,128)}, u32[]{:S(2)}) copy-start(s32[4,512]{1,0:T(4,128)} %label_ref.1) | copy-start | bytes 24580
  17.6 8.3 %copy-start.13 = (s32[4,512]{1,0:T(4,128)S(1)}, s32[4,512]{1,0:T(4,128)}, u32[]{:S(2)}) copy-start(s32[4,512]{1,0:T(4,128)} %domain_ref.1) | copy-start | bytes 24580
  17.6 4.5 %collective-permute-start.3 = (bf16[32,1280]{1,0:T(8,128)(2,1)S(1)}, bf16[32,1280]{1,0:T(8,128)(2,1)S(1)}, u32[]{:S(2)}, u32[]{:S(2)}) collective-permute-start(bf16[32,1280]{1,0:T(8,128)(2,1)S(1)} %pad_maximum_fusion.11), channel_id=1, source_target_pairs={{0,8},{1,9},{2,10},{3,11},{4,12},{5,13},{6,14},{7,15},{8,0},{9,1},... | collective-permute-start | bytes 245768 | tf_op jit(solution)/shard_map/ppermute | solution.py:425
  22.4 11.4 %collective-permute-start.6 = (bf16[128,2176]{1,0:T(8,128)(2,1)S(1)}, bf16[128,2176]{1,0:T(8,128)(2,1)S(1)}, u32[]{:S(2)}, u32[]{:S(2)}) collective-permute-start(bf16[128,2176]{1,0:T(8,128)(2,1)S(1)} %pad_maximum_fusion.2), channel_id=1, source_target_pairs={{0,1},{1,0},{2,6},{3,7},{4,5},{5,4},{6,2},{7,3},{8,9},{9,8},{10,14... | collective-permute-start | bytes 1671176 | tf_op jit(solution)/shard_map/ppermute | solution.py:425
  24.2 9.5 %collective-permute-start.5 = (bf16[64,1280]{1,0:T(8,128)(2,1)S(1)}, bf16[64,1280]{1,0:T(8,128)(2,1)S(1)}, u32[]{:S(2)}, u32[]{:S(2)}) collective-permute-start(bf16[64,1280]{1,0:T(8,128)(2,1)S(1)} %pad_maximum_fusion.8), channel_id=1, source_target_pairs={{0,4},{1,5},{2,3},{3,2},{4,0},{5,1},{6,7},{7,6},{8,12},{9,13},{10,... | collective-permute-start | bytes 491528 | tf_op jit(solution)/shard_map/ppermute | solution.py:425
  33.8 2.8 %collective-permute-start.9 = (bf16[256,2176]{1,0:T(8,128)(2,1)S(1)}, bf16[256,2176]{1,0:T(8,128)(2,1)S(1)}, u32[]{:S(2)}, u32[]{:S(2)}) collective-permute-start(bf16[256,2176]{1,0:T(8,128)(2,1)S(1)} %constant_dynamic-update-slice_fusion.own_ref), channel_id=1, source_target_pairs={{0,2},{1,3},{2,0},{3,1},{4,6},{5,7},{6,4},{7,5},{8,10},{9,11},{10,... | collective-permute-start | bytes 3342344 | tf_op jit(solution)/shard_map/ppermute | solution.py:425
  34.2 7.1 %collective-permute-start.8 = (bf16[128,1280]{1,0:T(8,128)(2,1)S(1)}, bf16[128,1280]{1,0:T(8,128)(2,1)S(1)}, u32[]{:S(2)}, u32[]{:S(2)}) collective-permute-start(bf16[128,1280]{1,0:T(8,128)(2,1)S(1)} %pad_maximum_fusion.4), channel_id=1, source_target_pairs={{0,1},{1,0},{2,6},{3,7},{4,5},{5,4},{6,2},{7,3},{8,9},{9,8},{10,14... | collective-permute-start | bytes 983048 | tf_op jit(solution)/shard_map/ppermute | solution.py:425
  36.7 6.8 %copy-start.18 = (f32[2,128]{1,0:T(2,128)S(1)}, f32[2,128]{1,0:T(2,128)}, u32[]{:S(2)}) copy-start(f32[2,128]{1,0:T(2,128)} %refs_4_.1) | copy-start | bytes 3076
  41.3 2.2 %collective-permute-start.10 = (bf16[256,1280]{1,0:T(8,128)(2,1)S(1)}, bf16[256,1280]{1,0:T(8,128)(2,1)S(1)}, u32[]{:S(2)}, u32[]{:S(2)}) collective-permute-start(bf16[256,1280]{1,0:T(8,128)(2,1)S(1)} %constant_dynamic-update-slice_fusion.5.own_ref), channel_id=1, source_target_pairs={{0,2},{1,3},{2,0},{3,1},{4,6},{5,7},{6,4},{7,5},{8,10},{9,11},{10,... | collective-permute-start | bytes 1966088 | tf_op jit(solution)/shard_map/ppermute | solution.py:425
  47.8 4.2 %collective-permute-start.11 = (bf16[264,1152]{1,0:T(8,128)(2,1)S(1)}, bf16[264,1152]{1,0:T(8,128)(2,1)S(1)}, u32[]{:S(2)}, u32[]{:S(2)}) collective-permute-start(bf16[264,1152]{1,0:T(8,128)(2,1)S(1)} %pad_maximum_fusion.1), channel_id=1, source_target_pairs={{0,2},{1,3},{2,0},{3,1},{4,6},{5,7},{6,4},{7,5},{8,10},{9,11},{10,... | collective-permute-start | bytes 1824776 | tf_op jit(solution)/shard_map/ppermute | solution.py:425
  51.5 4.3 %collective-permute-start.14 = (bf16[256,1536]{1,0:T(8,128)(2,1)S(1)}, bf16[256,1536]{1,0:T(8,128)(2,1)S(1)}, u32[]{:S(2)}, u32[]{:S(2)}) collective-permute-start(bf16[256,1536]{1,0:T(8,128)(2,1)S(1)} %get-tuple-element.106), channel_id=1, source_target_pairs={{0,2},{1,3},{2,0},{3,1},{4,6},{5,7},{6,4},{7,5},{8,10},{9,11},{10,... | collective-permute-start | bytes 2359304 | tf_op jit(solution)/shard_map/ppermute | solution.py:425
  52.2 7.0 %collective-permute-start.12 = (bf16[136,1152]{1,0:T(8,128)(2,1)S(1)}, bf16[136,1152]{1,0:T(8,128)(2,1)S(1)}, u32[]{:S(2)}, u32[]{:S(2)}) collective-permute-start(bf16[136,1152]{1,0:T(8,128)(2,1)S(1)} %pad_maximum_fusion.5), channel_id=1, source_target_pairs={{0,1},{1,0},{2,6},{3,7},{4,5},{5,4},{6,2},{7,3},{8,9},{9,8},{10,14... | collective-permute-start | bytes 940040 | tf_op jit(solution)/shard_map/ppermute | solution.py:425
  55.7 1.8 %collective-permute-start.13 = (bf16[256,640]{1,0:T(8,128)(2,1)S(1)}, bf16[256,640]{1,0:T(8,128)(2,1)S(1)}, u32[]{:S(2)}, u32[]{:S(2)}) collective-permute-start(bf16[256,640]{1,0:T(8,128)(2,1)S(1)} %get-tuple-element.112), channel_id=1, source_target_pairs={{0,2},{1,3},{2,0},{3,1},{4,6},{5,7},{6,4},{7,5},{8,10},{9,11},{10,... | collective-permute-start | bytes 983048 | tf_op jit(solution)/shard_map/ppermute | solution.py:425
  56.1 11.4 %collective-permute-start.16 = (bf16[128,1536]{1,0:T(8,128)(2,1)S(1)}, bf16[128,1536]{1,0:T(8,128)(2,1)S(1)}, u32[]{:S(2)}, u32[]{:S(2)}) collective-permute-start(bf16[128,1536]{1,0:T(8,128)(2,1)S(1)} %slice.294), channel_id=1, source_target_pairs={{0,1},{1,0},{2,6},{3,7},{4,5},{5,4},{6,2},{7,3},{8,9},{9,8},{10,14... | collective-permute-start | bytes 1179656 | tf_op jit(solution)/shard_map/ppermute | solution.py:425
  59.3 8.2 %collective-permute-start.17 = (bf16[128,640]{1,0:T(8,128)(2,1)S(1)}, bf16[128,640]{1,0:T(8,128)(2,1)S(1)}, u32[]{:S(2)}, u32[]{:S(2)}) collective-permute-start(bf16[128,640]{1,0:T(8,128)(2,1)S(1)} %slice.297), channel_id=1, source_target_pairs={{0,1},{1,0},{2,6},{3,7},{4,5},{5,4},{6,2},{7,3},{8,9},{9,8},{10,14... | collective-permute-start | bytes 491528 | tf_op jit(solution)/shard_map/ppermute | solution.py:425
  61.1 6.4 %collective-permute-start.15 = (bf16[72,1152]{1,0:T(8,128)(2,1)S(1)}, bf16[72,1152]{1,0:T(8,128)(2,1)S(1)}, u32[]{:S(2)}, u32[]{:S(2)}) collective-permute-start(bf16[72,1152]{1,0:T(8,128)(2,1)S(1)} %pad_maximum_fusion.7), channel_id=1, source_target_pairs={{0,4},{1,5},{2,3},{3,2},{4,0},{5,1},{6,7},{7,6},{8,12},{9,13},{10,... | collective-permute-start | bytes 497672 | tf_op jit(solution)/shard_map/ppermute | solution.py:425
  67.7 6.6 %collective-permute-start.19 = (bf16[64,2176]{1,0:T(8,128)(2,1)S(1)}, bf16[64,2176]{1,0:T(8,128)(2,1)S(1)}, u32[]{:S(2)}, u32[]{:S(2)}) collective-permute-start(bf16[64,2176]{1,0:T(8,128)(2,1)S(1)} %slice.296), channel_id=1, source_target_pairs={{0,4},{1,5},{2,3},{3,2},{4,0},{5,1},{6,7},{7,6},{8,12},{9,13},{10,... | collective-permute-start | bytes 835592 | tf_op jit(solution)/shard_map/ppermute | solution.py:425
  69.3 4.6 %collective-permute-start.18 = (bf16[40,1152]{1,0:T(8,128)(2,1)S(1)}, bf16[40,1152]{1,0:T(8,128)(2,1)S(1)}, u32[]{:S(2)}, u32[]{:S(2)}) collective-permute-start(bf16[40,1152]{1,0:T(8,128)(2,1)S(1)} %pad_maximum_fusion.10), channel_id=1, source_target_pairs={{0,8},{1,9},{2,10},{3,11},{4,12},{5,13},{6,14},{7,15},{8,0},{9,1},... | collective-permute-start | bytes 276488 | tf_op jit(solution)/shard_map/ppermute | solution.py:425
  70.5 14.0 %collective-permute-start.21 = (bf16[512,256]{1,0:T(8,128)(2,1)S(1)}, bf16[512,256]{1,0:T(8,128)(2,1)S(1)}, u32[]{:S(2)}, u32[]{:S(2)}) collective-permute-start(bf16[512,256]{1,0:T(8,128)(2,1)S(1)} %get-tuple-element.130), channel_id=1, source_target_pairs={{0,1},{1,0},{2,3},{3,2},{4,5},{5,4},{6,7},{7,6},{8,9},{9,8},{10,11... | collective-permute-start | bytes 786440 | tf_op jit(solution)/shard_map/ppermute | solution.py:541
  74.4 6.5 %collective-permute-start.23 = (bf16[32,2176]{1,0:T(8,128)(2,1)S(1)}, bf16[32,2176]{1,0:T(8,128)(2,1)S(1)}, u32[]{:S(2)}, u32[]{:S(2)}) collective-permute-start(bf16[32,2176]{1,0:T(8,128)(2,1)S(1)} %slice.299), channel_id=1, source_target_pairs={{0,8},{1,9},{2,10},{3,11},{4,12},{5,13},{6,14},{7,15},{8,0},{9,1},... | collective-permute-start | bytes 417800 | tf_op jit(solution)/shard_map/ppermute | solution.py:425
  75.8 5.1 %collective-permute-start.20 = (bf16[24,1152]{1,0:T(8,128)(2,1)S(1)}, bf16[24,1152]{1,0:T(8,128)(2,1)S(1)}, u32[]{:S(2)}, u32[]{:S(2)}) collective-permute-start(bf16[24,1152]{1,0:T(8,128)(2,1)S(1)} %pad_maximum_fusion.12), channel_id=1, source_target_pairs={{0,16},{1,17},{2,18},{3,19},{4,20},{5,21},{6,22},{7,23},{8,24},{9,... | collective-permute-start | bytes 165896 | tf_op jit(solution)/shard_map/ppermute | solution.py:425
  78.3 6.4 %collective-permute-start.22 = (bf16[512,256]{1,0:T(8,128)(2,1)S(1)}, bf16[512,256]{1,0:T(8,128)(2,1)S(1)}, u32[]{:S(2)}, u32[]{:S(2)}) collective-permute-start(bf16[512,256]{1,0:T(8,128)(2,1)S(1)} %get-tuple-element.131), channel_id=1, source_target_pairs={{0,1},{1,0},{2,3},{3,2},{4,5},{5,4},{6,7},{7,6},{8,9},{9,8},{10,11... | collective-permute-start | bytes 786440 | tf_op jit(solution)/shard_map/ppermute | solution.py:541
  81.0 5.3 %collective-permute-start.24 = (bf16[16,2176]{1,0:T(8,128)(2,1)S(1)}, bf16[16,2176]{1,0:T(8,128)(2,1)S(1)}, u32[]{:S(2)}, u32[]{:S(2)}) collective-permute-start(bf16[16,2176]{1,0:T(8,128)(2,1)S(1)} %slice.301), channel_id=1, source_target_pairs={{0,16},{1,17},{2,18},{3,19},{4,20},{5,21},{6,22},{7,23},{8,24},{9,... | collective-permute-start | bytes 208904 | tf_op jit(solution)/shard_map/ppermute | solution.py:425
  84.3 1.9 %copy-start.2 = (f32[16,2048]{1,0:T(8,128)S(1)}, f32[16,2048]{1,0:T(8,128)}, u32[]{:S(2)}) copy-start(f32[16,2048]{1,0:T(8,128)} %refs_0_.1) | copy-start | bytes 393220
  84.3 1.9 %copy-start.4 = (f32[16,2048]{1,0:T(8,128)S(1)}, f32[16,2048]{1,0:T(8,128)}, u32[]{:S(2)}) copy-start(f32[16,2048]{1,0:T(8,128)} %refs_5_.1) | copy-start | bytes 393220
  84.3 1.9 %copy-start.5 = (f32[16,2048]{1,0:T(8,128)S(1)}, f32[16,2048]{1,0:T(8,128)}, u32[]{:S(2)}) copy-start(f32[16,2048]{1,0:T(8,128)} %refs_10_.1) | copy-start | bytes 393220
  84.3 1.9 %copy-start.6 = (f32[8,8,256]{2,1,0:T(8,128)S(1)}, f32[8,8,256]{2,1,0:T(8,128)}, u32[]{:S(2)}) copy-start(f32[8,8,256]{2,1,0:T(8,128)} %refs_7_.1) | copy-start | bytes 196612
  84.3 1.9 %copy-start.7 = (f32[8,8,256]{2,1,0:T(8,128)S(1)}, f32[8,8,256]{2,1,0:T(8,128)}, u32[]{:S(2)}) copy-start(f32[8,8,256]{2,1,0:T(8,128)} %refs_12_.1) | copy-start | bytes 196612
  84.4 1.9 %copy-start.9 = (f32[16,16]{1,0:T(8,128)S(1)}, f32[16,16]{1,0:T(8,128)}, u32[]{:S(2)}) copy-start(f32[16,16]{1,0:T(8,128)} %refs_1_.1) | copy-start | bytes 3076
  84.4 1.9 %copy-start.14 = (f32[16,16]{1,0:T(8,128)S(1)}, f32[16,16]{1,0:T(8,128)}, u32[]{:S(2)}) copy-start(f32[16,16]{1,0:T(8,128)} %refs_6_.1) | copy-start | bytes 3076
  84.4 1.9 %copy-start.15 = (f32[2,8,128]{2,1,0:T(8,128)S(1)}, f32[2,8,128]{2,1,0:T(8,128)}, u32[]{:S(2)}) copy-start(f32[2,8,128]{2,1,0:T(8,128)} %refs_8_.1) | copy-start | bytes 24580
  84.4 1.9 %copy-start.16 = (f32[16,16]{1,0:T(8,128)S(1)}, f32[16,16]{1,0:T(8,128)}, u32[]{:S(2)}) copy-start(f32[16,16]{1,0:T(8,128)} %refs_11_.1) | copy-start | bytes 3076
  84.4 1.9 %copy-start.17 = (f32[2,8,128]{2,1,0:T(8,128)S(1)}, f32[2,8,128]{2,1,0:T(8,128)}, u32[]{:S(2)}) copy-start(f32[2,8,128]{2,1,0:T(8,128)} %refs_13_.1) | copy-start | bytes 24580
  84.4 1.9 %copy-start.19 = (f32[2,128]{1,0:T(2,128)S(1)}, f32[2,128]{1,0:T(2,128)}, u32[]{:S(2)}) copy-start(f32[2,128]{1,0:T(2,128)} %refs_9_.1) | copy-start | bytes 3076
  84.4 1.9 %copy-start.20 = (f32[2,128]{1,0:T(2,128)S(1)}, f32[2,128]{1,0:T(2,128)}, u32[]{:S(2)}) copy-start(f32[2,128]{1,0:T(2,128)} %refs_14_.1) | copy-start | bytes 3076
